TPU v7x, 32 devices: a whole 2x2x4 slice. The times are simulated.
32 devices in a mesh: groups: 1, seq: 16 (over z, y, x), chan: 2 (over core).
Axes of the slice: x: 2, y: 2, z: 4, core: 2. Of those that a mesh axis runs over, the one named last changes fastest.
Arguments:
- q_proj: bfloat16 [4096, 2048], P('chan', ('groups', 'seq')), may hold values from -6 to 6
- k_proj: bfloat16 [4096, 2048], P('chan', ('groups', 'seq')), may hold values from -6 to 6
- value_projection: bfloat16 [4096, 2048], P('chan', ('groups', 'seq')), may hold values from -6 to 6
- residues: float32 [4096, 16], P(('chan', 'seq')), may hold values from -1.5 to 1.5
- rates: float32 [4096, 16], P(('chan', 'seq')), may hold values from 9.765625e-06 to 0.03
- direct_gain: float32 [4096], P('chan'), may hold values from 0.5 to 1.5
Outputs:
- mixed: bfloat16 [4096, 2048], P('chan', ('groups', 'seq'))
All inputs are finite; a program needn't handle non-finite values.
Results may differ from a plain program's by a relative error of at most 0.001.
Values sent between devices are 32-bit elements; how exact they have to be, the bound alone decides.
No kernel may reach another device: no remote copies, remote signals or barrier semaphores. Data moves between devices by JAX's collectives and lax.ppermute only.
A program may use at most 64 MiB of HBM per device.

v0:
```python
import jax
import jax.numpy as jnp
from jax import lax
from jax.sharding import PartitionSpec as P

TOP_PRECISION = lax.Precision.HIGHEST


def conv_local(signal, weights, decay, blk_max, group_maximum):
    channels, length = signal.shape
    blk = min(blk_max, length)
    block_list = length // blk
    group = min(channels, group_maximum)
    positions = jnp.arange(blk).astype(jnp.float32)
    lower = jnp.arange(blk)[:, None] - jnp.arange(blk)[None, :] >= 0
    block_index = jnp.arange(block_list)
    block_gap = block_index[:, None] - 1 - block_index[None, :]
    block_valid = block_gap >= 0
    gap_clipped = jnp.maximum(block_gap, 0).astype(jnp.float32)
    trailing_distance = (block_list - 1 - block_index).astype(jnp.float32)

    def one_group(pieces):
        values, weight_matrix, rate = pieces
        series = values.reshape(group, block_list, blk)
        decay_powers = jnp.exp(-rate[:, :, None] * positions[None, None, :])
        rising = jnp.exp(rate[:, :, None] * positions[None, None, :])
        scaled = weight_matrix[:, :, None] * decay_powers
        toeplitz = jnp.einsum("gri,grj->gij", scaled, rising, precision=TOP_PRECISION)
        toeplitz = jnp.where(lower[None], toeplitz, 0.0)
        inner = jnp.einsum("gij,gnj->gni", toeplitz, series, precision=TOP_PRECISION)
        ends = jnp.exp(-rate[:, :, None] * (blk - 1.0 - positions)[None, None, :])
        per_block_state = jnp.einsum("grj,gnj->gnr", ends, series, precision=TOP_PRECISION)
        span_rate = rate * blk
        linked_recurrence = jnp.where(
            block_valid[None, None],
            jnp.exp(-span_rate[:, :, None, None] * gap_clipped[None, None]),
            0.0,
        )
        carry_state = jnp.einsum(
            "pikz,pzi->pki", linked_recurrence, per_block_state, precision=TOP_PRECISION
        )
        trailing_weight = jnp.exp(-span_rate[:, :, None] * trailing_distance[None, None, :])
        last_output = jnp.einsum(
            "jpw,jwp->jp", trailing_weight, per_block_state, precision=TOP_PRECISION
        )
        reach = scaled * jnp.exp(-rate)[:, :, None]
        outer = jnp.einsum("gri,gnr->gni", reach, carry_state, precision=TOP_PRECISION)
        return ((inner + outer).reshape(group, length), last_output)

    result, last_output = lax.map(
        one_group,
        (
            signal.reshape(channels // group, group, length),
            weights.reshape(channels // group, group, -1),
            decay.reshape(channels // group, group, -1),
        ),
    )
    return (result.reshape(channels, length), last_output.reshape(channels, -1))


def shards(q_proj, k_proj, value_projection, residues, rates, direct_gain):
    gated = k_proj.astype(jnp.float32) * value_projection.astype(jnp.float32)
    weights = residues * jnp.sqrt(-jnp.expm1(-2.0 * rates))
    columns = lax.all_to_all(gated, "seq", split_axis=0, concat_axis=1, tiled=True)
    conv_cols, _ = conv_local(columns, weights, rates, 256, 32)
    conv = lax.all_to_all(conv_cols, "seq", split_axis=1, concat_axis=0, tiled=True)
    mixed = q_proj.astype(jnp.float32) * (conv + direct_gain[:, None] * gated)
    return mixed.astype(jnp.bfloat16)


def solution(mesh):
    return jax.shard_map(
        shards,
        mesh=mesh,
        in_specs=(
            P("chan", ("groups", "seq")),
            P("chan", ("groups", "seq")),
            P("chan", ("groups", "seq")),
            P(("chan", "seq"), None),
            P(("chan", "seq"), None),
            P("chan"),
        ),
        out_specs=P("chan", ("groups", "seq")),
        check_vma=False,
    )
```

profile of v0, /device:TPU:2, one launch (start us, length us, event | category | flops | bytes accessed | tf_op | source)
XLA Modules:
  0.0 136.6 jit_solution(14871511168569307633)
XLA Ops:
  0.0 2.3 %convert_multiply_fusion = f32[2048,128]{1,0:T(8,128)} fusion(bf16[2048,128]{1,0:T(8,128)(2,1)} %param.10, bf16[2048,128]{1,0:T(8,128)(2,1)} %param.9), kind=kLoop, calls=%fused_computation.44 | loop fusion | flops 786432 | bytes 2097152 | tf_op jit(solution)/shard_map/mul | solution.py:62
  2.3 7.3 %all-to-all-start = ((f32[16,128,128]{2,1,0:T(8,128)}), f32[16,128,128]{2,1,0:T(8,128)S(1)}, u32[]{:S(2)}, u32[]{:S(2)}) async-start(f32[16,128,128]{2,1,0:T(8,128)} %bitcast.2), calls=%async_computation | async-start | bytes 2097152 | tf_op jit(solution)/shard_map/all_to_all | solution.py:64
  9.6 0.8 reshape.61
  10.4 0.7 sqrt_multiply_fusion
  11.3 21.4 %all-to-all-done = f32[16,128,128]{2,1,0:T(8,128)S(1)} async-done(((f32[16,128,128]{2,1,0:T(8,128)}), f32[16,128,128]{2,1,0:T(8,128)S(1)}, u32[]{:S(2)}, u32[]{:S(2)}) %all-to-all-start) | async-done | bytes 1048608 | tf_op jit(solution)/shard_map/all_to_all | solution.py:64
  33.5 69.5 %while.13 = (s32[]{:T(128)}, f32[4,32,2048]{2,1,0:T(8,128)}, f32[4,32,2048]{2,1,0:T(8,128)S(1)}, f32[4,32,16]{2,1,0:T(8,128)S(1)}, f32[4,32,16]{1,0,2:T(4,128)S(1)}, /*index=5*/s32[8]{0:T(128)S(1)}, s32[]{:T(128)}) while((s32[]{:T(128)}, f32[4,32,2048]{2,1,0:T(8,128)}, f32[4,32,2048]{2,1,0:T(8,128)S(1)}, ...), condition=%wide.region_1.2_spmd.clone.clone.clone, body=%wide.region_0.1_spmd.clone.clone.clone.sunk | while | flops 632486464 | bytes 20498712 | solution.py:50
  33.7 7.1 %fusion.52 = f32[32,256,256]{2,1,0:T(8,128)S(1)} fusion(f32[32,16]{1,0:T(8,128)S(1)} %copy.44, f32[256]{0:T(256)S(1)} %iota_convert_fusion.2, f32[32,16]{1,0:T(8,128)S(1)} %copy.45, f32[32,16]{1,0:T(8,128)S(1)} %dynamic-slice_bitcast_fusion.2), kind=kOutput, calls=%fused_computation.14.clone.1 | convolution fusion | flops 403046400 | bytes 8395776 | tf_op jit(solution)/shard_map/while/body/eval_jaxpr/gri,grj->gij/dot_general | solution.py:28
  41.0 7.1 %fusion.53 = f32[32,8,256]{2,1,0:T(8,128)S(1)} fusion(f32[32,8,256]{2,1,0:T(8,128)S(1)} %bitcast.49, f32[32,256,256]{2,1,0:T(8,128)S(1)} %fusion.52, pred[256,256]{1,0:T(8,128)(4,1)S(1)} %subtract_compare_fusion.2), kind=kOutput, calls=%fused_computation.4.clone.1 | convolution fusion | flops 203423744 | bytes 8978432 | tf_op jit(solution)/shard_map/while/body/eval_jaxpr/gij,gnj->gni/dot_general | solution.py:30
  48.1 0.7 convolution_bitcast_fusion.2
  50.2 0.7 constant_dynamic-update-slice_fusion.2
  51.1 7.1 %fusion.52 = f32[32,256,256]{2,1,0:T(8,128)S(1)} fusion(f32[32,16]{1,0:T(8,128)S(1)} %copy.44, f32[256]{0:T(256)S(1)} %iota_convert_fusion.2, f32[32,16]{1,0:T(8,128)S(1)} %copy.45, f32[32,16]{1,0:T(8,128)S(1)} %dynamic-slice_bitcast_fusion.2), kind=kOutput, calls=%fused_computation.14.clone.1 | convolution fusion | flops 403046400 | bytes 8395776 | tf_op jit(solution)/shard_map/while/body/eval_jaxpr/gri,grj->gij/dot_general | solution.py:28
  58.4 7.1 %fusion.53 = f32[32,8,256]{2,1,0:T(8,128)S(1)} fusion(f32[32,8,256]{2,1,0:T(8,128)S(1)} %bitcast.49, f32[32,256,256]{2,1,0:T(8,128)S(1)} %fusion.52, pred[256,256]{1,0:T(8,128)(4,1)S(1)} %subtract_compare_fusion.2), kind=kOutput, calls=%fused_computation.4.clone.1 | convolution fusion | flops 203423744 | bytes 8978432 | tf_op jit(solution)/shard_map/while/body/eval_jaxpr/gij,gnj->gni/dot_general | solution.py:30
  65.5 0.7 convolution_bitcast_fusion.2
  67.6 0.7 constant_dynamic-update-slice_fusion.2
  68.5 7.1 %fusion.52 = f32[32,256,256]{2,1,0:T(8,128)S(1)} fusion(f32[32,16]{1,0:T(8,128)S(1)} %copy.44, f32[256]{0:T(256)S(1)} %iota_convert_fusion.2, f32[32,16]{1,0:T(8,128)S(1)} %copy.45, f32[32,16]{1,0:T(8,128)S(1)} %dynamic-slice_bitcast_fusion.2), kind=kOutput, calls=%fused_computation.14.clone.1 | convolution fusion | flops 403046400 | bytes 8395776 | tf_op jit(solution)/shard_map/while/body/eval_jaxpr/gri,grj->gij/dot_general | solution.py:28
  75.8 7.1 %fusion.53 = f32[32,8,256]{2,1,0:T(8,128)S(1)} fusion(f32[32,8,256]{2,1,0:T(8,128)S(1)} %bitcast.49, f32[32,256,256]{2,1,0:T(8,128)S(1)} %fusion.52, pred[256,256]{1,0:T(8,128)(4,1)S(1)} %subtract_compare_fusion.2), kind=kOutput, calls=%fused_computation.4.clone.1 | convolution fusion | flops 203423744 | bytes 8978432 | tf_op jit(solution)/shard_map/while/body/eval_jaxpr/gij,gnj->gni/dot_general | solution.py:30
  82.9 0.7 convolution_bitcast_fusion.2
  85.0 0.7 constant_dynamic-update-slice_fusion.2
  85.9 7.1 %fusion.52 = f32[32,256,256]{2,1,0:T(8,128)S(1)} fusion(f32[32,16]{1,0:T(8,128)S(1)} %copy.44, f32[256]{0:T(256)S(1)} %iota_convert_fusion.2, f32[32,16]{1,0:T(8,128)S(1)} %copy.45, f32[32,16]{1,0:T(8,128)S(1)} %dynamic-slice_bitcast_fusion.2), kind=kOutput, calls=%fused_computation.14.clone.1 | convolution fusion | flops 403046400 | bytes 8395776 | tf_op jit(solution)/shard_map/while/body/eval_jaxpr/gri,grj->gij/dot_general | solution.py:28
  93.1 7.1 %fusion.53 = f32[32,8,256]{2,1,0:T(8,128)S(1)} fusion(f32[32,8,256]{2,1,0:T(8,128)S(1)} %bitcast.49, f32[32,256,256]{2,1,0:T(8,128)S(1)} %fusion.52, pred[256,256]{1,0:T(8,128)(4,1)S(1)} %subtract_compare_fusion.2), kind=kOutput, calls=%fused_computation.4.clone.1 | convolution fusion | flops 203423744 | bytes 8978432 | tf_op jit(solution)/shard_map/while/body/eval_jaxpr/gij,gnj->gni/dot_general | solution.py:30
  102.3 0.7 constant_dynamic-update-slice_fusion.2
  103.1 1.4 %copy.36 = f32[16,8,16,128]{3,2,1,0:T(8,128)S(1)} copy(f32[16,8,16,128]{3,1,2,0:T(8,128)} %bitcast.56) | data formatting | bytes 2097152
  104.8 30.6 %all_to_all.35 = f32[128,16,128]{2,0,1:T(8,128)S(1)} all-to-all(f32[128,16,128]{2,0,1:T(8,128)S(1)} %copy.23), channel_id=1, replica_groups=mesh['groups'=1,'seq'=16,'chan'=2] {'seq'}, dimensions={1} | all-to-all | bytes 2097152 | tf_op jit(solution)/shard_map/all_to_all | solution.py:66
  135.4 1.1 fusion.31
  (87 shorter events, 8.7 us)
Async XLA Ops:
  2.3 30.4 %all-to-all-start = ((f32[16,128,128]{2,1,0:T(8,128)}), f32[16,128,128]{2,1,0:T(8,128)S(1)}, u32[]{:S(2)}, u32[]{:S(2)}) async-start(f32[16,128,128]{2,1,0:T(8,128)} %bitcast.2), calls=%async_computation | async-start | bytes 2097152 | tf_op jit(solution)/shard_map/all_to_all | solution.py:64
  33.5 101.9 %copy-start = (bf16[2048,128]{1,0:T(8,128)(2,1)S(1)}, bf16[2048,128]{1,0:T(8,128)(2,1)}, u32[]{:S(2)}) copy-start(bf16[2048,128]{1,0:T(8,128)(2,1)} %param.10) | copy-start | bytes 1572868
  33.5 101.9 %copy-start.1 = (bf16[2048,128]{1,0:T(8,128)(2,1)S(1)}, bf16[2048,128]{1,0:T(8,128)(2,1)}, u32[]{:S(2)}) copy-start(bf16[2048,128]{1,0:T(8,128)(2,1)} %param.9) | copy-start | bytes 1572868
  33.5 101.9 %copy-start.2 = (bf16[2048,128]{1,0:T(8,128)(2,1)S(1)}, bf16[2048,128]{1,0:T(8,128)(2,1)}, u32[]{:S(2)}) copy-start(bf16[2048,128]{1,0:T(8,128)(2,1)} %param.8) | copy-start | bytes 1572868
  33.5 101.9 %copy-start.3 = (f32[2048]{0:T(1024)S(1)}, f32[2048]{0:T(1024)}, u32[]{:S(2)}) copy-start(f32[2048]{0:T(1024)} %param.13) | copy-start | bytes 24580
where the time goes:
time: 139 us; the launch traced here: 137 us
  matrix products  61.8 us (44%)
  blocking collectives  30.6 us (22%)
  waiting for transfers between devices  21.4 us (15%)
  local copies, waits for them, and re-layouts  8.79 us (6%)
  starting transfers between devices  7.31 us (5%)
  other arithmetic  6.22 us (4%)
    all_to_all x1, blocking collectives, shards(): lax.all_to_all(conv_cols, 'seq', split_axis=1, concat_axis=0, tiled=True)  30.6 us
    dot_general x4, matrix products, one_group(): jnp.einsum('gij,gnj->gni', toeplitz, series, precision=TOP_PRECISION)  28.5 us
    dot_general x4, matrix products, one_group(): jnp.einsum('gri,grj->gij', scaled, rising, precision=TOP_PRECISION)  28.3 us
    all_to_all x1, waiting for transfers between devices, shards(): lax.all_to_all(gated, 'seq', split_axis=0, concat_axis=1, tiled=True)  21.4 us
    all_to_all x1, starting transfers between devices, shards(): lax.all_to_all(gated, 'seq', split_axis=0, concat_axis=1, tiled=True)  7.31 us
    dynamic_update_slice x4, local copies, waits for them, and re-layouts, conv_local(): lax.map(one_group, (signal.reshape(channels // group, group, length), wei...  2.89 us
  transfers between devices with their start and end apart: 1, of which 1 were waited for; matrix products, arithmetic and copies ran while one was open for 1% of the time, Pallas kernels for 0%

commit v1 on v0

v1 whole, which is shorter than its diff:
```python
import functools
import jax
import jax.numpy as jnp
from jax import lax
from jax.experimental import pallas as pl
from jax.experimental.pallas import tpu as pltpu
from jax.sharding import PartitionSpec as P

LANES = 128
SUBLANES = 8
UNROLL = 8
VMEM_LIMIT = 32 * 1024 * 1024


def prepare_kernel(chunks, k_ref, v_ref, series_ref):
    length = k_ref.shape[1]
    for chunk in range(chunks):
        rows = pl.ds(chunk * LANES, LANES)
        gated = k_ref[rows, :].astype(jnp.float32) * v_ref[rows, :].astype(jnp.float32)
        series_ref[pl.ds(chunk, length, stride=chunks), :] = gated.T


def mode_rows(ref, base, order, per_chunk, chunks, half):
    first = half * SUBLANES * per_chunk + base
    return [ref[pl.ds(first + r, SUBLANES, stride=per_chunk), :] for r in range(order)]


def state_kernel(chunks, order, params_ref, series_ref, state_ref):
    length = series_ref.shape[0] // chunks
    for half in range(chunks // SUBLANES):
        decay = [jnp.exp(-rate) for rate in mode_rows(params_ref, 0, order, 2 * order, chunks, half)]

        def steps(i, state):
            state = list(state)
            for u in range(UNROLL):
                row = pl.multiple_of((i * UNROLL + u) * chunks + half * SUBLANES, SUBLANES)
                x = series_ref[pl.ds(row, SUBLANES), :]
                for r in range(order):
                    state[r] = decay[r] * state[r] + x
            return tuple(state)

        zero = jnp.zeros((SUBLANES, LANES), jnp.float32)
        state = lax.fori_loop(0, length // UNROLL, steps, (zero,) * order)
        for r in range(order):
            state_ref[pl.ds(half * SUBLANES * order + r, SUBLANES, stride=order), :] = state[r]


def prefix_kernel(length, rate_ref, ends_ref, starts_ref):
    span_decay = jnp.exp(-float(length) * rate_ref[...])
    carry = jnp.zeros(rate_ref.shape, jnp.float32)
    for block in range(ends_ref.shape[0]):
        starts_ref[block] = carry
        carry = span_decay * carry + ends_ref[block]


def tree_sum(terms):
    terms = list(terms)
    while len(terms) > 1:
        terms = [terms[i] + terms[i + 1] if i + 1 < len(terms) else terms[i] for i in range(0, len(terms), 2)]
    return terms[0]


def output_kernel(chunks, order, params_ref, series_ref, carry_ref, gain_ref, q_ref, out_ref, conv_ref):
    length = series_ref.shape[0] // chunks
    for half in range(chunks // SUBLANES):
        decay = [jnp.exp(-rate) for rate in mode_rows(params_ref, 0, order, 2 * order, chunks, half)]
        weight = mode_rows(params_ref, order, order, 2 * order, chunks, half)
        carry = mode_rows(carry_ref, 0, order, order, chunks, half)
        gain = gain_ref[pl.ds(half * SUBLANES, SUBLANES), :]

        def steps(i, state):
            state = list(state)
            for u in range(UNROLL):
                row = pl.multiple_of((i * UNROLL + u) * chunks + half * SUBLANES, SUBLANES)
                x = series_ref[pl.ds(row, SUBLANES), :]
                for r in range(order):
                    state[r] = decay[r] * state[r] + x
                terms = [weight[r] * state[r] for r in range(order)]
                conv_ref[pl.ds(row, SUBLANES), :] = tree_sum(terms + [gain * x])
            return tuple(state)

        lax.fori_loop(0, length // UNROLL, steps, tuple(carry))
    for chunk in range(chunks):
        rows = pl.ds(chunk * LANES, LANES)
        conv = conv_ref[pl.ds(chunk, length, stride=chunks), :].T
        out_ref[rows, :] = (q_ref[rows, :].astype(jnp.float32) * conv).astype(jnp.bfloat16)


def call(kernel, out_shape, *args, scratch=(), flops=0):
    in_bytes = sum(a.size * a.dtype.itemsize for a in args)
    vmem = pl.BlockSpec(memory_space=pltpu.VMEM)
    return pl.pallas_call(
        kernel,
        out_shape=out_shape,
        in_specs=[vmem] * len(args),
        out_specs=vmem,
        scratch_shapes=list(scratch),
        compiler_params=pltpu.CompilerParams(vmem_limit_bytes=VMEM_LIMIT),
        cost_estimate=pl.CostEstimate(flops=flops, bytes_accessed=in_bytes, transcendentals=0),
    )(*args)


def to_chunks(pieces):
    owners, rows, own = pieces.shape
    if own == LANES:
        return pieces
    if own < LANES:
        group = LANES // own
        return pieces.reshape(owners // group, group, rows, own).swapaxes(1, 2).reshape(-1, rows, LANES)
    return pieces.reshape(owners, rows, own // LANES, LANES).swapaxes(1, 2).reshape(-1, rows, LANES)


def from_chunks(pieces, owners):
    chunks, rows, _ = pieces.shape
    own = chunks * LANES // owners
    if own == LANES:
        return pieces
    if own < LANES:
        group = LANES // own
        return pieces.reshape(chunks, rows, group, own).swapaxes(1, 2).reshape(owners, rows, own)
    return pieces.reshape(owners, own // LANES, rows, LANES).swapaxes(1, 2).reshape(owners, rows, own)


def shards(blocks, q_proj, k_proj, value_projection, residues, rates, direct_gain):
    channels, length = q_proj.shape
    order = residues.shape[1]
    chunks = channels // LANES
    f32 = jnp.float32

    weights = residues * jnp.sqrt(-jnp.expm1(-2.0 * rates))
    own_rates = rates.T
    packed = jnp.concatenate([own_rates, weights.T], axis=0)
    gathered = lax.all_gather(packed, "seq", axis=0)
    params = to_chunks(gathered).reshape(chunks * 2 * order, LANES)

    series = call(
        functools.partial(prepare_kernel, chunks),
        jax.ShapeDtypeStruct((length * chunks, LANES), f32),
        k_proj,
        value_projection,
        flops=channels * length,
    )
    ends = call(
        functools.partial(state_kernel, chunks, order),
        jax.ShapeDtypeStruct((chunks * order, LANES), f32),
        params,
        series,
        flops=2 * order * channels * length,
    )
    ends = from_chunks(ends.reshape(chunks, order, LANES), blocks)
    ends = lax.all_to_all(ends, "seq", split_axis=0, concat_axis=0, tiled=True)
    starts = call(
        functools.partial(prefix_kernel, length),
        jax.ShapeDtypeStruct(ends.shape, f32),
        own_rates,
        ends,
    )
    starts = lax.all_to_all(starts, "seq", split_axis=0, concat_axis=0, tiled=True)
    carry = to_chunks(starts).reshape(chunks * order, LANES)
    return call(
        functools.partial(output_kernel, chunks, order),
        jax.ShapeDtypeStruct((channels, length), jnp.bfloat16),
        params,
        series,
        carry,
        direct_gain.reshape(chunks, LANES),
        q_proj,
        scratch=[pltpu.VMEM((length * chunks, LANES), f32)],
        flops=4 * order * channels * length,
    )


def solution(mesh):
    return jax.shard_map(
        functools.partial(shards, mesh.shape["seq"]),
        mesh=mesh,
        in_specs=(
            P("chan", ("groups", "seq")),
            P("chan", ("groups", "seq")),
            P("chan", ("groups", "seq")),
            P(("chan", "seq"), None),
            P(("chan", "seq"), None),
            P("chan"),
        ),
        out_specs=P("chan", ("groups", "seq")),
        check_vma=False,
    )
```

time: 139 us -> 74.5 us (0.54)
  the two profiles are of different devices: /device:TPU:2 before, /device:TPU:0 now
where the time goes in v1:
time: 74.5 us; the launch traced here: 74.1 us
  blocking collectives  65.7 us (88%)
  Pallas kernels  5.47 us (7%)
  local copies, waits for them, and re-layouts  2.1 us (3%)
  other arithmetic  0.79 us (1%)
    all_gather x1, blocking collectives, shards(): gathered = lax.all_gather(packed, 'seq', axis=0)  43.8 us
    all_to_all x1, blocking collectives, shards(): lax.all_to_all(starts, 'seq', split_axis=0, concat_axis=0, tiled=True)  11.4 us
    all_to_all x1, blocking collectives, shards(): ends = lax.all_to_all(ends, 'seq', split_axis=0, concat_axis=0, tiled=True)  10.5 us
    pallas_call x4, Pallas kernels, call(): pl.pallas_call(kernel, out_shape=out_shape, in_specs=[vmem] * len(args),...  5.47 us
    unnamed x10, local copies, waits for them, and re-layouts  2.1 us

profile of v1, /device:TPU:0, one launch (start us, length us, event | category | flops | bytes accessed | tf_op | source)
XLA Modules:
  0.0 74.1 jit_solution(8187422257172893119)
XLA Ops:
  0.0 0.0 copy-start.3
  0.0 0.8 %multiply_bitcast_fusion = f32[16,128]{1,0:T(8,128)S(1)} fusion(f32[128,16]{0,1:T(8,128)} %param.9, f32[128,16]{0,1:T(8,128)} %param.10), kind=kLoop, calls=%fused_computation.1 | loop fusion | flops 6144 | bytes 24576 | tf_op jit(solution)/shard_map/transpose | solution.py:132
  0.8 0.0 copy-done.3
  0.8 43.8 %all-gather.params_ref = f32[512,128]{1,0:T(8,128)S(1)} all-gather(f32[32,128]{1,0:T(8,128)S(1)} %pad_maximum_fusion), channel_id=2, replica_groups=mesh['groups'=1,'seq'=16,'chan'=2] {'seq'}, dimensions={0}, use_global_device_ids=true | all-gather | bytes 278528 | tf_op jit(solution)/shard_map/all_gather | solution.py:133
  44.6 0.0 copy-start.1
  44.6 1.0 %copy-done.1 = bf16[2048,128]{1,0:T(8,128)(2,1)S(1)} copy-done((bf16[2048,128]{1,0:T(8,128)(2,1)S(1)}, bf16[2048,128]{1,0:T(8,128)(2,1)}, u32[]{:S(2)}) %copy-start.1) | copy-done | bytes 524312
  45.6 0.0 copy-start.2
  45.6 1.0 %copy-done.2 = bf16[2048,128]{1,0:T(8,128)(2,1)S(1)} copy-done((bf16[2048,128]{1,0:T(8,128)(2,1)S(1)}, bf16[2048,128]{1,0:T(8,128)(2,1)}, u32[]{:S(2)}) %copy-start.2) | copy-done | bytes 524312
  46.7 0.4 shard_map.64.series_ref
  47.1 1.3 %shard_map.65 = f32[256,128]{1,0:T(8,128)S(1)} custom-call(f32[512,128]{1,0:T(8,128)S(1)} %all-gather.params_ref, f32[2048,128]{1,0:T(8,128)S(1)} %shard_map.64.series_ref), custom_call_target="tpu_custom_call" | custom-call | flops 8388608 | bytes 1310720 | tf_op jit(solution)/shard_map/pallas_call | solution.py:92
  48.4 0.0 copy-start
  48.4 10.5 %all_to_all.10.ends_ref = f32[16,16,128]{2,1,0:T(8,128)S(1)} all-to-all(f32[16,16,128]{2,1,0:T(8,128)S(1)} %bitcast.7), channel_id=1, replica_groups=mesh['groups'=1,'seq'=16,'chan'=2] {'seq'}, dimensions={0} | all-to-all | bytes 262144 | tf_op jit(solution)/shard_map/all_to_all | solution.py:151
  59.0 0.0 copy-start.4
  59.0 11.4 %all_to_all.11 = f32[16,16,128]{2,1,0:T(8,128)S(1)} all-to-all(f32[16,16,128]{2,1,0:T(8,128)S(1)} %shard_map.66), channel_id=1, replica_groups=mesh['groups'=1,'seq'=16,'chan'=2] {'seq'}, dimensions={0} | all-to-all | bytes 262144 | tf_op jit(solution)/shard_map/all_to_all | solution.py:158
  70.4 0.0 copy-done
  70.4 0.0 copy-done.4
  70.4 3.7 %shard_map.67 = bf16[2048,128]{1,0:T(8,128)(2,1)} custom-call(f32[512,128]{1,0:T(8,128)S(1)} %all-gather.params_ref, f32[2048,128]{1,0:T(8,128)S(1)} %shard_map.64.series_ref, f32[256,128]{1,0:T(8,128)S(1)} %bitcast.6, f32[16,128]{1,0:T(8,128)S(1)} %bitcast.10, bf16[2048,128]{1,0:T(8,128)(2,1)S(1)} %copy-done), custom_call_target="tpu_custom_call" | custom-call | flops 16777216 | bytes 1974272 | tf_op jit(solution)/shard_map/pallas_call | solution.py:92
  (2 shorter events, 0.0 us)
Async XLA Ops:
  0.0 0.8 %copy-start.3 = (f32[128,16]{0,1:T(8,128)S(1)}, f32[128,16]{0,1:T(8,128)}, u32[]{:S(2)}) copy-start(f32[128,16]{0,1:T(8,128)} %param.10) | copy-start | bytes 24580
  44.6 1.0 %copy-start.1 = (bf16[2048,128]{1,0:T(8,128)(2,1)S(1)}, bf16[2048,128]{1,0:T(8,128)(2,1)}, u32[]{:S(2)}) copy-start(bf16[2048,128]{1,0:T(8,128)(2,1)} %k_ref.1) | copy-start | bytes 1572868
  45.6 1.0 %copy-start.2 = (bf16[2048,128]{1,0:T(8,128)(2,1)S(1)}, bf16[2048,128]{1,0:T(8,128)(2,1)}, u32[]{:S(2)}) copy-start(bf16[2048,128]{1,0:T(8,128)(2,1)} %v_ref.1) | copy-start | bytes 1572868
  48.4 22.0 %copy-start = (bf16[2048,128]{1,0:T(8,128)(2,1)S(1)}, bf16[2048,128]{1,0:T(8,128)(2,1)}, u32[]{:S(2)}) copy-start(bf16[2048,128]{1,0:T(8,128)(2,1)} %q_ref.1) | copy-start | bytes 1572868
  59.0 11.4 %copy-start.4 = (f32[2048]{0:T(1024)S(1)}, f32[2048]{0:T(1024)}, u32[]{:S(2)}) copy-start(f32[2048]{0:T(1024)} %param.11) | copy-start | bytes 24580

commit v2 on v1

--- a/solution.py
+++ b/solution.py
@@ -9,6 +9,7 @@
 LANES = 128
 SUBLANES = 8
 UNROLL = 8
+MOST_PERMUTES = 16
 VMEM_LIMIT = 32 * 1024 * 1024
 
 
@@ -25,8 +26,14 @@
     return [ref[pl.ds(first + r, SUBLANES, stride=per_chunk), :] for r in range(order)]
 
 
-def state_kernel(chunks, order, params_ref, series_ref, state_ref):
+def state_kernel(chunks, order, pieces, *refs):
+    piece_refs, (series_ref, params_ref, state_ref) = refs[:pieces], refs[pieces:]
     length = series_ref.shape[0] // chunks
+    rows = piece_refs[0].shape[0]
+    me = lax.axis_index("seq") if pieces > 1 else 0
+    for shift, piece_ref in enumerate(piece_refs):
+        owner = lax.rem(me + pieces - shift, pieces)
+        params_ref[pl.ds(pl.multiple_of(owner * rows, SUBLANES), rows), :] = piece_ref[...]
     for half in range(chunks // SUBLANES):
         decay = [jnp.exp(-rate) for rate in mode_rows(params_ref, 0, order, 2 * order, chunks, half)]
 
@@ -93,7 +100,7 @@
         kernel,
         out_shape=out_shape,
         in_specs=[vmem] * len(args),
-        out_specs=vmem,
+        out_specs=jax.tree.map(lambda _: vmem, out_shape),
         scratch_shapes=list(scratch),
         compiler_params=pltpu.CompilerParams(vmem_limit_bytes=VMEM_LIMIT),
         cost_estimate=pl.CostEstimate(flops=flops, bytes_accessed=in_bytes, transcendentals=0),
@@ -130,8 +137,14 @@
     weights = residues * jnp.sqrt(-jnp.expm1(-2.0 * rates))
     own_rates = rates.T
     packed = jnp.concatenate([own_rates, weights.T], axis=0)
-    gathered = lax.all_gather(packed, "seq", axis=0)
-    params = to_chunks(gathered).reshape(chunks * 2 * order, LANES)
+    if blocks <= MOST_PERMUTES and blocks == chunks:
+        pieces = [packed]
+        for shift in range(1, blocks):
+            pairs = [(i, (i + shift) % blocks) for i in range(blocks)]
+            pieces.append(lax.ppermute(packed, "seq", pairs))
+    else:
+        gathered = lax.all_gather(packed, "seq", axis=0)
+        pieces = [to_chunks(gathered).reshape(chunks * 2 * order, LANES)]
 
     series = call(
         functools.partial(prepare_kernel, chunks),
@@ -140,10 +153,13 @@
         value_projection,
         flops=channels * length,
     )
-    ends = call(
-        functools.partial(state_kernel, chunks, order),
-        jax.ShapeDtypeStruct((chunks * order, LANES), f32),
-        params,
+    params, ends = call(
+        functools.partial(state_kernel, chunks, order, len(pieces)),
+        (
+            jax.ShapeDtypeStruct((chunks * 2 * order, LANES), f32),
+            jax.ShapeDtypeStruct((chunks * order, LANES), f32),
+        ),
+        *pieces,
         series,
         flops=2 * order * channels * length,
     )

time: 74.5 us -> 62.6 us (0.84)
  blocking collectives: 65.7 us -> 21.2 us
  starting transfers between devices: 0 us -> 27.6 us
  waiting for transfers between devices: 0 us -> 4.85 us
    all_gather x1 -> x0, blocking collectives: 43.8 us -> none  [shards(): gathered = lax.all_gather(packed, 'seq', axis=0)]
    ppermute x0 -> x15, starting transfers between devices: none -> 27.6 us  [shards(): pieces.append(lax.ppermute(packed, 'seq', pairs))]
    ppermute x0 -> x15, waiting for transfers between devices: none -> 4.85 us  [shards(): pieces.append(lax.ppermute(packed, 'seq', pairs))]
    all_to_all x1, blocking collectives: 11.4 us -> 10.4 us  [shards(): lax.all_to_all(starts, 'seq', split_axis=0, concat_axis=0, tiled=True)]
  transfers between devices with their start and end apart: 0 -> 15, of which waited for: 0 -> 3; matrix products, arithmetic and copies ran while one was open for 0% -> 0% of each run, Pallas kernels for 0% -> 1%
where the time goes in v2:
time: 62.6 us; the launch traced here: 62.2 us
  starting transfers between devices  27.6 us (44%)
  blocking collectives  21.2 us (34%)
  Pallas kernels  5.58 us (9%)
  waiting for transfers between devices  4.85 us (8%)
  local copies, waits for them, and re-layouts  2.1 us (3%)
  other arithmetic  0.79 us (1%)
    ppermute x15, starting transfers between devices, shards(): pieces.append(lax.ppermute(packed, 'seq', pairs))  27.6 us
    all_to_all x1, blocking collectives, shards(): ends = lax.all_to_all(ends, 'seq', split_axis=0, concat_axis=0, tiled=True)  10.8 us
    all_to_all x1, blocking collectives, shards(): lax.all_to_all(starts, 'seq', split_axis=0, concat_axis=0, tiled=True)  10.4 us
    pallas_call x4, Pallas kernels, call(): pl.pallas_call(kernel, out_shape=out_shape, in_specs=[vmem] * len(args),...  5.58 us
    ppermute x15, waiting for transfers between devices, shards(): pieces.append(lax.ppermute(packed, 'seq', pairs))  4.85 us
    unnamed x10, local copies, waits for them, and re-layouts  2.1 us
  transfers between devices with their start and end apart: 15, of which 3 were waited for; matrix products, arithmetic and copies ran while one was open for 0% of the time, Pallas kernels for 1%

profile of v2, /device:TPU:0, one launch (start us, length us, event | category | flops | bytes accessed | tf_op | source)
XLA Modules:
  0.0 62.2 jit_solution(6193427624978616168)
XLA Ops:
  0.0 0.8 %multiply_bitcast_fusion = f32[16,128]{1,0:T(8,128)S(1)} fusion(f32[128,16]{0,1:T(8,128)} %param.9, f32[128,16]{0,1:T(8,128)} %param.10), kind=kLoop, calls=%fused_computation.1 | loop fusion | flops 6144 | bytes 24576 | tf_op jit(solution)/shard_map/transpose | solution.py:139
  0.8 7.0 %collective-permute-start.14 = (f32[32,128]{1,0:T(8,128)S(1)}, f32[32,128]{1,0:T(8,128)S(1)}, u32[]{:S(2)}, u32[]{:S(2)}) collective-permute-start(f32[32,128]{1,0:T(8,128)S(1)} %pad_maximum_fusion.refs_0_), channel_id=1, source_target_pairs={{0,30},{2,0},{4,2},{6,4},{8,6},{10,8},{12,10},{14,12},{16,14},{18,... | collective-permute-start | bytes 49160 | tf_op jit(solution)/shard_map/ppermute | solution.py:144
  7.8 0.5 collective-permute-start.13
  8.3 0.5 collective-permute-start.12
  8.8 0.4 collective-permute-start.11
  9.2 1.3 %collective-permute-start.10 = (f32[32,128]{1,0:T(8,128)S(1)}, f32[32,128]{1,0:T(8,128)S(1)}, u32[]{:S(2)}, u32[]{:S(2)}) collective-permute-start(f32[32,128]{1,0:T(8,128)S(1)} %pad_maximum_fusion.refs_0_), channel_id=1, source_target_pairs={{0,22},{2,24},{4,26},{6,28},{8,30},{10,0},{12,2},{14,4},{16,6},{18... | collective-permute-start | bytes 49160 | tf_op jit(solution)/shard_map/ppermute | solution.py:144
  10.6 4.4 %collective-permute-start.9 = (f32[32,128]{1,0:T(8,128)S(1)}, f32[32,128]{1,0:T(8,128)S(1)}, u32[]{:S(2)}, u32[]{:S(2)}) collective-permute-start(f32[32,128]{1,0:T(8,128)S(1)} %pad_maximum_fusion.refs_0_), channel_id=1, source_target_pairs={{0,20},{2,22},{4,24},{6,26},{8,28},{10,30},{12,0},{14,2},{16,4},{1... | collective-permute-start | bytes 49160 | tf_op jit(solution)/shard_map/ppermute | solution.py:144
  15.0 1.6 %collective-permute-start.7 = (f32[32,128]{1,0:T(8,128)S(1)}, f32[32,128]{1,0:T(8,128)S(1)}, u32[]{:S(2)}, u32[]{:S(2)}) collective-permute-start(f32[32,128]{1,0:T(8,128)S(1)} %pad_maximum_fusion.refs_0_), channel_id=1, source_target_pairs={{0,16},{2,18},{4,20},{6,22},{8,24},{10,26},{12,28},{14,30},{16,0},... | collective-permute-start | bytes 49160 | tf_op jit(solution)/shard_map/ppermute | solution.py:144
  16.6 2.6 %collective-permute-start.6 = (f32[32,128]{1,0:T(8,128)S(1)}, f32[32,128]{1,0:T(8,128)S(1)}, u32[]{:S(2)}, u32[]{:S(2)}) collective-permute-start(f32[32,128]{1,0:T(8,128)S(1)} %pad_maximum_fusion.refs_0_), channel_id=1, source_target_pairs={{0,14},{2,16},{4,18},{6,20},{8,22},{10,24},{12,26},{14,28},{16,30}... | collective-permute-start | bytes 49160 | tf_op jit(solution)/shard_map/ppermute | solution.py:144
  19.2 2.5 %collective-permute-start.5 = (f32[32,128]{1,0:T(8,128)S(1)}, f32[32,128]{1,0:T(8,128)S(1)}, u32[]{:S(2)}, u32[]{:S(2)}) collective-permute-start(f32[32,128]{1,0:T(8,128)S(1)} %pad_maximum_fusion.refs_0_), channel_id=1, source_target_pairs={{0,12},{2,14},{4,16},{6,18},{8,20},{10,22},{12,24},{14,26},{16,28}... | collective-permute-start | bytes 49160 | tf_op jit(solution)/shard_map/ppermute | solution.py:144
  21.7 0.7 %collective-permute-start.4 = (f32[32,128]{1,0:T(8,128)S(1)}, f32[32,128]{1,0:T(8,128)S(1)}, u32[]{:S(2)}, u32[]{:S(2)}) collective-permute-start(f32[32,128]{1,0:T(8,128)S(1)} %pad_maximum_fusion.refs_0_), channel_id=1, source_target_pairs={{0,10},{2,12},{4,14},{6,16},{8,18},{10,20},{12,22},{14,24},{16,26}... | collective-permute-start | bytes 49160 | tf_op jit(solution)/shard_map/ppermute | solution.py:144
  22.4 1.8 %collective-permute-start.3 = (f32[32,128]{1,0:T(8,128)S(1)}, f32[32,128]{1,0:T(8,128)S(1)}, u32[]{:S(2)}, u32[]{:S(2)}) collective-permute-start(f32[32,128]{1,0:T(8,128)S(1)} %pad_maximum_fusion.refs_0_), channel_id=1, source_target_pairs={{0,8},{2,10},{4,12},{6,14},{8,16},{10,18},{12,20},{14,22},{16,24},... | collective-permute-start | bytes 49160 | tf_op jit(solution)/shard_map/ppermute | solution.py:144
  24.3 3.3 %collective-permute-start.2 = (f32[32,128]{1,0:T(8,128)S(1)}, f32[32,128]{1,0:T(8,128)S(1)}, u32[]{:S(2)}, u32[]{:S(2)}) collective-permute-start(f32[32,128]{1,0:T(8,128)S(1)} %pad_maximum_fusion.refs_0_), channel_id=1, source_target_pairs={{0,6},{2,8},{4,10},{6,12},{8,14},{10,16},{12,18},{14,20},{16,22},{... | collective-permute-start | bytes 49160 | tf_op jit(solution)/shard_map/ppermute | solution.py:144
  27.5 0.9 %collective-permute-start.1 = (f32[32,128]{1,0:T(8,128)S(1)}, f32[32,128]{1,0:T(8,128)S(1)}, u32[]{:S(2)}, u32[]{:S(2)}) collective-permute-start(f32[32,128]{1,0:T(8,128)S(1)} %pad_maximum_fusion.refs_0_), channel_id=1, source_target_pairs={{0,4},{2,6},{4,8},{6,10},{8,12},{10,14},{12,16},{14,18},{16,20},{1... | collective-permute-start | bytes 49160 | tf_op jit(solution)/shard_map/ppermute | solution.py:144
  28.4 1.0 %copy-done.1 = bf16[2048,128]{1,0:T(8,128)(2,1)S(1)} copy-done((bf16[2048,128]{1,0:T(8,128)(2,1)S(1)}, bf16[2048,128]{1,0:T(8,128)(2,1)}, u32[]{:S(2)}) %copy-start.1) | copy-done | bytes 524312
  29.5 1.0 %copy-done.2 = bf16[2048,128]{1,0:T(8,128)(2,1)S(1)} copy-done((bf16[2048,128]{1,0:T(8,128)(2,1)S(1)}, bf16[2048,128]{1,0:T(8,128)(2,1)}, u32[]{:S(2)}) %copy-start.2) | copy-done | bytes 524312
  30.5 0.4 shard_map.64.refs_16_.series_ref
  30.9 0.8 %collective-permute-done.2.refs_3_ = f32[32,128]{1,0:T(8,128)S(1)} collective-permute-done((f32[32,128]{1,0:T(8,128)S(1)}, f32[32,128]{1,0:T(8,128)S(1)}, u32[]{:S(2)}, u32[]{:S(2)}) %collective-permute-start.2) | collective-permute-done | bytes 16416 | tf_op jit(solution)/shard_map/ppermute | solution.py:144
  31.8 2.2 %collective-permute-done.1.refs_2_ = f32[32,128]{1,0:T(8,128)S(1)} collective-permute-done((f32[32,128]{1,0:T(8,128)S(1)}, f32[32,128]{1,0:T(8,128)S(1)}, u32[]{:S(2)}, u32[]{:S(2)}) %collective-permute-start.1) | collective-permute-done | bytes 16416 | tf_op jit(solution)/shard_map/ppermute | solution.py:144
  34.0 1.8 %collective-permute-done.refs_1_ = f32[32,128]{1,0:T(8,128)S(1)} collective-permute-done((f32[32,128]{1,0:T(8,128)S(1)}, f32[32,128]{1,0:T(8,128)S(1)}, u32[]{:S(2)}, u32[]{:S(2)}) %collective-permute-start) | collective-permute-done | bytes 16416 | tf_op jit(solution)/shard_map/ppermute | solution.py:144
  35.8 1.4 %shard_map.65 = (f32[512,128]{1,0:T(8,128)S(1)}, f32[256,128]{1,0:T(8,128)S(1)}) custom-call(f32[32,128]{1,0:T(8,128)S(1)} %pad_maximum_fusion.refs_0_, f32[32,128]{1,0:T(8,128)S(1)} %collective-permute-done.refs_1_, f32[32,128]{1,0:T(8,128)S(1)} %collective-permute-done.1.refs_2_, f32[32,128]{1,0:T(8,128)S(1)} %collective-permute-done.2.refs_3_, ...), custom_call_target="tpu_custom_call" | custom-call | flops 8388608 | bytes 1310720 | tf_op jit(solution)/shard_map/pallas_call | solution.py:99
  37.2 10.8 %all_to_all.10.ends_ref = f32[16,16,128]{2,1,0:T(8,128)S(1)} all-to-all(f32[16,16,128]{2,1,0:T(8,128)S(1)} %bitcast.7), channel_id=1, replica_groups=mesh['groups'=1,'seq'=16,'chan'=2] {'seq'}, dimensions={0} | all-to-all | bytes 262144 | tf_op jit(solution)/shard_map/all_to_all | solution.py:167
  48.1 10.4 %all_to_all.11 = f32[16,16,128]{2,1,0:T(8,128)S(1)} all-to-all(f32[16,16,128]{2,1,0:T(8,128)S(1)} %shard_map.66), channel_id=1, replica_groups=mesh['groups'=1,'seq'=16,'chan'=2] {'seq'}, dimensions={0} | all-to-all | bytes 262144 | tf_op jit(solution)/shard_map/all_to_all | solution.py:174
  58.5 3.7 %shard_map.67 = bf16[2048,128]{1,0:T(8,128)(2,1)} custom-call(f32[512,128]{1,0:T(8,128)S(1)} %get-tuple-element.7.params_ref, f32[2048,128]{1,0:T(8,128)S(1)} %shard_map.64.refs_16_.series_ref, f32[256,128]{1,0:T(8,128)S(1)} %bitcast.6, f32[16,128]{1,0:T(8,128)S(1)} %bitcast.10, bf16[2048,128]{1,0:T(8,128)(2,1)S(1)} %copy-done), custom_call_target="tpu_custom_call" | custom-call | flops 16777216 | bytes 1974272 | tf_op jit(solution)/shard_map/pallas_call | solution.py:99
  (24 shorter events, 0.1 us)
Async XLA Ops:
  0.0 0.8 %copy-start.3 = (f32[128,16]{0,1:T(8,128)S(1)}, f32[128,16]{0,1:T(8,128)}, u32[]{:S(2)}) copy-start(f32[128,16]{0,1:T(8,128)} %param.10) | copy-start | bytes 24580
  0.8 9.7 %collective-permute-start.14 = (f32[32,128]{1,0:T(8,128)S(1)}, f32[32,128]{1,0:T(8,128)S(1)}, u32[]{:S(2)}, u32[]{:S(2)}) collective-permute-start(f32[32,128]{1,0:T(8,128)S(1)} %pad_maximum_fusion.refs_0_), channel_id=1, source_target_pairs={{0,30},{2,0},{4,2},{6,4},{8,6},{10,8},{12,10},{14,12},{16,14},{18,... | collective-permute-start | bytes 49160 | tf_op jit(solution)/shard_map/ppermute | solution.py:144
  7.8 7.2 %collective-permute-start.13 = (f32[32,128]{1,0:T(8,128)S(1)}, f32[32,128]{1,0:T(8,128)S(1)}, u32[]{:S(2)}, u32[]{:S(2)}) collective-permute-start(f32[32,128]{1,0:T(8,128)S(1)} %pad_maximum_fusion.refs_0_), channel_id=1, source_target_pairs={{0,28},{2,30},{4,0},{6,2},{8,4},{10,6},{12,8},{14,10},{16,12},{18,... | collective-permute-start | bytes 49160 | tf_op jit(solution)/shard_map/ppermute | solution.py:144
  8.3 6.7 %collective-permute-start.12 = (f32[32,128]{1,0:T(8,128)S(1)}, f32[32,128]{1,0:T(8,128)S(1)}, u32[]{:S(2)}, u32[]{:S(2)}) collective-permute-start(f32[32,128]{1,0:T(8,128)S(1)} %pad_maximum_fusion.refs_0_), channel_id=1, source_target_pairs={{0,26},{2,28},{4,30},{6,0},{8,2},{10,4},{12,6},{14,8},{16,10},{18,... | collective-permute-start | bytes 49160 | tf_op jit(solution)/shard_map/ppermute | solution.py:144
  8.8 7.8 %collective-permute-start.11 = (f32[32,128]{1,0:T(8,128)S(1)}, f32[32,128]{1,0:T(8,128)S(1)}, u32[]{:S(2)}, u32[]{:S(2)}) collective-permute-start(f32[32,128]{1,0:T(8,128)S(1)} %pad_maximum_fusion.refs_0_), channel_id=1, source_target_pairs={{0,24},{2,26},{4,28},{6,30},{8,0},{10,2},{12,4},{14,6},{16,8},{18,... | collective-permute-start | bytes 49160 | tf_op jit(solution)/shard_map/ppermute | solution.py:144
  9.2 9.9 %collective-permute-start.10 = (f32[32,128]{1,0:T(8,128)S(1)}, f32[32,128]{1,0:T(8,128)S(1)}, u32[]{:S(2)}, u32[]{:S(2)}) collective-permute-start(f32[32,128]{1,0:T(8,128)S(1)} %pad_maximum_fusion.refs_0_), channel_id=1, source_target_pairs={{0,22},{2,24},{4,26},{6,28},{8,30},{10,0},{12,2},{14,4},{16,6},{18... | collective-permute-start | bytes 49160 | tf_op jit(solution)/shard_map/ppermute | solution.py:144
  10.6 11.2 %collective-permute-start.9 = (f32[32,128]{1,0:T(8,128)S(1)}, f32[32,128]{1,0:T(8,128)S(1)}, u32[]{:S(2)}, u32[]{:S(2)}) collective-permute-start(f32[32,128]{1,0:T(8,128)S(1)} %pad_maximum_fusion.refs_0_), channel_id=1, source_target_pairs={{0,20},{2,22},{4,24},{6,26},{8,28},{10,30},{12,0},{14,2},{16,4},{1... | collective-permute-start | bytes 49160 | tf_op jit(solution)/shard_map/ppermute | solution.py:144
  15.0 7.4 %collective-permute-start.8 = (f32[32,128]{1,0:T(8,128)S(1)}, f32[32,128]{1,0:T(8,128)S(1)}, u32[]{:S(2)}, u32[]{:S(2)}) collective-permute-start(f32[32,128]{1,0:T(8,128)S(1)} %pad_maximum_fusion.refs_0_), channel_id=1, source_target_pairs={{0,18},{2,20},{4,22},{6,24},{8,26},{10,28},{12,30},{14,0},{16,2},{... | collective-permute-start | bytes 49160 | tf_op jit(solution)/shard_map/ppermute | solution.py:144
  15.0 9.2 %collective-permute-start.7 = (f32[32,128]{1,0:T(8,128)S(1)}, f32[32,128]{1,0:T(8,128)S(1)}, u32[]{:S(2)}, u32[]{:S(2)}) collective-permute-start(f32[32,128]{1,0:T(8,128)S(1)} %pad_maximum_fusion.refs_0_), channel_id=1, source_target_pairs={{0,16},{2,18},{4,20},{6,22},{8,24},{10,26},{12,28},{14,30},{16,0},... | collective-permute-start | bytes 49160 | tf_op jit(solution)/shard_map/ppermute | solution.py:144
  16.6 10.9 %collective-permute-start.6 = (f32[32,128]{1,0:T(8,128)S(1)}, f32[32,128]{1,0:T(8,128)S(1)}, u32[]{:S(2)}, u32[]{:S(2)}) collective-permute-start(f32[32,128]{1,0:T(8,128)S(1)} %pad_maximum_fusion.refs_0_), channel_id=1, source_target_pairs={{0,14},{2,16},{4,18},{6,20},{8,22},{10,24},{12,26},{14,28},{16,30}... | collective-permute-start | bytes 49160 | tf_op jit(solution)/shard_map/ppermute | solution.py:144
  19.2 9.2 %collective-permute-start.5 = (f32[32,128]{1,0:T(8,128)S(1)}, f32[32,128]{1,0:T(8,128)S(1)}, u32[]{:S(2)}, u32[]{:S(2)}) collective-permute-start(f32[32,128]{1,0:T(8,128)S(1)} %pad_maximum_fusion.refs_0_), channel_id=1, source_target_pairs={{0,12},{2,14},{4,16},{6,18},{8,20},{10,22},{12,24},{14,26},{16,28}... | collective-permute-start | bytes 49160 | tf_op jit(solution)/shard_map/ppermute | solution.py:144
  21.7 9.2 %collective-permute-start.4 = (f32[32,128]{1,0:T(8,128)S(1)}, f32[32,128]{1,0:T(8,128)S(1)}, u32[]{:S(2)}, u32[]{:S(2)}) collective-permute-start(f32[32,128]{1,0:T(8,128)S(1)} %pad_maximum_fusion.refs_0_), channel_id=1, source_target_pairs={{0,10},{2,12},{4,14},{6,16},{8,18},{10,20},{12,22},{14,24},{16,26}... | collective-permute-start | bytes 49160 | tf_op jit(solution)/shard_map/ppermute | solution.py:144
  22.4 8.5 %collective-permute-start.3 = (f32[32,128]{1,0:T(8,128)S(1)}, f32[32,128]{1,0:T(8,128)S(1)}, u32[]{:S(2)}, u32[]{:S(2)}) collective-permute-start(f32[32,128]{1,0:T(8,128)S(1)} %pad_maximum_fusion.refs_0_), channel_id=1, source_target_pairs={{0,8},{2,10},{4,12},{6,14},{8,16},{10,18},{12,20},{14,22},{16,24},... | collective-permute-start | bytes 49160 | tf_op jit(solution)/shard_map/ppermute | solution.py:144
  24.3 7.5 %collective-permute-start.2 = (f32[32,128]{1,0:T(8,128)S(1)}, f32[32,128]{1,0:T(8,128)S(1)}, u32[]{:S(2)}, u32[]{:S(2)}) collective-permute-start(f32[32,128]{1,0:T(8,128)S(1)} %pad_maximum_fusion.refs_0_), channel_id=1, source_target_pairs={{0,6},{2,8},{4,10},{6,12},{8,14},{10,16},{12,18},{14,20},{16,22},{... | collective-permute-start | bytes 49160 | tf_op jit(solution)/shard_map/ppermute | solution.py:144
  27.5 6.4 %collective-permute-start.1 = (f32[32,128]{1,0:T(8,128)S(1)}, f32[32,128]{1,0:T(8,128)S(1)}, u32[]{:S(2)}, u32[]{:S(2)}) collective-permute-start(f32[32,128]{1,0:T(8,128)S(1)} %pad_maximum_fusion.refs_0_), channel_id=1, source_target_pairs={{0,4},{2,6},{4,8},{6,10},{8,12},{10,14},{12,16},{14,18},{16,20},{1... | collective-permute-start | bytes 49160 | tf_op jit(solution)/shard_map/ppermute | solution.py:144
  28.4 7.3 %collective-permute-start = (f32[32,128]{1,0:T(8,128)S(1)}, f32[32,128]{1,0:T(8,128)S(1)}, u32[]{:S(2)}, u32[]{:S(2)}) collective-permute-start(f32[32,128]{1,0:T(8,128)S(1)} %pad_maximum_fusion.refs_0_), channel_id=1, source_target_pairs={{0,2},{2,4},{4,6},{6,8},{8,10},{10,12},{12,14},{14,16},{16,18},{18... | collective-permute-start | bytes 49160 | tf_op jit(solution)/shard_map/ppermute | solution.py:144
  28.4 1.0 %copy-start.1 = (bf16[2048,128]{1,0:T(8,128)(2,1)S(1)}, bf16[2048,128]{1,0:T(8,128)(2,1)}, u32[]{:S(2)}) copy-start(bf16[2048,128]{1,0:T(8,128)(2,1)} %k_ref.1) | copy-start | bytes 1572868
  29.5 1.0 %copy-start.2 = (bf16[2048,128]{1,0:T(8,128)(2,1)S(1)}, bf16[2048,128]{1,0:T(8,128)(2,1)}, u32[]{:S(2)}) copy-start(bf16[2048,128]{1,0:T(8,128)(2,1)} %v_ref.1) | copy-start | bytes 1572868
  37.2 21.3 %copy-start = (bf16[2048,128]{1,0:T(8,128)(2,1)S(1)}, bf16[2048,128]{1,0:T(8,128)(2,1)}, u32[]{:S(2)}) copy-start(bf16[2048,128]{1,0:T(8,128)(2,1)} %q_ref.1) | copy-start | bytes 1572868
  48.1 10.4 %copy-start.4 = (f32[2048]{0:T(1024)S(1)}, f32[2048]{0:T(1024)}, u32[]{:S(2)}) copy-start(f32[2048]{0:T(1024)} %param.11) | copy-start | bytes 24580

commit v3 on v1

--- a/solution.py
+++ b/solution.py
@@ -93,7 +93,7 @@
         kernel,
         out_shape=out_shape,
         in_specs=[vmem] * len(args),
-        out_specs=vmem,
+        out_specs=jax.tree.map(lambda _: vmem, out_shape),
         scratch_shapes=list(scratch),
         compiler_params=pltpu.CompilerParams(vmem_limit_bytes=VMEM_LIMIT),
         cost_estimate=pl.CostEstimate(flops=flops, bytes_accessed=in_bytes, transcendentals=0),
@@ -130,7 +130,8 @@
     weights = residues * jnp.sqrt(-jnp.expm1(-2.0 * rates))
     own_rates = rates.T
     packed = jnp.concatenate([own_rates, weights.T], axis=0)
-    gathered = lax.all_gather(packed, "seq", axis=0)
+    copies = jnp.broadcast_to(packed[None], (blocks,) + packed.shape)
+    gathered = lax.all_to_all(copies, "seq", split_axis=0, concat_axis=0, tiled=True)
     params = to_chunks(gathered).reshape(chunks * 2 * order, LANES)
 
     series = call(

time: 74.5 us -> 46.9 us (0.63)
  blocking collectives: 65.7 us -> 21.7 us
  waiting for transfers between devices: 0 us -> 8.41 us
  starting transfers between devices: 0 us -> 8.31 us
    all_gather x1 -> x0, blocking collectives: 43.8 us -> none  [shards(): gathered = lax.all_gather(packed, 'seq', axis=0)]
    all_to_all x0 -> x1, waiting for transfers between devices: none -> 8.41 us  [shards(): lax.all_to_all(copies, 'seq', split_axis=0, concat_axis=0, tiled=True)]
    all_to_all x0 -> x1, starting transfers between devices: none -> 8.31 us  [shards(): lax.all_to_all(copies, 'seq', split_axis=0, concat_axis=0, tiled=True)]
    unnamed x10, local copies, waits for them, and re-layouts: 2.1 us -> 1.06 us
    all_to_all x1, blocking collectives: 11.4 us -> 10.4 us  [shards(): lax.all_to_all(starts, 'seq', split_axis=0, concat_axis=0, tiled=True)]
    all_to_all x1, blocking collectives: 10.5 us -> 11.3 us  [shards(): ends = lax.all_to_all(ends, 'seq', split_axis=0, concat_axis=0, tiled=True)]
  transfers between devices with their start and end apart: 0 -> 1, of which waited for: 0 -> 1; matrix products, arithmetic and copies ran while one was open for 0% -> 0% of each run, Pallas kernels for 0% -> 1%
where the time goes in v3:
time: 46.9 us; the launch traced here: 46.5 us
  blocking collectives  21.7 us (46%)
  waiting for transfers between devices  8.41 us (18%)
  starting transfers between devices  8.31 us (18%)
  Pallas kernels  5.45 us (12%)
  local copies, waits for them, and re-layouts  1.79 us (4%)
  other arithmetic  0.79 us (2%)
    all_to_all x1, blocking collectives, shards(): ends = lax.all_to_all(ends, 'seq', split_axis=0, concat_axis=0, tiled=True)  11.3 us
    all_to_all x1, blocking collectives, shards(): lax.all_to_all(starts, 'seq', split_axis=0, concat_axis=0, tiled=True)  10.4 us
    all_to_all x1, waiting for transfers between devices, shards(): lax.all_to_all(copies, 'seq', split_axis=0, concat_axis=0, tiled=True)  8.41 us
    all_to_all x1, starting transfers between devices, shards(): lax.all_to_all(copies, 'seq', split_axis=0, concat_axis=0, tiled=True)  8.31 us
    pallas_call x4, Pallas kernels, call(): pl.pallas_call(kernel, out_shape=out_shape, in_specs=[vmem] * len(args),...  5.45 us
    unnamed x10, local copies, waits for them, and re-layouts  1.06 us
  transfers between devices with their start and end apart: 1, of which 1 were waited for; matrix products, arithmetic and copies ran while one was open for 0% of the time, Pallas kernels for 1%

profile of v3, /device:TPU:0, one launch (start us, length us, event | category | flops | bytes accessed | tf_op | source)
XLA Modules:
  0.0 46.5 jit_solution(8855639974552707549)
XLA Ops:
  0.0 0.0 copy-start.3
  0.0 0.0 copy-start.1
  0.0 0.8 %multiply_bitcast_fusion = f32[16,128]{1,0:T(8,128)S(1)} fusion(f32[128,16]{0,1:T(8,128)} %param.9, f32[128,16]{0,1:T(8,128)} %param.10), kind=kLoop, calls=%fused_computation.1 | loop fusion | flops 6144 | bytes 24576 | tf_op jit(solution)/shard_map/transpose | solution.py:132
  0.8 0.0 copy-done.3
  0.8 0.7 %broadcast_in_dim.2 = f32[16,32,128]{2,1,0:T(8,128)} broadcast(f32[32,128]{1,0:T(8,128)S(1)} %pad_maximum_fusion), dimensions={1,2} | broadcast | bytes 278528 | tf_op jit(solution)/shard_map/broadcast_in_dim | solution.py:133
  1.5 8.3 %all-to-all-start = ((f32[16,32,128]{2,1,0:T(8,128)}), f32[16,32,128]{2,1,0:T(8,128)S(1)}, u32[]{:S(2)}, u32[]{:S(2)}) async-start(f32[16,32,128]{2,1,0:T(8,128)} %broadcast_in_dim.2), calls=%async_computation | async-start | bytes 524288 | tf_op jit(solution)/shard_map/all_to_all | solution.py:134
  9.9 0.0 copy-done.1
  9.9 0.0 copy-start.2
  9.9 1.0 %copy-done.2 = bf16[2048,128]{1,0:T(8,128)(2,1)S(1)} copy-done((bf16[2048,128]{1,0:T(8,128)(2,1)S(1)}, bf16[2048,128]{1,0:T(8,128)(2,1)}, u32[]{:S(2)}) %copy-start.2) | copy-done | bytes 524312
  10.9 0.4 shard_map.64.series_ref
  11.3 8.4 %all-to-all-done = f32[16,32,128]{2,1,0:T(8,128)S(1)} async-done(((f32[16,32,128]{2,1,0:T(8,128)}), f32[16,32,128]{2,1,0:T(8,128)S(1)}, u32[]{:S(2)}, u32[]{:S(2)}) %all-to-all-start) | async-done | bytes 262176 | tf_op jit(solution)/shard_map/all_to_all | solution.py:134
  19.7 1.3 %shard_map.65 = f32[256,128]{1,0:T(8,128)S(1)} custom-call(f32[512,128]{1,0:T(8,128)S(1)} %bitcast.7, f32[2048,128]{1,0:T(8,128)S(1)} %shard_map.64.series_ref), custom_call_target="tpu_custom_call" | custom-call | flops 8388608 | bytes 1310720 | tf_op jit(solution)/shard_map/pallas_call | solution.py:92
  21.1 0.0 copy-start
  21.1 11.3 %all_to_all.15.ends_ref = f32[16,16,128]{2,1,0:T(8,128)S(1)} all-to-all(f32[16,16,128]{2,1,0:T(8,128)S(1)} %bitcast.10), channel_id=1, replica_groups=mesh['groups'=1,'seq'=16,'chan'=2] {'seq'}, dimensions={0} | all-to-all | bytes 262144 | tf_op jit(solution)/shard_map/all_to_all | solution.py:152
  32.4 0.0 copy-start.4
  32.4 10.4 %all_to_all.16 = f32[16,16,128]{2,1,0:T(8,128)S(1)} all-to-all(f32[16,16,128]{2,1,0:T(8,128)S(1)} %shard_map.66), channel_id=1, replica_groups=mesh['groups'=1,'seq'=16,'chan'=2] {'seq'}, dimensions={0} | all-to-all | bytes 262144 | tf_op jit(solution)/shard_map/all_to_all | solution.py:159
  42.8 0.0 copy-done
  42.8 0.0 copy-done.4
  42.8 3.7 %shard_map.67 = bf16[2048,128]{1,0:T(8,128)(2,1)} custom-call(f32[512,128]{1,0:T(8,128)S(1)} %bitcast.8, f32[2048,128]{1,0:T(8,128)S(1)} %shard_map.64.series_ref, f32[256,128]{1,0:T(8,128)S(1)} %bitcast.9, f32[16,128]{1,0:T(8,128)S(1)} %bitcast.13, bf16[2048,128]{1,0:T(8,128)(2,1)S(1)} %copy-done), custom_call_target="tpu_custom_call" | custom-call | flops 16777216 | bytes 1974272 | tf_op jit(solution)/shard_map/pallas_call | solution.py:92
  (2 shorter events, 0.0 us)
Async XLA Ops:
  0.0 0.8 %copy-start.3 = (f32[128,16]{0,1:T(8,128)S(1)}, f32[128,16]{0,1:T(8,128)}, u32[]{:S(2)}) copy-start(f32[128,16]{0,1:T(8,128)} %param.10) | copy-start | bytes 24580
  0.0 9.9 %copy-start.1 = (bf16[2048,128]{1,0:T(8,128)(2,1)S(1)}, bf16[2048,128]{1,0:T(8,128)(2,1)}, u32[]{:S(2)}) copy-start(bf16[2048,128]{1,0:T(8,128)(2,1)} %k_ref.1) | copy-start | bytes 1572868
  1.5 18.2 %all-to-all-start = ((f32[16,32,128]{2,1,0:T(8,128)}), f32[16,32,128]{2,1,0:T(8,128)S(1)}, u32[]{:S(2)}, u32[]{:S(2)}) async-start(f32[16,32,128]{2,1,0:T(8,128)} %broadcast_in_dim.2), calls=%async_computation | async-start | bytes 524288 | tf_op jit(solution)/shard_map/all_to_all | solution.py:134
  9.9 1.0 %copy-start.2 = (bf16[2048,128]{1,0:T(8,128)(2,1)S(1)}, bf16[2048,128]{1,0:T(8,128)(2,1)}, u32[]{:S(2)}) copy-start(bf16[2048,128]{1,0:T(8,128)(2,1)} %v_ref.1) | copy-start | bytes 1572868
  21.1 21.8 %copy-start = (bf16[2048,128]{1,0:T(8,128)(2,1)S(1)}, bf16[2048,128]{1,0:T(8,128)(2,1)}, u32[]{:S(2)}) copy-start(bf16[2048,128]{1,0:T(8,128)(2,1)} %q_ref.1) | copy-start | bytes 1572868
  32.4 10.4 %copy-start.4 = (f32[2048]{0:T(1024)S(1)}, f32[2048]{0:T(1024)}, u32[]{:S(2)}) copy-start(f32[2048]{0:T(1024)} %param.11) | copy-start | bytes 24580

commit v4 on v3

--- a/solution.py
+++ b/solution.py
@@ -9,13 +9,15 @@
 LANES = 128
 SUBLANES = 8
 UNROLL = 8
+MEMBERS = 4
 VMEM_LIMIT = 32 * 1024 * 1024
 
 
-def prepare_kernel(chunks, k_ref, v_ref, series_ref):
+def prepare_kernel(places, k_ref, v_ref, series_ref):
     length = k_ref.shape[1]
-    for chunk in range(chunks):
-        rows = pl.ds(chunk * LANES, LANES)
+    chunks = len(places)
+    for chunk, place in enumerate(places):
+        rows = pl.ds(place * LANES, LANES)
         gated = k_ref[rows, :].astype(jnp.float32) * v_ref[rows, :].astype(jnp.float32)
         series_ref[pl.ds(chunk, length, stride=chunks), :] = gated.T
 
@@ -53,6 +55,31 @@
         carry = span_decay * carry + ends_ref[block]
 
 
+def plane_kernel(length, rate_ref, ends_ref, totals_ref):
+    order = ends_ref.shape[2]
+    span_decay = jnp.exp(-float(length) * rate_ref[:, :order, :])
+    total = ends_ref[0]
+    for block in range(1, ends_ref.shape[0]):
+        total = span_decay * total + ends_ref[block]
+    for plane in range(totals_ref.shape[0]):
+        totals_ref[plane] = total
+
+
+def planes_kernel(length, rate_ref, ends_ref, totals_ref, starts_ref):
+    members, _, order, _ = ends_ref.shape
+    mine = lax.axis_index("seq") // members
+    rate = rate_ref[:, :order, :]
+    plane_decay = jnp.exp(-float(length * members) * rate)
+    carry = jnp.zeros(rate.shape, jnp.float32)
+    for plane in range(totals_ref.shape[0] - 1):
+        carry = jnp.where(plane < mine, plane_decay * carry + totals_ref[plane], carry)
+    span_decay = jnp.exp(-float(length) * rate)
+    for block in range(members):
+        starts_ref[block] = carry
+        if block + 1 < members:
+            carry = span_decay * carry + ends_ref[block]
+
+
 def tree_sum(terms):
     terms = list(terms)
     while len(terms) > 1:
@@ -60,13 +87,15 @@
     return terms[0]
 
 
-def output_kernel(chunks, order, params_ref, series_ref, carry_ref, gain_ref, q_ref, out_ref, conv_ref):
+def output_kernel(places, order, params_ref, series_ref, carry_ref, gain_ref, q_ref, out_ref, conv_ref):
+    chunks = len(places)
     length = series_ref.shape[0] // chunks
     for half in range(chunks // SUBLANES):
         decay = [jnp.exp(-rate) for rate in mode_rows(params_ref, 0, order, 2 * order, chunks, half)]
         weight = mode_rows(params_ref, order, order, 2 * order, chunks, half)
         carry = mode_rows(carry_ref, 0, order, order, chunks, half)
-        gain = gain_ref[pl.ds(half * SUBLANES, SUBLANES), :]
+        own = places[half * SUBLANES : (half + 1) * SUBLANES]
+        gain = jnp.concatenate([gain_ref[pl.ds(place, 1), :] for place in own], axis=0)
 
         def steps(i, state):
             state = list(state)
@@ -80,8 +109,8 @@
             return tuple(state)
 
         lax.fori_loop(0, length // UNROLL, steps, tuple(carry))
-    for chunk in range(chunks):
-        rows = pl.ds(chunk * LANES, LANES)
+    for chunk, place in enumerate(places):
+        rows = pl.ds(place * LANES, LANES)
         conv = conv_ref[pl.ds(chunk, length, stride=chunks), :].T
         out_ref[rows, :] = (q_ref[rows, :].astype(jnp.float32) * conv).astype(jnp.bfloat16)
 
@@ -121,21 +150,40 @@
     return pieces.reshape(owners, own // LANES, rows, LANES).swapaxes(1, 2).reshape(owners, rows, own)
 
 
+def all_to_all(pieces, groups=None):
+    return lax.all_to_all(pieces, "seq", split_axis=0, concat_axis=0, axis_index_groups=groups, tiled=True)
+
+
+def copies(array, count):
+    return jnp.broadcast_to(array[None], (count,) + array.shape)
+
+
 def shards(blocks, q_proj, k_proj, value_projection, residues, rates, direct_gain):
     channels, length = q_proj.shape
-    order = residues.shape[1]
+    own, order = residues.shape
     chunks = channels // LANES
     f32 = jnp.float32
+    two_level = own == LANES and blocks % MEMBERS == 0
+    planes = blocks // MEMBERS
+    if two_level:
+        lines = [[plane * MEMBERS + member for plane in range(planes)] for member in range(MEMBERS)]
+        layers = [[plane * MEMBERS + member for member in range(MEMBERS)] for plane in range(planes)]
+        places = [plane * MEMBERS + member for member in range(MEMBERS) for plane in range(planes)]
+    else:
+        places = list(range(chunks))
 
     weights = residues * jnp.sqrt(-jnp.expm1(-2.0 * rates))
     own_rates = rates.T
     packed = jnp.concatenate([own_rates, weights.T], axis=0)
-    copies = jnp.broadcast_to(packed[None], (blocks,) + packed.shape)
-    gathered = lax.all_to_all(copies, "seq", split_axis=0, concat_axis=0, tiled=True)
-    params = to_chunks(gathered).reshape(chunks * 2 * order, LANES)
+    if two_level:
+        line_params = all_to_all(copies(packed, planes), lines)
+        params = all_to_all(copies(line_params, MEMBERS), layers)
+    else:
+        params = to_chunks(all_to_all(copies(packed, blocks)))
+    params = params.reshape(chunks * 2 * order, LANES)
 
     series = call(
-        functools.partial(prepare_kernel, chunks),
+        functools.partial(prepare_kernel, places),
         jax.ShapeDtypeStruct((length * chunks, LANES), f32),
         k_proj,
         value_projection,
@@ -148,22 +196,39 @@
         series,
         flops=2 * order * channels * length,
     )
-    ends = from_chunks(ends.reshape(chunks, order, LANES), blocks)
-    ends = lax.all_to_all(ends, "seq", split_axis=0, concat_axis=0, tiled=True)
-    starts = call(
-        functools.partial(prefix_kernel, length),
-        jax.ShapeDtypeStruct(ends.shape, f32),
-        own_rates,
-        ends,
-    )
-    starts = lax.all_to_all(starts, "seq", split_axis=0, concat_axis=0, tiled=True)
-    carry = to_chunks(starts).reshape(chunks * order, LANES)
+    ends = ends.reshape(chunks, order, LANES)
+    if two_level:
+        ends = all_to_all(ends.reshape(MEMBERS, planes, order, LANES), layers)
+        totals = call(
+            functools.partial(plane_kernel, length),
+            jax.ShapeDtypeStruct((planes, planes, order, LANES), f32),
+            line_params,
+            ends,
+        )
+        totals = all_to_all(totals, lines)
+        starts = call(
+            functools.partial(planes_kernel, length),
+            jax.ShapeDtypeStruct(ends.shape, f32),
+            line_params,
+            ends,
+            totals,
+        )
+        carry = all_to_all(starts, layers)
+    else:
+        ends = all_to_all(from_chunks(ends, blocks))
+        starts = call(
+            functools.partial(prefix_kernel, length),
+            jax.ShapeDtypeStruct(ends.shape, f32),
+            own_rates,
+            ends,
+        )
+        carry = to_chunks(all_to_all(starts))
     return call(
-        functools.partial(output_kernel, chunks, order),
+        functools.partial(output_kernel, places, order),
         jax.ShapeDtypeStruct((channels, length), jnp.bfloat16),
         params,
         series,
-        carry,
+        carry.reshape(chunks * order, LANES),
         direct_gain.reshape(chunks, LANES),
         q_proj,
         scratch=[pltpu.VMEM((length * chunks, LANES), f32)],

time: 46.9 us -> 51.5 us (1.098)
  blocking collectives: 21.7 us -> 35.3 us
  starting transfers between devices: 8.31 us -> 3.72 us
  waiting for transfers between devices: 8.41 us -> 4.96 us
  local copies, waits for them, and re-layouts: 1.79 us -> 0.76 us
    all_to_all x2 -> x4, blocking collectives: 21.7 us -> 35.3 us  [all_to_all(): lax.all_to_all(pieces, 'seq', split_axis=0, concat_axis=0, axis_index_gro...]
    all_to_all x1, starting transfers between devices: 8.31 us -> 3.72 us  [all_to_all(): lax.all_to_all(pieces, 'seq', split_axis=0, concat_axis=0, axis_index_gro...]
    all_to_all x1, waiting for transfers between devices: 8.41 us -> 4.96 us  [all_to_all(): lax.all_to_all(pieces, 'seq', split_axis=0, concat_axis=0, axis_index_gro...]
    unnamed x10, local copies, waits for them, and re-layouts: 1.06 us -> 0.03 us
    pallas_call x4 -> x5, Pallas kernels: 5.45 us -> 5.48 us  [call(): pl.pallas_call(kernel, out_shape=out_shape, in_specs=[vmem] * len(args),...]
where the time goes in v4:
time: 51.5 us; the launch traced here: 51 us
  blocking collectives  35.3 us (69%)
  Pallas kernels  5.48 us (11%)
  waiting for transfers between devices  4.96 us (10%)
  starting transfers between devices  3.72 us (7%)
  other arithmetic  0.79 us (2%)
  local copies, waits for them, and re-layouts  0.76 us (1%)
    all_to_all x4, blocking collectives, all_to_all(): lax.all_to_all(pieces, 'seq', split_axis=0, concat_axis=0, axis_index_gro...  35.3 us
    pallas_call x5, Pallas kernels, call(): pl.pallas_call(kernel, out_shape=out_shape, in_specs=[vmem] * len(args),...  5.48 us
    all_to_all x1, waiting for transfers between devices, all_to_all(): lax.all_to_all(pieces, 'seq', split_axis=0, concat_axis=0, axis_index_gro...  4.96 us
    all_to_all x1, starting transfers between devices, all_to_all(): lax.all_to_all(pieces, 'seq', split_axis=0, concat_axis=0, axis_index_gro...  3.72 us
  transfers between devices with their start and end apart: 1, of which 1 were waited for; matrix products, arithmetic and copies ran while one was open for 0% of the time, Pallas kernels for 1%

profile of v4, /device:TPU:0, one launch (start us, length us, event | category | flops | bytes accessed | tf_op | source)
XLA Modules:
  0.0 51.0 jit_solution(8064360217298759840)
XLA Ops:
  0.0 0.0 copy-start.4
  0.0 0.8 %multiply_bitcast_fusion = f32[16,128]{1,0:T(8,128)S(1)} fusion(f32[128,16]{0,1:T(8,128)} %param.9, f32[128,16]{0,1:T(8,128)} %param.10), kind=kLoop, calls=%fused_computation.1 | loop fusion | flops 6144 | bytes 24576 | tf_op jit(solution)/shard_map/transpose | solution.py:177
  0.8 0.0 copy-done.4
  0.8 0.0 copy-start.1
  0.8 0.0 copy-start.2
  0.9 12.0 %all_to_all.25.rate_ref = f32[4,32,128]{2,1,0:T(8,128)S(1)} all-to-all(f32[4,32,128]{2,1,0:T(8,128)S(1)} %broadcast_in_dim.4), channel_id=1, replica_groups={{0,8,16,24},{2,10,18,26},{4,12,20,28},{6,14,22,30},{1,9,17,25},{3,11,19..., dimensions={0} | all-to-all | bytes 131072 | tf_op jit(solution)/shard_map/all_to_all | solution.py:154
  12.8 0.7 %broadcast_in_dim.5 = f32[4,4,32,128]{3,2,1,0:T(8,128)} broadcast(f32[4,32,128]{2,1,0:T(8,128)S(1)} %all_to_all.25.rate_ref), dimensions={1,2,3} | broadcast | bytes 327680 | tf_op jit(solution)/shard_map/broadcast_in_dim | solution.py:158
  13.6 3.7 %all-to-all-start.1 = ((f32[4,4,32,128]{3,2,1,0:T(8,128)}), f32[4,4,32,128]{3,2,1,0:T(8,128)S(1)}, u32[]{:S(2)}, u32[]{:S(2)}) async-start(f32[4,4,32,128]{3,2,1,0:T(8,128)} %broadcast_in_dim.5), calls=%async_computation.1 | async-start | bytes 524288 | tf_op jit(solution)/shard_map/all_to_all | solution.py:154
  17.3 0.0 copy-done.1
  17.3 0.0 copy-done.2
  17.3 0.4 shard_map.64.series_ref
  17.7 5.0 %all-to-all-done.1 = f32[4,4,32,128]{3,2,1,0:T(8,128)S(1)} async-done(((f32[4,4,32,128]{3,2,1,0:T(8,128)}), f32[4,4,32,128]{3,2,1,0:T(8,128)S(1)}, u32[]{:S(2)}, u32[]{:S(2)}) %all-to-all-start.1) | async-done | bytes 262176 | tf_op jit(solution)/shard_map/all_to_all | solution.py:154
  22.7 1.3 %shard_map.65 = f32[256,128]{1,0:T(8,128)S(1)} custom-call(f32[512,128]{1,0:T(8,128)S(1)} %bitcast.7, f32[2048,128]{1,0:T(8,128)S(1)} %shard_map.64.series_ref), custom_call_target="tpu_custom_call" | custom-call | flops 8388608 | bytes 1310720 | tf_op jit(solution)/shard_map/pallas_call | solution.py:121
  24.0 7.4 %all_to_all.26.ends_ref = f32[4,4,16,128]{3,2,1,0:T(8,128)S(1)} all-to-all(f32[4,4,16,128]{3,2,1,0:T(8,128)S(1)} %bitcast.10), channel_id=1, replica_groups={{0,2,4,6},{8,10,12,14},{16,18,20,22},{24,26,28,30},{1,3,5,7},{9,11,13,1..., dimensions={0} | all-to-all | bytes 262144 | tf_op jit(solution)/shard_map/all_to_all | solution.py:154
  31.4 0.0 copy-start
  31.4 8.4 %all_to_all.27.totals_ref = f32[4,4,16,128]{3,2,1,0:T(8,128)S(1)} all-to-all(f32[4,4,16,128]{3,2,1,0:T(8,128)S(1)} %shard_map.66), channel_id=1, replica_groups={{0,8,16,24},{2,10,18,26},{4,12,20,28},{6,14,22,30},{1,9,17,25},{3,11,19..., dimensions={0} | all-to-all | bytes 262144 | tf_op jit(solution)/shard_map/all_to_all | solution.py:154
  39.9 0.0 copy-start.3
  39.9 7.4 %all_to_all.28 = f32[4,4,16,128]{3,2,1,0:T(8,128)S(1)} all-to-all(f32[4,4,16,128]{3,2,1,0:T(8,128)S(1)} %shard_map.67), channel_id=1, replica_groups={{0,2,4,6},{8,10,12,14},{16,18,20,22},{24,26,28,30},{1,3,5,7},{9,11,13,1..., dimensions={0} | all-to-all | bytes 262144 | tf_op jit(solution)/shard_map/all_to_all | solution.py:154
  47.3 0.0 copy-done
  47.3 0.0 copy-done.3
  47.3 3.7 %shard_map.68 = bf16[2048,128]{1,0:T(8,128)(2,1)} custom-call(f32[512,128]{1,0:T(8,128)S(1)} %bitcast.8, f32[2048,128]{1,0:T(8,128)S(1)} %shard_map.64.series_ref, f32[256,128]{1,0:T(8,128)S(1)} %bitcast.9, f32[16,128]{1,0:T(8,128)S(1)} %bitcast.11, bf16[2048,128]{1,0:T(8,128)(2,1)S(1)} %copy-done), custom_call_target="tpu_custom_call" | custom-call | flops 16777216 | bytes 1974272 | tf_op jit(solution)/shard_map/pallas_call | solution.py:121
  (4 shorter events, 0.1 us)
Async XLA Ops:
  0.0 0.8 %copy-start.4 = (f32[128,16]{0,1:T(8,128)S(1)}, f32[128,16]{0,1:T(8,128)}, u32[]{:S(2)}) copy-start(f32[128,16]{0,1:T(8,128)} %param.10) | copy-start | bytes 24580
  0.8 16.5 %copy-start.1 = (bf16[2048,128]{1,0:T(8,128)(2,1)S(1)}, bf16[2048,128]{1,0:T(8,128)(2,1)}, u32[]{:S(2)}) copy-start(bf16[2048,128]{1,0:T(8,128)(2,1)} %k_ref.1) | copy-start | bytes 1572868
  0.8 16.5 %copy-start.2 = (bf16[2048,128]{1,0:T(8,128)(2,1)S(1)}, bf16[2048,128]{1,0:T(8,128)(2,1)}, u32[]{:S(2)}) copy-start(bf16[2048,128]{1,0:T(8,128)(2,1)} %v_ref.1) | copy-start | bytes 1572868
  13.6 9.1 %all-to-all-start.1 = ((f32[4,4,32,128]{3,2,1,0:T(8,128)}), f32[4,4,32,128]{3,2,1,0:T(8,128)S(1)}, u32[]{:S(2)}, u32[]{:S(2)}) async-start(f32[4,4,32,128]{3,2,1,0:T(8,128)} %broadcast_in_dim.5), calls=%async_computation.1 | async-start | bytes 524288 | tf_op jit(solution)/shard_map/all_to_all | solution.py:154
  31.4 15.9 %copy-start = (bf16[2048,128]{1,0:T(8,128)(2,1)S(1)}, bf16[2048,128]{1,0:T(8,128)(2,1)}, u32[]{:S(2)}) copy-start(bf16[2048,128]{1,0:T(8,128)(2,1)} %q_ref.1) | copy-start | bytes 1572868
  39.9 7.4 %copy-start.3 = (f32[2048]{0:T(1024)S(1)}, f32[2048]{0:T(1024)}, u32[]{:S(2)}) copy-start(f32[2048]{0:T(1024)} %param.11) | copy-start | bytes 24580

commit v5 on v3

--- a/solution.py
+++ b/solution.py
@@ -60,12 +60,22 @@
     return terms[0]
 
 
-def output_kernel(chunks, order, params_ref, series_ref, carry_ref, gain_ref, q_ref, out_ref, conv_ref):
+def one_minus_exp(y):
+    series = jnp.ones_like(y)
+    for k in range(11, 1, -1):
+        series = 1.0 - (y * (1.0 / k)) * series
+    return jnp.where(y < 0.5, y * series, 1.0 - jnp.exp(-y))
+
+
+def local_kernel(chunks, order, gathered_ref, series_ref, gain_ref, conv_ref, weight_ref):
     length = series_ref.shape[0] // chunks
     for half in range(chunks // SUBLANES):
-        decay = [jnp.exp(-rate) for rate in mode_rows(params_ref, 0, order, 2 * order, chunks, half)]
-        weight = mode_rows(params_ref, order, order, 2 * order, chunks, half)
-        carry = mode_rows(carry_ref, 0, order, order, chunks, half)
+        rate = mode_rows(gathered_ref, 0, order, 2 * order, chunks, half)
+        residue = mode_rows(gathered_ref, order, order, 2 * order, chunks, half)
+        decay = [jnp.exp(-rate[r]) for r in range(order)]
+        weight = [residue[r] * jnp.sqrt(one_minus_exp(2.0 * rate[r])) for r in range(order)]
+        for r in range(order):
+            weight_ref[pl.ds(half * SUBLANES * order + r, SUBLANES, stride=order), :] = weight[r]
         gain = gain_ref[pl.ds(half * SUBLANES, SUBLANES), :]
 
         def steps(i, state):
@@ -79,11 +89,30 @@
                 conv_ref[pl.ds(row, SUBLANES), :] = tree_sum(terms + [gain * x])
             return tuple(state)
 
-        lax.fori_loop(0, length // UNROLL, steps, tuple(carry))
-    for chunk in range(chunks):
-        rows = pl.ds(chunk * LANES, LANES)
-        conv = conv_ref[pl.ds(chunk, length, stride=chunks), :].T
-        out_ref[rows, :] = (q_ref[rows, :].astype(jnp.float32) * conv).astype(jnp.bfloat16)
+        zero = jnp.zeros((SUBLANES, LANES), jnp.float32)
+        lax.fori_loop(0, length // UNROLL, steps, (zero,) * order)
+
+
+def output_kernel(chunks, order, gathered_ref, weight_ref, carry_ref, local_ref, q_ref, out_ref, conv_ref):
+    length = local_ref.shape[0] // chunks
+    for half in range(chunks // SUBLANES):
+        decay = [jnp.exp(-rate) for rate in mode_rows(gathered_ref, 0, order, 2 * order, chunks, half)]
+        weight = mode_rows(weight_ref, 0, order, order, chunks, half)
+        carry = mode_rows(carry_ref, 0, order, order, chunks, half)
+
+        def steps(i, fading):
+            fading = list(fading)
+            for u in range(UNROLL):
+                row = pl.multiple_of((i * UNROLL + u) * chunks + half * SUBLANES, SUBLANES)
+                fading = [decay[r] * fading[r] for r in range(order)]
+                conv_ref[pl.ds(row, SUBLANES), :] = tree_sum(fading + [local_ref[pl.ds(row, SUBLANES), :]])
+            return tuple(fading)
+
+        lax.fori_loop(0, length // UNROLL, steps, tuple(weight[r] * carry[r] for r in range(order)))
+        for chunk in range(half * SUBLANES, (half + 1) * SUBLANES):
+            rows = pl.ds(chunk * LANES, LANES)
+            conv = conv_ref[pl.ds(chunk, length, stride=chunks), :].T
+            out_ref[rows, :] = (q_ref[rows, :].astype(jnp.float32) * conv).astype(jnp.bfloat16)
 
 
 def call(kernel, out_shape, *args, scratch=(), flops=0):
@@ -127,9 +156,8 @@
     chunks = channels // LANES
     f32 = jnp.float32
 
-    weights = residues * jnp.sqrt(-jnp.expm1(-2.0 * rates))
     own_rates = rates.T
-    packed = jnp.concatenate([own_rates, weights.T], axis=0)
+    packed = jnp.concatenate([own_rates, residues.T], axis=0)
     copies = jnp.broadcast_to(packed[None], (blocks,) + packed.shape)
     gathered = lax.all_to_all(copies, "seq", split_axis=0, concat_axis=0, tiled=True)
     params = to_chunks(gathered).reshape(chunks * 2 * order, LANES)
@@ -148,7 +176,19 @@
         series,
         flops=2 * order * channels * length,
     )
+    local_series, ends = lax.optimization_barrier((series, ends))
     ends = from_chunks(ends.reshape(chunks, order, LANES), blocks)
+    local, weights = call(
+        functools.partial(local_kernel, chunks, order),
+        (
+            jax.ShapeDtypeStruct((length * chunks, LANES), f32),
+            jax.ShapeDtypeStruct((chunks * order, LANES), f32),
+        ),
+        params,
+        local_series,
+        direct_gain.reshape(chunks, LANES),
+        flops=4 * order * channels * length,
+    )
     ends = lax.all_to_all(ends, "seq", split_axis=0, concat_axis=0, tiled=True)
     starts = call(
         functools.partial(prefix_kernel, length),
@@ -162,12 +202,12 @@
         functools.partial(output_kernel, chunks, order),
         jax.ShapeDtypeStruct((channels, length), jnp.bfloat16),
         params,
-        series,
+        weights,
         carry,
-        direct_gain.reshape(chunks, LANES),
+        local,
         q_proj,
         scratch=[pltpu.VMEM((length * chunks, LANES), f32)],
-        flops=4 * order * channels * length,
+        flops=2 * order * channels * length,
     )
 
 

time: 46.9 us -> 47.3 us (level)
  blocking collectives: 21.7 us -> 11.1 us
  waiting for transfers between devices: 8.41 us -> 13.5 us
  starting transfers between devices: 8.31 us -> 12 us
  Pallas kernels: 5.45 us -> 7.61 us
    all_to_all x1 -> x0, blocking collectives: 10.4 us -> none  [shards(): lax.all_to_all(starts, 'seq', split_axis=0, concat_axis=0, tiled=True)]
    all_to_all x0 -> x1, waiting for transfers between devices: none -> 5.07 us  [shards(): lax.all_to_all(starts, 'seq', split_axis=0, concat_axis=0, tiled=True)]
    all_to_all x0 -> x1, starting transfers between devices: none -> 3.64 us  [shards(): lax.all_to_all(starts, 'seq', split_axis=0, concat_axis=0, tiled=True)]
    pallas_call x4 -> x5, Pallas kernels: 5.45 us -> 7.61 us  [call(): pl.pallas_call(kernel, out_shape=out_shape, in_specs=[vmem] * len(args),...]
    transpose x1 -> x0, other arithmetic: 0.79 us -> none  [shards(): packed = jnp.concatenate([own_rates, weights.T], axis=0)]
    concatenate x1, other arithmetic: 0.01 us -> 0.77 us  [shards(): packed = jnp.concatenate([own_rates, residues.T], axis=0)]
  transfers between devices with their start and end apart: 1 -> 2, of which waited for: 1 -> 2; matrix products, arithmetic and copies ran while one was open for 0% -> 0% of each run, Pallas kernels for 1% -> 7%
where the time goes in v5:
time: 47.3 us; the launch traced here: 46.8 us
  waiting for transfers between devices  13.5 us (29%)
  starting transfers between devices  12 us (25%)
  blocking collectives  11.1 us (23%)
  Pallas kernels  7.61 us (16%)
  local copies, waits for them, and re-layouts  1.79 us (4%)
  other arithmetic  0.77 us (2%)
    all_to_all x1, blocking collectives, shards(): ends = lax.all_to_all(ends, 'seq', split_axis=0, concat_axis=0, tiled=True)  11.1 us
    all_to_all x1, waiting for transfers between devices, shards(): lax.all_to_all(copies, 'seq', split_axis=0, concat_axis=0, tiled=True)  8.41 us
    all_to_all x1, starting transfers between devices, shards(): lax.all_to_all(copies, 'seq', split_axis=0, concat_axis=0, tiled=True)  8.31 us
    pallas_call x5, Pallas kernels, call(): pl.pallas_call(kernel, out_shape=out_shape, in_specs=[vmem] * len(args),...  7.61 us
    all_to_all x1, waiting for transfers between devices, shards(): lax.all_to_all(starts, 'seq', split_axis=0, concat_axis=0, tiled=True)  5.07 us
    all_to_all x1, starting transfers between devices, shards(): lax.all_to_all(starts, 'seq', split_axis=0, concat_axis=0, tiled=True)  3.64 us
    unnamed x10, local copies, waits for them, and re-layouts  1.06 us
  transfers between devices with their start and end apart: 2, of which 2 were waited for; matrix products, arithmetic and copies ran while one was open for 0% of the time, Pallas kernels for 7%

profile of v5, /device:TPU:0, one launch (start us, length us, event | category | flops | bytes accessed | tf_op | source)
XLA Modules:
  0.0 46.8 jit_solution(6953597561580393820)
XLA Ops:
  0.0 0.0 copy-start.1
  0.0 0.8 %pad_maximum_fusion = f32[32,128]{1,0:T(8,128)S(1)} fusion(f32[16,128]{1,0:T(8,128)} %bitcast.14, f32[16,128]{1,0:T(8,128)} %bitcast.11), kind=kLoop, calls=%fused_computation | loop fusion | flops 4096 | bytes 32768 | tf_op jit(solution)/shard_map/concatenate | solution.py:160
  0.8 0.7 %broadcast_in_dim.2 = f32[16,32,128]{2,1,0:T(8,128)} broadcast(f32[32,128]{1,0:T(8,128)S(1)} %pad_maximum_fusion), dimensions={1,2} | broadcast | bytes 278528 | tf_op jit(solution)/shard_map/broadcast_in_dim | solution.py:161
  1.5 8.3 %all-to-all-start = ((f32[16,32,128]{2,1,0:T(8,128)}), f32[16,32,128]{2,1,0:T(8,128)S(1)}, u32[]{:S(2)}, u32[]{:S(2)}) async-start(f32[16,32,128]{2,1,0:T(8,128)} %broadcast_in_dim.2), calls=%async_computation | async-start | bytes 524288 | tf_op jit(solution)/shard_map/all_to_all | solution.py:162
  9.8 0.0 copy-done.1
  9.8 0.0 copy-start.2
  9.8 1.0 %copy-done.2 = bf16[2048,128]{1,0:T(8,128)(2,1)S(1)} copy-done((bf16[2048,128]{1,0:T(8,128)(2,1)S(1)}, bf16[2048,128]{1,0:T(8,128)(2,1)}, u32[]{:S(2)}) %copy-start.2) | copy-done | bytes 524312
  10.9 0.4 shard_map.64.series_ref
  11.3 8.4 %all-to-all-done = f32[16,32,128]{2,1,0:T(8,128)S(1)} async-done(((f32[16,32,128]{2,1,0:T(8,128)}), f32[16,32,128]{2,1,0:T(8,128)S(1)}, u32[]{:S(2)}, u32[]{:S(2)}) %all-to-all-start) | async-done | bytes 262176 | tf_op jit(solution)/shard_map/all_to_all | solution.py:162
  19.7 1.3 %shard_map.65 = f32[256,128]{1,0:T(8,128)S(1)} custom-call(f32[512,128]{1,0:T(8,128)S(1)} %bitcast.6, f32[2048,128]{1,0:T(8,128)S(1)} %shard_map.64.series_ref), custom_call_target="tpu_custom_call" | custom-call | flops 8388608 | bytes 1310720 | tf_op jit(solution)/shard_map/pallas_call | solution.py:121
  21.0 0.0 copy-start.3
  21.0 11.1 %all_to_all.15.ends_ref = f32[16,16,128]{2,1,0:T(8,128)S(1)} all-to-all(f32[16,16,128]{2,1,0:T(8,128)S(1)} %bitcast.10), channel_id=1, replica_groups=mesh['groups'=1,'seq'=16,'chan'=2] {'seq'}, dimensions={0} | all-to-all | bytes 262144 | tf_op jit(solution)/shard_map/all_to_all | solution.py:192
  32.2 0.0 copy-done.3
  32.2 0.7 %shard_map.67 = f32[16,16,128]{2,1,0:T(8,128)} custom-call(f32[16,128]{1,0:T(8,128)S(1)} %bitcast.12, f32[16,16,128]{2,1,0:T(8,128)S(1)} %all_to_all.15.ends_ref), custom_call_target="tpu_custom_call" | custom-call | bytes 139264 | tf_op jit(solution)/shard_map/pallas_call | solution.py:121
  32.9 0.0 copy-start.4
  32.9 3.6 %all-to-all-start.2 = ((f32[16,16,128]{2,1,0:T(8,128)}), f32[16,16,128]{2,1,0:T(8,128)S(1)}, u32[]{:S(2)}, u32[]{:S(2)}) async-start(f32[16,16,128]{2,1,0:T(8,128)} %shard_map.67), calls=%async_computation.2 | async-start | bytes 262144 | tf_op jit(solution)/shard_map/all_to_all | solution.py:199
  36.5 0.0 copy-done.4
  36.5 0.0 copy-start
  36.5 2.7 %shard_map.66 = (f32[2048,128]{1,0:T(8,128)S(1)}, f32[256,128]{1,0:T(8,128)S(1)}) custom-call(f32[512,128]{1,0:T(8,128)S(1)} %bitcast.7, f32[2048,128]{1,0:T(8,128)S(1)} %shard_map.64.series_ref, f32[16,128]{1,0:T(8,128)S(1)} %bitcast.13), custom_call_target="tpu_custom_call" | custom-call | flops 16777216 | bytes 1318912 | tf_op jit(solution)/shard_map/pallas_call | solution.py:121
  39.2 5.1 %all-to-all-done.2 = f32[16,16,128]{2,1,0:T(8,128)S(1)} async-done(((f32[16,16,128]{2,1,0:T(8,128)}), f32[16,16,128]{2,1,0:T(8,128)S(1)}, u32[]{:S(2)}, u32[]{:S(2)}) %all-to-all-start.2) | async-done | bytes 131104 | tf_op jit(solution)/shard_map/all_to_all | solution.py:199
  44.3 0.0 copy-done
  44.3 2.5 %shard_map.68 = bf16[2048,128]{1,0:T(8,128)(2,1)} custom-call(f32[512,128]{1,0:T(8,128)S(1)} %bitcast.8, f32[256,128]{1,0:T(8,128)S(1)} %get-tuple-element.10.weight_ref, f32[256,128]{1,0:T(8,128)S(1)} %bitcast.9, f32[2048,128]{1,0:T(8,128)S(1)} %get-tuple-element.12.local_ref, bf16[2048,128]{1,0:T(8,128)(2,1)S(1)} %copy-done), custom_call_target="tpu_custom_call" | custom-call | flops 8388608 | bytes 2097152 | tf_op jit(solution)/shard_map/pallas_call | solution.py:121
Async XLA Ops:
  0.0 9.8 %copy-start.1 = (bf16[2048,128]{1,0:T(8,128)(2,1)S(1)}, bf16[2048,128]{1,0:T(8,128)(2,1)}, u32[]{:S(2)}) copy-start(bf16[2048,128]{1,0:T(8,128)(2,1)} %k_ref.1) | copy-start | bytes 1572868
  1.5 18.2 %all-to-all-start = ((f32[16,32,128]{2,1,0:T(8,128)}), f32[16,32,128]{2,1,0:T(8,128)S(1)}, u32[]{:S(2)}, u32[]{:S(2)}) async-start(f32[16,32,128]{2,1,0:T(8,128)} %broadcast_in_dim.2), calls=%async_computation | async-start | bytes 524288 | tf_op jit(solution)/shard_map/all_to_all | solution.py:162
  9.8 1.0 %copy-start.2 = (bf16[2048,128]{1,0:T(8,128)(2,1)S(1)}, bf16[2048,128]{1,0:T(8,128)(2,1)}, u32[]{:S(2)}) copy-start(bf16[2048,128]{1,0:T(8,128)(2,1)} %v_ref.1) | copy-start | bytes 1572868
  21.0 11.2 %copy-start.3 = (f32[128,16]{0,1:T(8,128)S(1)}, f32[128,16]{0,1:T(8,128)}, u32[]{:S(2)}) copy-start(f32[128,16]{0,1:T(8,128)} %param.10) | copy-start | bytes 24580
  32.9 3.7 %copy-start.4 = (f32[2048]{0:T(1024)S(1)}, f32[2048]{0:T(1024)}, u32[]{:S(2)}) copy-start(f32[2048]{0:T(1024)} %param.11) | copy-start | bytes 24580
  32.9 11.4 %all-to-all-start.2 = ((f32[16,16,128]{2,1,0:T(8,128)}), f32[16,16,128]{2,1,0:T(8,128)S(1)}, u32[]{:S(2)}, u32[]{:S(2)}) async-start(f32[16,16,128]{2,1,0:T(8,128)} %shard_map.67), calls=%async_computation.2 | async-start | bytes 262144 | tf_op jit(solution)/shard_map/all_to_all | solution.py:199
  36.5 7.8 %copy-start = (bf16[2048,128]{1,0:T(8,128)(2,1)S(1)}, bf16[2048,128]{1,0:T(8,128)(2,1)}, u32[]{:S(2)}) copy-start(bf16[2048,128]{1,0:T(8,128)(2,1)} %q_ref.1) | copy-start | bytes 1572868

commit v6 on v3

--- a/solution.py
+++ b/solution.py
@@ -12,21 +12,17 @@
 VMEM_LIMIT = 32 * 1024 * 1024
 
 
-def prepare_kernel(chunks, k_ref, v_ref, series_ref):
+def mode_rows(ref, base, order, per_chunk, chunks, half):
+    first = half * SUBLANES * per_chunk + base
+    return [ref[pl.ds(first + r, SUBLANES, stride=per_chunk), :] for r in range(order)]
+
+
+def state_kernel(chunks, order, params_ref, k_ref, v_ref, series_ref, state_ref):
     length = k_ref.shape[1]
     for chunk in range(chunks):
         rows = pl.ds(chunk * LANES, LANES)
         gated = k_ref[rows, :].astype(jnp.float32) * v_ref[rows, :].astype(jnp.float32)
         series_ref[pl.ds(chunk, length, stride=chunks), :] = gated.T
-
-
-def mode_rows(ref, base, order, per_chunk, chunks, half):
-    first = half * SUBLANES * per_chunk + base
-    return [ref[pl.ds(first + r, SUBLANES, stride=per_chunk), :] for r in range(order)]
-
-
-def state_kernel(chunks, order, params_ref, series_ref, state_ref):
-    length = series_ref.shape[0] // chunks
     for half in range(chunks // SUBLANES):
         decay = [jnp.exp(-rate) for rate in mode_rows(params_ref, 0, order, 2 * order, chunks, half)]
 
@@ -60,11 +56,20 @@
     return terms[0]
 
 
+def one_minus_exp(y):
+    series = jnp.ones_like(y)
+    for k in range(11, 1, -1):
+        series = 1.0 - (y * (1.0 / k)) * series
+    return jnp.where(y < 0.5, y * series, 1.0 - jnp.exp(-y))
+
+
 def output_kernel(chunks, order, params_ref, series_ref, carry_ref, gain_ref, q_ref, out_ref, conv_ref):
     length = series_ref.shape[0] // chunks
     for half in range(chunks // SUBLANES):
-        decay = [jnp.exp(-rate) for rate in mode_rows(params_ref, 0, order, 2 * order, chunks, half)]
-        weight = mode_rows(params_ref, order, order, 2 * order, chunks, half)
+        rate = mode_rows(params_ref, 0, order, 2 * order, chunks, half)
+        residue = mode_rows(params_ref, order, order, 2 * order, chunks, half)
+        decay = [jnp.exp(-rate[r]) for r in range(order)]
+        weight = [residue[r] * jnp.sqrt(one_minus_exp(2.0 * rate[r])) for r in range(order)]
         carry = mode_rows(carry_ref, 0, order, order, chunks, half)
         gain = gain_ref[pl.ds(half * SUBLANES, SUBLANES), :]
 
@@ -80,10 +85,10 @@
             return tuple(state)
 
         lax.fori_loop(0, length // UNROLL, steps, tuple(carry))
-    for chunk in range(chunks):
-        rows = pl.ds(chunk * LANES, LANES)
-        conv = conv_ref[pl.ds(chunk, length, stride=chunks), :].T
-        out_ref[rows, :] = (q_ref[rows, :].astype(jnp.float32) * conv).astype(jnp.bfloat16)
+        for chunk in range(half * SUBLANES, (half + 1) * SUBLANES):
+            rows = pl.ds(chunk * LANES, LANES)
+            conv = conv_ref[pl.ds(chunk, length, stride=chunks), :].T
+            out_ref[rows, :] = (q_ref[rows, :].astype(jnp.float32) * conv).astype(jnp.bfloat16)
 
 
 def call(kernel, out_shape, *args, scratch=(), flops=0):
@@ -127,25 +132,21 @@
     chunks = channels // LANES
     f32 = jnp.float32
 
-    weights = residues * jnp.sqrt(-jnp.expm1(-2.0 * rates))
     own_rates = rates.T
-    packed = jnp.concatenate([own_rates, weights.T], axis=0)
+    packed = jnp.concatenate([own_rates, residues.T], axis=0)
     copies = jnp.broadcast_to(packed[None], (blocks,) + packed.shape)
     gathered = lax.all_to_all(copies, "seq", split_axis=0, concat_axis=0, tiled=True)
     params = to_chunks(gathered).reshape(chunks * 2 * order, LANES)
 
-    series = call(
-        functools.partial(prepare_kernel, chunks),
-        jax.ShapeDtypeStruct((length * chunks, LANES), f32),
+    series, ends = call(
+        functools.partial(state_kernel, chunks, order),
+        (
+            jax.ShapeDtypeStruct((length * chunks, LANES), f32),
+            jax.ShapeDtypeStruct((chunks * order, LANES), f32),
+        ),
+        params,
         k_proj,
         value_projection,
-        flops=channels * length,
-    )
-    ends = call(
-        functools.partial(state_kernel, chunks, order),
-        jax.ShapeDtypeStruct((chunks * order, LANES), f32),
-        params,
-        series,
         flops=2 * order * channels * length,
     )
     ends = from_chunks(ends.reshape(chunks, order, LANES), blocks)

time: 46.9 us -> 47.6 us (1.015)
  blocking collectives: 21.7 us -> 39.7 us
  waiting for transfers between devices: 8.41 us -> 0 us
  starting transfers between devices: 8.31 us -> 0 us
  local copies, waits for them, and re-layouts: 1.79 us -> 1.08 us
    all_to_all x0 -> x1, blocking collectives: none -> 18 us  [shards(): lax.all_to_all(copies, 'seq', split_axis=0, concat_axis=0, tiled=True)]
    all_to_all x1 -> x0, waiting for transfers between devices: 8.41 us -> none  [shards(): lax.all_to_all(copies, 'seq', split_axis=0, concat_axis=0, tiled=True)]
    all_to_all x1 -> x0, starting transfers between devices: 8.31 us -> none  [shards(): lax.all_to_all(copies, 'seq', split_axis=0, concat_axis=0, tiled=True)]
    transpose x1 -> x0, other arithmetic: 0.79 us -> none  [shards(): packed = jnp.concatenate([own_rates, weights.T], axis=0)]
    concatenate x1, other arithmetic: 0.01 us -> 0.77 us  [shards(): packed = jnp.concatenate([own_rates, residues.T], axis=0)]
    broadcast_in_dim x1, local copies, waits for them, and re-layouts: 0.73 us -> 0.02 us  [shards(): copies = jnp.broadcast_to(packed[None], (blocks,) + packed.shape)]
    pallas_call x4 -> x3, Pallas kernels: 5.45 us -> 5.7 us  [call(): pl.pallas_call(kernel, out_shape=out_shape, in_specs=[vmem] * len(args),...]
  transfers between devices with their start and end apart: 1 -> 0, of which waited for: 1 -> 0; matrix products, arithmetic and copies ran while one was open for 0% -> 0% of each run, Pallas kernels for 1% -> 0%
where the time goes in v6:
time: 47.6 us; the launch traced here: 47.3 us
  blocking collectives  39.7 us (83%)
  Pallas kernels  5.7 us (12%)
  local copies, waits for them, and re-layouts  1.08 us (2%)
  other arithmetic  0.77 us (2%)
    all_to_all x1, blocking collectives, shards(): lax.all_to_all(copies, 'seq', split_axis=0, concat_axis=0, tiled=True)  18 us
    all_to_all x1, blocking collectives, shards(): ends = lax.all_to_all(ends, 'seq', split_axis=0, concat_axis=0, tiled=True)  11.3 us
    all_to_all x1, blocking collectives, shards(): lax.all_to_all(starts, 'seq', split_axis=0, concat_axis=0, tiled=True)  10.4 us
    pallas_call x3, Pallas kernels, call(): pl.pallas_call(kernel, out_shape=out_shape, in_specs=[vmem] * len(args),...  5.7 us
    unnamed x10, local copies, waits for them, and re-layouts  1.06 us

profile of v6, /device:TPU:0, one launch (start us, length us, event | category | flops | bytes accessed | tf_op | source)
XLA Modules:
  0.0 47.3 jit_solution(13122093412223507098)
XLA Ops:
  0.0 0.0 copy-start.1
  0.0 0.8 %pad_maximum_fusion = f32[32,128]{1,0:T(8,128)S(1)} fusion(f32[16,128]{1,0:T(8,128)} %bitcast.13, f32[16,128]{1,0:T(8,128)} %bitcast.10), kind=kLoop, calls=%fused_computation | loop fusion | flops 4096 | bytes 32768 | tf_op jit(solution)/shard_map/concatenate | solution.py:136
  0.8 18.0 %all_to_all.15 = f32[16,32,128]{2,1,0:T(8,128)S(1)} all-to-all(f32[16,32,128]{2,1,0:T(8,128)S(1)} %broadcast_in_dim.2), channel_id=1, replica_groups=mesh['groups'=1,'seq'=16,'chan'=2] {'seq'}, dimensions={0} | all-to-all | bytes 524288 | tf_op jit(solution)/shard_map/all_to_all | solution.py:138
  18.8 0.0 copy-done.1
  18.8 0.0 copy-start.2
  18.8 1.0 %copy-done.2 = bf16[2048,128]{1,0:T(8,128)(2,1)S(1)} copy-done((bf16[2048,128]{1,0:T(8,128)(2,1)S(1)}, bf16[2048,128]{1,0:T(8,128)(2,1)}, u32[]{:S(2)}) %copy-start.2) | copy-done | bytes 524312
  19.8 0.0 copy-start.3
  19.8 1.7 %shard_map.64 = (f32[2048,128]{1,0:T(8,128)S(1)}, f32[256,128]{1,0:T(8,128)S(1)}) custom-call(f32[512,128]{1,0:T(8,128)S(1)} %bitcast.6, bf16[2048,128]{1,0:T(8,128)(2,1)S(1)} %copy-done.1, bf16[2048,128]{1,0:T(8,128)(2,1)S(1)} %copy-done.2), custom_call_target="tpu_custom_call" | custom-call | flops 8388608 | bytes 1310720 | tf_op jit(solution)/shard_map/pallas_call | solution.py:97
  21.6 0.0 copy-start
  21.6 11.3 %all_to_all.16.ends_ref = f32[16,16,128]{2,1,0:T(8,128)S(1)} all-to-all(f32[16,16,128]{2,1,0:T(8,128)S(1)} %bitcast.9), channel_id=1, replica_groups=mesh['groups'=1,'seq'=16,'chan'=2] {'seq'}, dimensions={0} | all-to-all | bytes 262144 | tf_op jit(solution)/shard_map/all_to_all | solution.py:153
  32.8 0.0 copy-done.3
  32.9 0.0 copy-start.4
  32.9 10.4 %all_to_all.17 = f32[16,16,128]{2,1,0:T(8,128)S(1)} all-to-all(f32[16,16,128]{2,1,0:T(8,128)S(1)} %shard_map.65), channel_id=1, replica_groups=mesh['groups'=1,'seq'=16,'chan'=2] {'seq'}, dimensions={0} | all-to-all | bytes 262144 | tf_op jit(solution)/shard_map/all_to_all | solution.py:160
  43.3 0.0 copy-done
  43.3 0.0 copy-done.4
  43.3 3.9 %shard_map.66 = bf16[2048,128]{1,0:T(8,128)(2,1)} custom-call(f32[512,128]{1,0:T(8,128)S(1)} %bitcast.7, f32[2048,128]{1,0:T(8,128)S(1)} %get-tuple-element.7.series_ref, f32[256,128]{1,0:T(8,128)S(1)} %bitcast.8, f32[16,128]{1,0:T(8,128)S(1)} %bitcast.12, bf16[2048,128]{1,0:T(8,128)(2,1)S(1)} %copy-done), custom_call_target="tpu_custom_call" | custom-call | flops 16777216 | bytes 1974272 | tf_op jit(solution)/shard_map/pallas_call | solution.py:97
  (2 shorter events, 0.1 us)
Async XLA Ops:
  0.0 18.8 %copy-start.1 = (bf16[2048,128]{1,0:T(8,128)(2,1)S(1)}, bf16[2048,128]{1,0:T(8,128)(2,1)}, u32[]{:S(2)}) copy-start(bf16[2048,128]{1,0:T(8,128)(2,1)} %k_ref.1) | copy-start | bytes 1572868
  18.8 1.0 %copy-start.2 = (bf16[2048,128]{1,0:T(8,128)(2,1)S(1)}, bf16[2048,128]{1,0:T(8,128)(2,1)}, u32[]{:S(2)}) copy-start(bf16[2048,128]{1,0:T(8,128)(2,1)} %v_ref.1) | copy-start | bytes 1572868
  19.8 13.0 %copy-start.3 = (f32[128,16]{0,1:T(8,128)S(1)}, f32[128,16]{0,1:T(8,128)}, u32[]{:S(2)}) copy-start(f32[128,16]{0,1:T(8,128)} %param.10) | copy-start | bytes 24580
  21.6 21.8 %copy-start = (bf16[2048,128]{1,0:T(8,128)(2,1)S(1)}, bf16[2048,128]{1,0:T(8,128)(2,1)}, u32[]{:S(2)}) copy-start(bf16[2048,128]{1,0:T(8,128)(2,1)} %q_ref.1) | copy-start | bytes 1572868
  32.9 10.4 %copy-start.4 = (f32[2048]{0:T(1024)S(1)}, f32[2048]{0:T(1024)}, u32[]{:S(2)}) copy-start(f32[2048]{0:T(1024)} %param.11) | copy-start | bytes 24580

commit v7 on v6

--- a/solution.py
+++ b/solution.py
@@ -12,19 +12,25 @@
 VMEM_LIMIT = 32 * 1024 * 1024
 
 
-def mode_rows(ref, base, order, per_chunk, chunks, half):
-    first = half * SUBLANES * per_chunk + base
-    return [ref[pl.ds(first + r, SUBLANES, stride=per_chunk), :] for r in range(order)]
-
-
-def state_kernel(chunks, order, params_ref, k_ref, v_ref, series_ref, state_ref):
+def half_rows(half, per_chunk, interleaved):
+    if interleaved:
+        return half * per_chunk, 2 * per_chunk
+    return half * SUBLANES * per_chunk, per_chunk
+
+
+def mode_rows(ref, base, order, per_chunk, half, interleaved):
+    first, stride = half_rows(half, per_chunk, interleaved)
+    return [ref[pl.ds(first + base + r, SUBLANES, stride=stride), :] for r in range(order)]
+
+
+def state_kernel(chunks, order, interleaved, params_ref, k_ref, v_ref, series_ref, state_ref):
     length = k_ref.shape[1]
     for chunk in range(chunks):
         rows = pl.ds(chunk * LANES, LANES)
         gated = k_ref[rows, :].astype(jnp.float32) * v_ref[rows, :].astype(jnp.float32)
         series_ref[pl.ds(chunk, length, stride=chunks), :] = gated.T
     for half in range(chunks // SUBLANES):
-        decay = [jnp.exp(-rate) for rate in mode_rows(params_ref, 0, order, 2 * order, chunks, half)]
+        decay = [jnp.exp(-rate) for rate in mode_rows(params_ref, 0, order, 2 * order, half, interleaved)]
 
         def steps(i, state):
             state = list(state)
@@ -37,16 +43,39 @@
 
         zero = jnp.zeros((SUBLANES, LANES), jnp.float32)
         state = lax.fori_loop(0, length // UNROLL, steps, (zero,) * order)
+        first, stride = half_rows(half, order, interleaved)
         for r in range(order):
-            state_ref[pl.ds(half * SUBLANES * order + r, SUBLANES, stride=order), :] = state[r]
-
-
-def prefix_kernel(length, rate_ref, ends_ref, starts_ref):
-    span_decay = jnp.exp(-float(length) * rate_ref[...])
-    carry = jnp.zeros(rate_ref.shape, jnp.float32)
+            state_ref[pl.ds(first + r, SUBLANES, stride=stride), :] = state[r]
+
+
+def copies_kernel(members, own_ref, other_ref, copies_ref):
+    own, other = own_ref[...], other_ref[...]
+    lower = jnp.broadcast_to(lax.axis_index("seq") < members, own.shape)
+    pair = (jnp.where(lower, own, other), jnp.where(lower, other, own))
+    for member in range(members):
+        for half in range(2):
+            copies_ref[member, half] = pair[half]
+
+
+def span_decay(length, order, rate_ref):
+    rate = rate_ref[0, :, :order, :] if len(rate_ref.shape) == 4 else rate_ref[...]
+    return jnp.exp(-float(length) * rate)
+
+
+def total_kernel(length, rate_ref, ends_ref, total_ref):
+    decay = span_decay(length, ends_ref.shape[-2], rate_ref)
+    total = ends_ref[0]
+    for block in range(1, ends_ref.shape[0]):
+        total = decay * total + ends_ref[block]
+    total_ref[...] = total
+
+
+def prefix_kernel(length, rate_ref, ends_ref, carry_ref, starts_ref):
+    decay = span_decay(length, ends_ref.shape[-2], rate_ref)
+    carry = carry_ref[...]
     for block in range(ends_ref.shape[0]):
         starts_ref[block] = carry
-        carry = span_decay * carry + ends_ref[block]
+        carry = decay * carry + ends_ref[block]
 
 
 def tree_sum(terms):
@@ -63,14 +92,14 @@
     return jnp.where(y < 0.5, y * series, 1.0 - jnp.exp(-y))
 
 
-def output_kernel(chunks, order, params_ref, series_ref, carry_ref, gain_ref, q_ref, out_ref, conv_ref):
+def output_kernel(chunks, order, interleaved, params_ref, series_ref, carry_ref, gain_ref, q_ref, out_ref, conv_ref):
     length = series_ref.shape[0] // chunks
     for half in range(chunks // SUBLANES):
-        rate = mode_rows(params_ref, 0, order, 2 * order, chunks, half)
-        residue = mode_rows(params_ref, order, order, 2 * order, chunks, half)
+        rate = mode_rows(params_ref, 0, order, 2 * order, half, interleaved)
+        residue = mode_rows(params_ref, order, order, 2 * order, half, interleaved)
         decay = [jnp.exp(-rate[r]) for r in range(order)]
         weight = [residue[r] * jnp.sqrt(one_minus_exp(2.0 * rate[r])) for r in range(order)]
-        carry = mode_rows(carry_ref, 0, order, order, chunks, half)
+        carry = mode_rows(carry_ref, 0, order, order, half, interleaved)
         gain = gain_ref[pl.ds(half * SUBLANES, SUBLANES), :]
 
         def steps(i, state):
@@ -126,6 +155,10 @@
     return pieces.reshape(owners, own // LANES, rows, LANES).swapaxes(1, 2).reshape(owners, rows, own)
 
 
+def all_to_all(pieces, groups=None):
+    return lax.all_to_all(pieces, "seq", split_axis=0, concat_axis=0, axis_index_groups=groups, tiled=True)
+
+
 def shards(blocks, q_proj, k_proj, value_projection, residues, rates, direct_gain):
     channels, length = q_proj.shape
     order = residues.shape[1]
@@ -134,12 +167,25 @@
 
     own_rates = rates.T
     packed = jnp.concatenate([own_rates, residues.T], axis=0)
-    copies = jnp.broadcast_to(packed[None], (blocks,) + packed.shape)
-    gathered = lax.all_to_all(copies, "seq", split_axis=0, concat_axis=0, tiled=True)
-    params = to_chunks(gathered).reshape(chunks * 2 * order, LANES)
+    members = blocks // 2
+    halves = blocks == chunks and members == SUBLANES
+    if halves:
+        groups = [list(range(members)), list(range(members, blocks))]
+        other = lax.ppermute(packed, "seq", [(i, (i + members) % blocks) for i in range(blocks)])
+        copies = call(
+            functools.partial(copies_kernel, members),
+            jax.ShapeDtypeStruct((members, 2) + packed.shape, f32),
+            packed,
+            other,
+        )
+        params = all_to_all(copies, groups)
+    else:
+        copies = jnp.broadcast_to(packed[None], (blocks,) + packed.shape)
+        params = to_chunks(all_to_all(copies))
+    params = params.reshape(chunks * 2 * order, LANES)
 
     series, ends = call(
-        functools.partial(state_kernel, chunks, order),
+        functools.partial(state_kernel, chunks, order, halves),
         (
             jax.ShapeDtypeStruct((length * chunks, LANES), f32),
             jax.ShapeDtypeStruct((chunks * order, LANES), f32),
@@ -149,18 +195,34 @@
         value_projection,
         flops=2 * order * channels * length,
     )
-    ends = from_chunks(ends.reshape(chunks, order, LANES), blocks)
-    ends = lax.all_to_all(ends, "seq", split_axis=0, concat_axis=0, tiled=True)
+    if halves:
+        ends = all_to_all(ends.reshape(members, 2, order, LANES), groups)
+        total = call(
+            functools.partial(total_kernel, length),
+            jax.ShapeDtypeStruct(ends.shape[1:], f32),
+            copies,
+            ends,
+        )
+        before = lax.ppermute(total, "seq", [(i, i + members) for i in range(members)])
+        rates_here = copies
+    else:
+        ends = all_to_all(from_chunks(ends.reshape(chunks, order, LANES), blocks))
+        before = jnp.zeros(ends.shape[1:], f32)
+        rates_here = own_rates
     starts = call(
         functools.partial(prefix_kernel, length),
         jax.ShapeDtypeStruct(ends.shape, f32),
-        own_rates,
+        rates_here,
         ends,
-    )
-    starts = lax.all_to_all(starts, "seq", split_axis=0, concat_axis=0, tiled=True)
-    carry = to_chunks(starts).reshape(chunks * order, LANES)
+        before,
+    )
+    if halves:
+        carry = all_to_all(starts, groups)
+    else:
+        carry = to_chunks(all_to_all(starts))
+    carry = carry.reshape(chunks * order, LANES)
     return call(
-        functools.partial(output_kernel, chunks, order),
+        functools.partial(output_kernel, chunks, order, halves),
         jax.ShapeDtypeStruct((channels, length), jnp.bfloat16),
         params,
         series,

time: 47.6 us -> 48.3 us (1.015)
  blocking collectives: 39.7 us -> 28.5 us
  starting transfers between devices: 0 us -> 8.72 us
  waiting for transfers between devices: 0 us -> 3.14 us
    all_to_all x3, blocking collectives: 39.7 us -> 28.5 us  [all_to_all(): lax.all_to_all(pieces, 'seq', split_axis=0, concat_axis=0, axis_index_gro...]
    ppermute x0 -> x2, starting transfers between devices: none -> 8.72 us  [the longest x1 4.69 us: shards(): lax.ppermute(total, 'seq', [(i, i + members) for i in range(members)])]
    ppermute x0 -> x2, waiting for transfers between devices: none -> 3.14 us  [the longest x1 1.72 us: shards(): lax.ppermute(packed, 'seq', [(i, (i + members) % blocks) for i in range(b...]
    pallas_call x3 -> x5, Pallas kernels: 5.7 us -> 5.79 us  [call(): pl.pallas_call(kernel, out_shape=out_shape, in_specs=[vmem] * len(args),...]
    unnamed x10 -> x8, local copies, waits for them, and re-layouts: 1.06 us -> 1.06 us
  transfers between devices with their start and end apart: 0 -> 2, of which waited for: 0 -> 2; matrix products, arithmetic and copies ran while one was open for 0% -> 0% of each run, Pallas kernels for 0% -> 0%
where the time goes in v7:
time: 48.3 us; the launch traced here: 48 us
  blocking collectives  28.5 us (59%)
  starting transfers between devices  8.72 us (18%)
  Pallas kernels  5.79 us (12%)
  waiting for transfers between devices  3.14 us (7%)
  local copies, waits for them, and re-layouts  1.06 us (2%)
  other arithmetic  0.77 us (2%)
    all_to_all x3, blocking collectives, all_to_all(): lax.all_to_all(pieces, 'seq', split_axis=0, concat_axis=0, axis_index_gro...  28.5 us
    pallas_call x5, Pallas kernels, call(): pl.pallas_call(kernel, out_shape=out_shape, in_specs=[vmem] * len(args),...  5.79 us
    ppermute x1, starting transfers between devices, shards(): lax.ppermute(total, 'seq', [(i, i + members) for i in range(members)])  4.69 us
    ppermute x1, starting transfers between devices, shards(): lax.ppermute(packed, 'seq', [(i, (i + members) % blocks) for i in range(b...  4.04 us
    ppermute x1, waiting for transfers between devices, shards(): lax.ppermute(packed, 'seq', [(i, (i + members) % blocks) for i in range(b...  1.72 us
    ppermute x1, waiting for transfers between devices, shards(): lax.ppermute(total, 'seq', [(i, i + members) for i in range(members)])  1.43 us
    unnamed x8, local copies, waits for them, and re-layouts  1.06 us
  transfers between devices with their start and end apart: 2, of which 2 were waited for; matrix products, arithmetic and copies ran while one was open for 0% of the time, Pallas kernels for 0%

profile of v7, /device:TPU:0, one launch (start us, length us, event | category | flops | bytes accessed | tf_op | source)
XLA Modules:
  0.0 48.0 jit_solution(1788790615005544563)
XLA Ops:
  0.0 0.0 copy-start.1
  0.0 0.8 %pad_maximum_fusion.own_ref = f32[32,128]{1,0:T(8,128)S(1)} fusion(f32[16,128]{1,0:T(8,128)} %bitcast.11, f32[16,128]{1,0:T(8,128)} %bitcast.12), kind=kLoop, calls=%fused_computation | loop fusion | flops 4096 | bytes 32768 | tf_op jit(solution)/shard_map/concatenate | solution.py:169
  0.8 4.0 %collective-permute-start = (f32[32,128]{1,0:T(8,128)S(1)}, f32[32,128]{1,0:T(8,128)S(1)}, u32[]{:S(2)}, u32[]{:S(2)}) collective-permute-start(f32[32,128]{1,0:T(8,128)S(1)} %pad_maximum_fusion.own_ref), channel_id=1, source_target_pairs={{0,16},{2,18},{4,20},{6,22},{8,24},{10,26},{12,28},{14,30},{16,0},... | collective-permute-start | bytes 49160 | tf_op jit(solution)/shard_map/ppermute | solution.py:174
  4.8 1.7 %collective-permute-done.other_ref = f32[32,128]{1,0:T(8,128)S(1)} collective-permute-done((f32[32,128]{1,0:T(8,128)S(1)}, f32[32,128]{1,0:T(8,128)S(1)}, u32[]{:S(2)}, u32[]{:S(2)}) %collective-permute-start) | collective-permute-done | bytes 16416 | tf_op jit(solution)/shard_map/ppermute | solution.py:174
  6.6 11.5 %all_to_all.15 = f32[8,2,32,128]{3,2,1,0:T(8,128)S(1)} all-to-all(f32[8,2,32,128]{3,2,1,0:T(8,128)S(1)} %shard_map.64.rate_ref), channel_id=1, replica_groups={{0,2,4,6,8,10,12,14},{16,18,20,22,24,26,28,30},{1,3,5,7,9,11,13,15},{17..., dimensions={0} | all-to-all | bytes 524288 | tf_op jit(solution)/shard_map/all_to_all | solution.py:159
  18.0 0.0 copy-done.1
  18.0 0.0 copy-start.2
  18.0 1.0 %copy-done.2 = bf16[2048,128]{1,0:T(8,128)(2,1)S(1)} copy-done((bf16[2048,128]{1,0:T(8,128)(2,1)S(1)}, bf16[2048,128]{1,0:T(8,128)(2,1)}, u32[]{:S(2)}) %copy-start.2) | copy-done | bytes 524312
  19.1 1.7 %shard_map.65 = (f32[2048,128]{1,0:T(8,128)S(1)}, f32[256,128]{1,0:T(8,128)S(1)}) custom-call(f32[512,128]{1,0:T(8,128)S(1)} %bitcast.6, bf16[2048,128]{1,0:T(8,128)(2,1)S(1)} %copy-done.1, bf16[2048,128]{1,0:T(8,128)(2,1)S(1)} %copy-done.2), custom_call_target="tpu_custom_call" | custom-call | flops 8388608 | bytes 1310720 | tf_op jit(solution)/shard_map/pallas_call | solution.py:126
  20.8 8.5 %all_to_all.16.ends_ref = f32[8,2,16,128]{3,2,1,0:T(8,128)S(1)} all-to-all(f32[8,2,16,128]{3,2,1,0:T(8,128)S(1)} %bitcast.9), channel_id=1, replica_groups={{0,2,4,6,8,10,12,14},{16,18,20,22,24,26,28,30},{1,3,5,7,9,11,13,15},{17..., dimensions={0} | all-to-all | bytes 262144 | tf_op jit(solution)/shard_map/all_to_all | solution.py:159
  29.3 0.0 copy-start
  29.4 4.7 %collective-permute-start.1 = (f32[2,16,128]{2,1,0:T(8,128)S(1)}, f32[2,16,128]{2,1,0:T(8,128)S(1)}, u32[]{:S(2)}, u32[]{:S(2)}) collective-permute-start(f32[2,16,128]{2,1,0:T(8,128)S(1)} %shard_map.66), channel_id=1, source_target_pairs={{0,16},{2,18},{4,20},{6,22},{8,24},{10,26},{12,28},{14,30},{1,17},... | collective-permute-start | bytes 49160 | tf_op jit(solution)/shard_map/ppermute | solution.py:206
  34.0 1.4 %collective-permute-done.1.carry_ref = f32[2,16,128]{2,1,0:T(8,128)S(1)} collective-permute-done((f32[2,16,128]{2,1,0:T(8,128)S(1)}, f32[2,16,128]{2,1,0:T(8,128)S(1)}, u32[]{:S(2)}, u32[]{:S(2)}) %collective-permute-start.1) | collective-permute-done | bytes 16416 | tf_op jit(solution)/shard_map/ppermute | solution.py:206
  35.5 0.0 copy-start.3
  35.5 8.5 %all_to_all.17 = f32[8,2,16,128]{3,2,1,0:T(8,128)S(1)} all-to-all(f32[8,2,16,128]{3,2,1,0:T(8,128)S(1)} %shard_map.67), channel_id=1, replica_groups={{0,2,4,6,8,10,12,14},{16,18,20,22,24,26,28,30},{1,3,5,7,9,11,13,15},{17..., dimensions={0} | all-to-all | bytes 262144 | tf_op jit(solution)/shard_map/all_to_all | solution.py:159
  44.0 0.0 copy-done
  44.0 0.0 copy-done.3
  44.0 4.0 %shard_map.68 = bf16[2048,128]{1,0:T(8,128)(2,1)} custom-call(f32[512,128]{1,0:T(8,128)S(1)} %bitcast.7, f32[2048,128]{1,0:T(8,128)S(1)} %get-tuple-element.7.series_ref, f32[256,128]{1,0:T(8,128)S(1)} %bitcast.8, f32[16,128]{1,0:T(8,128)S(1)} %bitcast.10, bf16[2048,128]{1,0:T(8,128)(2,1)S(1)} %copy-done), custom_call_target="tpu_custom_call" | custom-call | flops 16777216 | bytes 1974272 | tf_op jit(solution)/shard_map/pallas_call | solution.py:126
  (3 shorter events, 0.1 us)
Async XLA Ops:
  0.0 18.0 %copy-start.1 = (bf16[2048,128]{1,0:T(8,128)(2,1)S(1)}, bf16[2048,128]{1,0:T(8,128)(2,1)}, u32[]{:S(2)}) copy-start(bf16[2048,128]{1,0:T(8,128)(2,1)} %k_ref.1) | copy-start | bytes 1572868
  0.8 5.8 %collective-permute-start = (f32[32,128]{1,0:T(8,128)S(1)}, f32[32,128]{1,0:T(8,128)S(1)}, u32[]{:S(2)}, u32[]{:S(2)}) collective-permute-start(f32[32,128]{1,0:T(8,128)S(1)} %pad_maximum_fusion.own_ref), channel_id=1, source_target_pairs={{0,16},{2,18},{4,20},{6,22},{8,24},{10,26},{12,28},{14,30},{16,0},... | collective-permute-start | bytes 49160 | tf_op jit(solution)/shard_map/ppermute | solution.py:174
  18.0 1.0 %copy-start.2 = (bf16[2048,128]{1,0:T(8,128)(2,1)S(1)}, bf16[2048,128]{1,0:T(8,128)(2,1)}, u32[]{:S(2)}) copy-start(bf16[2048,128]{1,0:T(8,128)(2,1)} %v_ref.1) | copy-start | bytes 1572868
  29.3 14.7 %copy-start = (bf16[2048,128]{1,0:T(8,128)(2,1)S(1)}, bf16[2048,128]{1,0:T(8,128)(2,1)}, u32[]{:S(2)}) copy-start(bf16[2048,128]{1,0:T(8,128)(2,1)} %q_ref.1) | copy-start | bytes 1572868
  29.4 6.1 %collective-permute-start.1 = (f32[2,16,128]{2,1,0:T(8,128)S(1)}, f32[2,16,128]{2,1,0:T(8,128)S(1)}, u32[]{:S(2)}, u32[]{:S(2)}) collective-permute-start(f32[2,16,128]{2,1,0:T(8,128)S(1)} %shard_map.66), channel_id=1, source_target_pairs={{0,16},{2,18},{4,20},{6,22},{8,24},{10,26},{12,28},{14,30},{1,17},... | collective-permute-start | bytes 49160 | tf_op jit(solution)/shard_map/ppermute | solution.py:206
  35.5 8.5 %copy-start.3 = (f32[2048]{0:T(1024)S(1)}, f32[2048]{0:T(1024)}, u32[]{:S(2)}) copy-start(f32[2048]{0:T(1024)} %param.11) | copy-start | bytes 24580

commit v8 on v5

--- a/solution.py
+++ b/solution.py
@@ -93,8 +93,22 @@
         lax.fori_loop(0, length // UNROLL, steps, (zero,) * order)
 
 
-def output_kernel(chunks, order, gathered_ref, weight_ref, carry_ref, local_ref, q_ref, out_ref, conv_ref):
+def output_kernel(
+    chunks, order, gathered_ref, weight_ref, carry_ref, local_ref, q_ref, out_ref, conv_ref, gated_ref, sems
+):
     length = local_ref.shape[0] // chunks
+    tokens = length // SUBLANES
+
+    def leave(chunk):
+        rows = pl.ds(pl.multiple_of(chunk * LANES, LANES), LANES)
+        return pltpu.make_async_copy(gated_ref.at[rows, :], out_ref.at[rows, :], sems.at[chunk])
+
+    def finish(chunk):
+        rows = pl.ds(pl.multiple_of(chunk * LANES, LANES), LANES)
+        conv = conv_ref[pl.ds(chunk, length, stride=chunks), :].T
+        gated_ref[rows, :] = (q_ref[rows, :].astype(jnp.float32) * conv).astype(jnp.bfloat16)
+        leave(chunk).start()
+
     for half in range(chunks // SUBLANES):
         decay = [jnp.exp(-rate) for rate in mode_rows(gathered_ref, 0, order, 2 * order, chunks, half)]
         weight = mode_rows(weight_ref, 0, order, order, chunks, half)
@@ -102,27 +116,43 @@
 
         def steps(i, fading):
             fading = list(fading)
-            for u in range(UNROLL):
-                row = pl.multiple_of((i * UNROLL + u) * chunks + half * SUBLANES, SUBLANES)
+            for u in range(tokens):
+                row = pl.multiple_of((i * tokens + u) * chunks + half * SUBLANES, SUBLANES)
                 fading = [decay[r] * fading[r] for r in range(order)]
                 conv_ref[pl.ds(row, SUBLANES), :] = tree_sum(fading + [local_ref[pl.ds(row, SUBLANES), :]])
+            if half > 0:
+                finish((half - 1) * SUBLANES + i)
             return tuple(fading)
 
-        lax.fori_loop(0, length // UNROLL, steps, tuple(weight[r] * carry[r] for r in range(order)))
-        for chunk in range(half * SUBLANES, (half + 1) * SUBLANES):
-            rows = pl.ds(chunk * LANES, LANES)
-            conv = conv_ref[pl.ds(chunk, length, stride=chunks), :].T
-            out_ref[rows, :] = (q_ref[rows, :].astype(jnp.float32) * conv).astype(jnp.bfloat16)
-
-
-def call(kernel, out_shape, *args, scratch=(), flops=0):
+        lax.fori_loop(0, SUBLANES, steps, tuple(weight[r] * carry[r] for r in range(order)))
+    for chunk in range(chunks - SUBLANES, chunks):
+        finish(chunk)
+    for chunk in range(chunks):
+        leave(chunk).wait()
+
+
+def copies_kernel(rate_hbm, residue_hbm, copies_ref, rate_ref, residue_ref, sems):
+    pairs = ((rate_hbm, rate_ref), (residue_hbm, residue_ref))
+    loads = [pltpu.make_async_copy(source, target, sems.at[i]) for i, (source, target) in enumerate(pairs)]
+    for load in loads:
+        load.start()
+    for load in loads:
+        load.wait()
+    order = rate_ref.shape[0]
+    for copy in range(copies_ref.shape[0]):
+        copies_ref[copy, :order] = rate_ref[...]
+        copies_ref[copy, order:] = residue_ref[...]
+
+
+def call(kernel, out_shape, *args, in_space=pltpu.VMEM, out_space=pltpu.VMEM, scratch=(), flops=0):
     in_bytes = sum(a.size * a.dtype.itemsize for a in args)
-    vmem = pl.BlockSpec(memory_space=pltpu.VMEM)
+    in_spec = pl.BlockSpec(memory_space=in_space)
+    out_spec = pl.BlockSpec(memory_space=out_space)
     return pl.pallas_call(
         kernel,
         out_shape=out_shape,
-        in_specs=[vmem] * len(args),
-        out_specs=jax.tree.map(lambda _: vmem, out_shape),
+        in_specs=[in_spec] * len(args),
+        out_specs=jax.tree.map(lambda _: out_spec, out_shape),
         scratch_shapes=list(scratch),
         compiler_params=pltpu.CompilerParams(vmem_limit_bytes=VMEM_LIMIT),
         cost_estimate=pl.CostEstimate(flops=flops, bytes_accessed=in_bytes, transcendentals=0),
@@ -157,8 +187,14 @@
     f32 = jnp.float32
 
     own_rates = rates.T
-    packed = jnp.concatenate([own_rates, residues.T], axis=0)
-    copies = jnp.broadcast_to(packed[None], (blocks,) + packed.shape)
+    copies = call(
+        copies_kernel,
+        pltpu.VMEM((blocks, 2 * order, rates.shape[0]), f32),
+        own_rates,
+        residues.T,
+        in_space=pltpu.HBM,
+        scratch=[pltpu.VMEM(own_rates.shape, f32)] * 2 + [pltpu.SemaphoreType.DMA((2,))],
+    )
     gathered = lax.all_to_all(copies, "seq", split_axis=0, concat_axis=0, tiled=True)
     params = to_chunks(gathered).reshape(chunks * 2 * order, LANES)
 
@@ -192,7 +228,7 @@
     ends = lax.all_to_all(ends, "seq", split_axis=0, concat_axis=0, tiled=True)
     starts = call(
         functools.partial(prefix_kernel, length),
-        jax.ShapeDtypeStruct(ends.shape, f32),
+        pltpu.VMEM(ends.shape, f32),
         own_rates,
         ends,
     )
@@ -206,7 +242,12 @@
         carry,
         local,
         q_proj,
-        scratch=[pltpu.VMEM((length * chunks, LANES), f32)],
+        out_space=pl.ANY,
+        scratch=[
+            pltpu.VMEM((length * chunks, LANES), f32),
+            pltpu.VMEM((channels, length), jnp.bfloat16),
+            pltpu.SemaphoreType.DMA((chunks,)),
+        ],
         flops=2 * order * channels * length,
     )
 

time: 47.3 us -> 48.6 us (1.027)
  Pallas kernels: 7.61 us -> 8.93 us
  other arithmetic: 0.77 us -> 0 us
  local copies, waits for them, and re-layouts: 1.79 us -> 2.51 us
    unnamed x10 -> x14, local copies, waits for them, and re-layouts: 1.06 us -> 2.51 us
    pallas_call x5 -> x6, Pallas kernels: 7.61 us -> 8.93 us  [call(): pl.pallas_call(kernel, out_shape=out_shape, in_specs=[in_spec] * len(args...]
    concatenate x1 -> x0, other arithmetic: 0.77 us -> none  [shards(): packed = jnp.concatenate([own_rates, residues.T], axis=0)]
    broadcast_in_dim x1 -> x0, local copies, waits for them, and re-layouts: 0.73 us -> none  [shards(): copies = jnp.broadcast_to(packed[None], (blocks,) + packed.shape)]
  transfers between devices with their start and end apart: 2 -> 2, of which waited for: 2 -> 2; matrix products, arithmetic and copies ran while one was open for 0% -> 0% of each run, Pallas kernels for 7% -> 6%
where the time goes in v8:
time: 48.6 us; the launch traced here: 48.1 us
  waiting for transfers between devices  13.5 us (28%)
  starting transfers between devices  12 us (25%)
  blocking collectives  11.1 us (23%)
  Pallas kernels  8.93 us (18%)
  local copies, waits for them, and re-layouts  2.51 us (5%)
    all_to_all x1, blocking collectives, shards(): ends = lax.all_to_all(ends, 'seq', split_axis=0, concat_axis=0, tiled=True)  11.1 us
    pallas_call x6, Pallas kernels, call(): pl.pallas_call(kernel, out_shape=out_shape, in_specs=[in_spec] * len(args...  8.93 us
    all_to_all x1, waiting for transfers between devices, shards(): lax.all_to_all(copies, 'seq', split_axis=0, concat_axis=0, tiled=True)  8.41 us
    all_to_all x1, starting transfers between devices, shards(): lax.all_to_all(copies, 'seq', split_axis=0, concat_axis=0, tiled=True)  8.32 us
    all_to_all x1, waiting for transfers between devices, shards(): lax.all_to_all(starts, 'seq', split_axis=0, concat_axis=0, tiled=True)  5.07 us
    all_to_all x1, starting transfers between devices, shards(): lax.all_to_all(starts, 'seq', split_axis=0, concat_axis=0, tiled=True)  3.64 us
    unnamed x14, local copies, waits for them, and re-layouts  2.51 us
  transfers between devices with their start and end apart: 2, of which 2 were waited for; matrix products, arithmetic and copies ran while one was open for 0% of the time, Pallas kernels for 6%

profile of v8, /device:TPU:0, one launch (start us, length us, event | category | flops | bytes accessed | tf_op | source)
XLA Modules:
  0.0 48.1 jit_solution(4376440516585271769)
XLA Ops:
  0.0 0.0 copy-start.1
  0.0 0.0 copy-start.3
  0.0 0.8 %copy-done.3 = f32[128,16]{0,1:T(8,128)S(1)} copy-done((f32[128,16]{0,1:T(8,128)S(1)}, f32[128,16]{0,1:T(8,128)}, u32[]{:S(2)}) %copy-start.3) | copy-done | bytes 8216
  0.8 0.0 copy-start.6
  0.8 0.7 %copy-done.6 = f32[128,16]{0,1:T(8,128)S(1)} copy-done((f32[128,16]{0,1:T(8,128)S(1)}, f32[128,16]{0,1:T(8,128)}, u32[]{:S(2)}) %copy-start.6) | copy-done | bytes 8216
  1.5 0.7 %shard_map.64 = f32[16,32,128]{2,1,0:T(8,128)} custom-call(f32[16,128]{1,0:T(8,128)S(1)} %bitcast.11, f32[16,128]{1,0:T(8,128)S(1)} %bitcast.14), custom_call_target="tpu_custom_call" | custom-call | bytes 16384 | tf_op jit(solution)/shard_map/pallas_call | solution.py:151
  2.2 8.3 %all-to-all-start = ((f32[16,32,128]{2,1,0:T(8,128)}), f32[16,32,128]{2,1,0:T(8,128)S(1)}, u32[]{:S(2)}, u32[]{:S(2)}) async-start(f32[16,32,128]{2,1,0:T(8,128)} %shard_map.64), calls=%async_computation | async-start | bytes 524288 | tf_op jit(solution)/shard_map/all_to_all | solution.py:198
  10.5 0.0 copy-done.1
  10.6 0.0 copy-start.2
  10.6 1.0 %copy-done.2 = bf16[2048,128]{1,0:T(8,128)(2,1)S(1)} copy-done((bf16[2048,128]{1,0:T(8,128)(2,1)S(1)}, bf16[2048,128]{1,0:T(8,128)(2,1)}, u32[]{:S(2)}) %copy-start.2) | copy-done | bytes 524312
  11.6 0.4 shard_map.65.series_ref
  12.0 8.4 %all-to-all-done = f32[16,32,128]{2,1,0:T(8,128)S(1)} async-done(((f32[16,32,128]{2,1,0:T(8,128)}), f32[16,32,128]{2,1,0:T(8,128)S(1)}, u32[]{:S(2)}, u32[]{:S(2)}) %all-to-all-start) | async-done | bytes 262176 | tf_op jit(solution)/shard_map/all_to_all | solution.py:198
  20.4 1.3 %shard_map.66 = f32[256,128]{1,0:T(8,128)S(1)} custom-call(f32[512,128]{1,0:T(8,128)S(1)} %bitcast.6, f32[2048,128]{1,0:T(8,128)S(1)} %shard_map.65.series_ref), custom_call_target="tpu_custom_call" | custom-call | flops 8388608 | bytes 1310720 | tf_op jit(solution)/shard_map/pallas_call | solution.py:151
  21.7 0.0 copy-start.4
  21.7 11.1 %all_to_all.15.ends_ref = f32[16,16,128]{2,1,0:T(8,128)S(1)} all-to-all(f32[16,16,128]{2,1,0:T(8,128)S(1)} %bitcast.10), channel_id=1, replica_groups=mesh['groups'=1,'seq'=16,'chan'=2] {'seq'}, dimensions={0} | all-to-all | bytes 262144 | tf_op jit(solution)/shard_map/all_to_all | solution.py:228
  32.9 0.0 copy-done.4
  32.9 0.7 %shard_map.68 = f32[16,16,128]{2,1,0:T(8,128)} custom-call(f32[16,128]{1,0:T(8,128)S(1)} %bitcast.12, f32[16,16,128]{2,1,0:T(8,128)S(1)} %all_to_all.15.ends_ref), custom_call_target="tpu_custom_call" | custom-call | bytes 139264 | tf_op jit(solution)/shard_map/pallas_call | solution.py:151
  33.6 3.6 %all-to-all-start.2 = ((f32[16,16,128]{2,1,0:T(8,128)}), f32[16,16,128]{2,1,0:T(8,128)S(1)}, u32[]{:S(2)}, u32[]{:S(2)}) async-start(f32[16,16,128]{2,1,0:T(8,128)} %shard_map.68), calls=%async_computation.2 | async-start | bytes 262144 | tf_op jit(solution)/shard_map/all_to_all | solution.py:235
  37.2 0.0 copy-done.5
  37.2 0.0 copy-start
  37.3 2.7 %shard_map.67 = (f32[2048,128]{1,0:T(8,128)S(1)}, f32[256,128]{1,0:T(8,128)S(1)}) custom-call(f32[512,128]{1,0:T(8,128)S(1)} %bitcast.7, f32[2048,128]{1,0:T(8,128)S(1)} %shard_map.65.series_ref, f32[16,128]{1,0:T(8,128)S(1)} %bitcast.13), custom_call_target="tpu_custom_call" | custom-call | flops 16777216 | bytes 1318912 | tf_op jit(solution)/shard_map/pallas_call | solution.py:151
  39.9 5.1 %all-to-all-done.2 = f32[16,16,128]{2,1,0:T(8,128)S(1)} async-done(((f32[16,16,128]{2,1,0:T(8,128)}), f32[16,16,128]{2,1,0:T(8,128)S(1)}, u32[]{:S(2)}, u32[]{:S(2)}) %all-to-all-start.2) | async-done | bytes 131104 | tf_op jit(solution)/shard_map/all_to_all | solution.py:235
  45.0 0.0 copy-done
  45.0 3.1 %shard_map.69 = bf16[2048,128]{1,0:T(8,128)(2,1)} custom-call(f32[512,128]{1,0:T(8,128)S(1)} %bitcast.8, f32[256,128]{1,0:T(8,128)S(1)} %get-tuple-element.10.weight_ref, f32[256,128]{1,0:T(8,128)S(1)} %bitcast.9, f32[2048,128]{1,0:T(8,128)S(1)} %get-tuple-element.12.local_ref, bf16[2048,128]{1,0:T(8,128)(2,1)S(1)} %copy-done), custom_call_target="tpu_custom_call" | custom-call | flops 8388608 | bytes 2097152 | tf_op jit(solution)/shard_map/pallas_call | solution.py:151
  (1 shorter events, 0.0 us)
Async XLA Ops:
  0.0 10.5 %copy-start.1 = (bf16[2048,128]{1,0:T(8,128)(2,1)S(1)}, bf16[2048,128]{1,0:T(8,128)(2,1)}, u32[]{:S(2)}) copy-start(bf16[2048,128]{1,0:T(8,128)(2,1)} %k_ref.1) | copy-start | bytes 1572868
  0.0 0.8 %copy-start.3 = (f32[128,16]{0,1:T(8,128)S(1)}, f32[128,16]{0,1:T(8,128)}, u32[]{:S(2)}) copy-start(f32[128,16]{0,1:T(8,128)} %param.10) | copy-start | bytes 24580
  0.8 0.7 %copy-start.6 = (f32[128,16]{0,1:T(8,128)S(1)}, f32[128,16]{0,1:T(8,128)}, u32[]{:S(2)}) copy-start(f32[128,16]{0,1:T(8,128)} %param.9) | copy-start | bytes 24580
  2.2 18.2 %all-to-all-start = ((f32[16,32,128]{2,1,0:T(8,128)}), f32[16,32,128]{2,1,0:T(8,128)S(1)}, u32[]{:S(2)}, u32[]{:S(2)}) async-start(f32[16,32,128]{2,1,0:T(8,128)} %shard_map.64), calls=%async_computation | async-start | bytes 524288 | tf_op jit(solution)/shard_map/all_to_all | solution.py:198
  10.6 1.0 %copy-start.2 = (bf16[2048,128]{1,0:T(8,128)(2,1)S(1)}, bf16[2048,128]{1,0:T(8,128)(2,1)}, u32[]{:S(2)}) copy-start(bf16[2048,128]{1,0:T(8,128)(2,1)} %v_ref.1) | copy-start | bytes 1572868
  21.7 11.2 %copy-start.4 = (f32[128,16]{0,1:T(8,128)S(1)}, f32[128,16]{0,1:T(8,128)}, u32[]{:S(2)}) copy-start(f32[128,16]{0,1:T(8,128)} %param.10) | copy-start | bytes 24580
  33.6 3.7 %copy-start.5 = (f32[2048]{0:T(1024)S(1)}, f32[2048]{0:T(1024)}, u32[]{:S(2)}) copy-start(f32[2048]{0:T(1024)} %param.11) | copy-start | bytes 24580
  33.6 11.4 %all-to-all-start.2 = ((f32[16,16,128]{2,1,0:T(8,128)}), f32[16,16,128]{2,1,0:T(8,128)S(1)}, u32[]{:S(2)}, u32[]{:S(2)}) async-start(f32[16,16,128]{2,1,0:T(8,128)} %shard_map.68), calls=%async_computation.2 | async-start | bytes 262144 | tf_op jit(solution)/shard_map/all_to_all | solution.py:235
  37.2 7.8 %copy-start = (bf16[2048,128]{1,0:T(8,128)(2,1)S(1)}, bf16[2048,128]{1,0:T(8,128)(2,1)}, u32[]{:S(2)}) copy-start(bf16[2048,128]{1,0:T(8,128)(2,1)} %q_ref.1) | copy-start | bytes 1572868

commit v9 on v5

--- a/solution.py
+++ b/solution.py
@@ -67,7 +67,22 @@
     return jnp.where(y < 0.5, y * series, 1.0 - jnp.exp(-y))
 
 
-def local_kernel(chunks, order, gathered_ref, series_ref, gain_ref, conv_ref, weight_ref):
+def leaving(chunk, gated_ref, out_ref, sems):
+    rows = pl.ds(chunk * LANES, LANES)
+    return pltpu.make_async_copy(gated_ref.at[rows, :], out_ref.at[rows, :], sems.at[chunk])
+
+
+def finish(chunk, chunks, conv_ref, q_ref, gated_ref, out_ref, sems):
+    length = conv_ref.shape[0] // chunks
+    rows = pl.ds(chunk * LANES, LANES)
+    conv = conv_ref[pl.ds(chunk, length, stride=chunks), :].T
+    gated_ref[rows, :] = (q_ref[rows, :].astype(jnp.float32) * conv).astype(jnp.bfloat16)
+    leaving(chunk, gated_ref, out_ref, sems).start()
+
+
+def local_kernel(
+    chunks, order, gathered_ref, series_ref, gain_ref, q_ref, conv_ref, weight_ref, out_ref, gated_ref, sems
+):
     length = series_ref.shape[0] // chunks
     for half in range(chunks // SUBLANES):
         rate = mode_rows(gathered_ref, 0, order, 2 * order, chunks, half)
@@ -92,38 +107,64 @@
         zero = jnp.zeros((SUBLANES, LANES), jnp.float32)
         lax.fori_loop(0, length // UNROLL, steps, (zero,) * order)
 
-
-def output_kernel(chunks, order, gathered_ref, weight_ref, carry_ref, local_ref, q_ref, out_ref, conv_ref):
+    @pl.when(lax.axis_index("seq") == 0)
+    def _():
+        for chunk in range(chunks):
+            finish(chunk, chunks, conv_ref, q_ref, gated_ref, out_ref, sems)
+        for chunk in range(chunks):
+            leaving(chunk, gated_ref, out_ref, sems).wait()
+
+
+def output_kernel(
+    chunks, order, gathered_ref, weight_ref, carry_ref, local_ref, q_ref, _, out_ref, conv_ref, gated_ref, sems
+):
     length = local_ref.shape[0] // chunks
-    for half in range(chunks // SUBLANES):
-        decay = [jnp.exp(-rate) for rate in mode_rows(gathered_ref, 0, order, 2 * order, chunks, half)]
-        weight = mode_rows(weight_ref, 0, order, order, chunks, half)
-        carry = mode_rows(carry_ref, 0, order, order, chunks, half)
-
-        def steps(i, fading):
-            fading = list(fading)
-            for u in range(UNROLL):
-                row = pl.multiple_of((i * UNROLL + u) * chunks + half * SUBLANES, SUBLANES)
-                fading = [decay[r] * fading[r] for r in range(order)]
-                conv_ref[pl.ds(row, SUBLANES), :] = tree_sum(fading + [local_ref[pl.ds(row, SUBLANES), :]])
-            return tuple(fading)
-
-        lax.fori_loop(0, length // UNROLL, steps, tuple(weight[r] * carry[r] for r in range(order)))
-        for chunk in range(half * SUBLANES, (half + 1) * SUBLANES):
-            rows = pl.ds(chunk * LANES, LANES)
-            conv = conv_ref[pl.ds(chunk, length, stride=chunks), :].T
-            out_ref[rows, :] = (q_ref[rows, :].astype(jnp.float32) * conv).astype(jnp.bfloat16)
-
-
-def call(kernel, out_shape, *args, scratch=(), flops=0):
+    tokens = length // SUBLANES
+
+    @pl.when(lax.axis_index("seq") > 0)
+    def _():
+        for half in range(chunks // SUBLANES):
+            decay = [jnp.exp(-rate) for rate in mode_rows(gathered_ref, 0, order, 2 * order, chunks, half)]
+            weight = mode_rows(weight_ref, 0, order, order, chunks, half)
+            carry = mode_rows(carry_ref, 0, order, order, chunks, half)
+
+            def steps(i, fading):
+                fading = list(fading)
+                for u in range(tokens):
+                    row = (i * tokens + u) * chunks + half * SUBLANES
+                    if not isinstance(row, int):
+                        row = pl.multiple_of(row, SUBLANES)
+                    fading = [decay[r] * fading[r] for r in range(order)]
+                    conv_ref[pl.ds(row, SUBLANES), :] = tree_sum(fading + [local_ref[pl.ds(row, SUBLANES), :]])
+                return tuple(fading)
+
+            fading = tuple(weight[r] * carry[r] for r in range(order))
+            if half == 0:
+                lax.fori_loop(0, SUBLANES, steps, fading)
+            else:
+                for i in range(SUBLANES):
+                    fading = steps(i, fading)
+                    finish((half - 1) * SUBLANES + i, chunks, conv_ref, q_ref, gated_ref, out_ref, sems)
+        for chunk in range(chunks - SUBLANES, chunks):
+            finish(chunk, chunks, conv_ref, q_ref, gated_ref, out_ref, sems)
+        for chunk in range(chunks):
+            leaving(chunk, gated_ref, out_ref, sems).wait()
+
+
+def call(kernel, out_shape, *args, out_spaces=None, aliases=None, scratch=(), flops=0):
     in_bytes = sum(a.size * a.dtype.itemsize for a in args)
     vmem = pl.BlockSpec(memory_space=pltpu.VMEM)
+    in_specs = [vmem] * len(args)
+    for i in aliases or {}:
+        in_specs[i] = pl.BlockSpec(memory_space=pl.ANY)
+    out_spaces = out_spaces or jax.tree.map(lambda _: pltpu.VMEM, out_shape)
     return pl.pallas_call(
         kernel,
         out_shape=out_shape,
-        in_specs=[vmem] * len(args),
-        out_specs=jax.tree.map(lambda _: vmem, out_shape),
+        in_specs=in_specs,
+        out_specs=jax.tree.map(lambda space: pl.BlockSpec(memory_space=space), out_spaces),
         scratch_shapes=list(scratch),
+        input_output_aliases=aliases or {},
         compiler_params=pltpu.CompilerParams(vmem_limit_bytes=VMEM_LIMIT),
         cost_estimate=pl.CostEstimate(flops=flops, bytes_accessed=in_bytes, transcendentals=0),
     )(*args)
@@ -157,8 +198,9 @@
     f32 = jnp.float32
 
     own_rates = rates.T
-    packed = jnp.concatenate([own_rates, residues.T], axis=0)
-    copies = jnp.broadcast_to(packed[None], (blocks,) + packed.shape)
+    copies_of = (blocks, 2, order, rates.shape[0])
+    first = lax.broadcasted_iota(jnp.int32, copies_of, 1) == 0
+    copies = jnp.where(first, own_rates, residues.T).reshape(blocks, 2 * order, -1)
     gathered = lax.all_to_all(copies, "seq", split_axis=0, concat_axis=0, tiled=True)
     params = to_chunks(gathered).reshape(chunks * 2 * order, LANES)
 
@@ -178,15 +220,21 @@
     )
     local_series, ends = lax.optimization_barrier((series, ends))
     ends = from_chunks(ends.reshape(chunks, order, LANES), blocks)
-    local, weights = call(
+    out_shape = jax.ShapeDtypeStruct((channels, length), jnp.bfloat16)
+    out_scratch = [pltpu.VMEM(out_shape.shape, out_shape.dtype), pltpu.SemaphoreType.DMA((chunks,))]
+    local, weights, out = call(
         functools.partial(local_kernel, chunks, order),
         (
             jax.ShapeDtypeStruct((length * chunks, LANES), f32),
             jax.ShapeDtypeStruct((chunks * order, LANES), f32),
+            out_shape,
         ),
         params,
         local_series,
         direct_gain.reshape(chunks, LANES),
+        q_proj,
+        out_spaces=(pltpu.VMEM, pltpu.VMEM, pl.ANY),
+        scratch=out_scratch,
         flops=4 * order * channels * length,
     )
     ends = lax.all_to_all(ends, "seq", split_axis=0, concat_axis=0, tiled=True)
@@ -200,13 +248,16 @@
     carry = to_chunks(starts).reshape(chunks * order, LANES)
     return call(
         functools.partial(output_kernel, chunks, order),
-        jax.ShapeDtypeStruct((channels, length), jnp.bfloat16),
+        out_shape,
         params,
         weights,
         carry,
         local,
         q_proj,
-        scratch=[pltpu.VMEM((length * chunks, LANES), f32)],
+        out,
+        out_spaces=pl.ANY,
+        aliases={5: 0},
+        scratch=[pltpu.VMEM((length * chunks, LANES), f32)] + out_scratch,
         flops=2 * order * channels * length,
     )
 

time: 47.3 us -> 46.3 us (0.979)
  the two profiles are of different devices: /device:TPU:0 before, /device:TPU:2 now
where the time goes in v9:
time: 46.3 us; the launch traced here: 45.8 us
  starting transfers between devices  11.7 us (25%)
  blocking collectives  11.6 us (25%)
  waiting for transfers between devices  11.5 us (25%)
  Pallas kernels  7.65 us (17%)
  local copies, waits for them, and re-layouts  2.61 us (6%)
  other arithmetic  0.8 us (2%)
    all_to_all x1, blocking collectives, shards(): ends = lax.all_to_all(ends, 'seq', split_axis=0, concat_axis=0, tiled=True)  11.6 us
    pallas_call x5, Pallas kernels, call(): pl.pallas_call(kernel, out_shape=out_shape, in_specs=in_specs, out_specs=...  7.65 us
    all_to_all x1, starting transfers between devices, shards(): lax.all_to_all(copies, 'seq', split_axis=0, concat_axis=0, tiled=True)  7.31 us
    all_to_all x1, waiting for transfers between devices, shards(): lax.all_to_all(copies, 'seq', split_axis=0, concat_axis=0, tiled=True)  7.26 us
    all_to_all x1, starting transfers between devices, shards(): lax.all_to_all(starts, 'seq', split_axis=0, concat_axis=0, tiled=True)  4.36 us
    all_to_all x1, waiting for transfers between devices, shards(): lax.all_to_all(starts, 'seq', split_axis=0, concat_axis=0, tiled=True)  4.2 us
    broadcast_in_dim x2, local copies, waits for them, and re-layouts, shards(): jnp.where(first, own_rates, residues.T).reshape(blocks, 2 * order, -1)  1.4 us
    unnamed x10, local copies, waits for them, and re-layouts  1.05 us
  transfers between devices with their start and end apart: 2, of which 2 were waited for; matrix products, arithmetic and copies ran while one was open for 0% of the time, Pallas kernels for 7%

profile of v9, /device:TPU:2, one launch (start us, length us, event | category | flops | bytes accessed | tf_op | source)
XLA Modules:
  0.0 45.8 jit_solution(11836081909874069256)
XLA Ops:
  0.0 0.0 copy-start.1
  0.0 0.1 iota.11
  0.1 0.1 iota.12
  0.2 0.7 %broadcast_in_dim.19 = f32[2,16,128]{2,1,0:T(8,128)S(1)} broadcast(f32[16,128]{1,0:T(8,128)} %bitcast.18), dimensions={1,2} | broadcast | bytes 24576 | tf_op jit(solution)/shard_map/jit(_where)/broadcast_in_dim | solution.py:203
  0.9 0.7 %broadcast_in_dim.16 = f32[2,16,128]{2,1,0:T(8,128)S(1)} broadcast(f32[16,128]{1,0:T(8,128)} %bitcast.13), dimensions={1,2} | broadcast | bytes 24576 | tf_op jit(solution)/shard_map/jit(_where)/broadcast_in_dim | solution.py:203
  1.6 0.8 %broadcast_select_fusion = f32[16,32,128]{2,1,0:T(8,128)} fusion(f32[32,128]{1,0:T(8,128)S(1)} %bitcast.16, f32[32,128]{1,0:T(8,128)S(1)} %bitcast.17, pred[32]{0:T(512)(128)(4,1)S(1)} %iota.12), kind=kLoop, calls=%fused_computation | loop fusion | flops 65536 | bytes 294944 | tf_op jit(solution)/shard_map/jit(_where)/select_n | solution.py:203
  2.4 7.3 %all-to-all-start = ((f32[16,32,128]{2,1,0:T(8,128)}), f32[16,32,128]{2,1,0:T(8,128)S(1)}, u32[]{:S(2)}, u32[]{:S(2)}) async-start(f32[16,32,128]{2,1,0:T(8,128)} %broadcast_select_fusion), calls=%async_computation | async-start | bytes 524288 | tf_op jit(solution)/shard_map/all_to_all | solution.py:204
  9.7 0.0 copy-done.1
  9.7 0.0 copy-start.2
  9.7 1.0 %copy-done.2 = bf16[2048,128]{1,0:T(8,128)(2,1)S(1)} copy-done((bf16[2048,128]{1,0:T(8,128)(2,1)S(1)}, bf16[2048,128]{1,0:T(8,128)(2,1)}, u32[]{:S(2)}) %copy-start.2) | copy-done | bytes 524312
  10.7 0.4 shard_map.64.series_ref
  11.1 7.3 %all-to-all-done = f32[16,32,128]{2,1,0:T(8,128)S(1)} async-done(((f32[16,32,128]{2,1,0:T(8,128)}), f32[16,32,128]{2,1,0:T(8,128)S(1)}, u32[]{:S(2)}, u32[]{:S(2)}) %all-to-all-start) | async-done | bytes 262176 | tf_op jit(solution)/shard_map/all_to_all | solution.py:204
  18.4 0.0 copy-start.3
  18.4 1.3 %shard_map.65 = f32[256,128]{1,0:T(8,128)S(1)} custom-call(f32[512,128]{1,0:T(8,128)S(1)} %bitcast.8, f32[2048,128]{1,0:T(8,128)S(1)} %shard_map.64.series_ref), custom_call_target="tpu_custom_call" | custom-call | flops 8388608 | bytes 1310720 | tf_op jit(solution)/shard_map/pallas_call | solution.py:161
  19.7 0.0 copy-start
  19.7 11.6 %all_to_all.15.ends_ref = f32[16,16,128]{2,1,0:T(8,128)S(1)} all-to-all(f32[16,16,128]{2,1,0:T(8,128)S(1)} %bitcast.12), channel_id=1, replica_groups=mesh['groups'=1,'seq'=16,'chan'=2] {'seq'}, dimensions={0} | all-to-all | bytes 262144 | tf_op jit(solution)/shard_map/all_to_all | solution.py:240
  31.3 0.0 copy-done.3
  31.3 0.7 %shard_map.67 = f32[16,16,128]{2,1,0:T(8,128)} custom-call(f32[16,128]{1,0:T(8,128)S(1)} %bitcast.14, f32[16,16,128]{2,1,0:T(8,128)S(1)} %all_to_all.15.ends_ref), custom_call_target="tpu_custom_call" | custom-call | bytes 139264 | tf_op jit(solution)/shard_map/pallas_call | solution.py:161
  32.0 4.4 %all-to-all-start.2 = ((f32[16,16,128]{2,1,0:T(8,128)}), f32[16,16,128]{2,1,0:T(8,128)S(1)}, u32[]{:S(2)}, u32[]{:S(2)}) async-start(f32[16,16,128]{2,1,0:T(8,128)} %shard_map.67), calls=%async_computation.2 | async-start | bytes 262144 | tf_op jit(solution)/shard_map/all_to_all | solution.py:247
  36.4 0.0 copy-done
  36.4 0.0 copy-done.4
  36.4 2.8 %shard_map.66 = (f32[2048,128]{1,0:T(8,128)S(1)}, f32[256,128]{1,0:T(8,128)S(1)}, bf16[2048,128]{1,0:T(8,128)(2,1)}) custom-call(f32[512,128]{1,0:T(8,128)S(1)} %bitcast.9, f32[2048,128]{1,0:T(8,128)S(1)} %shard_map.64.series_ref, f32[16,128]{1,0:T(8,128)S(1)} %bitcast.15, bf16[2048,128]{1,0:T(8,128)(2,1)S(1)} %copy-done), custom_call_target="tpu_custom_call" | custom-call | flops 16777216 | bytes 1843200 | tf_op jit(solution)/shard_map/pallas_call | solution.py:161
  39.2 4.2 %all-to-all-done.2 = f32[16,16,128]{2,1,0:T(8,128)S(1)} async-done(((f32[16,16,128]{2,1,0:T(8,128)}), f32[16,16,128]{2,1,0:T(8,128)S(1)}, u32[]{:S(2)}, u32[]{:S(2)}) %all-to-all-start.2) | async-done | bytes 131104 | tf_op jit(solution)/shard_map/all_to_all | solution.py:247
  43.4 2.4 %shard_map.68 = bf16[2048,128]{1,0:T(8,128)(2,1)} custom-call(f32[512,128]{1,0:T(8,128)S(1)} %bitcast.10, f32[256,128]{1,0:T(8,128)S(1)} %get-tuple-element.11.weight_ref, f32[256,128]{1,0:T(8,128)S(1)} %bitcast.11, f32[2048,128]{1,0:T(8,128)S(1)} %get-tuple-element.13.local_ref, bf16[2048,128]{1,0:T(8,128)(2,1)S(1)} %copy-done, ...), custom_call_target="tpu_custom_call", output_to_operand_aliasing={{}: (5, {})} | custom-call | flops 8388608 | bytes 2621440 | tf_op jit(solution)/shard_map/pallas_call | solution.py:161
  (2 shorter events, 0.0 us)
Async XLA Ops:
  0.0 9.7 %copy-start.1 = (bf16[2048,128]{1,0:T(8,128)(2,1)S(1)}, bf16[2048,128]{1,0:T(8,128)(2,1)}, u32[]{:S(2)}) copy-start(bf16[2048,128]{1,0:T(8,128)(2,1)} %k_ref.1) | copy-start | bytes 1572868
  2.4 16.0 %all-to-all-start = ((f32[16,32,128]{2,1,0:T(8,128)}), f32[16,32,128]{2,1,0:T(8,128)S(1)}, u32[]{:S(2)}, u32[]{:S(2)}) async-start(f32[16,32,128]{2,1,0:T(8,128)} %broadcast_select_fusion), calls=%async_computation | async-start | bytes 524288 | tf_op jit(solution)/shard_map/all_to_all | solution.py:204
  9.7 1.0 %copy-start.2 = (bf16[2048,128]{1,0:T(8,128)(2,1)S(1)}, bf16[2048,128]{1,0:T(8,128)(2,1)}, u32[]{:S(2)}) copy-start(bf16[2048,128]{1,0:T(8,128)(2,1)} %v_ref.1) | copy-start | bytes 1572868
  18.4 12.9 %copy-start.3 = (f32[128,16]{0,1:T(8,128)S(1)}, f32[128,16]{0,1:T(8,128)}, u32[]{:S(2)}) copy-start(f32[128,16]{0,1:T(8,128)} %param.10) | copy-start | bytes 24580
  19.7 16.7 %copy-start = (bf16[2048,128]{1,0:T(8,128)(2,1)S(1)}, bf16[2048,128]{1,0:T(8,128)(2,1)}, u32[]{:S(2)}) copy-start(bf16[2048,128]{1,0:T(8,128)(2,1)} %q_ref.3) | copy-start | bytes 1572868
  32.0 4.4 %copy-start.4 = (f32[2048]{0:T(1024)S(1)}, f32[2048]{0:T(1024)}, u32[]{:S(2)}) copy-start(f32[2048]{0:T(1024)} %param.11) | copy-start | bytes 24580
  32.0 11.4 %all-to-all-start.2 = ((f32[16,16,128]{2,1,0:T(8,128)}), f32[16,16,128]{2,1,0:T(8,128)S(1)}, u32[]{:S(2)}, u32[]{:S(2)}) async-start(f32[16,16,128]{2,1,0:T(8,128)} %shard_map.67), calls=%async_computation.2 | async-start | bytes 262144 | tf_op jit(solution)/shard_map/all_to_all | solution.py:247

commit v10 on v9

--- a/solution.py
+++ b/solution.py
@@ -151,17 +151,27 @@
             leaving(chunk, gated_ref, out_ref, sems).wait()
 
 
-def call(kernel, out_shape, *args, out_spaces=None, aliases=None, scratch=(), flops=0):
+def copies_kernel(rate_ref, residue_ref, copies_ref, sems):
+    order = rate_ref.shape[0]
+    copies = []
+    for piece in range(copies_ref.shape[0]):
+        for part, source in enumerate((rate_ref, residue_ref)):
+            target = copies_ref.at[piece, pl.ds(part * order, order)]
+            copies.append(pltpu.make_async_copy(source, target, sems.at[piece, part]))
+    for copy in copies:
+        copy.start()
+    for copy in copies:
+        copy.wait()
+
+
+def call(kernel, out_shape, *args, in_spaces=None, out_spaces=None, aliases=None, scratch=(), flops=0):
     in_bytes = sum(a.size * a.dtype.itemsize for a in args)
-    vmem = pl.BlockSpec(memory_space=pltpu.VMEM)
-    in_specs = [vmem] * len(args)
-    for i in aliases or {}:
-        in_specs[i] = pl.BlockSpec(memory_space=pl.ANY)
+    in_spaces = in_spaces or [pl.ANY if i in (aliases or {}) else pltpu.VMEM for i in range(len(args))]
     out_spaces = out_spaces or jax.tree.map(lambda _: pltpu.VMEM, out_shape)
     return pl.pallas_call(
         kernel,
         out_shape=out_shape,
-        in_specs=in_specs,
+        in_specs=[pl.BlockSpec(memory_space=space) for space in in_spaces],
         out_specs=jax.tree.map(lambda space: pl.BlockSpec(memory_space=space), out_spaces),
         scratch_shapes=list(scratch),
         input_output_aliases=aliases or {},
@@ -198,9 +208,15 @@
     f32 = jnp.float32
 
     own_rates = rates.T
-    copies_of = (blocks, 2, order, rates.shape[0])
-    first = lax.broadcasted_iota(jnp.int32, copies_of, 1) == 0
-    copies = jnp.where(first, own_rates, residues.T).reshape(blocks, 2 * order, -1)
+    in_hbm = [pltpu.with_memory_space_constraint(array, pltpu.HBM) for array in (own_rates, residues.T)]
+    copies = call(
+        copies_kernel,
+        jax.ShapeDtypeStruct((blocks, 2 * order, rates.shape[0]), f32),
+        *in_hbm,
+        in_spaces=[pl.ANY] * 2,
+        out_spaces=pl.ANY,
+        scratch=[pltpu.SemaphoreType.DMA((blocks, 2))],
+    )
     gathered = lax.all_to_all(copies, "seq", split_axis=0, concat_axis=0, tiled=True)
     params = to_chunks(gathered).reshape(chunks * 2 * order, LANES)
 

time: 46.3 us -> 53.2 us (1.15)
  Pallas kernels: 7.65 us -> 17 us
  local copies, waits for them, and re-layouts: 2.61 us -> 1.05 us
  other arithmetic: 0.8 us -> 0 us
    pallas_call x5 -> x6, Pallas kernels: 7.65 us -> 17 us  [call(): pl.pallas_call(kernel, out_shape=out_shape, in_specs=[pl.BlockSpec(memory...]
    broadcast_in_dim x2 -> x0, local copies, waits for them, and re-layouts: 1.4 us -> none  [shards(): jnp.where(first, own_rates, residues.T).reshape(blocks, 2 * order, -1)]
    select_n x1 -> x0, other arithmetic: 0.8 us -> none  [shards(): jnp.where(first, own_rates, residues.T).reshape(blocks, 2 * order, -1)]
  transfers between devices with their start and end apart: 2 -> 2, of which waited for: 2 -> 2; matrix products, arithmetic and copies ran while one was open for 0% -> 0% of each run, Pallas kernels for 7% -> 6%
where the time goes in v10:
time: 53.2 us; the launch traced here: 52.8 us
  Pallas kernels  17 us (32%)
  starting transfers between devices  11.7 us (22%)
  blocking collectives  11.6 us (22%)
  waiting for transfers between devices  11.5 us (22%)
  local copies, waits for them, and re-layouts  1.05 us (2%)
    pallas_call x6, Pallas kernels, call(): pl.pallas_call(kernel, out_shape=out_shape, in_specs=[pl.BlockSpec(memory...  17 us
    all_to_all x1, blocking collectives, shards(): ends = lax.all_to_all(ends, 'seq', split_axis=0, concat_axis=0, tiled=True)  11.6 us
    all_to_all x1, starting transfers between devices, shards(): lax.all_to_all(copies, 'seq', split_axis=0, concat_axis=0, tiled=True)  7.32 us
    all_to_all x1, waiting for transfers between devices, shards(): lax.all_to_all(copies, 'seq', split_axis=0, concat_axis=0, tiled=True)  7.26 us
    all_to_all x1, starting transfers between devices, shards(): lax.all_to_all(starts, 'seq', split_axis=0, concat_axis=0, tiled=True)  4.36 us
    all_to_all x1, waiting for transfers between devices, shards(): lax.all_to_all(starts, 'seq', split_axis=0, concat_axis=0, tiled=True)  4.2 us
  transfers between devices with their start and end apart: 2, of which 2 were waited for; matrix products, arithmetic and copies ran while one was open for 0% of the time, Pallas kernels for 6%

profile of v10, /device:TPU:2, one launch (start us, length us, event | category | flops | bytes accessed | tf_op | source)
XLA Modules:
  0.0 52.8 jit_solution(14724759778234299067)
XLA Ops:
  0.0 0.0 copy-start.1
  0.0 9.3 %shard_map.64 = f32[16,32,128]{2,1,0:T(8,128)} custom-call(f32[16,128]{1,0:T(8,128)} %bitcast.11, f32[16,128]{1,0:T(8,128)} %bitcast.14), custom_call_target="tpu_custom_call" | custom-call | bytes 16384 | tf_op jit(solution)/shard_map/pallas_call | solution.py:171
  9.3 7.3 %all-to-all-start = ((f32[16,32,128]{2,1,0:T(8,128)}), f32[16,32,128]{2,1,0:T(8,128)S(1)}, u32[]{:S(2)}, u32[]{:S(2)}) async-start(f32[16,32,128]{2,1,0:T(8,128)} %shard_map.64), calls=%async_computation | async-start | bytes 524288 | tf_op jit(solution)/shard_map/all_to_all | solution.py:220
  16.7 0.0 copy-done.1
  16.7 0.0 copy-start.2
  16.7 1.0 %copy-done.2 = bf16[2048,128]{1,0:T(8,128)(2,1)S(1)} copy-done((bf16[2048,128]{1,0:T(8,128)(2,1)S(1)}, bf16[2048,128]{1,0:T(8,128)(2,1)}, u32[]{:S(2)}) %copy-start.2) | copy-done | bytes 524312
  17.7 0.4 shard_map.65.series_ref
  18.1 7.3 %all-to-all-done = f32[16,32,128]{2,1,0:T(8,128)S(1)} async-done(((f32[16,32,128]{2,1,0:T(8,128)}), f32[16,32,128]{2,1,0:T(8,128)S(1)}, u32[]{:S(2)}, u32[]{:S(2)}) %all-to-all-start) | async-done | bytes 262176 | tf_op jit(solution)/shard_map/all_to_all | solution.py:220
  25.4 0.0 copy-start.3
  25.4 1.3 %shard_map.66 = f32[256,128]{1,0:T(8,128)S(1)} custom-call(f32[512,128]{1,0:T(8,128)S(1)} %bitcast.6, f32[2048,128]{1,0:T(8,128)S(1)} %shard_map.65.series_ref), custom_call_target="tpu_custom_call" | custom-call | flops 8388608 | bytes 1310720 | tf_op jit(solution)/shard_map/pallas_call | solution.py:171
  26.7 0.0 copy-start
  26.7 11.6 %all_to_all.15.ends_ref = f32[16,16,128]{2,1,0:T(8,128)S(1)} all-to-all(f32[16,16,128]{2,1,0:T(8,128)S(1)} %bitcast.10), channel_id=1, replica_groups=mesh['groups'=1,'seq'=16,'chan'=2] {'seq'}, dimensions={0} | all-to-all | bytes 262144 | tf_op jit(solution)/shard_map/all_to_all | solution.py:256
  38.3 0.0 copy-done.3
  38.3 0.7 %shard_map.68 = f32[16,16,128]{2,1,0:T(8,128)} custom-call(f32[16,128]{1,0:T(8,128)S(1)} %bitcast.12, f32[16,16,128]{2,1,0:T(8,128)S(1)} %all_to_all.15.ends_ref), custom_call_target="tpu_custom_call" | custom-call | bytes 139264 | tf_op jit(solution)/shard_map/pallas_call | solution.py:171
  39.0 0.0 copy-start.4
  39.0 4.4 %all-to-all-start.2 = ((f32[16,16,128]{2,1,0:T(8,128)}), f32[16,16,128]{2,1,0:T(8,128)S(1)}, u32[]{:S(2)}, u32[]{:S(2)}) async-start(f32[16,16,128]{2,1,0:T(8,128)} %shard_map.68), calls=%async_computation.2 | async-start | bytes 262144 | tf_op jit(solution)/shard_map/all_to_all | solution.py:263
  43.4 0.0 copy-done
  43.4 0.0 copy-done.4
  43.4 2.8 %shard_map.67 = (f32[2048,128]{1,0:T(8,128)S(1)}, f32[256,128]{1,0:T(8,128)S(1)}, bf16[2048,128]{1,0:T(8,128)(2,1)}) custom-call(f32[512,128]{1,0:T(8,128)S(1)} %bitcast.7, f32[2048,128]{1,0:T(8,128)S(1)} %shard_map.65.series_ref, f32[16,128]{1,0:T(8,128)S(1)} %bitcast.13, bf16[2048,128]{1,0:T(8,128)(2,1)S(1)} %copy-done), custom_call_target="tpu_custom_call" | custom-call | flops 16777216 | bytes 1843200 | tf_op jit(solution)/shard_map/pallas_call | solution.py:171
  46.2 4.2 %all-to-all-done.2 = f32[16,16,128]{2,1,0:T(8,128)S(1)} async-done(((f32[16,16,128]{2,1,0:T(8,128)}), f32[16,16,128]{2,1,0:T(8,128)S(1)}, u32[]{:S(2)}, u32[]{:S(2)}) %all-to-all-start.2) | async-done | bytes 131104 | tf_op jit(solution)/shard_map/all_to_all | solution.py:263
  50.4 2.4 %shard_map.69 = bf16[2048,128]{1,0:T(8,128)(2,1)} custom-call(f32[512,128]{1,0:T(8,128)S(1)} %bitcast.8, f32[256,128]{1,0:T(8,128)S(1)} %get-tuple-element.11.weight_ref, f32[256,128]{1,0:T(8,128)S(1)} %bitcast.9, f32[2048,128]{1,0:T(8,128)S(1)} %get-tuple-element.13.local_ref, bf16[2048,128]{1,0:T(8,128)(2,1)S(1)} %copy-done, ...), custom_call_target="tpu_custom_call", output_to_operand_aliasing={{}: (5, {})} | custom-call | flops 8388608 | bytes 2621440 | tf_op jit(solution)/shard_map/pallas_call | solution.py:171
Async XLA Ops:
  0.0 16.7 %copy-start.1 = (bf16[2048,128]{1,0:T(8,128)(2,1)S(1)}, bf16[2048,128]{1,0:T(8,128)(2,1)}, u32[]{:S(2)}) copy-start(bf16[2048,128]{1,0:T(8,128)(2,1)} %k_ref.1) | copy-start | bytes 1572868
  9.3 16.0 %all-to-all-start = ((f32[16,32,128]{2,1,0:T(8,128)}), f32[16,32,128]{2,1,0:T(8,128)S(1)}, u32[]{:S(2)}, u32[]{:S(2)}) async-start(f32[16,32,128]{2,1,0:T(8,128)} %shard_map.64), calls=%async_computation | async-start | bytes 524288 | tf_op jit(solution)/shard_map/all_to_all | solution.py:220
  16.7 1.0 %copy-start.2 = (bf16[2048,128]{1,0:T(8,128)(2,1)S(1)}, bf16[2048,128]{1,0:T(8,128)(2,1)}, u32[]{:S(2)}) copy-start(bf16[2048,128]{1,0:T(8,128)(2,1)} %v_ref.1) | copy-start | bytes 1572868
  25.4 12.9 %copy-start.3 = (f32[128,16]{0,1:T(8,128)S(1)}, f32[128,16]{0,1:T(8,128)}, u32[]{:S(2)}) copy-start(f32[128,16]{0,1:T(8,128)} %param.10) | copy-start | bytes 24580
  26.7 16.7 %copy-start = (bf16[2048,128]{1,0:T(8,128)(2,1)S(1)}, bf16[2048,128]{1,0:T(8,128)(2,1)}, u32[]{:S(2)}) copy-start(bf16[2048,128]{1,0:T(8,128)(2,1)} %q_ref.3) | copy-start | bytes 1572868
  39.0 4.4 %copy-start.4 = (f32[2048]{0:T(1024)S(1)}, f32[2048]{0:T(1024)}, u32[]{:S(2)}) copy-start(f32[2048]{0:T(1024)} %param.11) | copy-start | bytes 24580
  39.0 11.4 %all-to-all-start.2 = ((f32[16,16,128]{2,1,0:T(8,128)}), f32[16,16,128]{2,1,0:T(8,128)S(1)}, u32[]{:S(2)}, u32[]{:S(2)}) async-start(f32[16,16,128]{2,1,0:T(8,128)} %shard_map.68), calls=%async_computation.2 | async-start | bytes 262144 | tf_op jit(solution)/shard_map/all_to_all | solution.py:263

commit v11 on v10

--- a/solution.py
+++ b/solution.py
@@ -12,10 +12,10 @@
 VMEM_LIMIT = 32 * 1024 * 1024
 
 
-def prepare_kernel(chunks, k_ref, v_ref, series_ref):
-    length = k_ref.shape[1]
-    for chunk in range(chunks):
-        rows = pl.ds(chunk * LANES, LANES)
+def prepare_kernel(places, k_ref, v_ref, series_ref):
+    chunks, length = len(places), k_ref.shape[1]
+    for chunk, place in enumerate(places):
+        rows = pl.ds(place * LANES, LANES)
         gated = k_ref[rows, :].astype(jnp.float32) * v_ref[rows, :].astype(jnp.float32)
         series_ref[pl.ds(chunk, length, stride=chunks), :] = gated.T
 
@@ -45,12 +45,12 @@
             state_ref[pl.ds(half * SUBLANES * order + r, SUBLANES, stride=order), :] = state[r]
 
 
-def prefix_kernel(length, rate_ref, ends_ref, starts_ref):
+def prefix_kernel(length, members, rate_ref, ends_ref, starts_ref):
     span_decay = jnp.exp(-float(length) * rate_ref[...])
     carry = jnp.zeros(rate_ref.shape, jnp.float32)
-    for block in range(ends_ref.shape[0]):
-        starts_ref[block] = carry
-        carry = span_decay * carry + ends_ref[block]
+    for block in range(len(members)):
+        starts_ref[members.index(block)] = carry
+        carry = span_decay * carry + ends_ref[members.index(block)]
 
 
 def tree_sum(terms):
@@ -67,22 +67,24 @@
     return jnp.where(y < 0.5, y * series, 1.0 - jnp.exp(-y))
 
 
-def leaving(chunk, gated_ref, out_ref, sems):
-    rows = pl.ds(chunk * LANES, LANES)
+def leaving(chunk, places, gated_ref, out_ref, sems):
+    rows = pl.ds(places[chunk] * LANES, LANES)
     return pltpu.make_async_copy(gated_ref.at[rows, :], out_ref.at[rows, :], sems.at[chunk])
 
 
-def finish(chunk, chunks, conv_ref, q_ref, gated_ref, out_ref, sems):
+def finish(chunk, places, conv_ref, q_ref, gated_ref, out_ref, sems):
+    chunks = len(places)
     length = conv_ref.shape[0] // chunks
-    rows = pl.ds(chunk * LANES, LANES)
+    rows = pl.ds(places[chunk] * LANES, LANES)
     conv = conv_ref[pl.ds(chunk, length, stride=chunks), :].T
     gated_ref[rows, :] = (q_ref[rows, :].astype(jnp.float32) * conv).astype(jnp.bfloat16)
-    leaving(chunk, gated_ref, out_ref, sems).start()
+    leaving(chunk, places, gated_ref, out_ref, sems).start()
 
 
 def local_kernel(
-    chunks, order, gathered_ref, series_ref, gain_ref, q_ref, conv_ref, weight_ref, out_ref, gated_ref, sems
+    places, order, gathered_ref, series_ref, gain_ref, q_ref, conv_ref, weight_ref, out_ref, gated_ref, sems
 ):
+    chunks = len(places)
     length = series_ref.shape[0] // chunks
     for half in range(chunks // SUBLANES):
         rate = mode_rows(gathered_ref, 0, order, 2 * order, chunks, half)
@@ -91,7 +93,8 @@
         weight = [residue[r] * jnp.sqrt(one_minus_exp(2.0 * rate[r])) for r in range(order)]
         for r in range(order):
             weight_ref[pl.ds(half * SUBLANES * order + r, SUBLANES, stride=order), :] = weight[r]
-        gain = gain_ref[pl.ds(half * SUBLANES, SUBLANES), :]
+        own = places[half * SUBLANES : (half + 1) * SUBLANES]
+        gain = jnp.concatenate([gain_ref[pl.ds(place, 1), :] for place in own], axis=0)
 
         def steps(i, state):
             state = list(state)
@@ -110,14 +113,15 @@
     @pl.when(lax.axis_index("seq") == 0)
     def _():
         for chunk in range(chunks):
-            finish(chunk, chunks, conv_ref, q_ref, gated_ref, out_ref, sems)
+            finish(chunk, places, conv_ref, q_ref, gated_ref, out_ref, sems)
         for chunk in range(chunks):
-            leaving(chunk, gated_ref, out_ref, sems).wait()
+            leaving(chunk, places, gated_ref, out_ref, sems).wait()
 
 
 def output_kernel(
-    chunks, order, gathered_ref, weight_ref, carry_ref, local_ref, q_ref, _, out_ref, conv_ref, gated_ref, sems
+    places, order, gathered_ref, weight_ref, carry_ref, local_ref, q_ref, _, out_ref, conv_ref, gated_ref, sems
 ):
+    chunks = len(places)
     length = local_ref.shape[0] // chunks
     tokens = length // SUBLANES
 
@@ -144,24 +148,24 @@
             else:
                 for i in range(SUBLANES):
                     fading = steps(i, fading)
-                    finish((half - 1) * SUBLANES + i, chunks, conv_ref, q_ref, gated_ref, out_ref, sems)
+                    finish((half - 1) * SUBLANES + i, places, conv_ref, q_ref, gated_ref, out_ref, sems)
         for chunk in range(chunks - SUBLANES, chunks):
-            finish(chunk, chunks, conv_ref, q_ref, gated_ref, out_ref, sems)
+            finish(chunk, places, conv_ref, q_ref, gated_ref, out_ref, sems)
         for chunk in range(chunks):
-            leaving(chunk, gated_ref, out_ref, sems).wait()
-
-
-def copies_kernel(rate_ref, residue_ref, copies_ref, sems):
+            leaving(chunk, places, gated_ref, out_ref, sems).wait()
+
+
+def copies_kernel(rate_hbm, residue_hbm, copies_ref, rate_ref, residue_ref, sems):
+    pairs = ((rate_hbm, rate_ref), (residue_hbm, residue_ref))
+    loads = [pltpu.make_async_copy(source, target, sems.at[i]) for i, (source, target) in enumerate(pairs)]
+    for load in loads:
+        load.start()
+    for load in loads:
+        load.wait()
     order = rate_ref.shape[0]
-    copies = []
     for piece in range(copies_ref.shape[0]):
-        for part, source in enumerate((rate_ref, residue_ref)):
-            target = copies_ref.at[piece, pl.ds(part * order, order)]
-            copies.append(pltpu.make_async_copy(source, target, sems.at[piece, part]))
-    for copy in copies:
-        copy.start()
-    for copy in copies:
-        copy.wait()
+        copies_ref[piece, :order] = rate_ref[...]
+        copies_ref[piece, order:] = residue_ref[...]
 
 
 def call(kernel, out_shape, *args, in_spaces=None, out_spaces=None, aliases=None, scratch=(), flops=0):
@@ -201,11 +205,19 @@
     return pieces.reshape(owners, own // LANES, rows, LANES).swapaxes(1, 2).reshape(owners, rows, own)
 
 
+def all_to_all(pieces, members):
+    return lax.all_to_all(pieces, "seq", split_axis=0, concat_axis=0, axis_index_groups=[members], tiled=True)
+
+
 def shards(blocks, q_proj, k_proj, value_projection, residues, rates, direct_gain):
     channels, length = q_proj.shape
     order = residues.shape[1]
     chunks = channels // LANES
     f32 = jnp.float32
+
+    members, places = list(range(blocks)), list(range(chunks))
+    if blocks == chunks:
+        members, places = members[::-1], places[::-1]
 
     own_rates = rates.T
     in_hbm = [pltpu.with_memory_space_constraint(array, pltpu.HBM) for array in (own_rates, residues.T)]
@@ -214,14 +226,13 @@
         jax.ShapeDtypeStruct((blocks, 2 * order, rates.shape[0]), f32),
         *in_hbm,
         in_spaces=[pl.ANY] * 2,
-        out_spaces=pl.ANY,
-        scratch=[pltpu.SemaphoreType.DMA((blocks, 2))],
-    )
-    gathered = lax.all_to_all(copies, "seq", split_axis=0, concat_axis=0, tiled=True)
+        scratch=[pltpu.VMEM(own_rates.shape, f32)] * 2 + [pltpu.SemaphoreType.DMA((2,))],
+    )
+    gathered = all_to_all(copies, members)
     params = to_chunks(gathered).reshape(chunks * 2 * order, LANES)
 
     series = call(
-        functools.partial(prepare_kernel, chunks),
+        functools.partial(prepare_kernel, places),
         jax.ShapeDtypeStruct((length * chunks, LANES), f32),
         k_proj,
         value_projection,
@@ -239,7 +250,7 @@
     out_shape = jax.ShapeDtypeStruct((channels, length), jnp.bfloat16)
     out_scratch = [pltpu.VMEM(out_shape.shape, out_shape.dtype), pltpu.SemaphoreType.DMA((chunks,))]
     local, weights, out = call(
-        functools.partial(local_kernel, chunks, order),
+        functools.partial(local_kernel, places, order),
         (
             jax.ShapeDtypeStruct((length * chunks, LANES), f32),
             jax.ShapeDtypeStruct((chunks * order, LANES), f32),
@@ -253,17 +264,17 @@
         scratch=out_scratch,
         flops=4 * order * channels * length,
     )
-    ends = lax.all_to_all(ends, "seq", split_axis=0, concat_axis=0, tiled=True)
+    ends = all_to_all(ends, members)
     starts = call(
-        functools.partial(prefix_kernel, length),
+        functools.partial(prefix_kernel, length, members),
         jax.ShapeDtypeStruct(ends.shape, f32),
         own_rates,
         ends,
     )
-    starts = lax.all_to_all(starts, "seq", split_axis=0, concat_axis=0, tiled=True)
+    starts = all_to_all(starts, members)
     carry = to_chunks(starts).reshape(chunks * order, LANES)
     return call(
-        functools.partial(output_kernel, chunks, order),
+        functools.partial(output_kernel, places, order),
         out_shape,
         params,
         weights,

time: 53.2 us -> 43.9 us (0.83)
  Pallas kernels: 17 us -> 9.16 us
  waiting for transfers between devices: 11.5 us -> 7.86 us
  starting transfers between devices: 11.7 us -> 14.8 us
  blocking collectives: 11.6 us -> 10.5 us
    pallas_call x6, Pallas kernels: 17 us -> 9.16 us  [call(): pl.pallas_call(kernel, out_shape=out_shape, in_specs=[pl.BlockSpec(memory...]
    all_to_all x2, waiting for transfers between devices: 11.5 us -> 7.86 us  [all_to_all(): lax.all_to_all(pieces, 'seq', split_axis=0, concat_axis=0, axis_index_gro...]
    all_to_all x2, starting transfers between devices: 11.7 us -> 14.8 us  [all_to_all(): lax.all_to_all(pieces, 'seq', split_axis=0, concat_axis=0, axis_index_gro...]
    all_to_all x1, blocking collectives: 11.6 us -> 10.5 us  [all_to_all(): lax.all_to_all(pieces, 'seq', split_axis=0, concat_axis=0, axis_index_gro...]
  transfers between devices with their start and end apart: 2 -> 2, of which waited for: 2 -> 2; matrix products, arithmetic and copies ran while one was open for 0% -> 0% of each run, Pallas kernels for 6% -> 7%
where the time goes in v11:
time: 43.9 us; the launch traced here: 43.5 us
  starting transfers between devices  14.8 us (34%)
  blocking collectives  10.5 us (24%)
  Pallas kernels  9.16 us (21%)
  waiting for transfers between devices  7.86 us (18%)
  local copies, waits for them, and re-layouts  1.05 us (2%)
    all_to_all x2, starting transfers between devices, all_to_all(): lax.all_to_all(pieces, 'seq', split_axis=0, concat_axis=0, axis_index_gro...  14.8 us
    all_to_all x1, blocking collectives, all_to_all(): lax.all_to_all(pieces, 'seq', split_axis=0, concat_axis=0, axis_index_gro...  10.5 us
    pallas_call x6, Pallas kernels, call(): pl.pallas_call(kernel, out_shape=out_shape, in_specs=[pl.BlockSpec(memory...  9.16 us
    all_to_all x2, waiting for transfers between devices, all_to_all(): lax.all_to_all(pieces, 'seq', split_axis=0, concat_axis=0, axis_index_gro...  7.86 us
    unnamed x10, local copies, waits for them, and re-layouts  1.05 us
  transfers between devices with their start and end apart: 2, of which 2 were waited for; matrix products, arithmetic and copies ran while one was open for 0% of the time, Pallas kernels for 7%

profile of v11, /device:TPU:2, one launch (start us, length us, event | category | flops | bytes accessed | tf_op | source)
XLA Modules:
  0.0 43.5 jit_solution(10916339831221979853)
XLA Ops:
  0.0 0.0 copy-start.1
  0.0 1.5 %shard_map.64 = f32[16,32,128]{2,1,0:T(8,128)} custom-call(f32[16,128]{1,0:T(8,128)} %bitcast.11, f32[16,128]{1,0:T(8,128)} %bitcast.14), custom_call_target="tpu_custom_call" | custom-call | bytes 16384 | tf_op jit(solution)/shard_map/pallas_call | solution.py:175
  1.5 8.0 %all-to-all-start = ((f32[16,32,128]{2,1,0:T(8,128)}), f32[16,32,128]{2,1,0:T(8,128)S(1)}, u32[]{:S(2)}, u32[]{:S(2)}) async-start(f32[16,32,128]{2,1,0:T(8,128)} %shard_map.64), calls=%async_computation | async-start | bytes 524288 | tf_op jit(solution)/shard_map/all_to_all | solution.py:209
  9.5 0.0 copy-done.1
  9.5 0.0 copy-start.2
  9.5 1.0 %copy-done.2 = bf16[2048,128]{1,0:T(8,128)(2,1)S(1)} copy-done((bf16[2048,128]{1,0:T(8,128)(2,1)S(1)}, bf16[2048,128]{1,0:T(8,128)(2,1)}, u32[]{:S(2)}) %copy-start.2) | copy-done | bytes 524312
  10.5 0.4 shard_map.65.series_ref
  11.0 6.2 %all-to-all-done = f32[16,32,128]{2,1,0:T(8,128)S(1)} async-done(((f32[16,32,128]{2,1,0:T(8,128)}), f32[16,32,128]{2,1,0:T(8,128)S(1)}, u32[]{:S(2)}, u32[]{:S(2)}) %all-to-all-start) | async-done | bytes 262176 | tf_op jit(solution)/shard_map/all_to_all | solution.py:209
  17.1 0.0 copy-start.3
  17.1 1.3 %shard_map.66 = f32[256,128]{1,0:T(8,128)S(1)} custom-call(f32[512,128]{1,0:T(8,128)S(1)} %bitcast.6, f32[2048,128]{1,0:T(8,128)S(1)} %shard_map.65.series_ref), custom_call_target="tpu_custom_call" | custom-call | flops 8388608 | bytes 1310720 | tf_op jit(solution)/shard_map/pallas_call | solution.py:175
  18.4 0.0 copy-start
  18.5 10.5 %all_to_all.15.ends_ref = f32[16,16,128]{2,1,0:T(8,128)S(1)} all-to-all(f32[16,16,128]{2,1,0:T(8,128)S(1)} %bitcast.10), channel_id=1, replica_groups={{30,28,26,24,22,20,18,16,14,12,10,8,6,4,2,0},{31,29,27,25,23,21,19,17,1..., dimensions={0} | all-to-all | bytes 262144 | tf_op jit(solution)/shard_map/all_to_all | solution.py:209
  29.0 0.0 copy-done.3
  29.0 0.7 %shard_map.68 = f32[16,16,128]{2,1,0:T(8,128)} custom-call(f32[16,128]{1,0:T(8,128)S(1)} %bitcast.12, f32[16,16,128]{2,1,0:T(8,128)S(1)} %all_to_all.15.ends_ref), custom_call_target="tpu_custom_call" | custom-call | bytes 139264 | tf_op jit(solution)/shard_map/pallas_call | solution.py:175
  29.7 0.0 copy-start.4
  29.7 6.8 %all-to-all-start.2 = ((f32[16,16,128]{2,1,0:T(8,128)}), f32[16,16,128]{2,1,0:T(8,128)S(1)}, u32[]{:S(2)}, u32[]{:S(2)}) async-start(f32[16,16,128]{2,1,0:T(8,128)} %shard_map.68), calls=%async_computation.2 | async-start | bytes 262144 | tf_op jit(solution)/shard_map/all_to_all | solution.py:209
  36.5 0.0 copy-done
  36.5 0.0 copy-done.4
  36.5 2.8 %shard_map.67 = (f32[2048,128]{1,0:T(8,128)S(1)}, f32[256,128]{1,0:T(8,128)S(1)}, bf16[2048,128]{1,0:T(8,128)(2,1)}) custom-call(f32[512,128]{1,0:T(8,128)S(1)} %bitcast.7, f32[2048,128]{1,0:T(8,128)S(1)} %shard_map.65.series_ref, f32[16,128]{1,0:T(8,128)S(1)} %bitcast.13, bf16[2048,128]{1,0:T(8,128)(2,1)S(1)} %copy-done), custom_call_target="tpu_custom_call" | custom-call | flops 16777216 | bytes 1843200 | tf_op jit(solution)/shard_map/pallas_call | solution.py:175
  39.4 1.7 %all-to-all-done.2 = f32[16,16,128]{2,1,0:T(8,128)S(1)} async-done(((f32[16,16,128]{2,1,0:T(8,128)}), f32[16,16,128]{2,1,0:T(8,128)S(1)}, u32[]{:S(2)}, u32[]{:S(2)}) %all-to-all-start.2) | async-done | bytes 131104 | tf_op jit(solution)/shard_map/all_to_all | solution.py:209
  41.0 2.4 %shard_map.69 = bf16[2048,128]{1,0:T(8,128)(2,1)} custom-call(f32[512,128]{1,0:T(8,128)S(1)} %bitcast.8, f32[256,128]{1,0:T(8,128)S(1)} %get-tuple-element.11.weight_ref, f32[256,128]{1,0:T(8,128)S(1)} %bitcast.9, f32[2048,128]{1,0:T(8,128)S(1)} %get-tuple-element.13.local_ref, bf16[2048,128]{1,0:T(8,128)(2,1)S(1)} %copy-done, ...), custom_call_target="tpu_custom_call", output_to_operand_aliasing={{}: (5, {})} | custom-call | flops 8388608 | bytes 2621440 | tf_op jit(solution)/shard_map/pallas_call | solution.py:175
Async XLA Ops:
  0.0 9.5 %copy-start.1 = (bf16[2048,128]{1,0:T(8,128)(2,1)S(1)}, bf16[2048,128]{1,0:T(8,128)(2,1)}, u32[]{:S(2)}) copy-start(bf16[2048,128]{1,0:T(8,128)(2,1)} %k_ref.1) | copy-start | bytes 1572868
  1.5 15.6 %all-to-all-start = ((f32[16,32,128]{2,1,0:T(8,128)}), f32[16,32,128]{2,1,0:T(8,128)S(1)}, u32[]{:S(2)}, u32[]{:S(2)}) async-start(f32[16,32,128]{2,1,0:T(8,128)} %shard_map.64), calls=%async_computation | async-start | bytes 524288 | tf_op jit(solution)/shard_map/all_to_all | solution.py:209
  9.5 1.0 %copy-start.2 = (bf16[2048,128]{1,0:T(8,128)(2,1)S(1)}, bf16[2048,128]{1,0:T(8,128)(2,1)}, u32[]{:S(2)}) copy-start(bf16[2048,128]{1,0:T(8,128)(2,1)} %v_ref.1) | copy-start | bytes 1572868
  17.1 11.9 %copy-start.3 = (f32[128,16]{0,1:T(8,128)S(1)}, f32[128,16]{0,1:T(8,128)}, u32[]{:S(2)}) copy-start(f32[128,16]{0,1:T(8,128)} %param.10) | copy-start | bytes 24580
  18.4 18.1 %copy-start = (bf16[2048,128]{1,0:T(8,128)(2,1)S(1)}, bf16[2048,128]{1,0:T(8,128)(2,1)}, u32[]{:S(2)}) copy-start(bf16[2048,128]{1,0:T(8,128)(2,1)} %q_ref.3) | copy-start | bytes 1572868
  29.7 6.8 %copy-start.4 = (f32[2048]{0:T(1024)S(1)}, f32[2048]{0:T(1024)}, u32[]{:S(2)}) copy-start(f32[2048]{0:T(1024)} %param.11) | copy-start | bytes 24580
  29.7 11.4 %all-to-all-start.2 = ((f32[16,16,128]{2,1,0:T(8,128)}), f32[16,16,128]{2,1,0:T(8,128)S(1)}, u32[]{:S(2)}, u32[]{:S(2)}) async-start(f32[16,16,128]{2,1,0:T(8,128)} %shard_map.68), calls=%async_computation.2 | async-start | bytes 262144 | tf_op jit(solution)/shard_map/all_to_all | solution.py:209

commit v12 on v11

--- a/solution.py
+++ b/solution.py
@@ -25,10 +25,12 @@
     return [ref[pl.ds(first + r, SUBLANES, stride=per_chunk), :] for r in range(order)]
 
 
-def state_kernel(chunks, order, params_ref, series_ref, state_ref):
+def state_kernel(chunks, order, rates_ref, residue_ref, series_ref, state_ref):
     length = series_ref.shape[0] // chunks
+    for chunk in range(chunks):
+        state_ref[pl.ds((2 * chunk + 1) * order, order), :] = residue_ref[...]
     for half in range(chunks // SUBLANES):
-        decay = [jnp.exp(-rate) for rate in mode_rows(params_ref, 0, order, 2 * order, chunks, half)]
+        decay = [jnp.exp(-rate) for rate in mode_rows(rates_ref, 0, order, order, chunks, half)]
 
         def steps(i, state):
             state = list(state)
@@ -42,7 +44,7 @@
         zero = jnp.zeros((SUBLANES, LANES), jnp.float32)
         state = lax.fori_loop(0, length // UNROLL, steps, (zero,) * order)
         for r in range(order):
-            state_ref[pl.ds(half * SUBLANES * order + r, SUBLANES, stride=order), :] = state[r]
+            state_ref[pl.ds(half * SUBLANES * 2 * order + r, SUBLANES, stride=2 * order), :] = state[r]
 
 
 def prefix_kernel(length, members, rate_ref, ends_ref, starts_ref):
@@ -50,7 +52,7 @@
     carry = jnp.zeros(rate_ref.shape, jnp.float32)
     for block in range(len(members)):
         starts_ref[members.index(block)] = carry
-        carry = span_decay * carry + ends_ref[members.index(block)]
+        carry = span_decay * carry + ends_ref[members.index(block), : rate_ref.shape[0]]
 
 
 def tree_sum(terms):
@@ -82,13 +84,13 @@
 
 
 def local_kernel(
-    places, order, gathered_ref, series_ref, gain_ref, q_ref, conv_ref, weight_ref, out_ref, gated_ref, sems
+    places, order, rates_ref, residues_ref, series_ref, gain_ref, q_ref, conv_ref, weight_ref, out_ref, gated_ref, sems
 ):
     chunks = len(places)
     length = series_ref.shape[0] // chunks
     for half in range(chunks // SUBLANES):
-        rate = mode_rows(gathered_ref, 0, order, 2 * order, chunks, half)
-        residue = mode_rows(gathered_ref, order, order, 2 * order, chunks, half)
+        rate = mode_rows(rates_ref, 0, order, order, chunks, half)
+        residue = mode_rows(residues_ref, order, order, 2 * order, chunks, half)
         decay = [jnp.exp(-rate[r]) for r in range(order)]
         weight = [residue[r] * jnp.sqrt(one_minus_exp(2.0 * rate[r])) for r in range(order)]
         for r in range(order):
@@ -119,7 +121,7 @@
 
 
 def output_kernel(
-    places, order, gathered_ref, weight_ref, carry_ref, local_ref, q_ref, _, out_ref, conv_ref, gated_ref, sems
+    places, order, rates_ref, weight_ref, carry_ref, local_ref, q_ref, _, out_ref, conv_ref, gated_ref, sems
 ):
     chunks = len(places)
     length = local_ref.shape[0] // chunks
@@ -128,7 +130,7 @@
     @pl.when(lax.axis_index("seq") > 0)
     def _():
         for half in range(chunks // SUBLANES):
-            decay = [jnp.exp(-rate) for rate in mode_rows(gathered_ref, 0, order, 2 * order, chunks, half)]
+            decay = [jnp.exp(-rate) for rate in mode_rows(rates_ref, 0, order, order, chunks, half)]
             weight = mode_rows(weight_ref, 0, order, order, chunks, half)
             carry = mode_rows(carry_ref, 0, order, order, chunks, half)
 
@@ -153,19 +155,6 @@
             finish(chunk, places, conv_ref, q_ref, gated_ref, out_ref, sems)
         for chunk in range(chunks):
             leaving(chunk, places, gated_ref, out_ref, sems).wait()
-
-
-def copies_kernel(rate_hbm, residue_hbm, copies_ref, rate_ref, residue_ref, sems):
-    pairs = ((rate_hbm, rate_ref), (residue_hbm, residue_ref))
-    loads = [pltpu.make_async_copy(source, target, sems.at[i]) for i, (source, target) in enumerate(pairs)]
-    for load in loads:
-        load.start()
-    for load in loads:
-        load.wait()
-    order = rate_ref.shape[0]
-    for piece in range(copies_ref.shape[0]):
-        copies_ref[piece, :order] = rate_ref[...]
-        copies_ref[piece, order:] = residue_ref[...]
 
 
 def call(kernel, out_shape, *args, in_spaces=None, out_spaces=None, aliases=None, scratch=(), flops=0):
@@ -219,17 +208,9 @@
     if blocks == chunks:
         members, places = members[::-1], places[::-1]
 
-    own_rates = rates.T
-    in_hbm = [pltpu.with_memory_space_constraint(array, pltpu.HBM) for array in (own_rates, residues.T)]
-    copies = call(
-        copies_kernel,
-        jax.ShapeDtypeStruct((blocks, 2 * order, rates.shape[0]), f32),
-        *in_hbm,
-        in_spaces=[pl.ANY] * 2,
-        scratch=[pltpu.VMEM(own_rates.shape, f32)] * 2 + [pltpu.SemaphoreType.DMA((2,))],
-    )
-    gathered = all_to_all(copies, members)
-    params = to_chunks(gathered).reshape(chunks * 2 * order, LANES)
+    own_rates, own_residues = rates.T, residues.T
+    copies = jnp.broadcast_to(own_rates[None], (blocks,) + own_rates.shape)
+    all_rates = to_chunks(all_to_all(copies, members)).reshape(chunks * order, LANES)
 
     series = call(
         functools.partial(prepare_kernel, places),
@@ -238,15 +219,21 @@
         value_projection,
         flops=channels * length,
     )
+    whole_chunk = own_residues.shape[1] == LANES
     ends = call(
         functools.partial(state_kernel, chunks, order),
-        jax.ShapeDtypeStruct((chunks * order, LANES), f32),
-        params,
+        jax.ShapeDtypeStruct((chunks * 2 * order, LANES), f32),
+        all_rates,
+        own_residues if whole_chunk else jnp.zeros((order, LANES), f32),
         series,
         flops=2 * order * channels * length,
     )
     local_series, ends = lax.optimization_barrier((series, ends))
-    ends = from_chunks(ends.reshape(chunks, order, LANES), blocks)
+    ends = from_chunks(ends.reshape(chunks, 2 * order, LANES), blocks)
+    if not whole_chunk:
+        ends = ends.at[:, order:].set(own_residues)
+    ends = all_to_all(ends, members)
+    all_residues = to_chunks(ends).reshape(chunks * 2 * order, LANES)
     out_shape = jax.ShapeDtypeStruct((channels, length), jnp.bfloat16)
     out_scratch = [pltpu.VMEM(out_shape.shape, out_shape.dtype), pltpu.SemaphoreType.DMA((chunks,))]
     local, weights, out = call(
@@ -256,7 +243,8 @@
             jax.ShapeDtypeStruct((chunks * order, LANES), f32),
             out_shape,
         ),
-        params,
+        all_rates,
+        all_residues,
         local_series,
         direct_gain.reshape(chunks, LANES),
         q_proj,
@@ -264,10 +252,9 @@
         scratch=out_scratch,
         flops=4 * order * channels * length,
     )
-    ends = all_to_all(ends, members)
     starts = call(
         functools.partial(prefix_kernel, length, members),
-        jax.ShapeDtypeStruct(ends.shape, f32),
+        jax.ShapeDtypeStruct((blocks,) + own_rates.shape, f32),
         own_rates,
         ends,
     )
@@ -276,7 +263,7 @@
     return call(
         functools.partial(output_kernel, places, order),
         out_shape,
-        params,
+        all_rates,
         weights,
         carry,
         local,

time: 43.9 us -> 42.8 us (0.975)
  waiting for transfers between devices: 7.86 us -> 4.11 us
  blocking collectives: 10.5 us -> 13 us
  local copies, waits for them, and re-layouts: 1.05 us -> 3.45 us
  Pallas kernels: 9.16 us -> 7.58 us
  starting transfers between devices: 14.8 us -> 14.1 us
    all_to_all x2, waiting for transfers between devices: 7.86 us -> 4.11 us  [all_to_all(): lax.all_to_all(pieces, 'seq', split_axis=0, concat_axis=0, axis_index_gro...]
    all_to_all x1, blocking collectives: 10.5 us -> 13 us  [all_to_all(): lax.all_to_all(pieces, 'seq', split_axis=0, concat_axis=0, axis_index_gro...]
    pallas_call x6 -> x5, Pallas kernels: 9.16 us -> 7.58 us  [call(): pl.pallas_call(kernel, out_shape=out_shape, in_specs=[pl.BlockSpec(memory...]
    broadcast_in_dim x0 -> x1, local copies, waits for them, and re-layouts: none -> 1.36 us  [shards(): copies = jnp.broadcast_to(own_rates[None], (blocks,) + own_rates.shape)]
    unnamed x10 -> x12, local copies, waits for them, and re-layouts: 1.05 us -> 2.09 us
    all_to_all x2, starting transfers between devices: 14.8 us -> 14.1 us  [all_to_all(): lax.all_to_all(pieces, 'seq', split_axis=0, concat_axis=0, axis_index_gro...]
  transfers between devices with their start and end apart: 2 -> 2, of which waited for: 2 -> 2; matrix products, arithmetic and copies ran while one was open for 0% -> 0% of each run, Pallas kernels for 7% -> 8%
where the time goes in v12:
time: 42.8 us; the launch traced here: 42.3 us
  starting transfers between devices  14.1 us (33%)
  blocking collectives  13 us (30%)
  Pallas kernels  7.58 us (18%)
  waiting for transfers between devices  4.11 us (10%)
  local copies, waits for them, and re-layouts  3.45 us (8%)
    all_to_all x2, starting transfers between devices, all_to_all(): lax.all_to_all(pieces, 'seq', split_axis=0, concat_axis=0, axis_index_gro...  14.1 us
    all_to_all x1, blocking collectives, all_to_all(): lax.all_to_all(pieces, 'seq', split_axis=0, concat_axis=0, axis_index_gro...  13 us
    pallas_call x5, Pallas kernels, call(): pl.pallas_call(kernel, out_shape=out_shape, in_specs=[pl.BlockSpec(memory...  7.58 us
    all_to_all x2, waiting for transfers between devices, all_to_all(): lax.all_to_all(pieces, 'seq', split_axis=0, concat_axis=0, axis_index_gro...  4.11 us
    unnamed x12, local copies, waits for them, and re-layouts  2.09 us
    broadcast_in_dim x1, local copies, waits for them, and re-layouts, shards(): copies = jnp.broadcast_to(own_rates[None], (blocks,) + own_rates.shape)  1.36 us
  transfers between devices with their start and end apart: 2, of which 2 were waited for; matrix products, arithmetic and copies ran while one was open for 0% of the time, Pallas kernels for 8%

profile of v12, /device:TPU:2, one launch (start us, length us, event | category | flops | bytes accessed | tf_op | source)
XLA Modules:
  0.0 42.3 jit_solution(5183509954896488505)
XLA Ops:
  0.0 1.4 %broadcast_in_dim.2 = f32[16,16,128]{2,1,0:T(8,128)} broadcast(f32[16,128]{1,0:T(8,128)} %bitcast.13), dimensions={1,2} | broadcast | bytes 139264 | tf_op jit(solution)/shard_map/broadcast_in_dim | solution.py:212
  1.4 7.9 %all-to-all-start = ((f32[16,16,128]{2,1,0:T(8,128)}), f32[16,16,128]{2,1,0:T(8,128)S(1)}, u32[]{:S(2)}, u32[]{:S(2)}) async-start(f32[16,16,128]{2,1,0:T(8,128)} %broadcast_in_dim.2), calls=%async_computation | async-start | bytes 262144 | tf_op jit(solution)/shard_map/all_to_all | solution.py:198
  9.3 0.0 copy-start.1
  9.3 1.0 %copy-done.1 = bf16[2048,128]{1,0:T(8,128)(2,1)S(1)} copy-done((bf16[2048,128]{1,0:T(8,128)(2,1)S(1)}, bf16[2048,128]{1,0:T(8,128)(2,1)}, u32[]{:S(2)}) %copy-start.1) | copy-done | bytes 524312
  10.3 0.0 copy-start.2
  10.4 1.0 %copy-done.2 = bf16[2048,128]{1,0:T(8,128)(2,1)S(1)} copy-done((bf16[2048,128]{1,0:T(8,128)(2,1)S(1)}, bf16[2048,128]{1,0:T(8,128)(2,1)}, u32[]{:S(2)}) %copy-start.2) | copy-done | bytes 524312
  11.4 0.0 copy-start.4
  11.4 0.4 shard_map.64.series_ref
  11.8 2.3 %all-to-all-done = f32[16,16,128]{2,1,0:T(8,128)S(1)} async-done(((f32[16,16,128]{2,1,0:T(8,128)}), f32[16,16,128]{2,1,0:T(8,128)S(1)}, u32[]{:S(2)}, u32[]{:S(2)}) %all-to-all-start) | async-done | bytes 131104 | tf_op jit(solution)/shard_map/all_to_all | solution.py:198
  14.1 0.0 copy-done.4
  14.1 0.0 copy-start.3
  14.1 1.3 %shard_map.65 = f32[512,128]{1,0:T(8,128)S(1)} custom-call(f32[256,128]{1,0:T(8,128)S(1)} %bitcast.8, f32[16,128]{1,0:T(8,128)S(1)} %bitcast.15, f32[2048,128]{1,0:T(8,128)S(1)} %shard_map.64.series_ref), custom_call_target="tpu_custom_call" | custom-call | flops 8388608 | bytes 1187840 | tf_op jit(solution)/shard_map/pallas_call | solution.py:164
  15.5 0.0 copy-start
  15.5 13.0 %all_to_all.15.ends_ref = f32[16,32,128]{2,1,0:T(8,128)S(1)} all-to-all(f32[16,32,128]{2,1,0:T(8,128)S(1)} %bitcast.11), channel_id=1, replica_groups={{30,28,26,24,22,20,18,16,14,12,10,8,6,4,2,0},{31,29,27,25,23,21,19,17,1..., dimensions={0} | all-to-all | bytes 524288 | tf_op jit(solution)/shard_map/all_to_all | solution.py:198
  28.4 0.0 copy-done.3
  28.4 0.7 %shard_map.67 = f32[16,16,128]{2,1,0:T(8,128)} custom-call(f32[16,128]{1,0:T(8,128)S(1)} %bitcast.14, f32[16,32,128]{2,1,0:T(8,128)S(1)} %all_to_all.15.ends_ref), custom_call_target="tpu_custom_call" | custom-call | bytes 270336 | tf_op jit(solution)/shard_map/pallas_call | solution.py:164
  29.1 0.0 copy-start.5
  29.1 6.1 %all-to-all-start.2 = ((f32[16,16,128]{2,1,0:T(8,128)}), f32[16,16,128]{2,1,0:T(8,128)S(1)}, u32[]{:S(2)}, u32[]{:S(2)}) async-start(f32[16,16,128]{2,1,0:T(8,128)} %shard_map.67), calls=%async_computation.2 | async-start | bytes 262144 | tf_op jit(solution)/shard_map/all_to_all | solution.py:198
  35.3 0.0 copy-done
  35.3 0.0 copy-done.5
  35.3 2.8 %shard_map.66 = (f32[2048,128]{1,0:T(8,128)S(1)}, f32[256,128]{1,0:T(8,128)S(1)}, bf16[2048,128]{1,0:T(8,128)(2,1)}) custom-call(f32[256,128]{1,0:T(8,128)S(1)} %bitcast.9, f32[512,128]{1,0:T(8,128)S(1)} %bitcast.7, f32[2048,128]{1,0:T(8,128)S(1)} %shard_map.64.series_ref, f32[16,128]{1,0:T(8,128)S(1)} %bitcast.16, bf16[2048,128]{1,0:T(8,128)(2,1)S(1)} %copy-done), custom_call_target="tpu_custom_call" | custom-call | flops 16777216 | bytes 1974272 | tf_op jit(solution)/shard_map/pallas_call | solution.py:164
  38.1 1.8 %all-to-all-done.2 = f32[16,16,128]{2,1,0:T(8,128)S(1)} async-done(((f32[16,16,128]{2,1,0:T(8,128)}), f32[16,16,128]{2,1,0:T(8,128)S(1)}, u32[]{:S(2)}, u32[]{:S(2)}) %all-to-all-start.2) | async-done | bytes 131104 | tf_op jit(solution)/shard_map/all_to_all | solution.py:198
  39.9 2.4 %shard_map.68 = bf16[2048,128]{1,0:T(8,128)(2,1)} custom-call(f32[256,128]{1,0:T(8,128)S(1)} %bitcast.10, f32[256,128]{1,0:T(8,128)S(1)} %get-tuple-element.12.weight_ref, f32[256,128]{1,0:T(8,128)S(1)} %bitcast.12, f32[2048,128]{1,0:T(8,128)S(1)} %get-tuple-element.13.local_ref, bf16[2048,128]{1,0:T(8,128)(2,1)S(1)} %copy-done, ...), custom_call_target="tpu_custom_call", output_to_operand_aliasing={{}: (5, {})} | custom-call | flops 8388608 | bytes 2490368 | tf_op jit(solution)/shard_map/pallas_call | solution.py:164
Async XLA Ops:
  1.4 12.8 %all-to-all-start = ((f32[16,16,128]{2,1,0:T(8,128)}), f32[16,16,128]{2,1,0:T(8,128)S(1)}, u32[]{:S(2)}, u32[]{:S(2)}) async-start(f32[16,16,128]{2,1,0:T(8,128)} %broadcast_in_dim.2), calls=%async_computation | async-start | bytes 262144 | tf_op jit(solution)/shard_map/all_to_all | solution.py:198
  9.3 1.0 %copy-start.1 = (bf16[2048,128]{1,0:T(8,128)(2,1)S(1)}, bf16[2048,128]{1,0:T(8,128)(2,1)}, u32[]{:S(2)}) copy-start(bf16[2048,128]{1,0:T(8,128)(2,1)} %k_ref.1) | copy-start | bytes 1572868
  10.3 1.0 %copy-start.2 = (bf16[2048,128]{1,0:T(8,128)(2,1)S(1)}, bf16[2048,128]{1,0:T(8,128)(2,1)}, u32[]{:S(2)}) copy-start(bf16[2048,128]{1,0:T(8,128)(2,1)} %v_ref.1) | copy-start | bytes 1572868
  11.4 2.7 %copy-start.4 = (f32[128,16]{0,1:T(8,128)S(1)}, f32[128,16]{0,1:T(8,128)}, u32[]{:S(2)}) copy-start(f32[128,16]{0,1:T(8,128)} %param.9) | copy-start | bytes 24580
  14.1 14.3 %copy-start.3 = (f32[128,16]{0,1:T(8,128)S(1)}, f32[128,16]{0,1:T(8,128)}, u32[]{:S(2)}) copy-start(f32[128,16]{0,1:T(8,128)} %param.10) | copy-start | bytes 24580
  15.5 19.8 %copy-start = (bf16[2048,128]{1,0:T(8,128)(2,1)S(1)}, bf16[2048,128]{1,0:T(8,128)(2,1)}, u32[]{:S(2)}) copy-start(bf16[2048,128]{1,0:T(8,128)(2,1)} %q_ref.3) | copy-start | bytes 1572868
  29.1 6.2 %copy-start.5 = (f32[2048]{0:T(1024)S(1)}, f32[2048]{0:T(1024)}, u32[]{:S(2)}) copy-start(f32[2048]{0:T(1024)} %param.11) | copy-start | bytes 24580
  29.1 10.8 %all-to-all-start.2 = ((f32[16,16,128]{2,1,0:T(8,128)}), f32[16,16,128]{2,1,0:T(8,128)S(1)}, u32[]{:S(2)}, u32[]{:S(2)}) async-start(f32[16,16,128]{2,1,0:T(8,128)} %shard_map.67), calls=%async_computation.2 | async-start | bytes 262144 | tf_op jit(solution)/shard_map/all_to_all | solution.py:198

commit v13 on v12

--- a/solution.py
+++ b/solution.py
@@ -25,10 +25,8 @@
     return [ref[pl.ds(first + r, SUBLANES, stride=per_chunk), :] for r in range(order)]
 
 
-def state_kernel(chunks, order, rates_ref, residue_ref, series_ref, state_ref):
+def state_kernel(chunks, order, rates_ref, series_ref, state_ref):
     length = series_ref.shape[0] // chunks
-    for chunk in range(chunks):
-        state_ref[pl.ds((2 * chunk + 1) * order, order), :] = residue_ref[...]
     for half in range(chunks // SUBLANES):
         decay = [jnp.exp(-rate) for rate in mode_rows(rates_ref, 0, order, order, chunks, half)]
 
@@ -44,7 +42,7 @@
         zero = jnp.zeros((SUBLANES, LANES), jnp.float32)
         state = lax.fori_loop(0, length // UNROLL, steps, (zero,) * order)
         for r in range(order):
-            state_ref[pl.ds(half * SUBLANES * 2 * order + r, SUBLANES, stride=2 * order), :] = state[r]
+            state_ref[pl.ds(half * SUBLANES * order + r, SUBLANES, stride=order), :] = state[r]
 
 
 def prefix_kernel(length, members, rate_ref, ends_ref, starts_ref):
@@ -52,7 +50,7 @@
     carry = jnp.zeros(rate_ref.shape, jnp.float32)
     for block in range(len(members)):
         starts_ref[members.index(block)] = carry
-        carry = span_decay * carry + ends_ref[members.index(block), : rate_ref.shape[0]]
+        carry = span_decay * carry + ends_ref[members.index(block)]
 
 
 def tree_sum(terms):
@@ -90,7 +88,7 @@
     length = series_ref.shape[0] // chunks
     for half in range(chunks // SUBLANES):
         rate = mode_rows(rates_ref, 0, order, order, chunks, half)
-        residue = mode_rows(residues_ref, order, order, 2 * order, chunks, half)
+        residue = mode_rows(residues_ref, 0, order, order, chunks, half)
         decay = [jnp.exp(-rate[r]) for r in range(order)]
         weight = [residue[r] * jnp.sqrt(one_minus_exp(2.0 * rate[r])) for r in range(order)]
         for r in range(order):
@@ -208,7 +206,9 @@
     if blocks == chunks:
         members, places = members[::-1], places[::-1]
 
-    own_rates, own_residues = rates.T, residues.T
+    own_rates = rates.T
+    all_residues = lax.all_gather(residues.T, "seq", axis=0, axis_index_groups=[members])
+    all_residues = to_chunks(all_residues).reshape(chunks * order, LANES)
     copies = jnp.broadcast_to(own_rates[None], (blocks,) + own_rates.shape)
     all_rates = to_chunks(all_to_all(copies, members)).reshape(chunks * order, LANES)
 
@@ -219,21 +219,15 @@
         value_projection,
         flops=channels * length,
     )
-    whole_chunk = own_residues.shape[1] == LANES
     ends = call(
         functools.partial(state_kernel, chunks, order),
-        jax.ShapeDtypeStruct((chunks * 2 * order, LANES), f32),
+        jax.ShapeDtypeStruct((chunks * order, LANES), f32),
         all_rates,
-        own_residues if whole_chunk else jnp.zeros((order, LANES), f32),
         series,
         flops=2 * order * channels * length,
     )
     local_series, ends = lax.optimization_barrier((series, ends))
-    ends = from_chunks(ends.reshape(chunks, 2 * order, LANES), blocks)
-    if not whole_chunk:
-        ends = ends.at[:, order:].set(own_residues)
-    ends = all_to_all(ends, members)
-    all_residues = to_chunks(ends).reshape(chunks * 2 * order, LANES)
+    ends = all_to_all(from_chunks(ends.reshape(chunks, order, LANES), blocks), members)
     out_shape = jax.ShapeDtypeStruct((channels, length), jnp.bfloat16)
     out_scratch = [pltpu.VMEM(out_shape.shape, out_shape.dtype), pltpu.SemaphoreType.DMA((chunks,))]
     local, weights, out = call(

time: 42.8 us -> 76.4 us (1.79)
  the two profiles are of different devices: /device:TPU:2 before, /device:TPU:30 now
where the time goes in v13:
time: 76.4 us; the launch traced here: 75.9 us
  blocking collectives  52.4 us (69%)
  Pallas kernels  7.54 us (10%)
  starting transfers between devices  7.15 us (9%)
  waiting for transfers between devices  5.27 us (7%)
  local copies, waits for them, and re-layouts  3.46 us (5%)
    all_gather x1, blocking collectives, shards(): lax.all_gather(residues.T, 'seq', axis=0, axis_index_groups=[members])  41.6 us
    all_to_all x1, blocking collectives, all_to_all(): lax.all_to_all(pieces, 'seq', split_axis=0, concat_axis=0, axis_index_gro...  10.8 us
    pallas_call x5, Pallas kernels, call(): pl.pallas_call(kernel, out_shape=out_shape, in_specs=[pl.BlockSpec(memory...  7.54 us
    all_to_all x2, starting transfers between devices, all_to_all(): lax.all_to_all(pieces, 'seq', split_axis=0, concat_axis=0, axis_index_gro...  7.15 us
    all_to_all x2, waiting for transfers between devices, all_to_all(): lax.all_to_all(pieces, 'seq', split_axis=0, concat_axis=0, axis_index_gro...  5.27 us
    unnamed x12, local copies, waits for them, and re-layouts  2.1 us
  transfers between devices with their start and end apart: 2, of which 1 were waited for; matrix products, arithmetic and copies ran while one was open for 0% of the time, Pallas kernels for 4%

profile of v13, /device:TPU:30, one launch (start us, length us, event | category | flops | bytes accessed | tf_op | source)
XLA Modules:
  0.0 75.9 jit_solution(7080139833992551674)
XLA Ops:
  0.0 1.4 %broadcast_in_dim.2 = f32[16,16,128]{2,1,0:T(8,128)} broadcast(f32[16,128]{1,0:T(8,128)} %bitcast.11), dimensions={1,2} | broadcast | bytes 139264 | tf_op jit(solution)/shard_map/broadcast_in_dim | solution.py:212
  1.4 3.5 %all-to-all-start = ((f32[16,16,128]{2,1,0:T(8,128)}), f32[16,16,128]{2,1,0:T(8,128)S(1)}, u32[]{:S(2)}, u32[]{:S(2)}) async-start(f32[16,16,128]{2,1,0:T(8,128)} %broadcast_in_dim.2), calls=%async_computation | async-start | bytes 262144 | tf_op jit(solution)/shard_map/all_to_all | solution.py:196
  4.9 0.0 copy-start.1
  4.9 1.0 %copy-done.1 = bf16[2048,128]{1,0:T(8,128)(2,1)S(1)} copy-done((bf16[2048,128]{1,0:T(8,128)(2,1)S(1)}, bf16[2048,128]{1,0:T(8,128)(2,1)}, u32[]{:S(2)}) %copy-start.1) | copy-done | bytes 524312
  5.9 0.0 copy-start.2
  5.9 1.0 %copy-done.2 = bf16[2048,128]{1,0:T(8,128)(2,1)S(1)} copy-done((bf16[2048,128]{1,0:T(8,128)(2,1)S(1)}, bf16[2048,128]{1,0:T(8,128)(2,1)}, u32[]{:S(2)}) %copy-start.2) | copy-done | bytes 524312
  7.0 0.4 shard_map.64.series_ref
  7.4 5.3 %all-to-all-done = f32[16,16,128]{2,1,0:T(8,128)S(1)} async-done(((f32[16,16,128]{2,1,0:T(8,128)}), f32[16,16,128]{2,1,0:T(8,128)S(1)}, u32[]{:S(2)}, u32[]{:S(2)}) %all-to-all-start) | async-done | bytes 131104 | tf_op jit(solution)/shard_map/all_to_all | solution.py:196
  12.6 0.0 copy-start.3
  12.6 1.3 %shard_map.65 = f32[256,128]{1,0:T(8,128)S(1)} custom-call(f32[256,128]{1,0:T(8,128)S(1)} %bitcast.6, f32[2048,128]{1,0:T(8,128)S(1)} %shard_map.64.series_ref), custom_call_target="tpu_custom_call" | custom-call | flops 8388608 | bytes 1179648 | tf_op jit(solution)/shard_map/pallas_call | solution.py:162
  13.9 0.0 copy-start
  13.9 10.8 %all_to_all.15.ends_ref = f32[16,16,128]{2,1,0:T(8,128)S(1)} all-to-all(f32[16,16,128]{2,1,0:T(8,128)S(1)} %bitcast.10), channel_id=1, replica_groups={{30,28,26,24,22,20,18,16,14,12,10,8,6,4,2,0},{31,29,27,25,23,21,19,17,1..., dimensions={0} | all-to-all | bytes 262144 | tf_op jit(solution)/shard_map/all_to_all | solution.py:196
  24.7 0.0 copy-done.3
  24.7 0.7 shard_map.67
  25.4 0.0 copy-start.5
  25.4 3.6 %all-to-all-start.2 = ((f32[16,16,128]{2,1,0:T(8,128)}), f32[16,16,128]{2,1,0:T(8,128)S(1)}, u32[]{:S(2)}, u32[]{:S(2)}) async-start(f32[16,16,128]{2,1,0:T(8,128)} %shard_map.67), calls=%async_computation.2 | async-start | bytes 262144 | tf_op jit(solution)/shard_map/all_to_all | solution.py:196
  29.0 0.0 copy-done.5
  29.0 0.0 copy-start.4
  29.1 41.6 %all-gather.residues_ref = f32[256,128]{1,0:T(8,128)S(1)} all-gather(f32[16,128]{1,0:T(8,128)S(1)} %bitcast.14), channel_id=2, replica_groups={{30,28,26,24,22,20,18,16,14,12,10,8,6,4,2,0},{31,29,27,25,23,21,19,17,1..., dimensions={0}, use_global_device_ids=true | all-gather | bytes 139264 | tf_op jit(solution)/shard_map/all_gather | solution.py:210
  70.7 0.0 copy-done
  70.7 0.0 copy-done.4
  70.7 2.8 %shard_map.66 = (f32[2048,128]{1,0:T(8,128)S(1)}, f32[256,128]{1,0:T(8,128)S(1)}, bf16[2048,128]{1,0:T(8,128)(2,1)}) custom-call(f32[256,128]{1,0:T(8,128)S(1)} %bitcast.7, f32[256,128]{1,0:T(8,128)S(1)} %all-gather.residues_ref, f32[2048,128]{1,0:T(8,128)S(1)} %shard_map.64.series_ref, f32[16,128]{1,0:T(8,128)S(1)} %bitcast.13, bf16[2048,128]{1,0:T(8,128)(2,1)S(1)} %copy-done), custom_call_target="tpu_custom_call" | custom-call | flops 16777216 | bytes 1843200 | tf_op jit(solution)/shard_map/pallas_call | solution.py:162
  73.5 0.0 all-to-all-done.2
  73.5 2.4 %shard_map.68 = bf16[2048,128]{1,0:T(8,128)(2,1)} custom-call(f32[256,128]{1,0:T(8,128)S(1)} %bitcast.8, f32[256,128]{1,0:T(8,128)S(1)} %get-tuple-element.11.weight_ref, f32[256,128]{1,0:T(8,128)S(1)} %bitcast.9, f32[2048,128]{1,0:T(8,128)S(1)} %get-tuple-element.13.local_ref, bf16[2048,128]{1,0:T(8,128)(2,1)S(1)} %copy-done, ...), custom_call_target="tpu_custom_call", output_to_operand_aliasing={{}: (5, {})} | custom-call | flops 8388608 | bytes 2490368 | tf_op jit(solution)/shard_map/pallas_call | solution.py:162
Async XLA Ops:
  1.4 11.3 %all-to-all-start = ((f32[16,16,128]{2,1,0:T(8,128)}), f32[16,16,128]{2,1,0:T(8,128)S(1)}, u32[]{:S(2)}, u32[]{:S(2)}) async-start(f32[16,16,128]{2,1,0:T(8,128)} %broadcast_in_dim.2), calls=%async_computation | async-start | bytes 262144 | tf_op jit(solution)/shard_map/all_to_all | solution.py:196
  4.9 1.0 %copy-start.1 = (bf16[2048,128]{1,0:T(8,128)(2,1)S(1)}, bf16[2048,128]{1,0:T(8,128)(2,1)}, u32[]{:S(2)}) copy-start(bf16[2048,128]{1,0:T(8,128)(2,1)} %k_ref.1) | copy-start | bytes 1572868
  5.9 1.0 %copy-start.2 = (bf16[2048,128]{1,0:T(8,128)(2,1)S(1)}, bf16[2048,128]{1,0:T(8,128)(2,1)}, u32[]{:S(2)}) copy-start(bf16[2048,128]{1,0:T(8,128)(2,1)} %v_ref.1) | copy-start | bytes 1572868
  12.6 12.1 %copy-start.3 = (f32[128,16]{0,1:T(8,128)S(1)}, f32[128,16]{0,1:T(8,128)}, u32[]{:S(2)}) copy-start(f32[128,16]{0,1:T(8,128)} %param.10) | copy-start | bytes 24580
  13.9 56.8 %copy-start = (bf16[2048,128]{1,0:T(8,128)(2,1)S(1)}, bf16[2048,128]{1,0:T(8,128)(2,1)}, u32[]{:S(2)}) copy-start(bf16[2048,128]{1,0:T(8,128)(2,1)} %q_ref.3) | copy-start | bytes 1572868
  25.4 3.7 %copy-start.5 = (f32[128,16]{0,1:T(8,128)S(1)}, f32[128,16]{0,1:T(8,128)}, u32[]{:S(2)}) copy-start(f32[128,16]{0,1:T(8,128)} %param.9) | copy-start | bytes 24580
  25.4 48.1 %all-to-all-start.2 = ((f32[16,16,128]{2,1,0:T(8,128)}), f32[16,16,128]{2,1,0:T(8,128)S(1)}, u32[]{:S(2)}, u32[]{:S(2)}) async-start(f32[16,16,128]{2,1,0:T(8,128)} %shard_map.67), calls=%async_computation.2 | async-start | bytes 262144 | tf_op jit(solution)/shard_map/all_to_all | solution.py:196
  29.0 41.6 %copy-start.4 = (f32[2048]{0:T(1024)S(1)}, f32[2048]{0:T(1024)}, u32[]{:S(2)}) copy-start(f32[2048]{0:T(1024)} %param.11) | copy-start | bytes 24580

commit v14 on v12

--- a/solution.py
+++ b/solution.py
@@ -9,15 +9,17 @@
 LANES = 128
 SUBLANES = 8
 UNROLL = 8
+COPIES_COST = 10**10
 VMEM_LIMIT = 32 * 1024 * 1024
 
 
-def prepare_kernel(places, k_ref, v_ref, series_ref):
-    chunks, length = len(places), k_ref.shape[1]
-    for chunk, place in enumerate(places):
-        rows = pl.ds(place * LANES, LANES)
-        gated = k_ref[rows, :].astype(jnp.float32) * v_ref[rows, :].astype(jnp.float32)
-        series_ref[pl.ds(chunk, length, stride=chunks), :] = gated.T
+def copies_kernel(rate_hbm, copies_ref, rate_ref, sem):
+    load = pltpu.make_async_copy(rate_hbm, rate_ref, sem)
+    load.start()
+    load.wait()
+    decay = jnp.exp(-rate_ref[...])
+    for piece in range(copies_ref.shape[0]):
+        copies_ref[piece] = decay
 
 
 def mode_rows(ref, base, order, per_chunk, chunks, half):
@@ -25,24 +27,53 @@
     return [ref[pl.ds(first + r, SUBLANES, stride=per_chunk), :] for r in range(order)]
 
 
-def state_kernel(chunks, order, rates_ref, residue_ref, series_ref, state_ref):
-    length = series_ref.shape[0] // chunks
+def one_minus_exp(y):
+    series = jnp.ones_like(y)
+    for k in range(11, 1, -1):
+        series = 1.0 - (y * (1.0 / k)) * series
+    return jnp.where(y < 0.5, y * series, 1.0 - jnp.exp(-y))
+
+
+def weights_of(residue, rate):
+    return residue * jnp.sqrt(one_minus_exp(2.0 * rate))
+
+
+def state_kernel(places, order, decays_ref, rate_ref, residue_ref, k_ref, v_ref, series_ref, state_ref):
+    chunks, length = len(places), k_ref.shape[1]
+    tokens = length // SUBLANES
+    halves = chunks // SUBLANES
+
+    def build(chunk):
+        rows = pl.ds(places[chunk] * LANES, LANES)
+        gated = k_ref[rows, :].astype(jnp.float32) * v_ref[rows, :].astype(jnp.float32)
+        series_ref[pl.ds(chunk, length, stride=chunks), :] = gated.T
+
+    weight = weights_of(residue_ref[...], rate_ref[...])
     for chunk in range(chunks):
-        state_ref[pl.ds((2 * chunk + 1) * order, order), :] = residue_ref[...]
-    for half in range(chunks // SUBLANES):
-        decay = [jnp.exp(-rate) for rate in mode_rows(rates_ref, 0, order, order, chunks, half)]
+        state_ref[pl.ds((2 * chunk + 1) * order, order), :] = weight
+    for chunk in range(SUBLANES):
+        build(chunk)
+    for half in range(halves):
+        decay = mode_rows(decays_ref, 0, order, order, chunks, half)
 
         def steps(i, state):
             state = list(state)
-            for u in range(UNROLL):
-                row = pl.multiple_of((i * UNROLL + u) * chunks + half * SUBLANES, SUBLANES)
+            for u in range(tokens):
+                row = (i * tokens + u) * chunks + half * SUBLANES
+                if not isinstance(row, int):
+                    row = pl.multiple_of(row, SUBLANES)
                 x = series_ref[pl.ds(row, SUBLANES), :]
                 for r in range(order):
                     state[r] = decay[r] * state[r] + x
             return tuple(state)
 
-        zero = jnp.zeros((SUBLANES, LANES), jnp.float32)
-        state = lax.fori_loop(0, length // UNROLL, steps, (zero,) * order)
+        state = (jnp.zeros((SUBLANES, LANES), jnp.float32),) * order
+        if half + 1 < halves:
+            for i in range(SUBLANES):
+                state = steps(i, state)
+                build((half + 1) * SUBLANES + i)
+        else:
+            state = lax.fori_loop(0, SUBLANES, steps, state)
         for r in range(order):
             state_ref[pl.ds(half * SUBLANES * 2 * order + r, SUBLANES, stride=2 * order), :] = state[r]
 
@@ -60,13 +91,6 @@
     while len(terms) > 1:
         terms = [terms[i] + terms[i + 1] if i + 1 < len(terms) else terms[i] for i in range(0, len(terms), 2)]
     return terms[0]
-
-
-def one_minus_exp(y):
-    series = jnp.ones_like(y)
-    for k in range(11, 1, -1):
-        series = 1.0 - (y * (1.0 / k)) * series
-    return jnp.where(y < 0.5, y * series, 1.0 - jnp.exp(-y))
 
 
 def leaving(chunk, places, gated_ref, out_ref, sems):
@@ -84,17 +108,13 @@
 
 
 def local_kernel(
-    places, order, rates_ref, residues_ref, series_ref, gain_ref, q_ref, conv_ref, weight_ref, out_ref, gated_ref, sems
+    places, order, decays_ref, weights_ref, series_ref, gain_ref, q_ref, conv_ref, out_ref, gated_ref, sems
 ):
     chunks = len(places)
     length = series_ref.shape[0] // chunks
     for half in range(chunks // SUBLANES):
-        rate = mode_rows(rates_ref, 0, order, order, chunks, half)
-        residue = mode_rows(residues_ref, order, order, 2 * order, chunks, half)
-        decay = [jnp.exp(-rate[r]) for r in range(order)]
-        weight = [residue[r] * jnp.sqrt(one_minus_exp(2.0 * rate[r])) for r in range(order)]
-        for r in range(order):
-            weight_ref[pl.ds(half * SUBLANES * order + r, SUBLANES, stride=order), :] = weight[r]
+        decay = mode_rows(decays_ref, 0, order, order, chunks, half)
+        weight = mode_rows(weights_ref, order, order, 2 * order, chunks, half)
         own = places[half * SUBLANES : (half + 1) * SUBLANES]
         gain = jnp.concatenate([gain_ref[pl.ds(place, 1), :] for place in own], axis=0)
 
@@ -121,7 +141,7 @@
 
 
 def output_kernel(
-    places, order, rates_ref, weight_ref, carry_ref, local_ref, q_ref, _, out_ref, conv_ref, gated_ref, sems
+    places, order, decays_ref, weights_ref, carry_ref, local_ref, q_ref, _, out_ref, conv_ref, gated_ref, sems
 ):
     chunks = len(places)
     length = local_ref.shape[0] // chunks
@@ -130,8 +150,8 @@
     @pl.when(lax.axis_index("seq") > 0)
     def _():
         for half in range(chunks // SUBLANES):
-            decay = [jnp.exp(-rate) for rate in mode_rows(rates_ref, 0, order, order, chunks, half)]
-            weight = mode_rows(weight_ref, 0, order, order, chunks, half)
+            decay = mode_rows(decays_ref, 0, order, order, chunks, half)
+            weight = mode_rows(weights_ref, order, order, 2 * order, chunks, half)
             carry = mode_rows(carry_ref, 0, order, order, chunks, half)
 
             def steps(i, fading):
@@ -209,46 +229,51 @@
         members, places = members[::-1], places[::-1]
 
     own_rates, own_residues = rates.T, residues.T
-    copies = jnp.broadcast_to(own_rates[None], (blocks,) + own_rates.shape)
-    all_rates = to_chunks(all_to_all(copies, members)).reshape(chunks * order, LANES)
-
-    series = call(
-        functools.partial(prepare_kernel, places),
-        jax.ShapeDtypeStruct((length * chunks, LANES), f32),
+    copies = call(
+        copies_kernel,
+        jax.ShapeDtypeStruct((blocks,) + own_rates.shape, f32),
+        pltpu.with_memory_space_constraint(own_rates, pltpu.HBM),
+        in_spaces=[pl.ANY],
+        scratch=[pltpu.VMEM(own_rates.shape, f32), pltpu.SemaphoreType.DMA],
+        flops=COPIES_COST,
+    )
+    decays = to_chunks(all_to_all(copies, members)).reshape(chunks * order, LANES)
+
+    whole_chunk = own_rates.shape[1] == LANES
+    unused = jnp.zeros((order, LANES), f32)
+    series, ends = call(
+        functools.partial(state_kernel, places, order),
+        (
+            jax.ShapeDtypeStruct((length * chunks, LANES), f32),
+            jax.ShapeDtypeStruct((chunks * 2 * order, LANES), f32),
+        ),
+        decays,
+        own_rates if whole_chunk else unused,
+        own_residues if whole_chunk else unused,
         k_proj,
         value_projection,
-        flops=channels * length,
-    )
-    whole_chunk = own_residues.shape[1] == LANES
-    ends = call(
-        functools.partial(state_kernel, chunks, order),
-        jax.ShapeDtypeStruct((chunks * 2 * order, LANES), f32),
-        all_rates,
-        own_residues if whole_chunk else jnp.zeros((order, LANES), f32),
-        series,
         flops=2 * order * channels * length,
     )
     local_series, ends = lax.optimization_barrier((series, ends))
     ends = from_chunks(ends.reshape(chunks, 2 * order, LANES), blocks)
     if not whole_chunk:
-        ends = ends.at[:, order:].set(own_residues)
+        ends = ends.at[:, order:].set(weights_of(own_residues, own_rates))
     ends = all_to_all(ends, members)
-    all_residues = to_chunks(ends).reshape(chunks * 2 * order, LANES)
+    weights = to_chunks(ends).reshape(chunks * 2 * order, LANES)
     out_shape = jax.ShapeDtypeStruct((channels, length), jnp.bfloat16)
     out_scratch = [pltpu.VMEM(out_shape.shape, out_shape.dtype), pltpu.SemaphoreType.DMA((chunks,))]
-    local, weights, out = call(
+    local, out = call(
         functools.partial(local_kernel, places, order),
         (
             jax.ShapeDtypeStruct((length * chunks, LANES), f32),
-            jax.ShapeDtypeStruct((chunks * order, LANES), f32),
             out_shape,
         ),
-        all_rates,
-        all_residues,
+        decays,
+        weights,
         local_series,
         direct_gain.reshape(chunks, LANES),
         q_proj,
-        out_spaces=(pltpu.VMEM, pltpu.VMEM, pl.ANY),
+        out_spaces=(pltpu.VMEM, pl.ANY),
         scratch=out_scratch,
         flops=4 * order * channels * length,
     )
@@ -263,7 +288,7 @@
     return call(
         functools.partial(output_kernel, places, order),
         out_shape,
-        all_rates,
+        decays,
         weights,
         carry,
         local,

time: 42.8 us -> 41.6 us (0.972)
  blocking collectives: 13 us -> 24.8 us
  starting transfers between devices: 14.1 us -> 6.15 us
  local copies, waits for them, and re-layouts: 3.45 us -> 0.03 us
  waiting for transfers between devices: 4.11 us -> 1.97 us
  Pallas kernels: 7.58 us -> 8.17 us
    all_to_all x1 -> x2, blocking collectives: 13 us -> 24.8 us  [all_to_all(): lax.all_to_all(pieces, 'seq', split_axis=0, concat_axis=0, axis_index_gro...]
    all_to_all x2 -> x1, starting transfers between devices: 14.1 us -> 6.15 us  [all_to_all(): lax.all_to_all(pieces, 'seq', split_axis=0, concat_axis=0, axis_index_gro...]
    all_to_all x2 -> x1, waiting for transfers between devices: 4.11 us -> 1.97 us  [all_to_all(): lax.all_to_all(pieces, 'seq', split_axis=0, concat_axis=0, axis_index_gro...]
    unnamed x12, local copies, waits for them, and re-layouts: 2.09 us -> 0.03 us
    broadcast_in_dim x1 -> x0, local copies, waits for them, and re-layouts: 1.36 us -> none  [shards(): copies = jnp.broadcast_to(own_rates[None], (blocks,) + own_rates.shape)]
    pallas_call x5, Pallas kernels: 7.58 us -> 8.17 us  [call(): pl.pallas_call(kernel, out_shape=out_shape, in_specs=[pl.BlockSpec(memory...]
  transfers between devices with their start and end apart: 2 -> 1, of which waited for: 2 -> 1; matrix products, arithmetic and copies ran while one was open for 0% -> 0% of each run, Pallas kernels for 8% -> 6%
where the time goes in v14:
time: 41.6 us; the launch traced here: 41.2 us
  blocking collectives  24.8 us (60%)
  Pallas kernels  8.17 us (20%)
  starting transfers between devices  6.15 us (15%)
  waiting for transfers between devices  1.97 us (5%)
    all_to_all x2, blocking collectives, all_to_all(): lax.all_to_all(pieces, 'seq', split_axis=0, concat_axis=0, axis_index_gro...  24.8 us
    pallas_call x5, Pallas kernels, call(): pl.pallas_call(kernel, out_shape=out_shape, in_specs=[pl.BlockSpec(memory...  8.17 us
    all_to_all x1, starting transfers between devices, all_to_all(): lax.all_to_all(pieces, 'seq', split_axis=0, concat_axis=0, axis_index_gro...  6.15 us
    all_to_all x1, waiting for transfers between devices, all_to_all(): lax.all_to_all(pieces, 'seq', split_axis=0, concat_axis=0, axis_index_gro...  1.97 us
  transfers between devices with their start and end apart: 1, of which 1 were waited for; matrix products, arithmetic and copies ran while one was open for 0% of the time, Pallas kernels for 6%

profile of v14, /device:TPU:2, one launch (start us, length us, event | category | flops | bytes accessed | tf_op | source)
XLA Modules:
  0.0 41.2 jit_solution(6364500408034374699)
XLA Ops:
  0.0 0.0 copy-start.1
  0.0 0.0 copy-start.2
  0.0 0.0 copy-start.3
  0.0 0.0 copy-start.4
  0.0 0.8 %shard_map.64 = f32[16,16,128]{2,1,0:T(8,128)S(1)} custom-call(f32[16,128]{1,0:T(8,128)} %bitcast.14), custom_call_target="tpu_custom_call" | custom-call | flops 10000000000 | bytes 8192 | tf_op jit(solution)/shard_map/pallas_call | solution.py:184
  0.8 11.9 %all_to_all.15 = f32[16,16,128]{2,1,0:T(8,128)S(1)} all-to-all(f32[16,16,128]{2,1,0:T(8,128)S(1)} %shard_map.64), channel_id=1, replica_groups={{30,28,26,24,22,20,18,16,14,12,10,8,6,4,2,0},{31,29,27,25,23,21,19,17,1..., dimensions={0} | all-to-all | bytes 262144 | tf_op jit(solution)/shard_map/all_to_all | solution.py:218
  12.7 0.0 copy-done.1
  12.7 0.0 copy-done.2
  12.7 0.0 copy-done.3
  12.7 0.0 copy-done.4
  12.7 1.7 %shard_map.65 = (f32[2048,128]{1,0:T(8,128)S(1)}, f32[512,128]{1,0:T(8,128)S(1)}) custom-call(f32[256,128]{1,0:T(8,128)S(1)} %bitcast.9, f32[16,128]{1,0:T(8,128)S(1)} %bitcast.15, f32[16,128]{1,0:T(8,128)S(1)} %bitcast.17, bf16[2048,128]{1,0:T(8,128)(2,1)S(1)} %copy-done.1, bf16[2048,128]{1,0:T(8,128)(2,1)S(1)} %copy-done.2), custom_call_target="tpu_custom_call" | custom-call | flops 8388608 | bytes 1196032 | tf_op jit(solution)/shard_map/pallas_call | solution.py:184
  14.4 0.0 copy-start
  14.4 13.0 %all_to_all.16.ends_ref = f32[16,32,128]{2,1,0:T(8,128)S(1)} all-to-all(f32[16,32,128]{2,1,0:T(8,128)S(1)} %bitcast.13), channel_id=1, replica_groups={{30,28,26,24,22,20,18,16,14,12,10,8,6,4,2,0},{31,29,27,25,23,21,19,17,1..., dimensions={0} | all-to-all | bytes 524288 | tf_op jit(solution)/shard_map/all_to_all | solution.py:218
  27.4 0.7 %shard_map.66 = f32[16,16,128]{2,1,0:T(8,128)} custom-call(f32[16,128]{1,0:T(8,128)S(1)} %bitcast.16, f32[16,32,128]{2,1,0:T(8,128)S(1)} %all_to_all.16.ends_ref), custom_call_target="tpu_custom_call" | custom-call | bytes 270336 | tf_op jit(solution)/shard_map/pallas_call | solution.py:184
  28.1 0.0 copy-start.5
  28.1 6.1 %all-to-all-start.2 = ((f32[16,16,128]{2,1,0:T(8,128)}), f32[16,16,128]{2,1,0:T(8,128)S(1)}, u32[]{:S(2)}, u32[]{:S(2)}) async-start(f32[16,16,128]{2,1,0:T(8,128)} %shard_map.66), calls=%async_computation.2 | async-start | bytes 262144 | tf_op jit(solution)/shard_map/all_to_all | solution.py:218
  34.2 0.0 copy-done
  34.2 0.0 copy-done.5
  34.2 2.6 %shard_map.67 = (f32[2048,128]{1,0:T(8,128)S(1)}, bf16[2048,128]{1,0:T(8,128)(2,1)}) custom-call(f32[256,128]{1,0:T(8,128)S(1)} %bitcast.10, f32[512,128]{1,0:T(8,128)S(1)} %bitcast.7, f32[2048,128]{1,0:T(8,128)S(1)} %get-tuple-element.10.series_ref, f32[16,128]{1,0:T(8,128)S(1)} %bitcast.18, bf16[2048,128]{1,0:T(8,128)(2,1)S(1)} %copy-done), custom_call_target="tpu_custom_call" | custom-call | flops 16777216 | bytes 1974272 | tf_op jit(solution)/shard_map/pallas_call | solution.py:184
  36.8 2.0 %all-to-all-done.2 = f32[16,16,128]{2,1,0:T(8,128)S(1)} async-done(((f32[16,16,128]{2,1,0:T(8,128)}), f32[16,16,128]{2,1,0:T(8,128)S(1)}, u32[]{:S(2)}, u32[]{:S(2)}) %all-to-all-start.2) | async-done | bytes 131104 | tf_op jit(solution)/shard_map/all_to_all | solution.py:218
  38.8 2.4 %shard_map.68 = bf16[2048,128]{1,0:T(8,128)(2,1)} custom-call(f32[256,128]{1,0:T(8,128)S(1)} %bitcast.11, f32[512,128]{1,0:T(8,128)S(1)} %bitcast.8, f32[256,128]{1,0:T(8,128)S(1)} %bitcast.12, f32[2048,128]{1,0:T(8,128)S(1)} %get-tuple-element.11.local_ref, bf16[2048,128]{1,0:T(8,128)(2,1)S(1)} %copy-done, ...), custom_call_target="tpu_custom_call", output_to_operand_aliasing={{}: (5, {})} | custom-call | flops 8388608 | bytes 2621440 | tf_op jit(solution)/shard_map/pallas_call | solution.py:184
Async XLA Ops:
  0.0 12.7 %copy-start.1 = (bf16[2048,128]{1,0:T(8,128)(2,1)S(1)}, bf16[2048,128]{1,0:T(8,128)(2,1)}, u32[]{:S(2)}) copy-start(bf16[2048,128]{1,0:T(8,128)(2,1)} %k_ref.1) | copy-start | bytes 1572868
  0.0 12.7 %copy-start.2 = (bf16[2048,128]{1,0:T(8,128)(2,1)S(1)}, bf16[2048,128]{1,0:T(8,128)(2,1)}, u32[]{:S(2)}) copy-start(bf16[2048,128]{1,0:T(8,128)(2,1)} %v_ref.1) | copy-start | bytes 1572868
  0.0 12.7 %copy-start.3 = (f32[128,16]{0,1:T(8,128)S(1)}, f32[128,16]{0,1:T(8,128)}, u32[]{:S(2)}) copy-start(f32[128,16]{0,1:T(8,128)} %param.10) | copy-start | bytes 24580
  0.0 12.7 %copy-start.4 = (f32[128,16]{0,1:T(8,128)S(1)}, f32[128,16]{0,1:T(8,128)}, u32[]{:S(2)}) copy-start(f32[128,16]{0,1:T(8,128)} %param.9) | copy-start | bytes 24580
  14.4 19.8 %copy-start = (bf16[2048,128]{1,0:T(8,128)(2,1)S(1)}, bf16[2048,128]{1,0:T(8,128)(2,1)}, u32[]{:S(2)}) copy-start(bf16[2048,128]{1,0:T(8,128)(2,1)} %q_ref.3) | copy-start | bytes 1572868
  28.1 6.2 %copy-start.5 = (f32[2048]{0:T(1024)S(1)}, f32[2048]{0:T(1024)}, u32[]{:S(2)}) copy-start(f32[2048]{0:T(1024)} %param.11) | copy-start | bytes 24580
  28.1 10.8 %all-to-all-start.2 = ((f32[16,16,128]{2,1,0:T(8,128)}), f32[16,16,128]{2,1,0:T(8,128)S(1)}, u32[]{:S(2)}, u32[]{:S(2)}) async-start(f32[16,16,128]{2,1,0:T(8,128)} %shard_map.66), calls=%async_computation.2 | async-start | bytes 262144 | tf_op jit(solution)/shard_map/all_to_all | solution.py:218

commit v15 on v14

--- a/solution.py
+++ b/solution.py
@@ -22,6 +22,15 @@
         copies_ref[piece] = decay
 
 
+def token_rows(half, length, token):
+    row = (half * length + token) * SUBLANES
+    return pl.ds(row if isinstance(row, int) else pl.multiple_of(row, SUBLANES), SUBLANES)
+
+
+def chunk_rows(chunk, length):
+    return pl.ds(chunk // SUBLANES * length * SUBLANES + chunk % SUBLANES, length, stride=SUBLANES)
+
+
 def mode_rows(ref, base, order, per_chunk, chunks, half):
     first = half * SUBLANES * per_chunk + base
     return [ref[pl.ds(first + r, SUBLANES, stride=per_chunk), :] for r in range(order)]
@@ -46,7 +55,7 @@
     def build(chunk):
         rows = pl.ds(places[chunk] * LANES, LANES)
         gated = k_ref[rows, :].astype(jnp.float32) * v_ref[rows, :].astype(jnp.float32)
-        series_ref[pl.ds(chunk, length, stride=chunks), :] = gated.T
+        series_ref[chunk_rows(chunk, length), :] = gated.T
 
     weight = weights_of(residue_ref[...], rate_ref[...])
     for chunk in range(chunks):
@@ -59,10 +68,7 @@
         def steps(i, state):
             state = list(state)
             for u in range(tokens):
-                row = (i * tokens + u) * chunks + half * SUBLANES
-                if not isinstance(row, int):
-                    row = pl.multiple_of(row, SUBLANES)
-                x = series_ref[pl.ds(row, SUBLANES), :]
+                x = series_ref[token_rows(half, length, i * tokens + u), :]
                 for r in range(order):
                     state[r] = decay[r] * state[r] + x
             return tuple(state)
@@ -99,10 +105,9 @@
 
 
 def finish(chunk, places, conv_ref, q_ref, gated_ref, out_ref, sems):
-    chunks = len(places)
-    length = conv_ref.shape[0] // chunks
+    length = conv_ref.shape[0] // len(places)
     rows = pl.ds(places[chunk] * LANES, LANES)
-    conv = conv_ref[pl.ds(chunk, length, stride=chunks), :].T
+    conv = conv_ref[chunk_rows(chunk, length), :].T
     gated_ref[rows, :] = (q_ref[rows, :].astype(jnp.float32) * conv).astype(jnp.bfloat16)
     leaving(chunk, places, gated_ref, out_ref, sems).start()
 
@@ -121,12 +126,12 @@
         def steps(i, state):
             state = list(state)
             for u in range(UNROLL):
-                row = pl.multiple_of((i * UNROLL + u) * chunks + half * SUBLANES, SUBLANES)
-                x = series_ref[pl.ds(row, SUBLANES), :]
+                rows = token_rows(half, length, i * UNROLL + u)
+                x = series_ref[rows, :]
                 for r in range(order):
                     state[r] = decay[r] * state[r] + x
                 terms = [weight[r] * state[r] for r in range(order)]
-                conv_ref[pl.ds(row, SUBLANES), :] = tree_sum(terms + [gain * x])
+                conv_ref[rows, :] = tree_sum(terms + [gain * x])
             return tuple(state)
 
         zero = jnp.zeros((SUBLANES, LANES), jnp.float32)
@@ -157,11 +162,9 @@
             def steps(i, fading):
                 fading = list(fading)
                 for u in range(tokens):
-                    row = (i * tokens + u) * chunks + half * SUBLANES
-                    if not isinstance(row, int):
-                        row = pl.multiple_of(row, SUBLANES)
+                    rows = token_rows(half, length, i * tokens + u)
                     fading = [decay[r] * fading[r] for r in range(order)]
-                    conv_ref[pl.ds(row, SUBLANES), :] = tree_sum(fading + [local_ref[pl.ds(row, SUBLANES), :]])
+                    conv_ref[rows, :] = tree_sum(fading + [local_ref[rows, :]])
                 return tuple(fading)
 
             fading = tuple(weight[r] * carry[r] for r in range(order))

time: 41.6 us -> 41.4 us (level)
  no operation moved by 1% of the time
where the time goes in v15:
time: 41.4 us; the launch traced here: 41.1 us
  blocking collectives  24.8 us (60%)
  Pallas kernels  8.02 us (19%)
  starting transfers between devices  6.15 us (15%)
  waiting for transfers between devices  1.97 us (5%)
    all_to_all x2, blocking collectives, all_to_all(): lax.all_to_all(pieces, 'seq', split_axis=0, concat_axis=0, axis_index_gro...  24.8 us
    pallas_call x5, Pallas kernels, call(): pl.pallas_call(kernel, out_shape=out_shape, in_specs=[pl.BlockSpec(memory...  8.02 us
    all_to_all x1, starting transfers between devices, all_to_all(): lax.all_to_all(pieces, 'seq', split_axis=0, concat_axis=0, axis_index_gro...  6.15 us
    all_to_all x1, waiting for transfers between devices, all_to_all(): lax.all_to_all(pieces, 'seq', split_axis=0, concat_axis=0, axis_index_gro...  1.97 us
  transfers between devices with their start and end apart: 1, of which 1 were waited for; matrix products, arithmetic and copies ran while one was open for 0% of the time, Pallas kernels for 6%

profile of v15, /device:TPU:2, one launch (start us, length us, event | category | flops | bytes accessed | tf_op | source)
XLA Modules:
  0.0 41.1 jit_solution(10071432192026399595)
XLA Ops:
  0.0 0.0 copy-start.1
  0.0 0.0 copy-start.2
  0.0 0.0 copy-start.3
  0.0 0.0 copy-start.4
  0.0 0.8 %shard_map.64 = f32[16,16,128]{2,1,0:T(8,128)S(1)} custom-call(f32[16,128]{1,0:T(8,128)} %bitcast.14), custom_call_target="tpu_custom_call" | custom-call | flops 10000000000 | bytes 8192 | tf_op jit(solution)/shard_map/pallas_call | solution.py:187
  0.8 11.9 %all_to_all.15 = f32[16,16,128]{2,1,0:T(8,128)S(1)} all-to-all(f32[16,16,128]{2,1,0:T(8,128)S(1)} %shard_map.64), channel_id=1, replica_groups={{30,28,26,24,22,20,18,16,14,12,10,8,6,4,2,0},{31,29,27,25,23,21,19,17,1..., dimensions={0} | all-to-all | bytes 262144 | tf_op jit(solution)/shard_map/all_to_all | solution.py:221
  12.7 0.0 copy-done.1
  12.7 0.0 copy-done.2
  12.7 0.0 copy-done.3
  12.7 0.0 copy-done.4
  12.7 1.6 %shard_map.65 = (f32[2048,128]{1,0:T(8,128)S(1)}, f32[512,128]{1,0:T(8,128)S(1)}) custom-call(f32[256,128]{1,0:T(8,128)S(1)} %bitcast.9, f32[16,128]{1,0:T(8,128)S(1)} %bitcast.15, f32[16,128]{1,0:T(8,128)S(1)} %bitcast.17, bf16[2048,128]{1,0:T(8,128)(2,1)S(1)} %copy-done.1, bf16[2048,128]{1,0:T(8,128)(2,1)S(1)} %copy-done.2), custom_call_target="tpu_custom_call" | custom-call | flops 8388608 | bytes 1196032 | tf_op jit(solution)/shard_map/pallas_call | solution.py:187
  14.3 0.0 copy-start
  14.3 13.0 %all_to_all.16.ends_ref = f32[16,32,128]{2,1,0:T(8,128)S(1)} all-to-all(f32[16,32,128]{2,1,0:T(8,128)S(1)} %bitcast.13), channel_id=1, replica_groups={{30,28,26,24,22,20,18,16,14,12,10,8,6,4,2,0},{31,29,27,25,23,21,19,17,1..., dimensions={0} | all-to-all | bytes 524288 | tf_op jit(solution)/shard_map/all_to_all | solution.py:221
  27.3 0.7 %shard_map.66 = f32[16,16,128]{2,1,0:T(8,128)} custom-call(f32[16,128]{1,0:T(8,128)S(1)} %bitcast.16, f32[16,32,128]{2,1,0:T(8,128)S(1)} %all_to_all.16.ends_ref), custom_call_target="tpu_custom_call" | custom-call | bytes 270336 | tf_op jit(solution)/shard_map/pallas_call | solution.py:187
  28.0 0.0 copy-start.5
  28.0 6.1 %all-to-all-start.2 = ((f32[16,16,128]{2,1,0:T(8,128)}), f32[16,16,128]{2,1,0:T(8,128)S(1)}, u32[]{:S(2)}, u32[]{:S(2)}) async-start(f32[16,16,128]{2,1,0:T(8,128)} %shard_map.66), calls=%async_computation.2 | async-start | bytes 262144 | tf_op jit(solution)/shard_map/all_to_all | solution.py:221
  34.1 0.0 copy-done
  34.1 0.0 copy-done.5
  34.1 2.6 %shard_map.67 = (f32[2048,128]{1,0:T(8,128)S(1)}, bf16[2048,128]{1,0:T(8,128)(2,1)}) custom-call(f32[256,128]{1,0:T(8,128)S(1)} %bitcast.10, f32[512,128]{1,0:T(8,128)S(1)} %bitcast.7, f32[2048,128]{1,0:T(8,128)S(1)} %get-tuple-element.10.series_ref, f32[16,128]{1,0:T(8,128)S(1)} %bitcast.18, bf16[2048,128]{1,0:T(8,128)(2,1)S(1)} %copy-done), custom_call_target="tpu_custom_call" | custom-call | flops 16777216 | bytes 1974272 | tf_op jit(solution)/shard_map/pallas_call | solution.py:187
  36.7 2.0 %all-to-all-done.2 = f32[16,16,128]{2,1,0:T(8,128)S(1)} async-done(((f32[16,16,128]{2,1,0:T(8,128)}), f32[16,16,128]{2,1,0:T(8,128)S(1)}, u32[]{:S(2)}, u32[]{:S(2)}) %all-to-all-start.2) | async-done | bytes 131104 | tf_op jit(solution)/shard_map/all_to_all | solution.py:221
  38.7 2.4 %shard_map.68 = bf16[2048,128]{1,0:T(8,128)(2,1)} custom-call(f32[256,128]{1,0:T(8,128)S(1)} %bitcast.11, f32[512,128]{1,0:T(8,128)S(1)} %bitcast.8, f32[256,128]{1,0:T(8,128)S(1)} %bitcast.12, f32[2048,128]{1,0:T(8,128)S(1)} %get-tuple-element.11.local_ref, bf16[2048,128]{1,0:T(8,128)(2,1)S(1)} %copy-done, ...), custom_call_target="tpu_custom_call", output_to_operand_aliasing={{}: (5, {})} | custom-call | flops 8388608 | bytes 2621440 | tf_op jit(solution)/shard_map/pallas_call | solution.py:187
Async XLA Ops:
  0.0 12.7 %copy-start.1 = (bf16[2048,128]{1,0:T(8,128)(2,1)S(1)}, bf16[2048,128]{1,0:T(8,128)(2,1)}, u32[]{:S(2)}) copy-start(bf16[2048,128]{1,0:T(8,128)(2,1)} %k_ref.1) | copy-start | bytes 1572868
  0.0 12.7 %copy-start.2 = (bf16[2048,128]{1,0:T(8,128)(2,1)S(1)}, bf16[2048,128]{1,0:T(8,128)(2,1)}, u32[]{:S(2)}) copy-start(bf16[2048,128]{1,0:T(8,128)(2,1)} %v_ref.1) | copy-start | bytes 1572868
  0.0 12.7 %copy-start.3 = (f32[128,16]{0,1:T(8,128)S(1)}, f32[128,16]{0,1:T(8,128)}, u32[]{:S(2)}) copy-start(f32[128,16]{0,1:T(8,128)} %param.10) | copy-start | bytes 24580
  0.0 12.7 %copy-start.4 = (f32[128,16]{0,1:T(8,128)S(1)}, f32[128,16]{0,1:T(8,128)}, u32[]{:S(2)}) copy-start(f32[128,16]{0,1:T(8,128)} %param.9) | copy-start | bytes 24580
  14.3 19.8 %copy-start = (bf16[2048,128]{1,0:T(8,128)(2,1)S(1)}, bf16[2048,128]{1,0:T(8,128)(2,1)}, u32[]{:S(2)}) copy-start(bf16[2048,128]{1,0:T(8,128)(2,1)} %q_ref.3) | copy-start | bytes 1572868
  28.0 6.2 %copy-start.5 = (f32[2048]{0:T(1024)S(1)}, f32[2048]{0:T(1024)}, u32[]{:S(2)}) copy-start(f32[2048]{0:T(1024)} %param.11) | copy-start | bytes 24580
  28.0 10.8 %all-to-all-start.2 = ((f32[16,16,128]{2,1,0:T(8,128)}), f32[16,16,128]{2,1,0:T(8,128)S(1)}, u32[]{:S(2)}, u32[]{:S(2)}) async-start(f32[16,16,128]{2,1,0:T(8,128)} %shard_map.66), calls=%async_computation.2 | async-start | bytes 262144 | tf_op jit(solution)/shard_map/all_to_all | solution.py:221

commit v16 on v15

--- a/solution.py
+++ b/solution.py
@@ -8,7 +8,6 @@
 
 LANES = 128
 SUBLANES = 8
-UNROLL = 8
 COPIES_COST = 10**10
 VMEM_LIMIT = 32 * 1024 * 1024
 
@@ -84,14 +83,6 @@
             state_ref[pl.ds(half * SUBLANES * 2 * order + r, SUBLANES, stride=2 * order), :] = state[r]
 
 
-def prefix_kernel(length, members, rate_ref, ends_ref, starts_ref):
-    span_decay = jnp.exp(-float(length) * rate_ref[...])
-    carry = jnp.zeros(rate_ref.shape, jnp.float32)
-    for block in range(len(members)):
-        starts_ref[members.index(block)] = carry
-        carry = span_decay * carry + ends_ref[members.index(block), : rate_ref.shape[0]]
-
-
 def tree_sum(terms):
     terms = list(terms)
     while len(terms) > 1:
@@ -112,12 +103,13 @@
     leaving(chunk, places, gated_ref, out_ref, sems).start()
 
 
-def local_kernel(
-    places, order, decays_ref, weights_ref, series_ref, gain_ref, q_ref, conv_ref, out_ref, gated_ref, sems
-):
+def convolve(halves, places, order, carry_ref, decays_ref, weights_ref, series_ref, gain_ref, q_ref, out):
+    out_ref, conv_ref, gated_ref, sems = out
     chunks = len(places)
     length = series_ref.shape[0] // chunks
-    for half in range(chunks // SUBLANES):
+    tokens = length // SUBLANES
+    todo = []
+    for half in halves:
         decay = mode_rows(decays_ref, 0, order, order, chunks, half)
         weight = mode_rows(weights_ref, order, order, 2 * order, chunks, half)
         own = places[half * SUBLANES : (half + 1) * SUBLANES]
@@ -125,59 +117,63 @@
 
         def steps(i, state):
             state = list(state)
-            for u in range(UNROLL):
-                rows = token_rows(half, length, i * UNROLL + u)
+            for u in range(tokens):
+                rows = token_rows(half, length, i * tokens + u)
                 x = series_ref[rows, :]
                 for r in range(order):
                     state[r] = decay[r] * state[r] + x
-                terms = [weight[r] * state[r] for r in range(order)]
-                conv_ref[rows, :] = tree_sum(terms + [gain * x])
+                conv_ref[rows, :] = tree_sum([weight[r] * state[r] for r in range(order)] + [gain * x])
             return tuple(state)
 
-        zero = jnp.zeros((SUBLANES, LANES), jnp.float32)
-        lax.fori_loop(0, length // UNROLL, steps, (zero,) * order)
+        if carry_ref is None:
+            state = (jnp.zeros((SUBLANES, LANES), jnp.float32),) * order
+        else:
+            state = tuple(mode_rows(carry_ref, 0, order, order, chunks, half))
+        if todo:
+            for i, chunk in enumerate(todo):
+                state = steps(i, state)
+                finish(chunk, places, conv_ref, q_ref, gated_ref, out_ref, sems)
+        else:
+            lax.fori_loop(0, SUBLANES, steps, state)
+        todo = range(half * SUBLANES, (half + 1) * SUBLANES)
+    for chunk in todo:
+        finish(chunk, places, conv_ref, q_ref, gated_ref, out_ref, sems)
+    for half in halves:
+        for chunk in range(half * SUBLANES, (half + 1) * SUBLANES):
+            leaving(chunk, places, gated_ref, out_ref, sems).wait()
+
+
+def prefix_kernel(
+    members, places, order, rate_ref, ends_ref, decays_ref, weights_ref, series_ref, gain_ref, q_ref,
+    starts_ref, out_ref, *scratch
+):
+    length = series_ref.shape[0] // len(places)
+    span_decay = jnp.exp(-float(length) * rate_ref[...])
+    carry = jnp.zeros(rate_ref.shape, jnp.float32)
+    for block in range(len(members)):
+        starts_ref[members.index(block)] = carry
+        carry = span_decay * carry + ends_ref[members.index(block), : rate_ref.shape[0]]
 
     @pl.when(lax.axis_index("seq") == 0)
     def _():
-        for chunk in range(chunks):
-            finish(chunk, places, conv_ref, q_ref, gated_ref, out_ref, sems)
-        for chunk in range(chunks):
-            leaving(chunk, places, gated_ref, out_ref, sems).wait()
+        halves = range(len(places) // SUBLANES // 2)
+        refs = (decays_ref, weights_ref, series_ref, gain_ref, q_ref, (out_ref,) + scratch)
+        convolve(halves, places, order, None, *refs)
 
 
 def output_kernel(
-    places, order, decays_ref, weights_ref, carry_ref, local_ref, q_ref, _, out_ref, conv_ref, gated_ref, sems
+    places, order, carry_ref, decays_ref, weights_ref, series_ref, gain_ref, q_ref, _, out_ref, *scratch
 ):
-    chunks = len(places)
-    length = local_ref.shape[0] // chunks
-    tokens = length // SUBLANES
+    halves = len(places) // SUBLANES
+    refs = (carry_ref, decays_ref, weights_ref, series_ref, gain_ref, q_ref, (out_ref,) + scratch)
+
+    @pl.when(lax.axis_index("seq") == 0)
+    def _():
+        convolve(range(halves // 2, halves), places, order, *refs)
 
     @pl.when(lax.axis_index("seq") > 0)
     def _():
-        for half in range(chunks // SUBLANES):
-            decay = mode_rows(decays_ref, 0, order, order, chunks, half)
-            weight = mode_rows(weights_ref, order, order, 2 * order, chunks, half)
-            carry = mode_rows(carry_ref, 0, order, order, chunks, half)
-
-            def steps(i, fading):
-                fading = list(fading)
-                for u in range(tokens):
-                    rows = token_rows(half, length, i * tokens + u)
-                    fading = [decay[r] * fading[r] for r in range(order)]
-                    conv_ref[rows, :] = tree_sum(fading + [local_ref[rows, :]])
-                return tuple(fading)
-
-            fading = tuple(weight[r] * carry[r] for r in range(order))
-            if half == 0:
-                lax.fori_loop(0, SUBLANES, steps, fading)
-            else:
-                for i in range(SUBLANES):
-                    fading = steps(i, fading)
-                    finish((half - 1) * SUBLANES + i, places, conv_ref, q_ref, gated_ref, out_ref, sems)
-        for chunk in range(chunks - SUBLANES, chunks):
-            finish(chunk, places, conv_ref, q_ref, gated_ref, out_ref, sems)
-        for chunk in range(chunks):
-            leaving(chunk, places, gated_ref, out_ref, sems).wait()
+        convolve(range(halves), places, order, *refs)
 
 
 def call(kernel, out_shape, *args, in_spaces=None, out_spaces=None, aliases=None, scratch=(), flops=0):
@@ -257,50 +253,39 @@
         value_projection,
         flops=2 * order * channels * length,
     )
-    local_series, ends = lax.optimization_barrier((series, ends))
     ends = from_chunks(ends.reshape(chunks, 2 * order, LANES), blocks)
     if not whole_chunk:
         ends = ends.at[:, order:].set(weights_of(own_residues, own_rates))
     ends = all_to_all(ends, members)
     weights = to_chunks(ends).reshape(chunks * 2 * order, LANES)
+
+    operands = (decays, weights, series, direct_gain.reshape(chunks, LANES), q_proj)
     out_shape = jax.ShapeDtypeStruct((channels, length), jnp.bfloat16)
-    out_scratch = [pltpu.VMEM(out_shape.shape, out_shape.dtype), pltpu.SemaphoreType.DMA((chunks,))]
-    local, out = call(
-        functools.partial(local_kernel, places, order),
-        (
-            jax.ShapeDtypeStruct((length * chunks, LANES), f32),
-            out_shape,
-        ),
-        decays,
-        weights,
-        local_series,
-        direct_gain.reshape(chunks, LANES),
-        q_proj,
-        out_spaces=(pltpu.VMEM, pl.ANY),
-        scratch=out_scratch,
-        flops=4 * order * channels * length,
-    )
-    starts = call(
-        functools.partial(prefix_kernel, length, members),
-        jax.ShapeDtypeStruct((blocks,) + own_rates.shape, f32),
+    scratch = [
+        pltpu.VMEM((length * chunks, LANES), f32),
+        pltpu.VMEM(out_shape.shape, out_shape.dtype),
+        pltpu.SemaphoreType.DMA((chunks,)),
+    ]
+    starts, out = call(
+        functools.partial(prefix_kernel, members, places, order),
+        (jax.ShapeDtypeStruct((blocks,) + own_rates.shape, f32), out_shape),
         own_rates,
         ends,
-    )
-    starts = all_to_all(starts, members)
-    carry = to_chunks(starts).reshape(chunks * order, LANES)
+        *operands,
+        out_spaces=(pltpu.VMEM, pl.ANY),
+        scratch=scratch,
+    )
+    carry = to_chunks(all_to_all(starts, members)).reshape(chunks * order, LANES)
     return call(
         functools.partial(output_kernel, places, order),
         out_shape,
-        decays,
-        weights,
         carry,
-        local,
-        q_proj,
+        *operands,
         out,
         out_spaces=pl.ANY,
-        aliases={5: 0},
-        scratch=[pltpu.VMEM((length * chunks, LANES), f32)] + out_scratch,
-        flops=2 * order * channels * length,
+        aliases={1 + len(operands): 0},
+        scratch=scratch,
+        flops=4 * order * channels * length,
     )
 
 

time: 41.4 us -> 43.8 us (1.058)
  blocking collectives: 24.8 us -> 37.3 us
  starting transfers between devices: 6.15 us -> 0 us
  Pallas kernels: 8.02 us -> 6.04 us
  waiting for transfers between devices: 1.97 us -> 0 us
    all_to_all x2 -> x3, blocking collectives: 24.8 us -> 37.3 us  [all_to_all(): lax.all_to_all(pieces, 'seq', split_axis=0, concat_axis=0, axis_index_gro...]
    all_to_all x1 -> x0, starting transfers between devices: 6.15 us -> none  [all_to_all(): lax.all_to_all(pieces, 'seq', split_axis=0, concat_axis=0, axis_index_gro...]
    pallas_call x5 -> x4, Pallas kernels: 8.02 us -> 6.04 us  [call(): pl.pallas_call(kernel, out_shape=out_shape, in_specs=[pl.BlockSpec(memory...]
    all_to_all x1 -> x0, waiting for transfers between devices: 1.97 us -> none  [all_to_all(): lax.all_to_all(pieces, 'seq', split_axis=0, concat_axis=0, axis_index_gro...]
  transfers between devices with their start and end apart: 1 -> 0, of which waited for: 1 -> 0; matrix products, arithmetic and copies ran while one was open for 0% -> 0% of each run, Pallas kernels for 6% -> 0%
where the time goes in v16:
time: 43.8 us; the launch traced here: 43.4 us
  blocking collectives  37.3 us (85%)
  Pallas kernels  6.04 us (14%)
    all_to_all x3, blocking collectives, all_to_all(): lax.all_to_all(pieces, 'seq', split_axis=0, concat_axis=0, axis_index_gro...  37.3 us
    pallas_call x4, Pallas kernels, call(): pl.pallas_call(kernel, out_shape=out_shape, in_specs=[pl.BlockSpec(memory...  6.04 us

profile of v16, /device:TPU:2, one launch (start us, length us, event | category | flops | bytes accessed | tf_op | source)
XLA Modules:
  0.0 43.4 jit_solution(17704018521199791577)
XLA Ops:
  0.0 0.0 copy-start.1
  0.0 0.0 copy-start.2
  0.0 0.0 copy-start.3
  0.0 0.0 copy-start.5
  0.0 0.8 %shard_map.64 = f32[16,16,128]{2,1,0:T(8,128)S(1)} custom-call(f32[16,128]{1,0:T(8,128)} %bitcast.14), custom_call_target="tpu_custom_call" | custom-call | flops 10000000000 | bytes 8192 | tf_op jit(solution)/shard_map/pallas_call | solution.py:183
  0.8 11.9 %all_to_all.15 = f32[16,16,128]{2,1,0:T(8,128)S(1)} all-to-all(f32[16,16,128]{2,1,0:T(8,128)S(1)} %shard_map.64), channel_id=1, replica_groups={{30,28,26,24,22,20,18,16,14,12,10,8,6,4,2,0},{31,29,27,25,23,21,19,17,1..., dimensions={0} | all-to-all | bytes 262144 | tf_op jit(solution)/shard_map/all_to_all | solution.py:217
  12.7 0.0 copy-done.1
  12.7 0.0 copy-done.2
  12.7 0.0 copy-done.3
  12.7 0.0 copy-done.5
  12.7 1.6 %shard_map.65 = (f32[2048,128]{1,0:T(8,128)S(1)}, f32[512,128]{1,0:T(8,128)S(1)}) custom-call(f32[256,128]{1,0:T(8,128)S(1)} %bitcast.9, f32[16,128]{1,0:T(8,128)S(1)} %bitcast.15, f32[16,128]{1,0:T(8,128)S(1)} %bitcast.19, bf16[2048,128]{1,0:T(8,128)(2,1)S(1)} %copy-done.1, bf16[2048,128]{1,0:T(8,128)(2,1)S(1)} %copy-done.2), custom_call_target="tpu_custom_call" | custom-call | flops 8388608 | bytes 1196032 | tf_op jit(solution)/shard_map/pallas_call | solution.py:183
  14.3 0.0 copy-start
  14.3 0.0 copy-start.4
  14.3 13.0 %all_to_all.16.ends_ref = f32[16,32,128]{2,1,0:T(8,128)S(1)} all-to-all(f32[16,32,128]{2,1,0:T(8,128)S(1)} %bitcast.13), channel_id=1, replica_groups={{30,28,26,24,22,20,18,16,14,12,10,8,6,4,2,0},{31,29,27,25,23,21,19,17,1..., dimensions={0} | all-to-all | bytes 524288 | tf_op jit(solution)/shard_map/all_to_all | solution.py:217
  27.3 0.0 copy-done
  27.3 0.0 copy-done.4
  27.3 0.2 shard_map.66
  27.5 12.4 %all_to_all.17 = f32[16,16,128]{2,1,0:T(8,128)S(1)} all-to-all(f32[16,16,128]{2,1,0:T(8,128)S(1)} %get-tuple-element.11), channel_id=1, replica_groups={{30,28,26,24,22,20,18,16,14,12,10,8,6,4,2,0},{31,29,27,25,23,21,19,17,1..., dimensions={0} | all-to-all | bytes 262144 | tf_op jit(solution)/shard_map/all_to_all | solution.py:217
  39.9 3.5 %shard_map.67 = bf16[2048,128]{1,0:T(8,128)(2,1)} custom-call(f32[256,128]{1,0:T(8,128)S(1)} %bitcast.12, f32[256,128]{1,0:T(8,128)S(1)} %bitcast.11, f32[512,128]{1,0:T(8,128)S(1)} %bitcast.8, f32[2048,128]{1,0:T(8,128)S(1)} %get-tuple-element.10.series_ref, f32[16,128]{1,0:T(8,128)S(1)} %bitcast.18, ...), custom_call_target="tpu_custom_call", output_to_operand_aliasing={{}: (6, {})} | custom-call | flops 16777216 | bytes 2629632 | tf_op jit(solution)/shard_map/pallas_call | solution.py:183
Async XLA Ops:
  0.0 12.7 %copy-start.1 = (bf16[2048,128]{1,0:T(8,128)(2,1)S(1)}, bf16[2048,128]{1,0:T(8,128)(2,1)}, u32[]{:S(2)}) copy-start(bf16[2048,128]{1,0:T(8,128)(2,1)} %k_ref.1) | copy-start | bytes 1572868
  0.0 12.7 %copy-start.2 = (bf16[2048,128]{1,0:T(8,128)(2,1)S(1)}, bf16[2048,128]{1,0:T(8,128)(2,1)}, u32[]{:S(2)}) copy-start(bf16[2048,128]{1,0:T(8,128)(2,1)} %v_ref.1) | copy-start | bytes 1572868
  0.0 12.7 %copy-start.3 = (f32[128,16]{0,1:T(8,128)S(1)}, f32[128,16]{0,1:T(8,128)}, u32[]{:S(2)}) copy-start(f32[128,16]{0,1:T(8,128)} %param.10) | copy-start | bytes 24580
  0.0 12.7 %copy-start.5 = (f32[128,16]{0,1:T(8,128)S(1)}, f32[128,16]{0,1:T(8,128)}, u32[]{:S(2)}) copy-start(f32[128,16]{0,1:T(8,128)} %param.9) | copy-start | bytes 24580
  14.3 13.0 %copy-start = (bf16[2048,128]{1,0:T(8,128)(2,1)S(1)}, bf16[2048,128]{1,0:T(8,128)(2,1)}, u32[]{:S(2)}) copy-start(bf16[2048,128]{1,0:T(8,128)(2,1)} %q_ref.3) | copy-start | bytes 1572868
  14.3 13.0 %copy-start.4 = (f32[2048]{0:T(1024)S(1)}, f32[2048]{0:T(1024)}, u32[]{:S(2)}) copy-start(f32[2048]{0:T(1024)} %param.11) | copy-start | bytes 24580

commit v17 on v15

--- a/solution.py
+++ b/solution.py
@@ -229,7 +229,9 @@
 
     members, places = list(range(blocks)), list(range(chunks))
     if blocks == chunks:
-        members, places = members[::-1], places[::-1]
+        middle = blocks * 11 // 16
+        members = [middle] + [block for block in members[::-1] if block != middle]
+        places = list(members)
 
     own_rates, own_residues = rates.T, residues.T
     copies = call(

time: 41.4 us -> 38.9 us (0.940); the launches traced: 41.1 us -> 38.1 us
  blocking collectives: 24.8 us -> 22.8 us
  starting transfers between devices: 6.15 us -> 5.25 us
    all_to_all x2, blocking collectives: 24.8 us -> 22.8 us  [all_to_all(): lax.all_to_all(pieces, 'seq', split_axis=0, concat_axis=0, axis_index_gro...]
    all_to_all x1, starting transfers between devices: 6.15 us -> 5.25 us  [all_to_all(): lax.all_to_all(pieces, 'seq', split_axis=0, concat_axis=0, axis_index_gro...]
  transfers between devices with their start and end apart: 1 -> 1, of which waited for: 1 -> 1; matrix products, arithmetic and copies ran while one was open for 0% -> 0% of each run, Pallas kernels for 6% -> 7%
where the time goes in v17:
time: 38.9 us; the launch traced here: 38.1 us
  blocking collectives  22.8 us (59%)
  Pallas kernels  8.02 us (21%)
  starting transfers between devices  5.25 us (13%)
  waiting for transfers between devices  1.9 us (5%)
    all_to_all x2, blocking collectives, all_to_all(): lax.all_to_all(pieces, 'seq', split_axis=0, concat_axis=0, axis_index_gro...  22.8 us
    pallas_call x5, Pallas kernels, call(): pl.pallas_call(kernel, out_shape=out_shape, in_specs=[pl.BlockSpec(memory...  8.02 us
    all_to_all x1, starting transfers between devices, all_to_all(): lax.all_to_all(pieces, 'seq', split_axis=0, concat_axis=0, axis_index_gro...  5.25 us
    all_to_all x1, waiting for transfers between devices, all_to_all(): lax.all_to_all(pieces, 'seq', split_axis=0, concat_axis=0, axis_index_gro...  1.9 us
  transfers between devices with their start and end apart: 1, of which 1 were waited for; matrix products, arithmetic and copies ran while one was open for 0% of the time, Pallas kernels for 7%

profile of v17, /device:TPU:2, one launch (start us, length us, event | category | flops | bytes accessed | tf_op | source)
XLA Modules:
  0.0 38.1 jit_solution(18309416101672686430)
XLA Ops:
  0.0 0.0 copy-start.1
  0.0 0.0 copy-start.2
  0.0 0.0 copy-start.3
  0.0 0.0 copy-start.4
  0.0 0.8 %shard_map.64 = f32[16,16,128]{2,1,0:T(8,128)S(1)} custom-call(f32[16,128]{1,0:T(8,128)} %bitcast.14), custom_call_target="tpu_custom_call" | custom-call | flops 10000000000 | bytes 8192 | tf_op jit(solution)/shard_map/pallas_call | solution.py:187
  0.8 10.8 %all_to_all.15 = f32[16,16,128]{2,1,0:T(8,128)S(1)} all-to-all(f32[16,16,128]{2,1,0:T(8,128)S(1)} %shard_map.64), channel_id=1, replica_groups={{22,30,28,26,24,20,18,16,14,12,10,8,6,4,2,0},{23,31,29,27,25,21,19,17,1..., dimensions={0} | all-to-all | bytes 262144 | tf_op jit(solution)/shard_map/all_to_all | solution.py:221
  11.6 0.0 copy-done.1
  11.7 0.0 copy-done.2
  11.7 0.0 copy-done.3
  11.7 0.0 copy-done.4
  11.7 1.6 %shard_map.65 = (f32[2048,128]{1,0:T(8,128)S(1)}, f32[512,128]{1,0:T(8,128)S(1)}) custom-call(f32[256,128]{1,0:T(8,128)S(1)} %bitcast.9, f32[16,128]{1,0:T(8,128)S(1)} %bitcast.15, f32[16,128]{1,0:T(8,128)S(1)} %bitcast.17, bf16[2048,128]{1,0:T(8,128)(2,1)S(1)} %copy-done.1, bf16[2048,128]{1,0:T(8,128)(2,1)S(1)} %copy-done.2), custom_call_target="tpu_custom_call" | custom-call | flops 8388608 | bytes 1196032 | tf_op jit(solution)/shard_map/pallas_call | solution.py:187
  13.2 0.0 copy-start
  13.3 12.0 %all_to_all.16.ends_ref = f32[16,32,128]{2,1,0:T(8,128)S(1)} all-to-all(f32[16,32,128]{2,1,0:T(8,128)S(1)} %bitcast.13), channel_id=1, replica_groups={{22,30,28,26,24,20,18,16,14,12,10,8,6,4,2,0},{23,31,29,27,25,21,19,17,1..., dimensions={0} | all-to-all | bytes 524288 | tf_op jit(solution)/shard_map/all_to_all | solution.py:221
  25.3 0.7 %shard_map.66 = f32[16,16,128]{2,1,0:T(8,128)} custom-call(f32[16,128]{1,0:T(8,128)S(1)} %bitcast.16, f32[16,32,128]{2,1,0:T(8,128)S(1)} %all_to_all.16.ends_ref), custom_call_target="tpu_custom_call" | custom-call | bytes 270336 | tf_op jit(solution)/shard_map/pallas_call | solution.py:187
  25.9 0.0 copy-start.5
  25.9 5.2 %all-to-all-start.2 = ((f32[16,16,128]{2,1,0:T(8,128)}), f32[16,16,128]{2,1,0:T(8,128)S(1)}, u32[]{:S(2)}, u32[]{:S(2)}) async-start(f32[16,16,128]{2,1,0:T(8,128)} %shard_map.66), calls=%async_computation.2 | async-start | bytes 262144 | tf_op jit(solution)/shard_map/all_to_all | solution.py:221
  31.2 0.0 copy-done
  31.2 0.0 copy-done.5
  31.2 2.6 %shard_map.67 = (f32[2048,128]{1,0:T(8,128)S(1)}, bf16[2048,128]{1,0:T(8,128)(2,1)}) custom-call(f32[256,128]{1,0:T(8,128)S(1)} %bitcast.10, f32[512,128]{1,0:T(8,128)S(1)} %bitcast.7, f32[2048,128]{1,0:T(8,128)S(1)} %get-tuple-element.10.series_ref, f32[16,128]{1,0:T(8,128)S(1)} %bitcast.18, bf16[2048,128]{1,0:T(8,128)(2,1)S(1)} %copy-done), custom_call_target="tpu_custom_call" | custom-call | flops 16777216 | bytes 1974272 | tf_op jit(solution)/shard_map/pallas_call | solution.py:187
  33.8 1.9 %all-to-all-done.2 = f32[16,16,128]{2,1,0:T(8,128)S(1)} async-done(((f32[16,16,128]{2,1,0:T(8,128)}), f32[16,16,128]{2,1,0:T(8,128)S(1)}, u32[]{:S(2)}, u32[]{:S(2)}) %all-to-all-start.2) | async-done | bytes 131104 | tf_op jit(solution)/shard_map/all_to_all | solution.py:221
  35.7 2.4 %shard_map.68 = bf16[2048,128]{1,0:T(8,128)(2,1)} custom-call(f32[256,128]{1,0:T(8,128)S(1)} %bitcast.11, f32[512,128]{1,0:T(8,128)S(1)} %bitcast.8, f32[256,128]{1,0:T(8,128)S(1)} %bitcast.12, f32[2048,128]{1,0:T(8,128)S(1)} %get-tuple-element.11.local_ref, bf16[2048,128]{1,0:T(8,128)(2,1)S(1)} %copy-done, ...), custom_call_target="tpu_custom_call", output_to_operand_aliasing={{}: (5, {})} | custom-call | flops 8388608 | bytes 2621440 | tf_op jit(solution)/shard_map/pallas_call | solution.py:187
Async XLA Ops:
  0.0 11.6 %copy-start.1 = (bf16[2048,128]{1,0:T(8,128)(2,1)S(1)}, bf16[2048,128]{1,0:T(8,128)(2,1)}, u32[]{:S(2)}) copy-start(bf16[2048,128]{1,0:T(8,128)(2,1)} %k_ref.1) | copy-start | bytes 1572868
  0.0 11.7 %copy-start.2 = (bf16[2048,128]{1,0:T(8,128)(2,1)S(1)}, bf16[2048,128]{1,0:T(8,128)(2,1)}, u32[]{:S(2)}) copy-start(bf16[2048,128]{1,0:T(8,128)(2,1)} %v_ref.1) | copy-start | bytes 1572868
  0.0 11.7 %copy-start.3 = (f32[128,16]{0,1:T(8,128)S(1)}, f32[128,16]{0,1:T(8,128)}, u32[]{:S(2)}) copy-start(f32[128,16]{0,1:T(8,128)} %param.10) | copy-start | bytes 24580
  0.0 11.7 %copy-start.4 = (f32[128,16]{0,1:T(8,128)S(1)}, f32[128,16]{0,1:T(8,128)}, u32[]{:S(2)}) copy-start(f32[128,16]{0,1:T(8,128)} %param.9) | copy-start | bytes 24580
  13.2 18.0 %copy-start = (bf16[2048,128]{1,0:T(8,128)(2,1)S(1)}, bf16[2048,128]{1,0:T(8,128)(2,1)}, u32[]{:S(2)}) copy-start(bf16[2048,128]{1,0:T(8,128)(2,1)} %q_ref.3) | copy-start | bytes 1572868
  25.9 5.3 %copy-start.5 = (f32[2048]{0:T(1024)S(1)}, f32[2048]{0:T(1024)}, u32[]{:S(2)}) copy-start(f32[2048]{0:T(1024)} %param.11) | copy-start | bytes 24580
  25.9 9.8 %all-to-all-start.2 = ((f32[16,16,128]{2,1,0:T(8,128)}), f32[16,16,128]{2,1,0:T(8,128)S(1)}, u32[]{:S(2)}, u32[]{:S(2)}) async-start(f32[16,16,128]{2,1,0:T(8,128)} %shard_map.66), calls=%async_computation.2 | async-start | bytes 262144 | tf_op jit(solution)/shard_map/all_to_all | solution.py:221

commit v18 on v17

--- a/solution.py
+++ b/solution.py
@@ -229,8 +229,9 @@
 
     members, places = list(range(blocks)), list(range(chunks))
     if blocks == chunks:
-        middle = blocks * 11 // 16
-        members = [middle] + [block for block in members[::-1] if block != middle]
+        far, middle = blocks // 2, blocks * 11 // 16
+        upper = [middle] + [block for block in members[:far - 1:-1] if block != middle]
+        members = [block for one in upper for block in (one, one - far)]
         places = list(members)
 
     own_rates, own_residues = rates.T, residues.T

time: 38.9 us -> 38.5 us (0.990); the launches traced: 38.1 us -> 38.2 us
  blocking collectives: 22.8 us -> 22.2 us
    all_to_all x2, blocking collectives: 22.8 us -> 22.2 us  [all_to_all(): lax.all_to_all(pieces, 'seq', split_axis=0, concat_axis=0, axis_index_gro...]
where the time goes in v18:
time: 38.5 us; the launch traced here: 38.2 us
  blocking collectives  22.2 us (58%)
  Pallas kernels  8.02 us (21%)
  starting transfers between devices  5.61 us (15%)
  waiting for transfers between devices  2.26 us (6%)
    all_to_all x2, blocking collectives, all_to_all(): lax.all_to_all(pieces, 'seq', split_axis=0, concat_axis=0, axis_index_gro...  22.2 us
    pallas_call x5, Pallas kernels, call(): pl.pallas_call(kernel, out_shape=out_shape, in_specs=[pl.BlockSpec(memory...  8.02 us
    all_to_all x1, starting transfers between devices, all_to_all(): lax.all_to_all(pieces, 'seq', split_axis=0, concat_axis=0, axis_index_gro...  5.61 us
    all_to_all x1, waiting for transfers between devices, all_to_all(): lax.all_to_all(pieces, 'seq', split_axis=0, concat_axis=0, axis_index_gro...  2.26 us
  transfers between devices with their start and end apart: 1, of which 1 were waited for; matrix products, arithmetic and copies ran while one was open for 0% of the time, Pallas kernels for 7%

profile of v18, /device:TPU:2, one launch (start us, length us, event | category | flops | bytes accessed | tf_op | source)
XLA Modules:
  0.0 38.2 jit_solution(13707765823706147861)
XLA Ops:
  0.0 0.0 copy-start.1
  0.0 0.0 copy-start.2
  0.0 0.0 copy-start.3
  0.0 0.0 copy-start.4
  0.0 0.8 %shard_map.64 = f32[16,16,128]{2,1,0:T(8,128)S(1)} custom-call(f32[16,128]{1,0:T(8,128)} %bitcast.14), custom_call_target="tpu_custom_call" | custom-call | flops 10000000000 | bytes 8192 | tf_op jit(solution)/shard_map/pallas_call | solution.py:187
  0.8 11.1 %all_to_all.15 = f32[16,16,128]{2,1,0:T(8,128)S(1)} all-to-all(f32[16,16,128]{2,1,0:T(8,128)S(1)} %shard_map.64), channel_id=1, replica_groups={{22,6,30,14,28,12,26,10,24,8,20,4,18,2,16,0},{23,7,31,15,29,13,27,11,25..., dimensions={0} | all-to-all | bytes 262144 | tf_op jit(solution)/shard_map/all_to_all | solution.py:221
  12.0 0.0 copy-done.1
  12.0 0.0 copy-done.2
  12.0 0.0 copy-done.3
  12.0 0.0 copy-done.4
  12.0 1.6 %shard_map.65 = (f32[2048,128]{1,0:T(8,128)S(1)}, f32[512,128]{1,0:T(8,128)S(1)}) custom-call(f32[256,128]{1,0:T(8,128)S(1)} %bitcast.9, f32[16,128]{1,0:T(8,128)S(1)} %bitcast.15, f32[16,128]{1,0:T(8,128)S(1)} %bitcast.17, bf16[2048,128]{1,0:T(8,128)(2,1)S(1)} %copy-done.1, bf16[2048,128]{1,0:T(8,128)(2,1)S(1)} %copy-done.2), custom_call_target="tpu_custom_call" | custom-call | flops 8388608 | bytes 1196032 | tf_op jit(solution)/shard_map/pallas_call | solution.py:187
  13.6 0.0 copy-start
  13.6 11.1 %all_to_all.16.ends_ref = f32[16,32,128]{2,1,0:T(8,128)S(1)} all-to-all(f32[16,32,128]{2,1,0:T(8,128)S(1)} %bitcast.13), channel_id=1, replica_groups={{22,6,30,14,28,12,26,10,24,8,20,4,18,2,16,0},{23,7,31,15,29,13,27,11,25..., dimensions={0} | all-to-all | bytes 524288 | tf_op jit(solution)/shard_map/all_to_all | solution.py:221
  24.6 0.7 %shard_map.66 = f32[16,16,128]{2,1,0:T(8,128)} custom-call(f32[16,128]{1,0:T(8,128)S(1)} %bitcast.16, f32[16,32,128]{2,1,0:T(8,128)S(1)} %all_to_all.16.ends_ref), custom_call_target="tpu_custom_call" | custom-call | bytes 270336 | tf_op jit(solution)/shard_map/pallas_call | solution.py:187
  25.3 0.0 copy-start.5
  25.3 5.6 %all-to-all-start.2 = ((f32[16,16,128]{2,1,0:T(8,128)}), f32[16,16,128]{2,1,0:T(8,128)S(1)}, u32[]{:S(2)}, u32[]{:S(2)}) async-start(f32[16,16,128]{2,1,0:T(8,128)} %shard_map.66), calls=%async_computation.2 | async-start | bytes 262144 | tf_op jit(solution)/shard_map/all_to_all | solution.py:221
  30.9 0.0 copy-done
  30.9 0.0 copy-done.5
  30.9 2.6 %shard_map.67 = (f32[2048,128]{1,0:T(8,128)S(1)}, bf16[2048,128]{1,0:T(8,128)(2,1)}) custom-call(f32[256,128]{1,0:T(8,128)S(1)} %bitcast.10, f32[512,128]{1,0:T(8,128)S(1)} %bitcast.7, f32[2048,128]{1,0:T(8,128)S(1)} %get-tuple-element.10.series_ref, f32[16,128]{1,0:T(8,128)S(1)} %bitcast.18, bf16[2048,128]{1,0:T(8,128)(2,1)S(1)} %copy-done), custom_call_target="tpu_custom_call" | custom-call | flops 16777216 | bytes 1974272 | tf_op jit(solution)/shard_map/pallas_call | solution.py:187
  33.6 2.3 %all-to-all-done.2 = f32[16,16,128]{2,1,0:T(8,128)S(1)} async-done(((f32[16,16,128]{2,1,0:T(8,128)}), f32[16,16,128]{2,1,0:T(8,128)S(1)}, u32[]{:S(2)}, u32[]{:S(2)}) %all-to-all-start.2) | async-done | bytes 131104 | tf_op jit(solution)/shard_map/all_to_all | solution.py:221
  35.8 2.4 %shard_map.68 = bf16[2048,128]{1,0:T(8,128)(2,1)} custom-call(f32[256,128]{1,0:T(8,128)S(1)} %bitcast.11, f32[512,128]{1,0:T(8,128)S(1)} %bitcast.8, f32[256,128]{1,0:T(8,128)S(1)} %bitcast.12, f32[2048,128]{1,0:T(8,128)S(1)} %get-tuple-element.11.local_ref, bf16[2048,128]{1,0:T(8,128)(2,1)S(1)} %copy-done, ...), custom_call_target="tpu_custom_call", output_to_operand_aliasing={{}: (5, {})} | custom-call | flops 8388608 | bytes 2621440 | tf_op jit(solution)/shard_map/pallas_call | solution.py:187
Async XLA Ops:
  0.0 12.0 %copy-start.1 = (bf16[2048,128]{1,0:T(8,128)(2,1)S(1)}, bf16[2048,128]{1,0:T(8,128)(2,1)}, u32[]{:S(2)}) copy-start(bf16[2048,128]{1,0:T(8,128)(2,1)} %k_ref.1) | copy-start | bytes 1572868
  0.0 12.0 %copy-start.2 = (bf16[2048,128]{1,0:T(8,128)(2,1)S(1)}, bf16[2048,128]{1,0:T(8,128)(2,1)}, u32[]{:S(2)}) copy-start(bf16[2048,128]{1,0:T(8,128)(2,1)} %v_ref.1) | copy-start | bytes 1572868
  0.0 12.0 %copy-start.3 = (f32[128,16]{0,1:T(8,128)S(1)}, f32[128,16]{0,1:T(8,128)}, u32[]{:S(2)}) copy-start(f32[128,16]{0,1:T(8,128)} %param.10) | copy-start | bytes 24580
  0.0 12.0 %copy-start.4 = (f32[128,16]{0,1:T(8,128)S(1)}, f32[128,16]{0,1:T(8,128)}, u32[]{:S(2)}) copy-start(f32[128,16]{0,1:T(8,128)} %param.9) | copy-start | bytes 24580
  13.6 17.4 %copy-start = (bf16[2048,128]{1,0:T(8,128)(2,1)S(1)}, bf16[2048,128]{1,0:T(8,128)(2,1)}, u32[]{:S(2)}) copy-start(bf16[2048,128]{1,0:T(8,128)(2,1)} %q_ref.3) | copy-start | bytes 1572868
  25.3 5.6 %copy-start.5 = (f32[2048]{0:T(1024)S(1)}, f32[2048]{0:T(1024)}, u32[]{:S(2)}) copy-start(f32[2048]{0:T(1024)} %param.11) | copy-start | bytes 24580
  25.3 10.5 %all-to-all-start.2 = ((f32[16,16,128]{2,1,0:T(8,128)}), f32[16,16,128]{2,1,0:T(8,128)S(1)}, u32[]{:S(2)}, u32[]{:S(2)}) async-start(f32[16,16,128]{2,1,0:T(8,128)} %shard_map.66), calls=%async_computation.2 | async-start | bytes 262144 | tf_op jit(solution)/shard_map/all_to_all | solution.py:221

commit v19 on v17

--- a/solution.py
+++ b/solution.py
@@ -228,9 +228,9 @@
     f32 = jnp.float32
 
     members, places = list(range(blocks)), list(range(chunks))
-    if blocks == chunks:
-        middle = blocks * 11 // 16
-        members = [middle] + [block for block in members[::-1] if block != middle]
+    if blocks == chunks and blocks % 4 == 0:
+        quarter = blocks // 4
+        members = [part * quarter + i for i in reversed(range(quarter)) for part in (2, 0, 3, 1)]
         places = list(members)
 
     own_rates, own_residues = rates.T, residues.T

time: 38.9 us -> 38.7 us (level); the launches traced: 38.1 us -> 38.4 us
  blocking collectives: 22.8 us -> 22.2 us
  starting transfers between devices: 5.25 us -> 5.77 us
    all_to_all x2, blocking collectives: 22.8 us -> 22.2 us  [all_to_all(): lax.all_to_all(pieces, 'seq', split_axis=0, concat_axis=0, axis_index_gro...]
    all_to_all x1, starting transfers between devices: 5.25 us -> 5.77 us  [all_to_all(): lax.all_to_all(pieces, 'seq', split_axis=0, concat_axis=0, axis_index_gro...]
where the time goes in v19:
time: 38.7 us; the launch traced here: 38.4 us
  blocking collectives  22.2 us (57%)
  Pallas kernels  8.02 us (21%)
  starting transfers between devices  5.77 us (15%)
  waiting for transfers between devices  2.27 us (6%)
    all_to_all x2, blocking collectives, all_to_all(): lax.all_to_all(pieces, 'seq', split_axis=0, concat_axis=0, axis_index_gro...  22.2 us
    pallas_call x5, Pallas kernels, call(): pl.pallas_call(kernel, out_shape=out_shape, in_specs=[pl.BlockSpec(memory...  8.02 us
    all_to_all x1, starting transfers between devices, all_to_all(): lax.all_to_all(pieces, 'seq', split_axis=0, concat_axis=0, axis_index_gro...  5.77 us
    all_to_all x1, waiting for transfers between devices, all_to_all(): lax.all_to_all(pieces, 'seq', split_axis=0, concat_axis=0, axis_index_gro...  2.27 us
  transfers between devices with their start and end apart: 1, of which 1 were waited for; matrix products, arithmetic and copies ran while one was open for 0% of the time, Pallas kernels for 7%

profile of v19, /device:TPU:2, one launch (start us, length us, event | category | flops | bytes accessed | tf_op | source)
XLA Modules:
  0.0 38.4 jit_solution(3008978663575102661)
XLA Ops:
  0.0 0.0 copy-start.1
  0.0 0.0 copy-start.2
  0.0 0.0 copy-start.3
  0.0 0.0 copy-start.4
  0.0 0.8 %shard_map.64 = f32[16,16,128]{2,1,0:T(8,128)S(1)} custom-call(f32[16,128]{1,0:T(8,128)} %bitcast.14), custom_call_target="tpu_custom_call" | custom-call | flops 10000000000 | bytes 8192 | tf_op jit(solution)/shard_map/pallas_call | solution.py:187
  0.8 11.2 %all_to_all.15 = f32[16,16,128]{2,1,0:T(8,128)S(1)} all-to-all(f32[16,16,128]{2,1,0:T(8,128)S(1)} %shard_map.64), channel_id=1, replica_groups={{22,6,30,14,20,4,28,12,18,2,26,10,16,0,24,8},{23,7,31,15,21,5,29,13,19,..., dimensions={0} | all-to-all | bytes 262144 | tf_op jit(solution)/shard_map/all_to_all | solution.py:221
  12.0 0.0 copy-done.1
  12.0 0.0 copy-done.2
  12.0 0.0 copy-done.3
  12.0 0.0 copy-done.4
  12.1 1.6 %shard_map.65 = (f32[2048,128]{1,0:T(8,128)S(1)}, f32[512,128]{1,0:T(8,128)S(1)}) custom-call(f32[256,128]{1,0:T(8,128)S(1)} %bitcast.9, f32[16,128]{1,0:T(8,128)S(1)} %bitcast.15, f32[16,128]{1,0:T(8,128)S(1)} %bitcast.17, bf16[2048,128]{1,0:T(8,128)(2,1)S(1)} %copy-done.1, bf16[2048,128]{1,0:T(8,128)(2,1)S(1)} %copy-done.2), custom_call_target="tpu_custom_call" | custom-call | flops 8388608 | bytes 1196032 | tf_op jit(solution)/shard_map/pallas_call | solution.py:187
  13.6 0.0 copy-start
  13.6 11.0 %all_to_all.16.ends_ref = f32[16,32,128]{2,1,0:T(8,128)S(1)} all-to-all(f32[16,32,128]{2,1,0:T(8,128)S(1)} %bitcast.13), channel_id=1, replica_groups={{22,6,30,14,20,4,28,12,18,2,26,10,16,0,24,8},{23,7,31,15,21,5,29,13,19,..., dimensions={0} | all-to-all | bytes 524288 | tf_op jit(solution)/shard_map/all_to_all | solution.py:221
  24.6 0.7 %shard_map.66 = f32[16,16,128]{2,1,0:T(8,128)} custom-call(f32[16,128]{1,0:T(8,128)S(1)} %bitcast.16, f32[16,32,128]{2,1,0:T(8,128)S(1)} %all_to_all.16.ends_ref), custom_call_target="tpu_custom_call" | custom-call | bytes 270336 | tf_op jit(solution)/shard_map/pallas_call | solution.py:187
  25.3 0.0 copy-start.5
  25.3 5.8 %all-to-all-start.2 = ((f32[16,16,128]{2,1,0:T(8,128)}), f32[16,16,128]{2,1,0:T(8,128)S(1)}, u32[]{:S(2)}, u32[]{:S(2)}) async-start(f32[16,16,128]{2,1,0:T(8,128)} %shard_map.66), calls=%async_computation.2 | async-start | bytes 262144 | tf_op jit(solution)/shard_map/all_to_all | solution.py:221
  31.1 0.0 copy-done
  31.1 0.0 copy-done.5
  31.1 2.6 %shard_map.67 = (f32[2048,128]{1,0:T(8,128)S(1)}, bf16[2048,128]{1,0:T(8,128)(2,1)}) custom-call(f32[256,128]{1,0:T(8,128)S(1)} %bitcast.10, f32[512,128]{1,0:T(8,128)S(1)} %bitcast.7, f32[2048,128]{1,0:T(8,128)S(1)} %get-tuple-element.10.series_ref, f32[16,128]{1,0:T(8,128)S(1)} %bitcast.18, bf16[2048,128]{1,0:T(8,128)(2,1)S(1)} %copy-done), custom_call_target="tpu_custom_call" | custom-call | flops 16777216 | bytes 1974272 | tf_op jit(solution)/shard_map/pallas_call | solution.py:187
  33.7 2.3 %all-to-all-done.2 = f32[16,16,128]{2,1,0:T(8,128)S(1)} async-done(((f32[16,16,128]{2,1,0:T(8,128)}), f32[16,16,128]{2,1,0:T(8,128)S(1)}, u32[]{:S(2)}, u32[]{:S(2)}) %all-to-all-start.2) | async-done | bytes 131104 | tf_op jit(solution)/shard_map/all_to_all | solution.py:221
  36.0 2.4 %shard_map.68 = bf16[2048,128]{1,0:T(8,128)(2,1)} custom-call(f32[256,128]{1,0:T(8,128)S(1)} %bitcast.11, f32[512,128]{1,0:T(8,128)S(1)} %bitcast.8, f32[256,128]{1,0:T(8,128)S(1)} %bitcast.12, f32[2048,128]{1,0:T(8,128)S(1)} %get-tuple-element.11.local_ref, bf16[2048,128]{1,0:T(8,128)(2,1)S(1)} %copy-done, ...), custom_call_target="tpu_custom_call", output_to_operand_aliasing={{}: (5, {})} | custom-call | flops 8388608 | bytes 2621440 | tf_op jit(solution)/shard_map/pallas_call | solution.py:187
Async XLA Ops:
  0.0 12.0 %copy-start.1 = (bf16[2048,128]{1,0:T(8,128)(2,1)S(1)}, bf16[2048,128]{1,0:T(8,128)(2,1)}, u32[]{:S(2)}) copy-start(bf16[2048,128]{1,0:T(8,128)(2,1)} %k_ref.1) | copy-start | bytes 1572868
  0.0 12.0 %copy-start.2 = (bf16[2048,128]{1,0:T(8,128)(2,1)S(1)}, bf16[2048,128]{1,0:T(8,128)(2,1)}, u32[]{:S(2)}) copy-start(bf16[2048,128]{1,0:T(8,128)(2,1)} %v_ref.1) | copy-start | bytes 1572868
  0.0 12.0 %copy-start.3 = (f32[128,16]{0,1:T(8,128)S(1)}, f32[128,16]{0,1:T(8,128)}, u32[]{:S(2)}) copy-start(f32[128,16]{0,1:T(8,128)} %param.10) | copy-start | bytes 24580
  0.0 12.0 %copy-start.4 = (f32[128,16]{0,1:T(8,128)S(1)}, f32[128,16]{0,1:T(8,128)}, u32[]{:S(2)}) copy-start(f32[128,16]{0,1:T(8,128)} %param.9) | copy-start | bytes 24580
  13.6 17.5 %copy-start = (bf16[2048,128]{1,0:T(8,128)(2,1)S(1)}, bf16[2048,128]{1,0:T(8,128)(2,1)}, u32[]{:S(2)}) copy-start(bf16[2048,128]{1,0:T(8,128)(2,1)} %q_ref.3) | copy-start | bytes 1572868
  25.3 5.8 %copy-start.5 = (f32[2048]{0:T(1024)S(1)}, f32[2048]{0:T(1024)}, u32[]{:S(2)}) copy-start(f32[2048]{0:T(1024)} %param.11) | copy-start | bytes 24580
  25.3 10.7 %all-to-all-start.2 = ((f32[16,16,128]{2,1,0:T(8,128)}), f32[16,16,128]{2,1,0:T(8,128)S(1)}, u32[]{:S(2)}, u32[]{:S(2)}) async-start(f32[16,16,128]{2,1,0:T(8,128)} %shard_map.66), calls=%async_computation.2 | async-start | bytes 262144 | tf_op jit(solution)/shard_map/all_to_all | solution.py:221

commit v20 on v18

--- a/solution.py
+++ b/solution.py
@@ -104,16 +104,24 @@
     return pltpu.make_async_copy(gated_ref.at[rows, :], out_ref.at[rows, :], sems.at[chunk])
 
 
-def finish(chunk, places, conv_ref, q_ref, gated_ref, out_ref, sems):
-    length = conv_ref.shape[0] // len(places)
+def finish(chunk, places, conv, q_ref, gated_ref, out_ref, sems):
     rows = pl.ds(places[chunk] * LANES, LANES)
-    conv = conv_ref[chunk_rows(chunk, length), :].T
-    gated_ref[rows, :] = (q_ref[rows, :].astype(jnp.float32) * conv).astype(jnp.bfloat16)
+    gated_ref[rows, :] = (q_ref[rows, :].astype(jnp.float32) * conv.T).astype(jnp.bfloat16)
     leaving(chunk, places, gated_ref, out_ref, sems).start()
 
 
+def power(base, exponent):
+    result = None
+    while exponent > 0:
+        if exponent % 2 == 1:
+            result = base if result is None else result * base
+        base = base * base
+        exponent //= 2
+    return result
+
+
 def local_kernel(
-    places, order, decays_ref, weights_ref, series_ref, gain_ref, q_ref, conv_ref, out_ref, gated_ref, sems
+    places, order, decays_ref, weights_ref, series_ref, gain_ref, q_ref, conv_ref, factors_ref, out_ref, gated_ref, sems
 ):
     chunks = len(places)
     length = series_ref.shape[0] // chunks
@@ -137,45 +145,64 @@
         zero = jnp.zeros((SUBLANES, LANES), jnp.float32)
         lax.fori_loop(0, length // UNROLL, steps, (zero,) * order)
 
-    @pl.when(lax.axis_index("seq") == 0)
+    first = lax.axis_index("seq") == 0
+
+    @pl.when(first)
     def _():
         for chunk in range(chunks):
-            finish(chunk, places, conv_ref, q_ref, gated_ref, out_ref, sems)
+            finish(chunk, places, conv_ref[chunk_rows(chunk, length), :], q_ref, gated_ref, out_ref, sems)
         for chunk in range(chunks):
             leaving(chunk, places, gated_ref, out_ref, sems).wait()
 
+    @pl.when(jnp.logical_not(first))
+    def _():
+        stretch = length // SUBLANES
+        index = lax.broadcasted_iota(jnp.int32, (SUBLANES, LANES), 0)
+
+        def one_row(row, _):
+            decay = jnp.broadcast_to(decays_ref[pl.ds(row, 1), :], (SUBLANES, LANES))
+            chunk = row // order
+            weight = weights_ref[pl.ds(chunk * 2 * order + order + row - chunk * order, 1), :]
+            factor = decay * weight
+            step = power(decay, stretch)
+            for bit in range(3):
+                factor = jnp.where(index & (1 << bit) != 0, factor * step, factor)
+                step = step * step
+            factors_ref[pl.ds(pl.multiple_of(row * SUBLANES, SUBLANES), SUBLANES), :] = factor
+            return 0
+
+        lax.fori_loop(0, chunks * order, one_row, 0, unroll=8)
+
 
 def output_kernel(
-    places, order, decays_ref, weights_ref, carry_ref, local_ref, q_ref, _, out_ref, conv_ref, gated_ref, sems
+    places, order, decays_ref, factors_ref, carry_ref, local_ref, q_ref, _, out_ref, conv_ref, gated_ref, sems
 ):
     chunks = len(places)
     length = local_ref.shape[0] // chunks
-    tokens = length // SUBLANES
+    stretch = length // SUBLANES
+
+    def scan(chunk):
+        rows = [chunk * order + r for r in range(order)]
+        decay = [jnp.broadcast_to(decays_ref[pl.ds(row, 1), :], (SUBLANES, LANES)) for row in rows]
+        fading = [factors_ref[pl.ds(row * SUBLANES, SUBLANES), :] * carry_ref[pl.ds(row, 1), :] for row in rows]
+        first = chunk // SUBLANES * length * SUBLANES + chunk % SUBLANES
+        for i in range(stretch):
+            local = local_ref[pl.ds(first + i * SUBLANES, SUBLANES, stride=stretch * SUBLANES), :]
+            conv_ref[pl.ds(chunk * length + i * SUBLANES, SUBLANES), :] = tree_sum(fading + [local])
+            if i + 1 < stretch:
+                fading = [decay[r] * fading[r] for r in range(order)]
+
+    def send(chunk):
+        parts = [conv_ref[pl.ds(chunk * length + i, stretch, stride=SUBLANES), :] for i in range(SUBLANES)]
+        finish(chunk, places, jnp.concatenate(parts, axis=0), q_ref, gated_ref, out_ref, sems)
 
     @pl.when(lax.axis_index("seq") > 0)
     def _():
-        for half in range(chunks // SUBLANES):
-            decay = mode_rows(decays_ref, 0, order, order, chunks, half)
-            weight = mode_rows(weights_ref, order, order, 2 * order, chunks, half)
-            carry = mode_rows(carry_ref, 0, order, order, chunks, half)
-
-            def steps(i, fading):
-                fading = list(fading)
-                for u in range(tokens):
-                    rows = token_rows(half, length, i * tokens + u)
-                    fading = [decay[r] * fading[r] for r in range(order)]
-                    conv_ref[rows, :] = tree_sum(fading + [local_ref[rows, :]])
-                return tuple(fading)
-
-            fading = tuple(weight[r] * carry[r] for r in range(order))
-            if half == 0:
-                lax.fori_loop(0, SUBLANES, steps, fading)
-            else:
-                for i in range(SUBLANES):
-                    fading = steps(i, fading)
-                    finish((half - 1) * SUBLANES + i, places, conv_ref, q_ref, gated_ref, out_ref, sems)
-        for chunk in range(chunks - SUBLANES, chunks):
-            finish(chunk, places, conv_ref, q_ref, gated_ref, out_ref, sems)
+        for chunk in range(chunks):
+            scan(chunk)
+            if chunk > 0:
+                send(chunk - 1)
+        send(chunks - 1)
         for chunk in range(chunks):
             leaving(chunk, places, gated_ref, out_ref, sems).wait()
 
@@ -268,10 +295,11 @@
     weights = to_chunks(ends).reshape(chunks * 2 * order, LANES)
     out_shape = jax.ShapeDtypeStruct((channels, length), jnp.bfloat16)
     out_scratch = [pltpu.VMEM(out_shape.shape, out_shape.dtype), pltpu.SemaphoreType.DMA((chunks,))]
-    local, out = call(
+    local, factors, out = call(
         functools.partial(local_kernel, places, order),
         (
             jax.ShapeDtypeStruct((length * chunks, LANES), f32),
+            jax.ShapeDtypeStruct((chunks * order * SUBLANES, LANES), f32),
             out_shape,
         ),
         decays,
@@ -279,7 +307,7 @@
         local_series,
         direct_gain.reshape(chunks, LANES),
         q_proj,
-        out_spaces=(pltpu.VMEM, pl.ANY),
+        out_spaces=(pltpu.VMEM, pltpu.VMEM, pl.ANY),
         scratch=out_scratch,
         flops=4 * order * channels * length,
     )
@@ -295,7 +323,7 @@
         functools.partial(output_kernel, places, order),
         out_shape,
         decays,
-        weights,
+        factors,
         carry,
         local,
         q_proj,

time: 38.5 us -> 40.4 us (1.049)
  waiting for transfers between devices: 2.26 us -> 0.01 us
  local copies, waits for them, and re-layouts: 0.03 us -> 2.21 us
  Pallas kernels: 8.02 us -> 9.92 us
    all_to_all x1, waiting for transfers between devices: 2.26 us -> 0.01 us  [all_to_all(): lax.all_to_all(pieces, 'seq', split_axis=0, concat_axis=0, axis_index_gro...]
    unnamed x12 -> x16, local copies, waits for them, and re-layouts: 0.03 us -> 2.21 us
    pallas_call x5, Pallas kernels: 8.02 us -> 9.92 us  [call(): pl.pallas_call(kernel, out_shape=out_shape, in_specs=[pl.BlockSpec(memory...]
  transfers between devices with their start and end apart: 1 -> 1, of which waited for: 1 -> 0; matrix products, arithmetic and copies ran while one was open for 0% -> 0% of each run, Pallas kernels for 7% -> 11%
where the time goes in v20:
time: 40.4 us; the launch traced here: 40 us
  blocking collectives  22.2 us (55%)
  Pallas kernels  9.92 us (25%)
  starting transfers between devices  5.61 us (14%)
  local copies, waits for them, and re-layouts  2.21 us (5%)
    all_to_all x2, blocking collectives, all_to_all(): lax.all_to_all(pieces, 'seq', split_axis=0, concat_axis=0, axis_index_gro...  22.2 us
    pallas_call x5, Pallas kernels, call(): pl.pallas_call(kernel, out_shape=out_shape, in_specs=[pl.BlockSpec(memory...  9.92 us
    all_to_all x1, starting transfers between devices, all_to_all(): lax.all_to_all(pieces, 'seq', split_axis=0, concat_axis=0, axis_index_gro...  5.61 us
    unnamed x16, local copies, waits for them, and re-layouts  2.21 us
  transfers between devices with their start and end apart: 1, of which 0 were waited for; matrix products, arithmetic and copies ran while one was open for 0% of the time, Pallas kernels for 11%

profile of v20, /device:TPU:2, one launch (start us, length us, event | category | flops | bytes accessed | tf_op | source)
XLA Modules:
  0.0 40.0 jit_solution(10154114194298138914)
XLA Ops:
  0.0 0.0 copy-start.3
  0.0 0.0 copy-start.4
  0.0 0.0 copy-start.5
  0.0 0.0 copy-start.6
  0.0 0.8 %shard_map.64 = f32[16,16,128]{2,1,0:T(8,128)S(1)} custom-call(f32[16,128]{1,0:T(8,128)} %bitcast.13), custom_call_target="tpu_custom_call" | custom-call | flops 10000000000 | bytes 8192 | tf_op jit(solution)/shard_map/pallas_call | solution.py:214
  0.8 11.1 %all_to_all.15 = f32[16,16,128]{2,1,0:T(8,128)S(1)} all-to-all(f32[16,16,128]{2,1,0:T(8,128)S(1)} %shard_map.64), channel_id=1, replica_groups={{22,6,30,14,28,12,26,10,24,8,20,4,18,2,16,0},{23,7,31,15,29,13,27,11,25..., dimensions={0} | all-to-all | bytes 262144 | tf_op jit(solution)/shard_map/all_to_all | solution.py:248
  12.0 0.0 copy-done.3
  12.0 0.0 copy-done.4
  12.0 0.0 copy-done.5
  12.0 0.0 copy-done.6
  12.0 1.6 %shard_map.65 = (f32[2048,128]{1,0:T(8,128)S(1)}, f32[512,128]{1,0:T(8,128)S(1)}) custom-call(f32[256,128]{1,0:T(8,128)S(1)} %bitcast.8, f32[16,128]{1,0:T(8,128)S(1)} %bitcast.14, f32[16,128]{1,0:T(8,128)S(1)} %bitcast.16, bf16[2048,128]{1,0:T(8,128)(2,1)S(1)} %copy-done.3, bf16[2048,128]{1,0:T(8,128)(2,1)S(1)} %copy-done.4), custom_call_target="tpu_custom_call" | custom-call | flops 8388608 | bytes 1196032 | tf_op jit(solution)/shard_map/pallas_call | solution.py:214
  13.6 0.0 copy-start
  13.6 11.1 %all_to_all.16.ends_ref = f32[16,32,128]{2,1,0:T(8,128)S(1)} all-to-all(f32[16,32,128]{2,1,0:T(8,128)S(1)} %bitcast.12), channel_id=1, replica_groups={{22,6,30,14,28,12,26,10,24,8,20,4,18,2,16,0},{23,7,31,15,29,13,27,11,25..., dimensions={0} | all-to-all | bytes 524288 | tf_op jit(solution)/shard_map/all_to_all | solution.py:248
  24.6 0.7 %shard_map.67 = f32[16,16,128]{2,1,0:T(8,128)} custom-call(f32[16,128]{1,0:T(8,128)S(1)} %bitcast.15, f32[16,32,128]{2,1,0:T(8,128)S(1)} %all_to_all.16.ends_ref), custom_call_target="tpu_custom_call" | custom-call | bytes 270336 | tf_op jit(solution)/shard_map/pallas_call | solution.py:214
  25.3 0.0 copy-start.7
  25.3 5.6 %all-to-all-start.2 = ((f32[16,16,128]{2,1,0:T(8,128)}), f32[16,16,128]{2,1,0:T(8,128)S(1)}, u32[]{:S(2)}, u32[]{:S(2)}) async-start(f32[16,16,128]{2,1,0:T(8,128)} %shard_map.67), calls=%async_computation.2 | async-start | bytes 262144 | tf_op jit(solution)/shard_map/all_to_all | solution.py:248
  30.9 0.0 copy-done
  30.9 0.0 copy-done.7
  30.9 4.5 %shard_map.66 = (f32[2048,128]{1,0:T(8,128)S(1)}, f32[2048,128]{1,0:T(8,128)S(1)}, bf16[2048,128]{1,0:T(8,128)(2,1)}) custom-call(f32[256,128]{1,0:T(8,128)S(1)} %bitcast.9, f32[512,128]{1,0:T(8,128)S(1)} %bitcast.7, f32[2048,128]{1,0:T(8,128)S(1)} %get-tuple-element.11.series_ref, f32[16,128]{1,0:T(8,128)S(1)} %bitcast.17, bf16[2048,128]{1,0:T(8,128)(2,1)S(1)} %copy-done), custom_call_target="tpu_custom_call" | custom-call | flops 16777216 | bytes 1974272 | tf_op jit(solution)/shard_map/pallas_call | solution.py:214
  35.4 0.0 copy-start.1
  35.4 1.0 %copy-done.1 = f32[2048,128]{1,0:T(8,128)} copy-done((f32[2048,128]{1,0:T(8,128)}, f32[2048,128]{1,0:T(8,128)S(1)}, u32[]{:S(2)}) %copy-start.1) | copy-done | bytes 1048600
  36.4 0.0 all-to-all-done.2
  36.4 1.2 %copy-done.2 = f32[2048,128]{1,0:T(8,128)S(1)} copy-done((f32[2048,128]{1,0:T(8,128)S(1)}, f32[2048,128]{1,0:T(8,128)}, u32[]{:S(2)}) %copy-start.2) | copy-done | bytes 1048600
  37.6 2.4 %shard_map.68 = bf16[2048,128]{1,0:T(8,128)(2,1)} custom-call(f32[256,128]{1,0:T(8,128)S(1)} %bitcast.10, f32[2048,128]{1,0:T(8,128)S(1)} %copy-done.2, f32[256,128]{1,0:T(8,128)S(1)} %bitcast.11, f32[2048,128]{1,0:T(8,128)S(1)} %get-tuple-element.13.local_ref, bf16[2048,128]{1,0:T(8,128)(2,1)S(1)} %copy-done, ...), custom_call_target="tpu_custom_call", output_to_operand_aliasing={{}: (5, {})} | custom-call | flops 8388608 | bytes 3407872 | tf_op jit(solution)/shard_map/pallas_call | solution.py:214
  (1 shorter events, 0.0 us)
Async XLA Ops:
  0.0 12.0 %copy-start.3 = (bf16[2048,128]{1,0:T(8,128)(2,1)S(1)}, bf16[2048,128]{1,0:T(8,128)(2,1)}, u32[]{:S(2)}) copy-start(bf16[2048,128]{1,0:T(8,128)(2,1)} %k_ref.1) | copy-start | bytes 1572868
  0.0 12.0 %copy-start.4 = (bf16[2048,128]{1,0:T(8,128)(2,1)S(1)}, bf16[2048,128]{1,0:T(8,128)(2,1)}, u32[]{:S(2)}) copy-start(bf16[2048,128]{1,0:T(8,128)(2,1)} %v_ref.1) | copy-start | bytes 1572868
  0.0 12.0 %copy-start.5 = (f32[128,16]{0,1:T(8,128)S(1)}, f32[128,16]{0,1:T(8,128)}, u32[]{:S(2)}) copy-start(f32[128,16]{0,1:T(8,128)} %param.10) | copy-start | bytes 24580
  0.0 12.0 %copy-start.6 = (f32[128,16]{0,1:T(8,128)S(1)}, f32[128,16]{0,1:T(8,128)}, u32[]{:S(2)}) copy-start(f32[128,16]{0,1:T(8,128)} %param.9) | copy-start | bytes 24580
  13.6 17.4 %copy-start = (bf16[2048,128]{1,0:T(8,128)(2,1)S(1)}, bf16[2048,128]{1,0:T(8,128)(2,1)}, u32[]{:S(2)}) copy-start(bf16[2048,128]{1,0:T(8,128)(2,1)} %q_ref.3) | copy-start | bytes 1572868
  25.3 5.6 %copy-start.7 = (f32[2048]{0:T(1024)S(1)}, f32[2048]{0:T(1024)}, u32[]{:S(2)}) copy-start(f32[2048]{0:T(1024)} %param.11) | copy-start | bytes 24580
  25.3 11.1 %all-to-all-start.2 = ((f32[16,16,128]{2,1,0:T(8,128)}), f32[16,16,128]{2,1,0:T(8,128)S(1)}, u32[]{:S(2)}, u32[]{:S(2)}) async-start(f32[16,16,128]{2,1,0:T(8,128)} %shard_map.67), calls=%async_computation.2 | async-start | bytes 262144 | tf_op jit(solution)/shard_map/all_to_all | solution.py:248
  35.4 1.0 %copy-start.1 = (f32[2048,128]{1,0:T(8,128)}, f32[2048,128]{1,0:T(8,128)S(1)}, u32[]{:S(2)}) copy-start(f32[2048,128]{1,0:T(8,128)S(1)} %get-tuple-element.12.factors_ref) | copy-start | bytes 3145732
  36.4 1.2 %copy-start.2 = (f32[2048,128]{1,0:T(8,128)S(1)}, f32[2048,128]{1,0:T(8,128)}, u32[]{:S(2)}) copy-start(f32[2048,128]{1,0:T(8,128)} %copy-done.1) | copy-start | bytes 3145732

commit v21 on v6

v21 whole, which is shorter than its diff:
```python
import functools
import jax
import jax.numpy as jnp
from jax import lax
from jax.experimental import pallas as pl
from jax.experimental.pallas import tpu as pltpu
from jax.sharding import PartitionSpec as P

LANES = 128
SUBLANES = 8
UNROLL = 8
COPIES_COST = 10**10
VMEM_LIMIT = 32 * 1024 * 1024


def one_minus_exp(y):
    series = jnp.ones_like(y)
    for k in range(11, 1, -1):
        series = 1.0 - (y * (1.0 / k)) * series
    return jnp.where(y < 0.5, y * series, 1.0 - jnp.exp(-y))


def weights_of(residue, rate):
    return residue * jnp.sqrt(one_minus_exp(2.0 * rate))


def copies_kernel(rate_hbm, residue_hbm, copies_ref, rate_ref, residue_ref, sems):
    pairs = ((rate_hbm, rate_ref), (residue_hbm, residue_ref))
    loads = [pltpu.make_async_copy(source, target, sems.at[i]) for i, (source, target) in enumerate(pairs)]
    for load in loads:
        load.start()
    for load in loads:
        load.wait()
    rate = rate_ref[...]
    order = rate.shape[0]
    decay, weight = jnp.exp(-rate), weights_of(residue_ref[...], rate)
    for piece in range(copies_ref.shape[0]):
        copies_ref[piece, :order] = decay
        copies_ref[piece, order:] = weight


def token_rows(half, length, token):
    row = (half * length + token) * SUBLANES
    return pl.ds(row if isinstance(row, int) else pl.multiple_of(row, SUBLANES), SUBLANES)


def chunk_rows(chunk, length):
    return pl.ds(chunk // SUBLANES * length * SUBLANES + chunk % SUBLANES, length, stride=SUBLANES)


def mode_rows(ref, base, order, per_chunk, half):
    first = half * SUBLANES * per_chunk + base
    return [ref[pl.ds(first + r, SUBLANES, stride=per_chunk), :] for r in range(order)]


def gain_rows(gain_ref, places, half):
    own = places[half * SUBLANES : (half + 1) * SUBLANES]
    return jnp.concatenate([gain_ref[pl.ds(place, 1), :] for place in own], axis=0)


def scan_half(half, places, order, state, params_ref, series_ref, gain_ref, conv_ref, beside=()):
    length = series_ref.shape[0] // len(places)
    tokens = length // SUBLANES
    decay = mode_rows(params_ref, 0, order, 2 * order, half)
    if conv_ref is not None:
        weight = mode_rows(params_ref, order, order, 2 * order, half)
        gain = gain_rows(gain_ref, places, half)

    def steps(i, state):
        state = list(state)
        for u in range(tokens):
            rows = token_rows(half, length, i * tokens + u)
            x = series_ref[rows, :]
            for r in range(order):
                state[r] = decay[r] * state[r] + x
            if conv_ref is not None:
                conv_ref[rows, :] = tree_sum([weight[r] * state[r] for r in range(order)] + [gain * x])
        return tuple(state)

    if not beside:
        return lax.fori_loop(0, SUBLANES, steps, tuple(state))
    for i, call_beside in enumerate(beside):
        state = steps(i, state)
        call_beside()
    return state


def state_kernel(places, order, params_ref, k_ref, v_ref, gain_ref, series_ref, state_ref, early_ref):
    chunks, length = len(places), k_ref.shape[1]
    halves = chunks // SUBLANES

    def build(chunk):
        rows = pl.ds(places[chunk] * LANES, LANES)
        gated = k_ref[rows, :].astype(jnp.float32) * v_ref[rows, :].astype(jnp.float32)
        series_ref[chunk_rows(chunk, length), :] = gated.T

    def scan(conv_ref):
        for half in range(halves):
            after = range((half + 1) * SUBLANES, min((half + 2) * SUBLANES, chunks))
            beside = [functools.partial(build, chunk) for chunk in after]
            state = (jnp.zeros((SUBLANES, LANES), jnp.float32),) * order
            state = scan_half(half, places, order, state, params_ref, series_ref, gain_ref, conv_ref, beside)
            for r in range(order):
                state_ref[pl.ds(half * SUBLANES * order + r, SUBLANES, stride=order), :] = state[r]

    for chunk in range(SUBLANES):
        build(chunk)
    first = lax.axis_index("seq") == 0

    @pl.when(first)
    def _():
        scan(early_ref)

    @pl.when(jnp.logical_not(first))
    def _():
        scan(None)


def prefix_kernel(length, members, rate_ref, ends_ref, starts_ref):
    span_decay = jnp.exp(-float(length) * rate_ref[...])
    carry = jnp.zeros(rate_ref.shape, jnp.float32)
    for block in range(len(members)):
        starts_ref[members.index(block)] = carry
        carry = span_decay * carry + ends_ref[members.index(block)]


def tree_sum(terms):
    terms = list(terms)
    while len(terms) > 1:
        terms = [terms[i] + terms[i + 1] if i + 1 < len(terms) else terms[i] for i in range(0, len(terms), 2)]
    return terms[0]


def leaving(chunk, places, gated_ref, out_ref, sems):
    rows = pl.ds(places[chunk] * LANES, LANES)
    return pltpu.make_async_copy(gated_ref.at[rows, :], out_ref.at[rows, :], sems.at[chunk])


def finish(chunk, places, conv_ref, q_ref, gated_ref, out_ref, sems):
    length = conv_ref.shape[0] // len(places)
    rows = pl.ds(places[chunk] * LANES, LANES)
    conv = conv_ref[chunk_rows(chunk, length), :].T
    gated_ref[rows, :] = (q_ref[rows, :].astype(jnp.float32) * conv).astype(jnp.bfloat16)
    leaving(chunk, places, gated_ref, out_ref, sems).start()


def output_kernel(
    places, order, carry_ref, params_ref, series_ref, early_ref, gain_ref, q_ref, out_ref, conv_ref, gated_ref, sems
):
    chunks = len(places)
    halves = chunks // SUBLANES
    first = lax.axis_index("seq") == 0

    def send(chunk, source_ref):
        finish(chunk, places, source_ref, q_ref, gated_ref, out_ref, sems)

    @pl.when(first)
    def _():
        for chunk in range(chunks):
            send(chunk, early_ref)

    @pl.when(jnp.logical_not(first))
    def _():
        for half in range(halves):
            before = range(max(half - 1, 0) * SUBLANES, half * SUBLANES)
            beside = [functools.partial(send, chunk, conv_ref) for chunk in before]
            state = mode_rows(carry_ref, 0, order, order, half)
            scan_half(half, places, order, state, params_ref, series_ref, gain_ref, conv_ref, beside)
        for chunk in range(chunks - SUBLANES, chunks):
            send(chunk, conv_ref)

    for chunk in range(chunks):
        leaving(chunk, places, gated_ref, out_ref, sems).wait()


def call(kernel, out_shape, *args, in_spaces=None, out_spaces=None, scratch=(), flops=0):
    in_bytes = sum(a.size * a.dtype.itemsize for a in args)
    in_spaces = in_spaces or [pltpu.VMEM] * len(args)
    out_spaces = out_spaces or jax.tree.map(lambda _: pltpu.VMEM, out_shape)
    return pl.pallas_call(
        kernel,
        out_shape=out_shape,
        in_specs=[pl.BlockSpec(memory_space=space) for space in in_spaces],
        out_specs=jax.tree.map(lambda space: pl.BlockSpec(memory_space=space), out_spaces),
        scratch_shapes=list(scratch),
        compiler_params=pltpu.CompilerParams(vmem_limit_bytes=VMEM_LIMIT),
        cost_estimate=pl.CostEstimate(flops=flops, bytes_accessed=in_bytes, transcendentals=0),
    )(*args)


def to_chunks(pieces):
    owners, rows, own = pieces.shape
    if own == LANES:
        return pieces
    if own < LANES:
        group = LANES // own
        return pieces.reshape(owners // group, group, rows, own).swapaxes(1, 2).reshape(-1, rows, LANES)
    return pieces.reshape(owners, rows, own // LANES, LANES).swapaxes(1, 2).reshape(-1, rows, LANES)


def from_chunks(pieces, owners):
    chunks, rows, _ = pieces.shape
    own = chunks * LANES // owners
    if own == LANES:
        return pieces
    if own < LANES:
        group = LANES // own
        return pieces.reshape(chunks, rows, group, own).swapaxes(1, 2).reshape(owners, rows, own)
    return pieces.reshape(owners, own // LANES, rows, LANES).swapaxes(1, 2).reshape(owners, rows, own)


def all_to_all(pieces, members):
    return lax.all_to_all(pieces, "seq", split_axis=0, concat_axis=0, axis_index_groups=[members], tiled=True)


def shards(blocks, q_proj, k_proj, value_projection, residues, rates, direct_gain):
    channels, length = q_proj.shape
    order = residues.shape[1]
    chunks = channels // LANES
    f32 = jnp.float32

    members, places = list(range(blocks)), list(range(chunks))
    if blocks == chunks:
        far, middle = blocks // 2, blocks * 11 // 16
        upper = [middle] + [block for block in members[:far - 1:-1] if block != middle]
        members = [block for one in upper for block in (one, one - far)]
        places = list(members)

    own_rates = rates.T
    copies = call(
        copies_kernel,
        jax.ShapeDtypeStruct((blocks, 2 * order, rates.shape[0]), f32),
        pltpu.with_memory_space_constraint(own_rates, pltpu.HBM),
        pltpu.with_memory_space_constraint(residues.T, pltpu.HBM),
        in_spaces=[pl.ANY] * 2,
        scratch=[pltpu.VMEM(own_rates.shape, f32)] * 2 + [pltpu.SemaphoreType.DMA((2,))],
        flops=COPIES_COST,
    )
    params = to_chunks(all_to_all(copies, members)).reshape(chunks * 2 * order, LANES)

    gain = direct_gain.reshape(chunks, LANES)
    rows = jax.ShapeDtypeStruct((length * chunks, LANES), f32)
    series, ends, early = call(
        functools.partial(state_kernel, places, order),
        (rows, jax.ShapeDtypeStruct((chunks * order, LANES), f32), rows),
        params,
        k_proj,
        value_projection,
        gain,
        flops=2 * order * channels * length,
    )
    ends = all_to_all(from_chunks(ends.reshape(chunks, order, LANES), blocks), members)
    starts = call(
        functools.partial(prefix_kernel, length, members),
        jax.ShapeDtypeStruct(ends.shape, f32),
        own_rates,
        ends,
    )
    carry = to_chunks(all_to_all(starts, members)).reshape(chunks * order, LANES)
    out_shape = jax.ShapeDtypeStruct((channels, length), jnp.bfloat16)
    return call(
        functools.partial(output_kernel, places, order),
        out_shape,
        carry,
        params,
        series,
        early,
        gain,
        q_proj,
        out_spaces=pl.ANY,
        scratch=[
            pltpu.VMEM(rows.shape, f32),
            pltpu.VMEM(out_shape.shape, out_shape.dtype),
            pltpu.SemaphoreType.DMA((chunks,)),
        ],
        flops=4 * order * channels * length,
    )


def solution(mesh):
    return jax.shard_map(
        functools.partial(shards, mesh.shape["seq"]),
        mesh=mesh,
        in_specs=(
            P("chan", ("groups", "seq")),
            P("chan", ("groups", "seq")),
            P("chan", ("groups", "seq")),
            P(("chan", "seq"), None),
            P(("chan", "seq"), None),
            P("chan"),
        ),
        out_specs=P("chan", ("groups", "seq")),
        check_vma=False,
    )
```

time: 47.6 us -> 41.1 us (0.86)
  the two profiles are of different devices: /device:TPU:0 before, /device:TPU:2 now
where the time goes in v21:
time: 41.1 us; the launch traced here: 40.8 us
  blocking collectives  34.8 us (85%)
  Pallas kernels  5.91 us (14%)
    all_to_all x3, blocking collectives, all_to_all(): lax.all_to_all(pieces, 'seq', split_axis=0, concat_axis=0, axis_index_gro...  34.8 us
    pallas_call x4, Pallas kernels, call(): pl.pallas_call(kernel, out_shape=out_shape, in_specs=[pl.BlockSpec(memory...  5.91 us

profile of v21, /device:TPU:2, one launch (start us, length us, event | category | flops | bytes accessed | tf_op | source)
XLA Modules:
  0.0 40.8 jit_solution(13788552444791422147)
XLA Ops:
  0.0 0.0 copy-start.2
  0.0 0.0 copy-start.3
  0.0 0.8 %shard_map.64 = f32[16,32,128]{2,1,0:T(8,128)S(1)} custom-call(f32[16,128]{1,0:T(8,128)} %bitcast.12, f32[16,128]{1,0:T(8,128)} %bitcast.14), custom_call_target="tpu_custom_call" | custom-call | flops 10000000000 | bytes 16384 | tf_op jit(solution)/shard_map/pallas_call | solution.py:180
  0.8 0.0 copy-start.1
  0.9 13.9 %all_to_all.15 = f32[16,32,128]{2,1,0:T(8,128)S(1)} all-to-all(f32[16,32,128]{2,1,0:T(8,128)S(1)} %shard_map.64), channel_id=1, replica_groups={{22,6,30,14,28,12,26,10,24,8,20,4,18,2,16,0},{23,7,31,15,29,13,27,11,25..., dimensions={0} | all-to-all | bytes 524288 | tf_op jit(solution)/shard_map/all_to_all | solution.py:213
  14.7 0.0 copy-done.2
  14.7 0.0 copy-done.3
  14.7 0.0 copy-done.1
  14.7 0.0 copy-start.4
  14.8 1.5 %shard_map.65 = (f32[2048,128]{1,0:T(8,128)S(1)}, f32[256,128]{1,0:T(8,128)S(1)}, f32[2048,128]{1,0:T(8,128)S(1)}) custom-call(f32[512,128]{1,0:T(8,128)S(1)} %bitcast.6, bf16[2048,128]{1,0:T(8,128)(2,1)S(1)} %copy-done.1, bf16[2048,128]{1,0:T(8,128)(2,1)S(1)} %copy-done.2, f32[16,128]{1,0:T(8,128)S(1)} %bitcast.10), custom_call_target="tpu_custom_call" | custom-call | flops 8388608 | bytes 1318912 | tf_op jit(solution)/shard_map/pallas_call | solution.py:180
  16.2 0.0 copy-start
  16.2 11.0 %all_to_all.16.ends_ref = f32[16,16,128]{2,1,0:T(8,128)S(1)} all-to-all(f32[16,16,128]{2,1,0:T(8,128)S(1)} %bitcast.9), channel_id=1, replica_groups={{22,6,30,14,28,12,26,10,24,8,20,4,18,2,16,0},{23,7,31,15,29,13,27,11,25..., dimensions={0} | all-to-all | bytes 262144 | tf_op jit(solution)/shard_map/all_to_all | solution.py:213
  27.2 0.0 copy-done.4
  27.3 10.0 %all_to_all.17 = f32[16,16,128]{2,1,0:T(8,128)S(1)} all-to-all(f32[16,16,128]{2,1,0:T(8,128)S(1)} %shard_map.66), channel_id=1, replica_groups={{22,6,30,14,28,12,26,10,24,8,20,4,18,2,16,0},{23,7,31,15,29,13,27,11,25..., dimensions={0} | all-to-all | bytes 262144 | tf_op jit(solution)/shard_map/all_to_all | solution.py:213
  37.3 0.0 copy-done
  37.3 3.6 %shard_map.67 = bf16[2048,128]{1,0:T(8,128)(2,1)} custom-call(f32[256,128]{1,0:T(8,128)S(1)} %bitcast.8, f32[512,128]{1,0:T(8,128)S(1)} %bitcast.7, f32[2048,128]{1,0:T(8,128)S(1)} %get-tuple-element.9.series_ref, f32[2048,128]{1,0:T(8,128)S(1)} %get-tuple-element.10.early_ref, f32[16,128]{1,0:T(8,128)S(1)} %bitcast.11, bf16[2048,128]{1,0:T(8,128)(2,1)S(1)} %copy-done), custom_call_target="tpu_custom_call" | custom-call | flops 16777216 | bytes 3022848 | tf_op jit(solution)/shard_map/pallas_call | solution.py:180
  (1 shorter events, 0.0 us)
Async XLA Ops:
  0.0 14.7 %copy-start.2 = (bf16[2048,128]{1,0:T(8,128)(2,1)S(1)}, bf16[2048,128]{1,0:T(8,128)(2,1)}, u32[]{:S(2)}) copy-start(bf16[2048,128]{1,0:T(8,128)(2,1)} %v_ref.1) | copy-start | bytes 1572868
  0.0 14.7 %copy-start.3 = (f32[2048]{0:T(1024)S(1)}, f32[2048]{0:T(1024)}, u32[]{:S(2)}) copy-start(f32[2048]{0:T(1024)} %param.11) | copy-start | bytes 24580
  0.8 13.9 %copy-start.1 = (bf16[2048,128]{1,0:T(8,128)(2,1)S(1)}, bf16[2048,128]{1,0:T(8,128)(2,1)}, u32[]{:S(2)}) copy-start(bf16[2048,128]{1,0:T(8,128)(2,1)} %k_ref.1) | copy-start | bytes 1572868
  14.7 12.5 %copy-start.4 = (f32[128,16]{0,1:T(8,128)S(1)}, f32[128,16]{0,1:T(8,128)}, u32[]{:S(2)}) copy-start(f32[128,16]{0,1:T(8,128)} %param.10) | copy-start | bytes 24580
  16.2 21.0 %copy-start = (bf16[2048,128]{1,0:T(8,128)(2,1)S(1)}, bf16[2048,128]{1,0:T(8,128)(2,1)}, u32[]{:S(2)}) copy-start(bf16[2048,128]{1,0:T(8,128)(2,1)} %q_ref.1) | copy-start | bytes 1572868

commit v22 on v18

--- a/solution.py
+++ b/solution.py
@@ -64,13 +64,15 @@
         build(chunk)
     for half in range(halves):
         decay = mode_rows(decays_ref, 0, order, order, chunks, half)
+        square = [one * one for one in decay]
 
         def steps(i, state):
             state = list(state)
-            for u in range(tokens):
+            for u in range(0, tokens, 2):
                 x = series_ref[token_rows(half, length, i * tokens + u), :]
+                y = series_ref[token_rows(half, length, i * tokens + u + 1), :]
                 for r in range(order):
-                    state[r] = decay[r] * state[r] + x
+                    state[r] = square[r] * state[r] + (decay[r] * x + y)
             return tuple(state)
 
         state = (jnp.zeros((SUBLANES, LANES), jnp.float32),) * order

time: 38.5 us -> 38.5 us (level)
  no operation moved by 1% of the time
where the time goes in v22:
time: 38.5 us; the launch traced here: 38.1 us
  blocking collectives  22.2 us (58%)
  Pallas kernels  7.99 us (21%)
  starting transfers between devices  5.61 us (15%)
  waiting for transfers between devices  2.26 us (6%)
    all_to_all x2, blocking collectives, all_to_all(): lax.all_to_all(pieces, 'seq', split_axis=0, concat_axis=0, axis_index_gro...  22.2 us
    pallas_call x5, Pallas kernels, call(): pl.pallas_call(kernel, out_shape=out_shape, in_specs=[pl.BlockSpec(memory...  7.99 us
    all_to_all x1, starting transfers between devices, all_to_all(): lax.all_to_all(pieces, 'seq', split_axis=0, concat_axis=0, axis_index_gro...  5.61 us
    all_to_all x1, waiting for transfers between devices, all_to_all(): lax.all_to_all(pieces, 'seq', split_axis=0, concat_axis=0, axis_index_gro...  2.26 us
  transfers between devices with their start and end apart: 1, of which 1 were waited for; matrix products, arithmetic and copies ran while one was open for 0% of the time, Pallas kernels for 7%

profile of v22, /device:TPU:2, one launch (start us, length us, event | category | flops | bytes accessed | tf_op | source)
XLA Modules:
  0.0 38.1 jit_solution(17798000761022376698)
XLA Ops:
  0.0 0.0 copy-start.1
  0.0 0.0 copy-start.2
  0.0 0.0 copy-start.3
  0.0 0.0 copy-start.4
  0.0 0.8 %shard_map.64 = f32[16,16,128]{2,1,0:T(8,128)S(1)} custom-call(f32[16,128]{1,0:T(8,128)} %bitcast.14), custom_call_target="tpu_custom_call" | custom-call | flops 10000000000 | bytes 8192 | tf_op jit(solution)/shard_map/pallas_call | solution.py:189
  0.8 11.1 %all_to_all.15 = f32[16,16,128]{2,1,0:T(8,128)S(1)} all-to-all(f32[16,16,128]{2,1,0:T(8,128)S(1)} %shard_map.64), channel_id=1, replica_groups={{22,6,30,14,28,12,26,10,24,8,20,4,18,2,16,0},{23,7,31,15,29,13,27,11,25..., dimensions={0} | all-to-all | bytes 262144 | tf_op jit(solution)/shard_map/all_to_all | solution.py:223
  12.0 0.0 copy-done.1
  12.0 0.0 copy-done.2
  12.0 0.0 copy-done.3
  12.0 0.0 copy-done.4
  12.0 1.5 %shard_map.65 = (f32[2048,128]{1,0:T(8,128)S(1)}, f32[512,128]{1,0:T(8,128)S(1)}) custom-call(f32[256,128]{1,0:T(8,128)S(1)} %bitcast.9, f32[16,128]{1,0:T(8,128)S(1)} %bitcast.15, f32[16,128]{1,0:T(8,128)S(1)} %bitcast.17, bf16[2048,128]{1,0:T(8,128)(2,1)S(1)} %copy-done.1, bf16[2048,128]{1,0:T(8,128)(2,1)S(1)} %copy-done.2), custom_call_target="tpu_custom_call" | custom-call | flops 8388608 | bytes 1196032 | tf_op jit(solution)/shard_map/pallas_call | solution.py:189
  13.5 0.0 copy-start
  13.5 11.1 %all_to_all.16.ends_ref = f32[16,32,128]{2,1,0:T(8,128)S(1)} all-to-all(f32[16,32,128]{2,1,0:T(8,128)S(1)} %bitcast.13), channel_id=1, replica_groups={{22,6,30,14,28,12,26,10,24,8,20,4,18,2,16,0},{23,7,31,15,29,13,27,11,25..., dimensions={0} | all-to-all | bytes 524288 | tf_op jit(solution)/shard_map/all_to_all | solution.py:223
  24.6 0.7 %shard_map.66 = f32[16,16,128]{2,1,0:T(8,128)} custom-call(f32[16,128]{1,0:T(8,128)S(1)} %bitcast.16, f32[16,32,128]{2,1,0:T(8,128)S(1)} %all_to_all.16.ends_ref), custom_call_target="tpu_custom_call" | custom-call | bytes 270336 | tf_op jit(solution)/shard_map/pallas_call | solution.py:189
  25.3 0.0 copy-start.5
  25.3 5.6 %all-to-all-start.2 = ((f32[16,16,128]{2,1,0:T(8,128)}), f32[16,16,128]{2,1,0:T(8,128)S(1)}, u32[]{:S(2)}, u32[]{:S(2)}) async-start(f32[16,16,128]{2,1,0:T(8,128)} %shard_map.66), calls=%async_computation.2 | async-start | bytes 262144 | tf_op jit(solution)/shard_map/all_to_all | solution.py:223
  30.9 0.0 copy-done
  30.9 0.0 copy-done.5
  30.9 2.6 %shard_map.67 = (f32[2048,128]{1,0:T(8,128)S(1)}, bf16[2048,128]{1,0:T(8,128)(2,1)}) custom-call(f32[256,128]{1,0:T(8,128)S(1)} %bitcast.10, f32[512,128]{1,0:T(8,128)S(1)} %bitcast.7, f32[2048,128]{1,0:T(8,128)S(1)} %get-tuple-element.10.series_ref, f32[16,128]{1,0:T(8,128)S(1)} %bitcast.18, bf16[2048,128]{1,0:T(8,128)(2,1)S(1)} %copy-done), custom_call_target="tpu_custom_call" | custom-call | flops 16777216 | bytes 1974272 | tf_op jit(solution)/shard_map/pallas_call | solution.py:189
  33.5 2.3 %all-to-all-done.2 = f32[16,16,128]{2,1,0:T(8,128)S(1)} async-done(((f32[16,16,128]{2,1,0:T(8,128)}), f32[16,16,128]{2,1,0:T(8,128)S(1)}, u32[]{:S(2)}, u32[]{:S(2)}) %all-to-all-start.2) | async-done | bytes 131104 | tf_op jit(solution)/shard_map/all_to_all | solution.py:223
  35.8 2.4 %shard_map.68 = bf16[2048,128]{1,0:T(8,128)(2,1)} custom-call(f32[256,128]{1,0:T(8,128)S(1)} %bitcast.11, f32[512,128]{1,0:T(8,128)S(1)} %bitcast.8, f32[256,128]{1,0:T(8,128)S(1)} %bitcast.12, f32[2048,128]{1,0:T(8,128)S(1)} %get-tuple-element.11.local_ref, bf16[2048,128]{1,0:T(8,128)(2,1)S(1)} %copy-done, ...), custom_call_target="tpu_custom_call", output_to_operand_aliasing={{}: (5, {})} | custom-call | flops 8388608 | bytes 2621440 | tf_op jit(solution)/shard_map/pallas_call | solution.py:189
Async XLA Ops:
  0.0 12.0 %copy-start.1 = (bf16[2048,128]{1,0:T(8,128)(2,1)S(1)}, bf16[2048,128]{1,0:T(8,128)(2,1)}, u32[]{:S(2)}) copy-start(bf16[2048,128]{1,0:T(8,128)(2,1)} %k_ref.1) | copy-start | bytes 1572868
  0.0 12.0 %copy-start.2 = (bf16[2048,128]{1,0:T(8,128)(2,1)S(1)}, bf16[2048,128]{1,0:T(8,128)(2,1)}, u32[]{:S(2)}) copy-start(bf16[2048,128]{1,0:T(8,128)(2,1)} %v_ref.1) | copy-start | bytes 1572868
  0.0 12.0 %copy-start.3 = (f32[128,16]{0,1:T(8,128)S(1)}, f32[128,16]{0,1:T(8,128)}, u32[]{:S(2)}) copy-start(f32[128,16]{0,1:T(8,128)} %param.10) | copy-start | bytes 24580
  0.0 12.0 %copy-start.4 = (f32[128,16]{0,1:T(8,128)S(1)}, f32[128,16]{0,1:T(8,128)}, u32[]{:S(2)}) copy-start(f32[128,16]{0,1:T(8,128)} %param.9) | copy-start | bytes 24580
  13.5 17.4 %copy-start = (bf16[2048,128]{1,0:T(8,128)(2,1)S(1)}, bf16[2048,128]{1,0:T(8,128)(2,1)}, u32[]{:S(2)}) copy-start(bf16[2048,128]{1,0:T(8,128)(2,1)} %q_ref.3) | copy-start | bytes 1572868
  25.3 5.6 %copy-start.5 = (f32[2048]{0:T(1024)S(1)}, f32[2048]{0:T(1024)}, u32[]{:S(2)}) copy-start(f32[2048]{0:T(1024)} %param.11) | copy-start | bytes 24580
  25.3 10.5 %all-to-all-start.2 = ((f32[16,16,128]{2,1,0:T(8,128)}), f32[16,16,128]{2,1,0:T(8,128)S(1)}, u32[]{:S(2)}, u32[]{:S(2)}) async-start(f32[16,16,128]{2,1,0:T(8,128)} %shard_map.66), calls=%async_computation.2 | async-start | bytes 262144 | tf_op jit(solution)/shard_map/all_to_all | solution.py:223

commit v23 on v22

--- a/solution.py
+++ b/solution.py
@@ -231,9 +231,9 @@
 
     members, places = list(range(blocks)), list(range(chunks))
     if blocks == chunks:
-        far, middle = blocks // 2, blocks * 11 // 16
-        upper = [middle] + [block for block in members[:far - 1:-1] if block != middle]
-        members = [block for one in upper for block in (one, one - far)]
+        far, middle = blocks // 2, blocks * 7 // 16
+        lower = [middle] + [block for block in members[far - 1 :: -1] if block != middle]
+        members = [block for one in lower for block in (one, one + far)]
         places = list(members)
 
     own_rates, own_residues = rates.T, residues.T

time: 38.5 us -> 39.6 us (1.029)
  blocking collectives: 22.2 us -> 23.1 us
  waiting for transfers between devices: 2.26 us -> 3.16 us
  starting transfers between devices: 5.61 us -> 4.91 us
    all_to_all x1, waiting for transfers between devices: 2.26 us -> 3.16 us  [all_to_all(): lax.all_to_all(pieces, 'seq', split_axis=0, concat_axis=0, axis_index_gro...]
    all_to_all x2, blocking collectives: 22.2 us -> 23.1 us  [all_to_all(): lax.all_to_all(pieces, 'seq', split_axis=0, concat_axis=0, axis_index_gro...]
    all_to_all x1, starting transfers between devices: 5.61 us -> 4.91 us  [all_to_all(): lax.all_to_all(pieces, 'seq', split_axis=0, concat_axis=0, axis_index_gro...]
where the time goes in v23:
time: 39.6 us; the launch traced here: 39.2 us
  blocking collectives  23.1 us (58%)
  Pallas kernels  7.99 us (20%)
  starting transfers between devices  4.91 us (12%)
  waiting for transfers between devices  3.16 us (8%)
    all_to_all x2, blocking collectives, all_to_all(): lax.all_to_all(pieces, 'seq', split_axis=0, concat_axis=0, axis_index_gro...  23.1 us
    pallas_call x5, Pallas kernels, call(): pl.pallas_call(kernel, out_shape=out_shape, in_specs=[pl.BlockSpec(memory...  7.99 us
    all_to_all x1, starting transfers between devices, all_to_all(): lax.all_to_all(pieces, 'seq', split_axis=0, concat_axis=0, axis_index_gro...  4.91 us
    all_to_all x1, waiting for transfers between devices, all_to_all(): lax.all_to_all(pieces, 'seq', split_axis=0, concat_axis=0, axis_index_gro...  3.16 us
  transfers between devices with their start and end apart: 1, of which 1 were waited for; matrix products, arithmetic and copies ran while one was open for 0% of the time, Pallas kernels for 7%

profile of v23, /device:TPU:2, one launch (start us, length us, event | category | flops | bytes accessed | tf_op | source)
XLA Modules:
  0.0 39.2 jit_solution(5531931813772547417)
XLA Ops:
  0.0 0.0 copy-start.1
  0.0 0.0 copy-start.2
  0.0 0.0 copy-start.3
  0.0 0.0 copy-start.4
  0.0 0.8 %shard_map.64 = f32[16,16,128]{2,1,0:T(8,128)S(1)} custom-call(f32[16,128]{1,0:T(8,128)} %bitcast.14), custom_call_target="tpu_custom_call" | custom-call | flops 10000000000 | bytes 8192 | tf_op jit(solution)/shard_map/pallas_call | solution.py:189
  0.8 12.0 %all_to_all.15 = f32[16,16,128]{2,1,0:T(8,128)S(1)} all-to-all(f32[16,16,128]{2,1,0:T(8,128)S(1)} %shard_map.64), channel_id=1, replica_groups={{14,30,12,28,10,26,8,24,6,22,4,20,2,18,0,16},{15,31,13,29,11,27,9,25,7,..., dimensions={0} | all-to-all | bytes 262144 | tf_op jit(solution)/shard_map/all_to_all | solution.py:223
  12.8 0.0 copy-done.1
  12.8 0.0 copy-done.2
  12.8 0.0 copy-done.3
  12.8 0.0 copy-done.4
  12.9 1.5 %shard_map.65 = (f32[2048,128]{1,0:T(8,128)S(1)}, f32[512,128]{1,0:T(8,128)S(1)}) custom-call(f32[256,128]{1,0:T(8,128)S(1)} %bitcast.9, f32[16,128]{1,0:T(8,128)S(1)} %bitcast.15, f32[16,128]{1,0:T(8,128)S(1)} %bitcast.17, bf16[2048,128]{1,0:T(8,128)(2,1)S(1)} %copy-done.1, bf16[2048,128]{1,0:T(8,128)(2,1)S(1)} %copy-done.2), custom_call_target="tpu_custom_call" | custom-call | flops 8388608 | bytes 1196032 | tf_op jit(solution)/shard_map/pallas_call | solution.py:189
  14.4 0.0 copy-start
  14.4 11.1 %all_to_all.16.ends_ref = f32[16,32,128]{2,1,0:T(8,128)S(1)} all-to-all(f32[16,32,128]{2,1,0:T(8,128)S(1)} %bitcast.13), channel_id=1, replica_groups={{14,30,12,28,10,26,8,24,6,22,4,20,2,18,0,16},{15,31,13,29,11,27,9,25,7,..., dimensions={0} | all-to-all | bytes 524288 | tf_op jit(solution)/shard_map/all_to_all | solution.py:223
  25.5 0.7 %shard_map.66 = f32[16,16,128]{2,1,0:T(8,128)} custom-call(f32[16,128]{1,0:T(8,128)S(1)} %bitcast.16, f32[16,32,128]{2,1,0:T(8,128)S(1)} %all_to_all.16.ends_ref), custom_call_target="tpu_custom_call" | custom-call | bytes 270336 | tf_op jit(solution)/shard_map/pallas_call | solution.py:189
  26.2 0.0 copy-start.5
  26.2 4.9 %all-to-all-start.2 = ((f32[16,16,128]{2,1,0:T(8,128)}), f32[16,16,128]{2,1,0:T(8,128)S(1)}, u32[]{:S(2)}, u32[]{:S(2)}) async-start(f32[16,16,128]{2,1,0:T(8,128)} %shard_map.66), calls=%async_computation.2 | async-start | bytes 262144 | tf_op jit(solution)/shard_map/all_to_all | solution.py:223
  31.1 0.0 copy-done
  31.1 0.0 copy-done.5
  31.1 2.6 %shard_map.67 = (f32[2048,128]{1,0:T(8,128)S(1)}, bf16[2048,128]{1,0:T(8,128)(2,1)}) custom-call(f32[256,128]{1,0:T(8,128)S(1)} %bitcast.10, f32[512,128]{1,0:T(8,128)S(1)} %bitcast.7, f32[2048,128]{1,0:T(8,128)S(1)} %get-tuple-element.10.series_ref, f32[16,128]{1,0:T(8,128)S(1)} %bitcast.18, bf16[2048,128]{1,0:T(8,128)(2,1)S(1)} %copy-done), custom_call_target="tpu_custom_call" | custom-call | flops 16777216 | bytes 1974272 | tf_op jit(solution)/shard_map/pallas_call | solution.py:189
  33.7 3.2 %all-to-all-done.2 = f32[16,16,128]{2,1,0:T(8,128)S(1)} async-done(((f32[16,16,128]{2,1,0:T(8,128)}), f32[16,16,128]{2,1,0:T(8,128)S(1)}, u32[]{:S(2)}, u32[]{:S(2)}) %all-to-all-start.2) | async-done | bytes 131104 | tf_op jit(solution)/shard_map/all_to_all | solution.py:223
  36.9 2.4 %shard_map.68 = bf16[2048,128]{1,0:T(8,128)(2,1)} custom-call(f32[256,128]{1,0:T(8,128)S(1)} %bitcast.11, f32[512,128]{1,0:T(8,128)S(1)} %bitcast.8, f32[256,128]{1,0:T(8,128)S(1)} %bitcast.12, f32[2048,128]{1,0:T(8,128)S(1)} %get-tuple-element.11.local_ref, bf16[2048,128]{1,0:T(8,128)(2,1)S(1)} %copy-done, ...), custom_call_target="tpu_custom_call", output_to_operand_aliasing={{}: (5, {})} | custom-call | flops 8388608 | bytes 2621440 | tf_op jit(solution)/shard_map/pallas_call | solution.py:189
Async XLA Ops:
  0.0 12.8 %copy-start.1 = (bf16[2048,128]{1,0:T(8,128)(2,1)S(1)}, bf16[2048,128]{1,0:T(8,128)(2,1)}, u32[]{:S(2)}) copy-start(bf16[2048,128]{1,0:T(8,128)(2,1)} %k_ref.1) | copy-start | bytes 1572868
  0.0 12.8 %copy-start.2 = (bf16[2048,128]{1,0:T(8,128)(2,1)S(1)}, bf16[2048,128]{1,0:T(8,128)(2,1)}, u32[]{:S(2)}) copy-start(bf16[2048,128]{1,0:T(8,128)(2,1)} %v_ref.1) | copy-start | bytes 1572868
  0.0 12.8 %copy-start.3 = (f32[128,16]{0,1:T(8,128)S(1)}, f32[128,16]{0,1:T(8,128)}, u32[]{:S(2)}) copy-start(f32[128,16]{0,1:T(8,128)} %param.10) | copy-start | bytes 24580
  0.0 12.8 %copy-start.4 = (f32[128,16]{0,1:T(8,128)S(1)}, f32[128,16]{0,1:T(8,128)}, u32[]{:S(2)}) copy-start(f32[128,16]{0,1:T(8,128)} %param.9) | copy-start | bytes 24580
  14.4 16.7 %copy-start = (bf16[2048,128]{1,0:T(8,128)(2,1)S(1)}, bf16[2048,128]{1,0:T(8,128)(2,1)}, u32[]{:S(2)}) copy-start(bf16[2048,128]{1,0:T(8,128)(2,1)} %q_ref.3) | copy-start | bytes 1572868
  26.2 4.9 %copy-start.5 = (f32[2048]{0:T(1024)S(1)}, f32[2048]{0:T(1024)}, u32[]{:S(2)}) copy-start(f32[2048]{0:T(1024)} %param.11) | copy-start | bytes 24580
  26.2 10.7 %all-to-all-start.2 = ((f32[16,16,128]{2,1,0:T(8,128)}), f32[16,16,128]{2,1,0:T(8,128)S(1)}, u32[]{:S(2)}, u32[]{:S(2)}) async-start(f32[16,16,128]{2,1,0:T(8,128)} %shard_map.66), calls=%async_computation.2 | async-start | bytes 262144 | tf_op jit(solution)/shard_map/all_to_all | solution.py:223

commit v24 on v22

--- a/solution.py
+++ b/solution.py
@@ -230,10 +230,11 @@
     f32 = jnp.float32
 
     members, places = list(range(blocks)), list(range(chunks))
-    if blocks == chunks:
+    if blocks == chunks and blocks >= 8:
         far, middle = blocks // 2, blocks * 11 // 16
-        upper = [middle] + [block for block in members[:far - 1:-1] if block != middle]
-        members = [block for one in upper for block in (one, one - far)]
+        upper = [block for block in members[: far - 1 : -1] if block not in (middle, blocks - 1)]
+        upper = [middle] + upper + [blocks - 1]
+        members = [block for pair in zip(upper, members[far - 1 :: -1]) for block in pair]
         places = list(members)
 
     own_rates, own_residues = rates.T, residues.T

time: 38.5 us -> 38.5 us (level)
  no operation moved by 1% of the time
where the time goes in v24:
time: 38.5 us; the launch traced here: 38.2 us
  blocking collectives  22.3 us (58%)
  Pallas kernels  7.99 us (21%)
  starting transfers between devices  5.43 us (14%)
  waiting for transfers between devices  2.34 us (6%)
    all_to_all x2, blocking collectives, all_to_all(): lax.all_to_all(pieces, 'seq', split_axis=0, concat_axis=0, axis_index_gro...  22.3 us
    pallas_call x5, Pallas kernels, call(): pl.pallas_call(kernel, out_shape=out_shape, in_specs=[pl.BlockSpec(memory...  7.99 us
    all_to_all x1, starting transfers between devices, all_to_all(): lax.all_to_all(pieces, 'seq', split_axis=0, concat_axis=0, axis_index_gro...  5.43 us
    all_to_all x1, waiting for transfers between devices, all_to_all(): lax.all_to_all(pieces, 'seq', split_axis=0, concat_axis=0, axis_index_gro...  2.34 us
  transfers between devices with their start and end apart: 1, of which 1 were waited for; matrix products, arithmetic and copies ran while one was open for 0% of the time, Pallas kernels for 7%

profile of v24, /device:TPU:2, one launch (start us, length us, event | category | flops | bytes accessed | tf_op | source)
XLA Modules:
  0.0 38.2 jit_solution(148143428533210222)
XLA Ops:
  0.0 0.0 copy-start.1
  0.0 0.0 copy-start.2
  0.0 0.0 copy-start.3
  0.0 0.0 copy-start.4
  0.0 0.8 %shard_map.64 = f32[16,16,128]{2,1,0:T(8,128)S(1)} custom-call(f32[16,128]{1,0:T(8,128)} %bitcast.14), custom_call_target="tpu_custom_call" | custom-call | flops 10000000000 | bytes 8192 | tf_op jit(solution)/shard_map/pallas_call | solution.py:189
  0.8 11.2 %all_to_all.15 = f32[16,16,128]{2,1,0:T(8,128)S(1)} all-to-all(f32[16,16,128]{2,1,0:T(8,128)S(1)} %shard_map.64), channel_id=1, replica_groups={{22,14,28,12,26,10,24,8,20,6,18,4,16,2,30,0},{23,15,29,13,27,11,25,9,21..., dimensions={0} | all-to-all | bytes 262144 | tf_op jit(solution)/shard_map/all_to_all | solution.py:223
  12.0 0.0 copy-done.1
  12.0 0.0 copy-done.2
  12.0 0.0 copy-done.3
  12.1 0.0 copy-done.4
  12.1 1.5 %shard_map.65 = (f32[2048,128]{1,0:T(8,128)S(1)}, f32[512,128]{1,0:T(8,128)S(1)}) custom-call(f32[256,128]{1,0:T(8,128)S(1)} %bitcast.9, f32[16,128]{1,0:T(8,128)S(1)} %bitcast.15, f32[16,128]{1,0:T(8,128)S(1)} %bitcast.17, bf16[2048,128]{1,0:T(8,128)(2,1)S(1)} %copy-done.1, bf16[2048,128]{1,0:T(8,128)(2,1)S(1)} %copy-done.2), custom_call_target="tpu_custom_call" | custom-call | flops 8388608 | bytes 1196032 | tf_op jit(solution)/shard_map/pallas_call | solution.py:189
  13.6 0.0 copy-start
  13.6 11.1 %all_to_all.16.ends_ref = f32[16,32,128]{2,1,0:T(8,128)S(1)} all-to-all(f32[16,32,128]{2,1,0:T(8,128)S(1)} %bitcast.13), channel_id=1, replica_groups={{22,14,28,12,26,10,24,8,20,6,18,4,16,2,30,0},{23,15,29,13,27,11,25,9,21..., dimensions={0} | all-to-all | bytes 524288 | tf_op jit(solution)/shard_map/all_to_all | solution.py:223
  24.7 0.7 %shard_map.66 = f32[16,16,128]{2,1,0:T(8,128)} custom-call(f32[16,128]{1,0:T(8,128)S(1)} %bitcast.16, f32[16,32,128]{2,1,0:T(8,128)S(1)} %all_to_all.16.ends_ref), custom_call_target="tpu_custom_call" | custom-call | bytes 270336 | tf_op jit(solution)/shard_map/pallas_call | solution.py:189
  25.4 0.0 copy-start.5
  25.4 5.4 %all-to-all-start.2 = ((f32[16,16,128]{2,1,0:T(8,128)}), f32[16,16,128]{2,1,0:T(8,128)S(1)}, u32[]{:S(2)}, u32[]{:S(2)}) async-start(f32[16,16,128]{2,1,0:T(8,128)} %shard_map.66), calls=%async_computation.2 | async-start | bytes 262144 | tf_op jit(solution)/shard_map/all_to_all | solution.py:223
  30.8 0.0 copy-done
  30.8 0.0 copy-done.5
  30.9 2.6 %shard_map.67 = (f32[2048,128]{1,0:T(8,128)S(1)}, bf16[2048,128]{1,0:T(8,128)(2,1)}) custom-call(f32[256,128]{1,0:T(8,128)S(1)} %bitcast.10, f32[512,128]{1,0:T(8,128)S(1)} %bitcast.7, f32[2048,128]{1,0:T(8,128)S(1)} %get-tuple-element.10.series_ref, f32[16,128]{1,0:T(8,128)S(1)} %bitcast.18, bf16[2048,128]{1,0:T(8,128)(2,1)S(1)} %copy-done), custom_call_target="tpu_custom_call" | custom-call | flops 16777216 | bytes 1974272 | tf_op jit(solution)/shard_map/pallas_call | solution.py:189
  33.5 2.3 %all-to-all-done.2 = f32[16,16,128]{2,1,0:T(8,128)S(1)} async-done(((f32[16,16,128]{2,1,0:T(8,128)}), f32[16,16,128]{2,1,0:T(8,128)S(1)}, u32[]{:S(2)}, u32[]{:S(2)}) %all-to-all-start.2) | async-done | bytes 131104 | tf_op jit(solution)/shard_map/all_to_all | solution.py:223
  35.8 2.4 %shard_map.68 = bf16[2048,128]{1,0:T(8,128)(2,1)} custom-call(f32[256,128]{1,0:T(8,128)S(1)} %bitcast.11, f32[512,128]{1,0:T(8,128)S(1)} %bitcast.8, f32[256,128]{1,0:T(8,128)S(1)} %bitcast.12, f32[2048,128]{1,0:T(8,128)S(1)} %get-tuple-element.11.local_ref, bf16[2048,128]{1,0:T(8,128)(2,1)S(1)} %copy-done, ...), custom_call_target="tpu_custom_call", output_to_operand_aliasing={{}: (5, {})} | custom-call | flops 8388608 | bytes 2621440 | tf_op jit(solution)/shard_map/pallas_call | solution.py:189
Async XLA Ops:
  0.0 12.0 %copy-start.1 = (bf16[2048,128]{1,0:T(8,128)(2,1)S(1)}, bf16[2048,128]{1,0:T(8,128)(2,1)}, u32[]{:S(2)}) copy-start(bf16[2048,128]{1,0:T(8,128)(2,1)} %k_ref.1) | copy-start | bytes 1572868
  0.0 12.0 %copy-start.2 = (bf16[2048,128]{1,0:T(8,128)(2,1)S(1)}, bf16[2048,128]{1,0:T(8,128)(2,1)}, u32[]{:S(2)}) copy-start(bf16[2048,128]{1,0:T(8,128)(2,1)} %v_ref.1) | copy-start | bytes 1572868
  0.0 12.0 %copy-start.3 = (f32[128,16]{0,1:T(8,128)S(1)}, f32[128,16]{0,1:T(8,128)}, u32[]{:S(2)}) copy-start(f32[128,16]{0,1:T(8,128)} %param.10) | copy-start | bytes 24580
  0.0 12.0 %copy-start.4 = (f32[128,16]{0,1:T(8,128)S(1)}, f32[128,16]{0,1:T(8,128)}, u32[]{:S(2)}) copy-start(f32[128,16]{0,1:T(8,128)} %param.9) | copy-start | bytes 24580
  13.6 17.2 %copy-start = (bf16[2048,128]{1,0:T(8,128)(2,1)S(1)}, bf16[2048,128]{1,0:T(8,128)(2,1)}, u32[]{:S(2)}) copy-start(bf16[2048,128]{1,0:T(8,128)(2,1)} %q_ref.3) | copy-start | bytes 1572868
  25.4 5.4 %copy-start.5 = (f32[2048]{0:T(1024)S(1)}, f32[2048]{0:T(1024)}, u32[]{:S(2)}) copy-start(f32[2048]{0:T(1024)} %param.11) | copy-start | bytes 24580
  25.4 10.4 %all-to-all-start.2 = ((f32[16,16,128]{2,1,0:T(8,128)}), f32[16,16,128]{2,1,0:T(8,128)S(1)}, u32[]{:S(2)}, u32[]{:S(2)}) async-start(f32[16,16,128]{2,1,0:T(8,128)} %shard_map.66), calls=%async_computation.2 | async-start | bytes 262144 | tf_op jit(solution)/shard_map/all_to_all | solution.py:223

commit v25 on v22

--- a/solution.py
+++ b/solution.py
@@ -10,12 +10,13 @@
 SUBLANES = 8
 UNROLL = 8
 COPIES_COST = 10**10
+PARTS = 4
 VMEM_LIMIT = 32 * 1024 * 1024
 
 
 def copies_kernel(rate_hbm, copies_ref, rate_ref, sem):
     load = pltpu.make_async_copy(rate_hbm, rate_ref, sem)
-    load.start()
+    load.start(priority=1)
     load.wait()
     decay = jnp.exp(-rate_ref[...])
     for piece in range(copies_ref.shape[0]):
@@ -86,12 +87,21 @@
             state_ref[pl.ds(half * SUBLANES * 2 * order + r, SUBLANES, stride=2 * order), :] = state[r]
 
 
-def prefix_kernel(length, members, rate_ref, ends_ref, starts_ref):
+def prefix_kernel(length, members, rate_ref, ends_ref, starts_ref, held_ref, sems):
     span_decay = jnp.exp(-float(length) * rate_ref[...])
     carry = jnp.zeros(rate_ref.shape, jnp.float32)
     for block in range(len(members)):
-        starts_ref[members.index(block)] = carry
+        held_ref[members.index(block)] = carry
         carry = span_decay * carry + ends_ref[members.index(block), : rate_ref.shape[0]]
+    part = max(len(members) // PARTS, 1)
+    copies = []
+    for i in range(0, len(members), part):
+        rows = pl.ds(i, part)
+        copies.append(pltpu.make_async_copy(held_ref.at[rows], starts_ref.at[rows], sems.at[i // part]))
+    for i, copy in enumerate(copies):
+        copy.start(priority=i % 2)
+    for copy in copies:
+        copy.wait()
 
 
 def tree_sum(terms):
@@ -111,7 +121,7 @@
     rows = pl.ds(places[chunk] * LANES, LANES)
     conv = conv_ref[chunk_rows(chunk, length), :].T
     gated_ref[rows, :] = (q_ref[rows, :].astype(jnp.float32) * conv).astype(jnp.bfloat16)
-    leaving(chunk, places, gated_ref, out_ref, sems).start()
+    leaving(chunk, places, gated_ref, out_ref, sems).start(priority=chunk % 2)
 
 
 def local_kernel(
@@ -290,6 +300,8 @@
         jax.ShapeDtypeStruct((blocks,) + own_rates.shape, f32),
         own_rates,
         ends,
+        out_spaces=pl.ANY,
+        scratch=[pltpu.VMEM((blocks,) + own_rates.shape, f32), pltpu.SemaphoreType.DMA((PARTS,))],
     )
     starts = all_to_all(starts, members)
     carry = to_chunks(starts).reshape(chunks * order, LANES)

time: 38.5 us -> 38.4 us (level)
  no operation moved by 1% of the time
where the time goes in v25:
time: 38.4 us; the launch traced here: 38.1 us
  blocking collectives  22.2 us (58%)
  Pallas kernels  8.02 us (21%)
  starting transfers between devices  5.49 us (14%)
  waiting for transfers between devices  2.26 us (6%)
    all_to_all x2, blocking collectives, all_to_all(): lax.all_to_all(pieces, 'seq', split_axis=0, concat_axis=0, axis_index_gro...  22.2 us
    pallas_call x5, Pallas kernels, call(): pl.pallas_call(kernel, out_shape=out_shape, in_specs=[pl.BlockSpec(memory...  8.02 us
    all_to_all x1, starting transfers between devices, all_to_all(): lax.all_to_all(pieces, 'seq', split_axis=0, concat_axis=0, axis_index_gro...  5.49 us
    all_to_all x1, waiting for transfers between devices, all_to_all(): lax.all_to_all(pieces, 'seq', split_axis=0, concat_axis=0, axis_index_gro...  2.26 us
  transfers between devices with their start and end apart: 1, of which 1 were waited for; matrix products, arithmetic and copies ran while one was open for 0% of the time, Pallas kernels for 7%

profile of v25, /device:TPU:2, one launch (start us, length us, event | category | flops | bytes accessed | tf_op | source)
XLA Modules:
  0.0 38.1 jit_solution(1152807168722528581)
XLA Ops:
  0.0 0.0 copy-start.1
  0.0 0.0 copy-start.2
  0.0 0.0 copy-start.3
  0.0 0.0 copy-start.4
  0.0 0.8 %shard_map.64 = f32[16,16,128]{2,1,0:T(8,128)S(1)} custom-call(f32[16,128]{1,0:T(8,128)} %bitcast.14), custom_call_target="tpu_custom_call" | custom-call | flops 10000000000 | bytes 8192 | tf_op jit(solution)/shard_map/pallas_call | solution.py:199
  0.8 11.1 %all_to_all.15 = f32[16,16,128]{2,1,0:T(8,128)S(1)} all-to-all(f32[16,16,128]{2,1,0:T(8,128)S(1)} %shard_map.64), channel_id=1, replica_groups={{22,6,30,14,28,12,26,10,24,8,20,4,18,2,16,0},{23,7,31,15,29,13,27,11,25..., dimensions={0} | all-to-all | bytes 262144 | tf_op jit(solution)/shard_map/all_to_all | solution.py:233
  12.0 0.0 copy-done.1
  12.0 0.0 copy-done.2
  12.0 0.0 copy-done.3
  12.0 0.0 copy-done.4
  12.0 1.5 %shard_map.65 = (f32[2048,128]{1,0:T(8,128)S(1)}, f32[512,128]{1,0:T(8,128)S(1)}) custom-call(f32[256,128]{1,0:T(8,128)S(1)} %bitcast.9, f32[16,128]{1,0:T(8,128)S(1)} %bitcast.15, f32[16,128]{1,0:T(8,128)S(1)} %bitcast.17, bf16[2048,128]{1,0:T(8,128)(2,1)S(1)} %copy-done.1, bf16[2048,128]{1,0:T(8,128)(2,1)S(1)} %copy-done.2), custom_call_target="tpu_custom_call" | custom-call | flops 8388608 | bytes 1196032 | tf_op jit(solution)/shard_map/pallas_call | solution.py:199
  13.5 0.0 copy-start
  13.5 11.1 %all_to_all.16.ends_ref = f32[16,32,128]{2,1,0:T(8,128)S(1)} all-to-all(f32[16,32,128]{2,1,0:T(8,128)S(1)} %bitcast.13), channel_id=1, replica_groups={{22,6,30,14,28,12,26,10,24,8,20,4,18,2,16,0},{23,7,31,15,29,13,27,11,25..., dimensions={0} | all-to-all | bytes 524288 | tf_op jit(solution)/shard_map/all_to_all | solution.py:233
  24.6 0.7 %shard_map.66 = f32[16,16,128]{2,1,0:T(8,128)} custom-call(f32[16,128]{1,0:T(8,128)S(1)} %bitcast.16, f32[16,32,128]{2,1,0:T(8,128)S(1)} %all_to_all.16.ends_ref), custom_call_target="tpu_custom_call" | custom-call | bytes 270336 | tf_op jit(solution)/shard_map/pallas_call | solution.py:199
  25.3 0.0 copy-start.5
  25.3 5.5 %all-to-all-start.2 = ((f32[16,16,128]{2,1,0:T(8,128)}), f32[16,16,128]{2,1,0:T(8,128)S(1)}, u32[]{:S(2)}, u32[]{:S(2)}) async-start(f32[16,16,128]{2,1,0:T(8,128)} %shard_map.66), calls=%async_computation.2 | async-start | bytes 262144 | tf_op jit(solution)/shard_map/all_to_all | solution.py:233
  30.8 0.0 copy-done
  30.8 0.0 copy-done.5
  30.8 2.6 %shard_map.67 = (f32[2048,128]{1,0:T(8,128)S(1)}, bf16[2048,128]{1,0:T(8,128)(2,1)}) custom-call(f32[256,128]{1,0:T(8,128)S(1)} %bitcast.10, f32[512,128]{1,0:T(8,128)S(1)} %bitcast.7, f32[2048,128]{1,0:T(8,128)S(1)} %get-tuple-element.10.series_ref, f32[16,128]{1,0:T(8,128)S(1)} %bitcast.18, bf16[2048,128]{1,0:T(8,128)(2,1)S(1)} %copy-done), custom_call_target="tpu_custom_call" | custom-call | flops 16777216 | bytes 1974272 | tf_op jit(solution)/shard_map/pallas_call | solution.py:199
  33.5 2.3 %all-to-all-done.2 = f32[16,16,128]{2,1,0:T(8,128)S(1)} async-done(((f32[16,16,128]{2,1,0:T(8,128)}), f32[16,16,128]{2,1,0:T(8,128)S(1)}, u32[]{:S(2)}, u32[]{:S(2)}) %all-to-all-start.2) | async-done | bytes 131104 | tf_op jit(solution)/shard_map/all_to_all | solution.py:233
  35.7 2.4 %shard_map.68 = bf16[2048,128]{1,0:T(8,128)(2,1)} custom-call(f32[256,128]{1,0:T(8,128)S(1)} %bitcast.11, f32[512,128]{1,0:T(8,128)S(1)} %bitcast.8, f32[256,128]{1,0:T(8,128)S(1)} %bitcast.12, f32[2048,128]{1,0:T(8,128)S(1)} %get-tuple-element.11.local_ref, bf16[2048,128]{1,0:T(8,128)(2,1)S(1)} %copy-done, ...), custom_call_target="tpu_custom_call", output_to_operand_aliasing={{}: (5, {})} | custom-call | flops 8388608 | bytes 2621440 | tf_op jit(solution)/shard_map/pallas_call | solution.py:199
Async XLA Ops:
  0.0 12.0 %copy-start.1 = (bf16[2048,128]{1,0:T(8,128)(2,1)S(1)}, bf16[2048,128]{1,0:T(8,128)(2,1)}, u32[]{:S(2)}) copy-start(bf16[2048,128]{1,0:T(8,128)(2,1)} %k_ref.1) | copy-start | bytes 1572868
  0.0 12.0 %copy-start.2 = (bf16[2048,128]{1,0:T(8,128)(2,1)S(1)}, bf16[2048,128]{1,0:T(8,128)(2,1)}, u32[]{:S(2)}) copy-start(bf16[2048,128]{1,0:T(8,128)(2,1)} %v_ref.1) | copy-start | bytes 1572868
  0.0 12.0 %copy-start.3 = (f32[128,16]{0,1:T(8,128)S(1)}, f32[128,16]{0,1:T(8,128)}, u32[]{:S(2)}) copy-start(f32[128,16]{0,1:T(8,128)} %param.10) | copy-start | bytes 24580
  0.0 12.0 %copy-start.4 = (f32[128,16]{0,1:T(8,128)S(1)}, f32[128,16]{0,1:T(8,128)}, u32[]{:S(2)}) copy-start(f32[128,16]{0,1:T(8,128)} %param.9) | copy-start | bytes 24580
  13.5 17.3 %copy-start = (bf16[2048,128]{1,0:T(8,128)(2,1)S(1)}, bf16[2048,128]{1,0:T(8,128)(2,1)}, u32[]{:S(2)}) copy-start(bf16[2048,128]{1,0:T(8,128)(2,1)} %q_ref.3) | copy-start | bytes 1572868
  25.3 5.5 %copy-start.5 = (f32[2048]{0:T(1024)S(1)}, f32[2048]{0:T(1024)}, u32[]{:S(2)}) copy-start(f32[2048]{0:T(1024)} %param.11) | copy-start | bytes 24580
  25.3 10.4 %all-to-all-start.2 = ((f32[16,16,128]{2,1,0:T(8,128)}), f32[16,16,128]{2,1,0:T(8,128)S(1)}, u32[]{:S(2)}, u32[]{:S(2)}) async-start(f32[16,16,128]{2,1,0:T(8,128)} %shard_map.66), calls=%async_computation.2 | async-start | bytes 262144 | tf_op jit(solution)/shard_map/all_to_all | solution.py:233

commit v26 on v22

--- a/solution.py
+++ b/solution.py
@@ -115,13 +115,16 @@
 
 
 def local_kernel(
-    places, order, decays_ref, weights_ref, series_ref, gain_ref, q_ref, conv_ref, out_ref, gated_ref, sems
+    places, order, decays_ref, weights_ref, series_ref, gain_ref, q_ref, conv_ref, dense_ref, out_ref, gated_ref, sems
 ):
     chunks = len(places)
     length = series_ref.shape[0] // chunks
     for half in range(chunks // SUBLANES):
         decay = mode_rows(decays_ref, 0, order, order, chunks, half)
         weight = mode_rows(weights_ref, order, order, 2 * order, chunks, half)
+        for r in range(order):
+            dense_ref[half, 0, r] = decay[r]
+            dense_ref[half, 1, r] = weight[r]
         own = places[half * SUBLANES : (half + 1) * SUBLANES]
         gain = jnp.concatenate([gain_ref[pl.ds(place, 1), :] for place in own], axis=0)
 
@@ -148,7 +151,7 @@
 
 
 def output_kernel(
-    places, order, decays_ref, weights_ref, carry_ref, local_ref, q_ref, _, out_ref, conv_ref, gated_ref, sems
+    places, order, dense_ref, carry_ref, local_ref, q_ref, _, out_ref, conv_ref, gated_ref, sems
 ):
     chunks = len(places)
     length = local_ref.shape[0] // chunks
@@ -157,8 +160,8 @@
     @pl.when(lax.axis_index("seq") > 0)
     def _():
         for half in range(chunks // SUBLANES):
-            decay = mode_rows(decays_ref, 0, order, order, chunks, half)
-            weight = mode_rows(weights_ref, order, order, 2 * order, chunks, half)
+            decay = [dense_ref[half, 0, r] for r in range(order)]
+            weight = [dense_ref[half, 1, r] for r in range(order)]
             carry = mode_rows(carry_ref, 0, order, order, chunks, half)
 
             def steps(i, fading):
@@ -270,10 +273,11 @@
     weights = to_chunks(ends).reshape(chunks * 2 * order, LANES)
     out_shape = jax.ShapeDtypeStruct((channels, length), jnp.bfloat16)
     out_scratch = [pltpu.VMEM(out_shape.shape, out_shape.dtype), pltpu.SemaphoreType.DMA((chunks,))]
-    local, out = call(
+    local, dense, out = call(
         functools.partial(local_kernel, places, order),
         (
             jax.ShapeDtypeStruct((length * chunks, LANES), f32),
+            jax.ShapeDtypeStruct((chunks // SUBLANES, 2, order, SUBLANES, LANES), f32),
             out_shape,
         ),
         decays,
@@ -281,7 +285,7 @@
         local_series,
         direct_gain.reshape(chunks, LANES),
         q_proj,
-        out_spaces=(pltpu.VMEM, pl.ANY),
+        out_spaces=(pltpu.VMEM, pltpu.VMEM, pl.ANY),
         scratch=out_scratch,
         flops=4 * order * channels * length,
     )
@@ -296,14 +300,13 @@
     return call(
         functools.partial(output_kernel, places, order),
         out_shape,
-        decays,
-        weights,
+        dense,
         carry,
         local,
         q_proj,
         out,
         out_spaces=pl.ANY,
-        aliases={5: 0},
+        aliases={4: 0},
         scratch=[pltpu.VMEM((length * chunks, LANES), f32)] + out_scratch,
         flops=2 * order * channels * length,
     )

time: 38.5 us -> 38.4 us (level)
  no operation moved by 1% of the time
where the time goes in v26:
time: 38.4 us; the launch traced here: 38 us
  blocking collectives  22.2 us (58%)
  Pallas kernels  7.89 us (21%)
  starting transfers between devices  5.61 us (15%)
  waiting for transfers between devices  2.25 us (6%)
    all_to_all x2, blocking collectives, all_to_all(): lax.all_to_all(pieces, 'seq', split_axis=0, concat_axis=0, axis_index_gro...  22.2 us
    pallas_call x5, Pallas kernels, call(): pl.pallas_call(kernel, out_shape=out_shape, in_specs=[pl.BlockSpec(memory...  7.89 us
    all_to_all x1, starting transfers between devices, all_to_all(): lax.all_to_all(pieces, 'seq', split_axis=0, concat_axis=0, axis_index_gro...  5.61 us
    all_to_all x1, waiting for transfers between devices, all_to_all(): lax.all_to_all(pieces, 'seq', split_axis=0, concat_axis=0, axis_index_gro...  2.25 us
  transfers between devices with their start and end apart: 1, of which 1 were waited for; matrix products, arithmetic and copies ran while one was open for 0% of the time, Pallas kernels for 7%

profile of v26, /device:TPU:2, one launch (start us, length us, event | category | flops | bytes accessed | tf_op | source)
XLA Modules:
  0.0 38.0 jit_solution(11860121799875566046)
XLA Ops:
  0.0 0.0 copy-start.1
  0.0 0.0 copy-start.2
  0.0 0.0 copy-start.3
  0.0 0.0 copy-start.4
  0.0 0.8 %shard_map.64 = f32[16,16,128]{2,1,0:T(8,128)S(1)} custom-call(f32[16,128]{1,0:T(8,128)} %bitcast.12), custom_call_target="tpu_custom_call" | custom-call | flops 10000000000 | bytes 8192 | tf_op jit(solution)/shard_map/pallas_call | solution.py:192
  0.8 11.1 %all_to_all.15 = f32[16,16,128]{2,1,0:T(8,128)S(1)} all-to-all(f32[16,16,128]{2,1,0:T(8,128)S(1)} %shard_map.64), channel_id=1, replica_groups={{22,6,30,14,28,12,26,10,24,8,20,4,18,2,16,0},{23,7,31,15,29,13,27,11,25..., dimensions={0} | all-to-all | bytes 262144 | tf_op jit(solution)/shard_map/all_to_all | solution.py:226
  12.0 0.0 copy-done.1
  12.0 0.0 copy-done.2
  12.0 0.0 copy-done.3
  12.0 0.0 copy-done.4
  12.0 1.5 %shard_map.65 = (f32[2048,128]{1,0:T(8,128)S(1)}, f32[512,128]{1,0:T(8,128)S(1)}) custom-call(f32[256,128]{1,0:T(8,128)S(1)} %bitcast.8, f32[16,128]{1,0:T(8,128)S(1)} %bitcast.13, f32[16,128]{1,0:T(8,128)S(1)} %bitcast.15, bf16[2048,128]{1,0:T(8,128)(2,1)S(1)} %copy-done.1, bf16[2048,128]{1,0:T(8,128)(2,1)S(1)} %copy-done.2), custom_call_target="tpu_custom_call" | custom-call | flops 8388608 | bytes 1196032 | tf_op jit(solution)/shard_map/pallas_call | solution.py:192
  13.5 0.0 copy-start
  13.5 11.1 %all_to_all.16.ends_ref = f32[16,32,128]{2,1,0:T(8,128)S(1)} all-to-all(f32[16,32,128]{2,1,0:T(8,128)S(1)} %bitcast.11), channel_id=1, replica_groups={{22,6,30,14,28,12,26,10,24,8,20,4,18,2,16,0},{23,7,31,15,29,13,27,11,25..., dimensions={0} | all-to-all | bytes 524288 | tf_op jit(solution)/shard_map/all_to_all | solution.py:226
  24.6 0.7 %shard_map.67 = f32[16,16,128]{2,1,0:T(8,128)} custom-call(f32[16,128]{1,0:T(8,128)S(1)} %bitcast.14, f32[16,32,128]{2,1,0:T(8,128)S(1)} %all_to_all.16.ends_ref), custom_call_target="tpu_custom_call" | custom-call | bytes 270336 | tf_op jit(solution)/shard_map/pallas_call | solution.py:192
  25.3 0.0 copy-start.5
  25.3 5.6 %all-to-all-start.2 = ((f32[16,16,128]{2,1,0:T(8,128)}), f32[16,16,128]{2,1,0:T(8,128)S(1)}, u32[]{:S(2)}, u32[]{:S(2)}) async-start(f32[16,16,128]{2,1,0:T(8,128)} %shard_map.67), calls=%async_computation.2 | async-start | bytes 262144 | tf_op jit(solution)/shard_map/all_to_all | solution.py:226
  30.9 0.0 copy-done
  30.9 0.0 copy-done.5
  30.9 2.6 %shard_map.66 = (f32[2048,128]{1,0:T(8,128)S(1)}, f32[2,2,16,8,128]{4,3,2,1,0:T(8,128)S(1)}, bf16[2048,128]{1,0:T(8,128)(2,1)}) custom-call(f32[256,128]{1,0:T(8,128)S(1)} %bitcast.9, f32[512,128]{1,0:T(8,128)S(1)} %bitcast.7, f32[2048,128]{1,0:T(8,128)S(1)} %get-tuple-element.11.series_ref, f32[16,128]{1,0:T(8,128)S(1)} %bitcast.16, ...), custom_call_target="tpu_custom_call" | custom-call | flops 16777216 | bytes 1974272 | tf_op jit(solution)/shard_map/pallas_call | solution.py:192
  33.5 2.2 %all-to-all-done.2 = f32[16,16,128]{2,1,0:T(8,128)S(1)} async-done(((f32[16,16,128]{2,1,0:T(8,128)}), f32[16,16,128]{2,1,0:T(8,128)S(1)}, u32[]{:S(2)}, u32[]{:S(2)}) %all-to-all-start.2) | async-done | bytes 131104 | tf_op jit(solution)/shard_map/all_to_all | solution.py:226
  35.8 2.3 %shard_map.68 = bf16[2048,128]{1,0:T(8,128)(2,1)} custom-call(f32[2,2,16,8,128]{4,3,2,1,0:T(8,128)S(1)} %get-tuple-element.12.dense_ref, f32[256,128]{1,0:T(8,128)S(1)} %bitcast.10, f32[2048,128]{1,0:T(8,128)S(1)} %get-tuple-element.13.local_ref, bf16[2048,128]{1,0:T(8,128)(2,1)S(1)} %copy-done, ...), custom_call_target="tpu_custom_call", output_to_operand_aliasing={{}: (4, {})} | custom-call | flops 8388608 | bytes 2490368 | tf_op jit(solution)/shard_map/pallas_call | solution.py:192
Async XLA Ops:
  0.0 12.0 %copy-start.1 = (bf16[2048,128]{1,0:T(8,128)(2,1)S(1)}, bf16[2048,128]{1,0:T(8,128)(2,1)}, u32[]{:S(2)}) copy-start(bf16[2048,128]{1,0:T(8,128)(2,1)} %k_ref.1) | copy-start | bytes 1572868
  0.0 12.0 %copy-start.2 = (bf16[2048,128]{1,0:T(8,128)(2,1)S(1)}, bf16[2048,128]{1,0:T(8,128)(2,1)}, u32[]{:S(2)}) copy-start(bf16[2048,128]{1,0:T(8,128)(2,1)} %v_ref.1) | copy-start | bytes 1572868
  0.0 12.0 %copy-start.3 = (f32[128,16]{0,1:T(8,128)S(1)}, f32[128,16]{0,1:T(8,128)}, u32[]{:S(2)}) copy-start(f32[128,16]{0,1:T(8,128)} %param.10) | copy-start | bytes 24580
  0.0 12.0 %copy-start.4 = (f32[128,16]{0,1:T(8,128)S(1)}, f32[128,16]{0,1:T(8,128)}, u32[]{:S(2)}) copy-start(f32[128,16]{0,1:T(8,128)} %param.9) | copy-start | bytes 24580
  13.5 17.4 %copy-start = (bf16[2048,128]{1,0:T(8,128)(2,1)S(1)}, bf16[2048,128]{1,0:T(8,128)(2,1)}, u32[]{:S(2)}) copy-start(bf16[2048,128]{1,0:T(8,128)(2,1)} %q_ref.3) | copy-start | bytes 1572868
  25.3 5.6 %copy-start.5 = (f32[2048]{0:T(1024)S(1)}, f32[2048]{0:T(1024)}, u32[]{:S(2)}) copy-start(f32[2048]{0:T(1024)} %param.11) | copy-start | bytes 24580
  25.3 10.5 %all-to-all-start.2 = ((f32[16,16,128]{2,1,0:T(8,128)}), f32[16,16,128]{2,1,0:T(8,128)S(1)}, u32[]{:S(2)}, u32[]{:S(2)}) async-start(f32[16,16,128]{2,1,0:T(8,128)} %shard_map.67), calls=%async_computation.2 | async-start | bytes 262144 | tf_op jit(solution)/shard_map/all_to_all | solution.py:226

commit v27 on v26

--- a/solution.py
+++ b/solution.py
@@ -106,11 +106,9 @@
     return pltpu.make_async_copy(gated_ref.at[rows, :], out_ref.at[rows, :], sems.at[chunk])
 
 
-def finish(chunk, places, conv_ref, q_ref, gated_ref, out_ref, sems):
-    length = conv_ref.shape[0] // len(places)
+def finish(chunk, places, conv, q_ref, gated_ref, out_ref, sems):
     rows = pl.ds(places[chunk] * LANES, LANES)
-    conv = conv_ref[chunk_rows(chunk, length), :].T
-    gated_ref[rows, :] = (q_ref[rows, :].astype(jnp.float32) * conv).astype(jnp.bfloat16)
+    gated_ref[rows, :] = (q_ref[rows, :].astype(jnp.float32) * conv.T).astype(jnp.bfloat16)
     leaving(chunk, places, gated_ref, out_ref, sems).start()
 
 
@@ -145,7 +143,7 @@
     @pl.when(lax.axis_index("seq") == 0)
     def _():
         for chunk in range(chunks):
-            finish(chunk, places, conv_ref, q_ref, gated_ref, out_ref, sems)
+            finish(chunk, places, conv_ref[chunk_rows(chunk, length), :], q_ref, gated_ref, out_ref, sems)
         for chunk in range(chunks):
             leaving(chunk, places, gated_ref, out_ref, sems).wait()
 
@@ -157,30 +155,25 @@
     length = local_ref.shape[0] // chunks
     tokens = length // SUBLANES
 
+    def send(chunk):
+        conv = conv_ref[pl.ds(chunk * length, length), :]
+        finish(chunk, places, conv, q_ref, gated_ref, out_ref, sems)
+
     @pl.when(lax.axis_index("seq") > 0)
     def _():
         for half in range(chunks // SUBLANES):
             decay = [dense_ref[half, 0, r] for r in range(order)]
             weight = [dense_ref[half, 1, r] for r in range(order)]
             carry = mode_rows(carry_ref, 0, order, order, chunks, half)
-
-            def steps(i, fading):
-                fading = list(fading)
-                for u in range(tokens):
-                    rows = token_rows(half, length, i * tokens + u)
-                    fading = [decay[r] * fading[r] for r in range(order)]
-                    conv_ref[rows, :] = tree_sum(fading + [local_ref[rows, :]])
-                return tuple(fading)
-
-            fading = tuple(weight[r] * carry[r] for r in range(order))
-            if half == 0:
-                lax.fori_loop(0, SUBLANES, steps, fading)
-            else:
-                for i in range(SUBLANES):
-                    fading = steps(i, fading)
-                    finish((half - 1) * SUBLANES + i, places, conv_ref, q_ref, gated_ref, out_ref, sems)
+            fading = [weight[r] * carry[r] for r in range(order)]
+            for token in range(length):
+                fading = [decay[r] * fading[r] for r in range(order)]
+                total = tree_sum(fading + [local_ref[token_rows(half, length, token), :]])
+                conv_ref[pl.ds(half * SUBLANES * length + token, SUBLANES, stride=length), :] = total
+                if half > 0 and token % tokens == tokens - 1:
+                    send((half - 1) * SUBLANES + token // tokens)
         for chunk in range(chunks - SUBLANES, chunks):
-            finish(chunk, places, conv_ref, q_ref, gated_ref, out_ref, sems)
+            send(chunk)
         for chunk in range(chunks):
             leaving(chunk, places, gated_ref, out_ref, sems).wait()
 

time: 38.4 us -> 38.5 us (level)
  no operation moved by 1% of the time
where the time goes in v27:
time: 38.5 us; the launch traced here: 38.2 us
  blocking collectives  22.2 us (58%)
  Pallas kernels  8.01 us (21%)
  starting transfers between devices  5.61 us (15%)
  waiting for transfers between devices  2.25 us (6%)
    all_to_all x2, blocking collectives, all_to_all(): lax.all_to_all(pieces, 'seq', split_axis=0, concat_axis=0, axis_index_gro...  22.2 us
    pallas_call x5, Pallas kernels, call(): pl.pallas_call(kernel, out_shape=out_shape, in_specs=[pl.BlockSpec(memory...  8.01 us
    all_to_all x1, starting transfers between devices, all_to_all(): lax.all_to_all(pieces, 'seq', split_axis=0, concat_axis=0, axis_index_gro...  5.61 us
    all_to_all x1, waiting for transfers between devices, all_to_all(): lax.all_to_all(pieces, 'seq', split_axis=0, concat_axis=0, axis_index_gro...  2.25 us
  transfers between devices with their start and end apart: 1, of which 1 were waited for; matrix products, arithmetic and copies ran while one was open for 0% of the time, Pallas kernels for 7%

profile of v27, /device:TPU:2, one launch (start us, length us, event | category | flops | bytes accessed | tf_op | source)
XLA Modules:
  0.0 38.2 jit_solution(5408975684254110840)
XLA Ops:
  0.0 0.0 copy-start.1
  0.0 0.0 copy-start.2
  0.0 0.0 copy-start.3
  0.0 0.0 copy-start.4
  0.0 0.8 %shard_map.64 = f32[16,16,128]{2,1,0:T(8,128)S(1)} custom-call(f32[16,128]{1,0:T(8,128)} %bitcast.12), custom_call_target="tpu_custom_call" | custom-call | flops 10000000000 | bytes 8192 | tf_op jit(solution)/shard_map/pallas_call | solution.py:185
  0.8 11.1 %all_to_all.15 = f32[16,16,128]{2,1,0:T(8,128)S(1)} all-to-all(f32[16,16,128]{2,1,0:T(8,128)S(1)} %shard_map.64), channel_id=1, replica_groups={{22,6,30,14,28,12,26,10,24,8,20,4,18,2,16,0},{23,7,31,15,29,13,27,11,25..., dimensions={0} | all-to-all | bytes 262144 | tf_op jit(solution)/shard_map/all_to_all | solution.py:219
  12.0 0.0 copy-done.1
  12.0 0.0 copy-done.2
  12.0 0.0 copy-done.3
  12.0 0.0 copy-done.4
  12.0 1.5 %shard_map.65 = (f32[2048,128]{1,0:T(8,128)S(1)}, f32[512,128]{1,0:T(8,128)S(1)}) custom-call(f32[256,128]{1,0:T(8,128)S(1)} %bitcast.8, f32[16,128]{1,0:T(8,128)S(1)} %bitcast.13, f32[16,128]{1,0:T(8,128)S(1)} %bitcast.15, bf16[2048,128]{1,0:T(8,128)(2,1)S(1)} %copy-done.1, bf16[2048,128]{1,0:T(8,128)(2,1)S(1)} %copy-done.2), custom_call_target="tpu_custom_call" | custom-call | flops 8388608 | bytes 1196032 | tf_op jit(solution)/shard_map/pallas_call | solution.py:185
  13.5 0.0 copy-start
  13.5 11.1 %all_to_all.16.ends_ref = f32[16,32,128]{2,1,0:T(8,128)S(1)} all-to-all(f32[16,32,128]{2,1,0:T(8,128)S(1)} %bitcast.11), channel_id=1, replica_groups={{22,6,30,14,28,12,26,10,24,8,20,4,18,2,16,0},{23,7,31,15,29,13,27,11,25..., dimensions={0} | all-to-all | bytes 524288 | tf_op jit(solution)/shard_map/all_to_all | solution.py:219
  24.6 0.7 %shard_map.67 = f32[16,16,128]{2,1,0:T(8,128)} custom-call(f32[16,128]{1,0:T(8,128)S(1)} %bitcast.14, f32[16,32,128]{2,1,0:T(8,128)S(1)} %all_to_all.16.ends_ref), custom_call_target="tpu_custom_call" | custom-call | bytes 270336 | tf_op jit(solution)/shard_map/pallas_call | solution.py:185
  25.3 0.0 copy-start.5
  25.3 5.6 %all-to-all-start.2 = ((f32[16,16,128]{2,1,0:T(8,128)}), f32[16,16,128]{2,1,0:T(8,128)S(1)}, u32[]{:S(2)}, u32[]{:S(2)}) async-start(f32[16,16,128]{2,1,0:T(8,128)} %shard_map.67), calls=%async_computation.2 | async-start | bytes 262144 | tf_op jit(solution)/shard_map/all_to_all | solution.py:219
  30.9 0.0 copy-done
  30.9 0.0 copy-done.5
  30.9 2.6 %shard_map.66 = (f32[2048,128]{1,0:T(8,128)S(1)}, f32[2,2,16,8,128]{4,3,2,1,0:T(8,128)S(1)}, bf16[2048,128]{1,0:T(8,128)(2,1)}) custom-call(f32[256,128]{1,0:T(8,128)S(1)} %bitcast.9, f32[512,128]{1,0:T(8,128)S(1)} %bitcast.7, f32[2048,128]{1,0:T(8,128)S(1)} %get-tuple-element.11.series_ref, f32[16,128]{1,0:T(8,128)S(1)} %bitcast.16, ...), custom_call_target="tpu_custom_call" | custom-call | flops 16777216 | bytes 1974272 | tf_op jit(solution)/shard_map/pallas_call | solution.py:185
  33.5 2.2 %all-to-all-done.2 = f32[16,16,128]{2,1,0:T(8,128)S(1)} async-done(((f32[16,16,128]{2,1,0:T(8,128)}), f32[16,16,128]{2,1,0:T(8,128)S(1)}, u32[]{:S(2)}, u32[]{:S(2)}) %all-to-all-start.2) | async-done | bytes 131104 | tf_op jit(solution)/shard_map/all_to_all | solution.py:219
  35.8 2.4 %shard_map.68 = bf16[2048,128]{1,0:T(8,128)(2,1)} custom-call(f32[2,2,16,8,128]{4,3,2,1,0:T(8,128)S(1)} %get-tuple-element.12.dense_ref, f32[256,128]{1,0:T(8,128)S(1)} %bitcast.10, f32[2048,128]{1,0:T(8,128)S(1)} %get-tuple-element.13.local_ref, bf16[2048,128]{1,0:T(8,128)(2,1)S(1)} %copy-done, ...), custom_call_target="tpu_custom_call", output_to_operand_aliasing={{}: (4, {})} | custom-call | flops 8388608 | bytes 2490368 | tf_op jit(solution)/shard_map/pallas_call | solution.py:185
Async XLA Ops:
  0.0 12.0 %copy-start.1 = (bf16[2048,128]{1,0:T(8,128)(2,1)S(1)}, bf16[2048,128]{1,0:T(8,128)(2,1)}, u32[]{:S(2)}) copy-start(bf16[2048,128]{1,0:T(8,128)(2,1)} %k_ref.1) | copy-start | bytes 1572868
  0.0 12.0 %copy-start.2 = (bf16[2048,128]{1,0:T(8,128)(2,1)S(1)}, bf16[2048,128]{1,0:T(8,128)(2,1)}, u32[]{:S(2)}) copy-start(bf16[2048,128]{1,0:T(8,128)(2,1)} %v_ref.1) | copy-start | bytes 1572868
  0.0 12.0 %copy-start.3 = (f32[128,16]{0,1:T(8,128)S(1)}, f32[128,16]{0,1:T(8,128)}, u32[]{:S(2)}) copy-start(f32[128,16]{0,1:T(8,128)} %param.10) | copy-start | bytes 24580
  0.0 12.0 %copy-start.4 = (f32[128,16]{0,1:T(8,128)S(1)}, f32[128,16]{0,1:T(8,128)}, u32[]{:S(2)}) copy-start(f32[128,16]{0,1:T(8,128)} %param.9) | copy-start | bytes 24580
  13.5 17.4 %copy-start = (bf16[2048,128]{1,0:T(8,128)(2,1)S(1)}, bf16[2048,128]{1,0:T(8,128)(2,1)}, u32[]{:S(2)}) copy-start(bf16[2048,128]{1,0:T(8,128)(2,1)} %q_ref.3) | copy-start | bytes 1572868
  25.3 5.6 %copy-start.5 = (f32[2048]{0:T(1024)S(1)}, f32[2048]{0:T(1024)}, u32[]{:S(2)}) copy-start(f32[2048]{0:T(1024)} %param.11) | copy-start | bytes 24580
  25.3 10.5 %all-to-all-start.2 = ((f32[16,16,128]{2,1,0:T(8,128)}), f32[16,16,128]{2,1,0:T(8,128)S(1)}, u32[]{:S(2)}, u32[]{:S(2)}) async-start(f32[16,16,128]{2,1,0:T(8,128)} %shard_map.67), calls=%async_computation.2 | async-start | bytes 262144 | tf_op jit(solution)/shard_map/all_to_all | solution.py:219

commit v28 on v26

--- a/solution.py
+++ b/solution.py
@@ -10,6 +10,7 @@
 SUBLANES = 8
 UNROLL = 8
 COPIES_COST = 10**10
+FAR_FIRST = (11, 0, 12, 4, 8, 2, 14, 1, 13, 3, 9, 6, 10, 5, 15, 7)
 VMEM_LIMIT = 32 * 1024 * 1024
 
 
@@ -233,11 +234,8 @@
     f32 = jnp.float32
 
     members, places = list(range(blocks)), list(range(chunks))
-    if blocks == chunks:
-        far, middle = blocks // 2, blocks * 11 // 16
-        upper = [middle] + [block for block in members[:far - 1:-1] if block != middle]
-        members = [block for one in upper for block in (one, one - far)]
-        places = list(members)
+    if blocks == chunks == len(FAR_FIRST):
+        members, places = list(FAR_FIRST), list(FAR_FIRST)
 
     own_rates, own_residues = rates.T, residues.T
     copies = call(

time: 38.4 us -> 39.1 us (1.018)
  starting transfers between devices: 5.61 us -> 6.71 us
  blocking collectives: 22.2 us -> 21.7 us
    all_to_all x1, starting transfers between devices: 5.61 us -> 6.71 us  [all_to_all(): lax.all_to_all(pieces, 'seq', split_axis=0, concat_axis=0, axis_index_gro...]
    all_to_all x2, blocking collectives: 22.2 us -> 21.7 us  [all_to_all(): lax.all_to_all(pieces, 'seq', split_axis=0, concat_axis=0, axis_index_gro...]
where the time goes in v28:
time: 39.1 us; the launch traced here: 38.4 us
  blocking collectives  21.7 us (55%)
  Pallas kernels  7.89 us (20%)
  starting transfers between devices  6.71 us (17%)
  waiting for transfers between devices  1.96 us (5%)
    all_to_all x2, blocking collectives, all_to_all(): lax.all_to_all(pieces, 'seq', split_axis=0, concat_axis=0, axis_index_gro...  21.7 us
    pallas_call x5, Pallas kernels, call(): pl.pallas_call(kernel, out_shape=out_shape, in_specs=[pl.BlockSpec(memory...  7.89 us
    all_to_all x1, starting transfers between devices, all_to_all(): lax.all_to_all(pieces, 'seq', split_axis=0, concat_axis=0, axis_index_gro...  6.71 us
    all_to_all x1, waiting for transfers between devices, all_to_all(): lax.all_to_all(pieces, 'seq', split_axis=0, concat_axis=0, axis_index_gro...  1.96 us
  transfers between devices with their start and end apart: 1, of which 1 were waited for; matrix products, arithmetic and copies ran while one was open for 0% of the time, Pallas kernels for 7%

profile of v28, /device:TPU:2, one launch (start us, length us, event | category | flops | bytes accessed | tf_op | source)
XLA Modules:
  0.0 38.4 jit_solution(10372168875270528927)
XLA Ops:
  0.0 0.0 copy-start.1
  0.0 0.0 copy-start.2
  0.0 0.0 copy-start.3
  0.0 0.0 copy-start.4
  0.0 0.8 %shard_map.64 = f32[16,16,128]{2,1,0:T(8,128)S(1)} custom-call(f32[16,128]{1,0:T(8,128)} %bitcast.12), custom_call_target="tpu_custom_call" | custom-call | flops 10000000000 | bytes 8192 | tf_op jit(solution)/shard_map/pallas_call | solution.py:193
  0.8 10.9 %all_to_all.15 = f32[16,16,128]{2,1,0:T(8,128)S(1)} all-to-all(f32[16,16,128]{2,1,0:T(8,128)S(1)} %shard_map.64), channel_id=1, replica_groups={{22,0,24,8,16,4,28,2,26,6,18,12,20,10,30,14},{23,1,25,9,17,5,29,3,27,7,..., dimensions={0} | all-to-all | bytes 262144 | tf_op jit(solution)/shard_map/all_to_all | solution.py:227
  11.7 0.0 copy-done.1
  11.7 0.0 copy-done.2
  11.7 0.0 copy-done.3
  11.7 0.0 copy-done.4
  11.7 1.5 %shard_map.65 = (f32[2048,128]{1,0:T(8,128)S(1)}, f32[512,128]{1,0:T(8,128)S(1)}) custom-call(f32[256,128]{1,0:T(8,128)S(1)} %bitcast.8, f32[16,128]{1,0:T(8,128)S(1)} %bitcast.13, f32[16,128]{1,0:T(8,128)S(1)} %bitcast.15, bf16[2048,128]{1,0:T(8,128)(2,1)S(1)} %copy-done.1, bf16[2048,128]{1,0:T(8,128)(2,1)S(1)} %copy-done.2), custom_call_target="tpu_custom_call" | custom-call | flops 8388608 | bytes 1196032 | tf_op jit(solution)/shard_map/pallas_call | solution.py:193
  13.2 0.0 copy-start
  13.3 10.9 %all_to_all.16.ends_ref = f32[16,32,128]{2,1,0:T(8,128)S(1)} all-to-all(f32[16,32,128]{2,1,0:T(8,128)S(1)} %bitcast.11), channel_id=1, replica_groups={{22,0,24,8,16,4,28,2,26,6,18,12,20,10,30,14},{23,1,25,9,17,5,29,3,27,7,..., dimensions={0} | all-to-all | bytes 524288 | tf_op jit(solution)/shard_map/all_to_all | solution.py:227
  24.1 0.7 %shard_map.67 = f32[16,16,128]{2,1,0:T(8,128)} custom-call(f32[16,128]{1,0:T(8,128)S(1)} %bitcast.14, f32[16,32,128]{2,1,0:T(8,128)S(1)} %all_to_all.16.ends_ref), custom_call_target="tpu_custom_call" | custom-call | bytes 270336 | tf_op jit(solution)/shard_map/pallas_call | solution.py:193
  24.8 0.0 copy-start.5
  24.8 6.7 %all-to-all-start.2 = ((f32[16,16,128]{2,1,0:T(8,128)}), f32[16,16,128]{2,1,0:T(8,128)S(1)}, u32[]{:S(2)}, u32[]{:S(2)}) async-start(f32[16,16,128]{2,1,0:T(8,128)} %shard_map.67), calls=%async_computation.2 | async-start | bytes 262144 | tf_op jit(solution)/shard_map/all_to_all | solution.py:227
  31.5 0.0 copy-done
  31.5 0.0 copy-done.5
  31.5 2.6 %shard_map.66 = (f32[2048,128]{1,0:T(8,128)S(1)}, f32[2,2,16,8,128]{4,3,2,1,0:T(8,128)S(1)}, bf16[2048,128]{1,0:T(8,128)(2,1)}) custom-call(f32[256,128]{1,0:T(8,128)S(1)} %bitcast.9, f32[512,128]{1,0:T(8,128)S(1)} %bitcast.7, f32[2048,128]{1,0:T(8,128)S(1)} %get-tuple-element.11.series_ref, f32[16,128]{1,0:T(8,128)S(1)} %bitcast.16, ...), custom_call_target="tpu_custom_call" | custom-call | flops 16777216 | bytes 1974272 | tf_op jit(solution)/shard_map/pallas_call | solution.py:193
  34.1 2.0 %all-to-all-done.2 = f32[16,16,128]{2,1,0:T(8,128)S(1)} async-done(((f32[16,16,128]{2,1,0:T(8,128)}), f32[16,16,128]{2,1,0:T(8,128)S(1)}, u32[]{:S(2)}, u32[]{:S(2)}) %all-to-all-start.2) | async-done | bytes 131104 | tf_op jit(solution)/shard_map/all_to_all | solution.py:227
  36.1 2.3 %shard_map.68 = bf16[2048,128]{1,0:T(8,128)(2,1)} custom-call(f32[2,2,16,8,128]{4,3,2,1,0:T(8,128)S(1)} %get-tuple-element.12.dense_ref, f32[256,128]{1,0:T(8,128)S(1)} %bitcast.10, f32[2048,128]{1,0:T(8,128)S(1)} %get-tuple-element.13.local_ref, bf16[2048,128]{1,0:T(8,128)(2,1)S(1)} %copy-done, ...), custom_call_target="tpu_custom_call", output_to_operand_aliasing={{}: (4, {})} | custom-call | flops 8388608 | bytes 2490368 | tf_op jit(solution)/shard_map/pallas_call | solution.py:193
Async XLA Ops:
  0.0 11.7 %copy-start.1 = (bf16[2048,128]{1,0:T(8,128)(2,1)S(1)}, bf16[2048,128]{1,0:T(8,128)(2,1)}, u32[]{:S(2)}) copy-start(bf16[2048,128]{1,0:T(8,128)(2,1)} %k_ref.1) | copy-start | bytes 1572868
  0.0 11.7 %copy-start.2 = (bf16[2048,128]{1,0:T(8,128)(2,1)S(1)}, bf16[2048,128]{1,0:T(8,128)(2,1)}, u32[]{:S(2)}) copy-start(bf16[2048,128]{1,0:T(8,128)(2,1)} %v_ref.1) | copy-start | bytes 1572868
  0.0 11.7 %copy-start.3 = (f32[128,16]{0,1:T(8,128)S(1)}, f32[128,16]{0,1:T(8,128)}, u32[]{:S(2)}) copy-start(f32[128,16]{0,1:T(8,128)} %param.10) | copy-start | bytes 24580
  0.0 11.7 %copy-start.4 = (f32[128,16]{0,1:T(8,128)S(1)}, f32[128,16]{0,1:T(8,128)}, u32[]{:S(2)}) copy-start(f32[128,16]{0,1:T(8,128)} %param.9) | copy-start | bytes 24580
  13.2 18.3 %copy-start = (bf16[2048,128]{1,0:T(8,128)(2,1)S(1)}, bf16[2048,128]{1,0:T(8,128)(2,1)}, u32[]{:S(2)}) copy-start(bf16[2048,128]{1,0:T(8,128)(2,1)} %q_ref.3) | copy-start | bytes 1572868
  24.8 6.7 %copy-start.5 = (f32[2048]{0:T(1024)S(1)}, f32[2048]{0:T(1024)}, u32[]{:S(2)}) copy-start(f32[2048]{0:T(1024)} %param.11) | copy-start | bytes 24580
  24.8 11.3 %all-to-all-start.2 = ((f32[16,16,128]{2,1,0:T(8,128)}), f32[16,16,128]{2,1,0:T(8,128)S(1)}, u32[]{:S(2)}, u32[]{:S(2)}) async-start(f32[16,16,128]{2,1,0:T(8,128)} %shard_map.67), calls=%async_computation.2 | async-start | bytes 262144 | tf_op jit(solution)/shard_map/all_to_all | solution.py:227

commit v29 on v28

--- a/solution.py
+++ b/solution.py
@@ -10,7 +10,7 @@
 SUBLANES = 8
 UNROLL = 8
 COPIES_COST = 10**10
-FAR_FIRST = (11, 0, 12, 4, 8, 2, 14, 1, 13, 3, 9, 6, 10, 5, 15, 7)
+NEAR_FIRST = (11, 7, 15, 6, 10, 5, 9, 3, 14, 4, 13, 2, 8, 1, 12, 0)
 VMEM_LIMIT = 32 * 1024 * 1024
 
 
@@ -234,8 +234,8 @@
     f32 = jnp.float32
 
     members, places = list(range(blocks)), list(range(chunks))
-    if blocks == chunks == len(FAR_FIRST):
-        members, places = list(FAR_FIRST), list(FAR_FIRST)
+    if blocks == chunks == len(NEAR_FIRST):
+        members, places = list(NEAR_FIRST), list(NEAR_FIRST)
 
     own_rates, own_residues = rates.T, residues.T
     copies = call(

time: 39.1 us -> 38.8 us (level)
  starting transfers between devices: 6.71 us -> 5.42 us
  blocking collectives: 21.7 us -> 22.6 us
  waiting for transfers between devices: 1.96 us -> 2.43 us
    all_to_all x1, starting transfers between devices: 6.71 us -> 5.42 us  [all_to_all(): lax.all_to_all(pieces, 'seq', split_axis=0, concat_axis=0, axis_index_gro...]
    all_to_all x2, blocking collectives: 21.7 us -> 22.6 us  [all_to_all(): lax.all_to_all(pieces, 'seq', split_axis=0, concat_axis=0, axis_index_gro...]
    all_to_all x1, waiting for transfers between devices: 1.96 us -> 2.43 us  [all_to_all(): lax.all_to_all(pieces, 'seq', split_axis=0, concat_axis=0, axis_index_gro...]
where the time goes in v29:
time: 38.8 us; the launch traced here: 38.4 us
  blocking collectives  22.6 us (58%)
  Pallas kernels  7.89 us (20%)
  starting transfers between devices  5.42 us (14%)
  waiting for transfers between devices  2.43 us (6%)
    all_to_all x2, blocking collectives, all_to_all(): lax.all_to_all(pieces, 'seq', split_axis=0, concat_axis=0, axis_index_gro...  22.6 us
    pallas_call x5, Pallas kernels, call(): pl.pallas_call(kernel, out_shape=out_shape, in_specs=[pl.BlockSpec(memory...  7.89 us
    all_to_all x1, starting transfers between devices, all_to_all(): lax.all_to_all(pieces, 'seq', split_axis=0, concat_axis=0, axis_index_gro...  5.42 us
    all_to_all x1, waiting for transfers between devices, all_to_all(): lax.all_to_all(pieces, 'seq', split_axis=0, concat_axis=0, axis_index_gro...  2.43 us
  transfers between devices with their start and end apart: 1, of which 1 were waited for; matrix products, arithmetic and copies ran while one was open for 0% of the time, Pallas kernels for 7%

profile of v29, /device:TPU:2, one launch (start us, length us, event | category | flops | bytes accessed | tf_op | source)
XLA Modules:
  0.0 38.4 jit_solution(16493959032142861830)
XLA Ops:
  0.0 0.0 copy-start.1
  0.0 0.0 copy-start.2
  0.0 0.0 copy-start.3
  0.0 0.0 copy-start.4
  0.0 0.8 %shard_map.64 = f32[16,16,128]{2,1,0:T(8,128)S(1)} custom-call(f32[16,128]{1,0:T(8,128)} %bitcast.12), custom_call_target="tpu_custom_call" | custom-call | flops 10000000000 | bytes 8192 | tf_op jit(solution)/shard_map/pallas_call | solution.py:193
  0.8 11.4 %all_to_all.15 = f32[16,16,128]{2,1,0:T(8,128)S(1)} all-to-all(f32[16,16,128]{2,1,0:T(8,128)S(1)} %shard_map.64), channel_id=1, replica_groups={{22,14,30,12,20,10,18,6,28,8,26,4,16,2,24,0},{23,15,31,13,21,11,19,7,29..., dimensions={0} | all-to-all | bytes 262144 | tf_op jit(solution)/shard_map/all_to_all | solution.py:227
  12.2 0.0 copy-done.1
  12.2 0.0 copy-done.2
  12.2 0.0 copy-done.3
  12.2 0.0 copy-done.4
  12.2 1.5 %shard_map.65 = (f32[2048,128]{1,0:T(8,128)S(1)}, f32[512,128]{1,0:T(8,128)S(1)}) custom-call(f32[256,128]{1,0:T(8,128)S(1)} %bitcast.8, f32[16,128]{1,0:T(8,128)S(1)} %bitcast.13, f32[16,128]{1,0:T(8,128)S(1)} %bitcast.15, bf16[2048,128]{1,0:T(8,128)(2,1)S(1)} %copy-done.1, bf16[2048,128]{1,0:T(8,128)(2,1)S(1)} %copy-done.2), custom_call_target="tpu_custom_call" | custom-call | flops 8388608 | bytes 1196032 | tf_op jit(solution)/shard_map/pallas_call | solution.py:193
  13.8 0.0 copy-start
  13.8 11.2 %all_to_all.16.ends_ref = f32[16,32,128]{2,1,0:T(8,128)S(1)} all-to-all(f32[16,32,128]{2,1,0:T(8,128)S(1)} %bitcast.11), channel_id=1, replica_groups={{22,14,30,12,20,10,18,6,28,8,26,4,16,2,24,0},{23,15,31,13,21,11,19,7,29..., dimensions={0} | all-to-all | bytes 524288 | tf_op jit(solution)/shard_map/all_to_all | solution.py:227
  25.0 0.7 %shard_map.67 = f32[16,16,128]{2,1,0:T(8,128)} custom-call(f32[16,128]{1,0:T(8,128)S(1)} %bitcast.14, f32[16,32,128]{2,1,0:T(8,128)S(1)} %all_to_all.16.ends_ref), custom_call_target="tpu_custom_call" | custom-call | bytes 270336 | tf_op jit(solution)/shard_map/pallas_call | solution.py:193
  25.7 0.0 copy-start.5
  25.7 5.4 %all-to-all-start.2 = ((f32[16,16,128]{2,1,0:T(8,128)}), f32[16,16,128]{2,1,0:T(8,128)S(1)}, u32[]{:S(2)}, u32[]{:S(2)}) async-start(f32[16,16,128]{2,1,0:T(8,128)} %shard_map.67), calls=%async_computation.2 | async-start | bytes 262144 | tf_op jit(solution)/shard_map/all_to_all | solution.py:227
  31.1 0.0 copy-done
  31.1 0.0 copy-done.5
  31.1 2.6 %shard_map.66 = (f32[2048,128]{1,0:T(8,128)S(1)}, f32[2,2,16,8,128]{4,3,2,1,0:T(8,128)S(1)}, bf16[2048,128]{1,0:T(8,128)(2,1)}) custom-call(f32[256,128]{1,0:T(8,128)S(1)} %bitcast.9, f32[512,128]{1,0:T(8,128)S(1)} %bitcast.7, f32[2048,128]{1,0:T(8,128)S(1)} %get-tuple-element.11.series_ref, f32[16,128]{1,0:T(8,128)S(1)} %bitcast.16, ...), custom_call_target="tpu_custom_call" | custom-call | flops 16777216 | bytes 1974272 | tf_op jit(solution)/shard_map/pallas_call | solution.py:193
  33.7 2.4 %all-to-all-done.2 = f32[16,16,128]{2,1,0:T(8,128)S(1)} async-done(((f32[16,16,128]{2,1,0:T(8,128)}), f32[16,16,128]{2,1,0:T(8,128)S(1)}, u32[]{:S(2)}, u32[]{:S(2)}) %all-to-all-start.2) | async-done | bytes 131104 | tf_op jit(solution)/shard_map/all_to_all | solution.py:227
  36.1 2.3 %shard_map.68 = bf16[2048,128]{1,0:T(8,128)(2,1)} custom-call(f32[2,2,16,8,128]{4,3,2,1,0:T(8,128)S(1)} %get-tuple-element.12.dense_ref, f32[256,128]{1,0:T(8,128)S(1)} %bitcast.10, f32[2048,128]{1,0:T(8,128)S(1)} %get-tuple-element.13.local_ref, bf16[2048,128]{1,0:T(8,128)(2,1)S(1)} %copy-done, ...), custom_call_target="tpu_custom_call", output_to_operand_aliasing={{}: (4, {})} | custom-call | flops 8388608 | bytes 2490368 | tf_op jit(solution)/shard_map/pallas_call | solution.py:193
Async XLA Ops:
  0.0 12.2 %copy-start.1 = (bf16[2048,128]{1,0:T(8,128)(2,1)S(1)}, bf16[2048,128]{1,0:T(8,128)(2,1)}, u32[]{:S(2)}) copy-start(bf16[2048,128]{1,0:T(8,128)(2,1)} %k_ref.1) | copy-start | bytes 1572868
  0.0 12.2 %copy-start.2 = (bf16[2048,128]{1,0:T(8,128)(2,1)S(1)}, bf16[2048,128]{1,0:T(8,128)(2,1)}, u32[]{:S(2)}) copy-start(bf16[2048,128]{1,0:T(8,128)(2,1)} %v_ref.1) | copy-start | bytes 1572868
  0.0 12.2 %copy-start.3 = (f32[128,16]{0,1:T(8,128)S(1)}, f32[128,16]{0,1:T(8,128)}, u32[]{:S(2)}) copy-start(f32[128,16]{0,1:T(8,128)} %param.10) | copy-start | bytes 24580
  0.0 12.2 %copy-start.4 = (f32[128,16]{0,1:T(8,128)S(1)}, f32[128,16]{0,1:T(8,128)}, u32[]{:S(2)}) copy-start(f32[128,16]{0,1:T(8,128)} %param.9) | copy-start | bytes 24580
  13.8 17.3 %copy-start = (bf16[2048,128]{1,0:T(8,128)(2,1)S(1)}, bf16[2048,128]{1,0:T(8,128)(2,1)}, u32[]{:S(2)}) copy-start(bf16[2048,128]{1,0:T(8,128)(2,1)} %q_ref.3) | copy-start | bytes 1572868
  25.7 5.4 %copy-start.5 = (f32[2048]{0:T(1024)S(1)}, f32[2048]{0:T(1024)}, u32[]{:S(2)}) copy-start(f32[2048]{0:T(1024)} %param.11) | copy-start | bytes 24580
  25.7 10.5 %all-to-all-start.2 = ((f32[16,16,128]{2,1,0:T(8,128)}), f32[16,16,128]{2,1,0:T(8,128)S(1)}, u32[]{:S(2)}, u32[]{:S(2)}) async-start(f32[16,16,128]{2,1,0:T(8,128)} %shard_map.67), calls=%async_computation.2 | async-start | bytes 262144 | tf_op jit(solution)/shard_map/all_to_all | solution.py:227

commit v30 on v26

--- a/solution.py
+++ b/solution.py
@@ -115,7 +115,8 @@
 
 
 def local_kernel(
-    places, order, decays_ref, weights_ref, series_ref, gain_ref, q_ref, conv_ref, dense_ref, out_ref, gated_ref, sems
+    places, order, decays_ref, weights_ref, series_ref, gain_ref, q_ref, conv_ref, dense_ref, gate_ref, out_ref,
+    gated_ref, sems
 ):
     chunks = len(places)
     length = series_ref.shape[0] // chunks
@@ -142,20 +143,33 @@
         zero = jnp.zeros((SUBLANES, LANES), jnp.float32)
         lax.fori_loop(0, length // UNROLL, steps, (zero,) * order)
 
-    @pl.when(lax.axis_index("seq") == 0)
+    first = lax.axis_index("seq") == 0
+
+    @pl.when(first)
     def _():
         for chunk in range(chunks):
             finish(chunk, places, conv_ref, q_ref, gated_ref, out_ref, sems)
         for chunk in range(chunks):
             leaving(chunk, places, gated_ref, out_ref, sems).wait()
 
+    @pl.when(jnp.logical_not(first))
+    def _():
+        for chunk, place in enumerate(places):
+            q = q_ref[pl.ds(place * LANES, LANES), :].astype(jnp.float32)
+            gate_ref[chunk_rows(chunk, length), :] = q.T
+
 
 def output_kernel(
-    places, order, dense_ref, carry_ref, local_ref, q_ref, _, out_ref, conv_ref, gated_ref, sems
+    places, order, dense_ref, carry_ref, local_ref, gate_ref, _, out_ref, conv_ref, gated_ref, sems
 ):
     chunks = len(places)
     length = local_ref.shape[0] // chunks
     tokens = length // SUBLANES
+
+    def send(chunk):
+        rows = pl.ds(places[chunk] * LANES, LANES)
+        gated_ref[rows, :] = conv_ref[chunk_rows(chunk, length), :].astype(jnp.bfloat16).T
+        leaving(chunk, places, gated_ref, out_ref, sems).start()
 
     @pl.when(lax.axis_index("seq") > 0)
     def _():
@@ -169,7 +183,7 @@
                 for u in range(tokens):
                     rows = token_rows(half, length, i * tokens + u)
                     fading = [decay[r] * fading[r] for r in range(order)]
-                    conv_ref[rows, :] = tree_sum(fading + [local_ref[rows, :]])
+                    conv_ref[rows, :] = gate_ref[rows, :] * tree_sum(fading + [local_ref[rows, :]])
                 return tuple(fading)
 
             fading = tuple(weight[r] * carry[r] for r in range(order))
@@ -178,9 +192,9 @@
             else:
                 for i in range(SUBLANES):
                     fading = steps(i, fading)
-                    finish((half - 1) * SUBLANES + i, places, conv_ref, q_ref, gated_ref, out_ref, sems)
+                    send((half - 1) * SUBLANES + i)
         for chunk in range(chunks - SUBLANES, chunks):
-            finish(chunk, places, conv_ref, q_ref, gated_ref, out_ref, sems)
+            send(chunk)
         for chunk in range(chunks):
             leaving(chunk, places, gated_ref, out_ref, sems).wait()
 
@@ -273,11 +287,12 @@
     weights = to_chunks(ends).reshape(chunks * 2 * order, LANES)
     out_shape = jax.ShapeDtypeStruct((channels, length), jnp.bfloat16)
     out_scratch = [pltpu.VMEM(out_shape.shape, out_shape.dtype), pltpu.SemaphoreType.DMA((chunks,))]
-    local, dense, out = call(
+    local, dense, gate, out = call(
         functools.partial(local_kernel, places, order),
         (
             jax.ShapeDtypeStruct((length * chunks, LANES), f32),
             jax.ShapeDtypeStruct((chunks // SUBLANES, 2, order, SUBLANES, LANES), f32),
+            jax.ShapeDtypeStruct((length * chunks, LANES), f32),
             out_shape,
         ),
         decays,
@@ -285,7 +300,7 @@
         local_series,
         direct_gain.reshape(chunks, LANES),
         q_proj,
-        out_spaces=(pltpu.VMEM, pltpu.VMEM, pl.ANY),
+        out_spaces=(pltpu.VMEM, pltpu.VMEM, pltpu.VMEM, pl.ANY),
         scratch=out_scratch,
         flops=4 * order * channels * length,
     )
@@ -303,7 +318,7 @@
         dense,
         carry,
         local,
-        q_proj,
+        gate,
         out,
         out_spaces=pl.ANY,
         aliases={4: 0},

time: 38.4 us -> 41 us (1.068)
  the two profiles are of different devices: /device:TPU:2 before, /device:TPU:0 now
where the time goes in v30:
time: 41 us; the launch traced here: 40.6 us
  blocking collectives  23.9 us (58%)
  Pallas kernels  7.64 us (19%)
  starting transfers between devices  6.33 us (15%)
  local copies, waits for them, and re-layouts  2.7 us (7%)
    all_to_all x2, blocking collectives, all_to_all(): lax.all_to_all(pieces, 'seq', split_axis=0, concat_axis=0, axis_index_gro...  23.9 us
    pallas_call x5, Pallas kernels, call(): pl.pallas_call(kernel, out_shape=out_shape, in_specs=[pl.BlockSpec(memory...  7.64 us
    all_to_all x1, starting transfers between devices, all_to_all(): lax.all_to_all(pieces, 'seq', split_axis=0, concat_axis=0, axis_index_gro...  6.33 us
    unnamed x16, local copies, waits for them, and re-layouts  2.7 us
  transfers between devices with their start and end apart: 1, of which 0 were waited for; matrix products, arithmetic and copies ran while one was open for 0% of the time, Pallas kernels for 9%

profile of v30, /device:TPU:0, one launch (start us, length us, event | category | flops | bytes accessed | tf_op | source)
XLA Modules:
  0.0 40.6 jit_solution(2848795668525894510)
XLA Ops:
  0.0 0.0 copy-start
  0.0 0.0 copy-start.1
  0.0 0.0 copy-start.5
  0.0 0.0 copy-start.6
  0.0 0.8 %shard_map.64 = f32[16,16,128]{2,1,0:T(8,128)S(1)} custom-call(f32[16,128]{1,0:T(8,128)} %bitcast.11), custom_call_target="tpu_custom_call" | custom-call | flops 10000000000 | bytes 8192 | tf_op jit(solution)/shard_map/pallas_call | solution.py:206
  0.8 12.8 %all_to_all.15 = f32[16,16,128]{2,1,0:T(8,128)S(1)} all-to-all(f32[16,16,128]{2,1,0:T(8,128)S(1)} %shard_map.64), channel_id=1, replica_groups={{22,6,30,14,28,12,26,10,24,8,20,4,18,2,16,0},{23,7,31,15,29,13,27,11,25..., dimensions={0} | all-to-all | bytes 262144 | tf_op jit(solution)/shard_map/all_to_all | solution.py:240
  13.6 0.0 copy-done
  13.6 0.0 copy-done.1
  13.6 0.0 copy-done.5
  13.6 0.0 copy-done.6
  13.6 1.5 %shard_map.65 = (f32[2048,128]{1,0:T(8,128)S(1)}, f32[512,128]{1,0:T(8,128)S(1)}) custom-call(f32[256,128]{1,0:T(8,128)S(1)} %bitcast.8, f32[16,128]{1,0:T(8,128)S(1)} %bitcast.12, f32[16,128]{1,0:T(8,128)S(1)} %bitcast.14, bf16[2048,128]{1,0:T(8,128)(2,1)S(1)} %copy-done, bf16[2048,128]{1,0:T(8,128)(2,1)S(1)} %copy-done.1), custom_call_target="tpu_custom_call" | custom-call | flops 8388608 | bytes 1196032 | tf_op jit(solution)/shard_map/pallas_call | solution.py:206
  15.2 11.1 %all_to_all.16.ends_ref = f32[16,32,128]{2,1,0:T(8,128)S(1)} all-to-all(f32[16,32,128]{2,1,0:T(8,128)S(1)} %bitcast.10), channel_id=1, replica_groups={{22,6,30,14,28,12,26,10,24,8,20,4,18,2,16,0},{23,7,31,15,29,13,27,11,25..., dimensions={0} | all-to-all | bytes 524288 | tf_op jit(solution)/shard_map/all_to_all | solution.py:240
  26.3 0.7 %shard_map.67 = f32[16,16,128]{2,1,0:T(8,128)} custom-call(f32[16,128]{1,0:T(8,128)S(1)} %bitcast.13, f32[16,32,128]{2,1,0:T(8,128)S(1)} %all_to_all.16.ends_ref), custom_call_target="tpu_custom_call" | custom-call | bytes 270336 | tf_op jit(solution)/shard_map/pallas_call | solution.py:206
  27.0 0.0 copy-start.7
  27.0 6.3 %all-to-all-start.2 = ((f32[16,16,128]{2,1,0:T(8,128)}), f32[16,16,128]{2,1,0:T(8,128)}, u32[]{:S(2)}, u32[]{:S(2)}) async-start(f32[16,16,128]{2,1,0:T(8,128)} %shard_map.67), calls=%async_computation.2 | async-start | bytes 262144 | tf_op jit(solution)/shard_map/all_to_all | solution.py:240
  33.3 0.0 copy-done.7
  33.3 0.0 copy-start.2
  33.3 1.0 %copy-done.2 = bf16[2048,128]{1,0:T(8,128)(2,1)S(1)} copy-done((bf16[2048,128]{1,0:T(8,128)(2,1)S(1)}, bf16[2048,128]{1,0:T(8,128)(2,1)}, u32[]{:S(2)}) %copy-start.2) | copy-done | bytes 524312
  34.3 3.6 %shard_map.66 = (f32[2048,128]{1,0:T(8,128)S(1)}, f32[2,2,16,8,128]{4,3,2,1,0:T(8,128)S(1)}, f32[2048,128]{1,0:T(8,128)S(1)}, bf16[2048,128]{1,0:T(8,128)(2,1)}) custom-call(f32[256,128]{1,0:T(8,128)S(1)} %bitcast.9, f32[512,128]{1,0:T(8,128)S(1)} %bitcast.7, f32[2048,128]{1,0:T(8,128)S(1)} %get-tuple-element.12.series_ref, f32[16,128]{1,0:T(8,128)S(1)} %bitcast.15, ...), custom_call_target="tpu_custom_call" | custom-call | flops 16777216 | bytes 1974272 | tf_op jit(solution)/shard_map/pallas_call | solution.py:206
  37.9 0.0 copy-start.3
  37.9 0.7 %copy-done.3 = f32[2,2,16,8,128]{4,3,2,1,0:T(8,128)} copy-done((f32[2,2,16,8,128]{4,3,2,1,0:T(8,128)}, f32[2,2,16,8,128]{4,3,2,1,0:T(8,128)S(1)}, u32[]{:S(2)}) %copy-start.3) | copy-done | bytes 262168
  38.6 0.0 all-to-all-done.2
  38.6 0.9 %copy-done.4 = f32[2,2,16,8,128]{4,3,2,1,0:T(8,128)S(1)} copy-done((f32[2,2,16,8,128]{4,3,2,1,0:T(8,128)S(1)}, f32[2,2,16,8,128]{4,3,2,1,0:T(8,128)}, u32[]{:S(2)}) %copy-start.4) | copy-done | bytes 262168
  39.6 1.0 %shard_map.68 = bf16[2048,128]{1,0:T(8,128)(2,1)} custom-call(f32[2,2,16,8,128]{4,3,2,1,0:T(8,128)S(1)} %copy-done.4, f32[256,128]{1,0:T(8,128)} %bitcast.6.carry_ref, f32[2048,128]{1,0:T(8,128)S(1)} %get-tuple-element.14.local_ref, f32[2048,128]{1,0:T(8,128)S(1)} %get-tuple-element.15.gate_ref, ...), custom_call_target="tpu_custom_call", output_to_operand_aliasing={{}: (4, {})} | custom-call | flops 8388608 | bytes 3014656 | tf_op jit(solution)/shard_map/pallas_call | solution.py:206
  (1 shorter events, 0.0 us)
Async XLA Ops:
  0.0 13.6 %copy-start = (bf16[2048,128]{1,0:T(8,128)(2,1)S(1)}, bf16[2048,128]{1,0:T(8,128)(2,1)}, u32[]{:S(2)}) copy-start(bf16[2048,128]{1,0:T(8,128)(2,1)} %k_ref.1) | copy-start | bytes 1572868
  0.0 13.6 %copy-start.1 = (bf16[2048,128]{1,0:T(8,128)(2,1)S(1)}, bf16[2048,128]{1,0:T(8,128)(2,1)}, u32[]{:S(2)}) copy-start(bf16[2048,128]{1,0:T(8,128)(2,1)} %v_ref.1) | copy-start | bytes 1572868
  0.0 13.6 %copy-start.5 = (f32[128,16]{0,1:T(8,128)S(1)}, f32[128,16]{0,1:T(8,128)}, u32[]{:S(2)}) copy-start(f32[128,16]{0,1:T(8,128)} %param.10) | copy-start | bytes 24580
  0.0 13.6 %copy-start.6 = (f32[128,16]{0,1:T(8,128)S(1)}, f32[128,16]{0,1:T(8,128)}, u32[]{:S(2)}) copy-start(f32[128,16]{0,1:T(8,128)} %param.9) | copy-start | bytes 24580
  27.0 6.3 %copy-start.7 = (f32[2048]{0:T(1024)S(1)}, f32[2048]{0:T(1024)}, u32[]{:S(2)}) copy-start(f32[2048]{0:T(1024)} %param.11) | copy-start | bytes 24580
  27.0 11.7 %all-to-all-start.2 = ((f32[16,16,128]{2,1,0:T(8,128)}), f32[16,16,128]{2,1,0:T(8,128)}, u32[]{:S(2)}, u32[]{:S(2)}) async-start(f32[16,16,128]{2,1,0:T(8,128)} %shard_map.67), calls=%async_computation.2 | async-start | bytes 262144 | tf_op jit(solution)/shard_map/all_to_all | solution.py:240
  33.3 1.0 %copy-start.2 = (bf16[2048,128]{1,0:T(8,128)(2,1)S(1)}, bf16[2048,128]{1,0:T(8,128)(2,1)}, u32[]{:S(2)}) copy-start(bf16[2048,128]{1,0:T(8,128)(2,1)} %q_ref.1) | copy-start | bytes 1572868
  37.9 0.7 %copy-start.3 = (f32[2,2,16,8,128]{4,3,2,1,0:T(8,128)}, f32[2,2,16,8,128]{4,3,2,1,0:T(8,128)S(1)}, u32[]{:S(2)}) copy-start(f32[2,2,16,8,128]{4,3,2,1,0:T(8,128)S(1)} %get-tuple-element.13.dense_ref) | copy-start | bytes 786436
  38.6 1.0 %copy-start.4 = (f32[2,2,16,8,128]{4,3,2,1,0:T(8,128)S(1)}, f32[2,2,16,8,128]{4,3,2,1,0:T(8,128)}, u32[]{:S(2)}) copy-start(f32[2,2,16,8,128]{4,3,2,1,0:T(8,128)} %copy-done.3) | copy-start | bytes 786436

commit v31 on v26

--- a/solution.py
+++ b/solution.py
@@ -106,12 +106,13 @@
     return pltpu.make_async_copy(gated_ref.at[rows, :], out_ref.at[rows, :], sems.at[chunk])
 
 
-def finish(chunk, places, conv_ref, q_ref, gated_ref, out_ref, sems):
+def finish(chunk, places, conv_ref, q_ref, gated_ref, out_ref, sems, start=True):
     length = conv_ref.shape[0] // len(places)
     rows = pl.ds(places[chunk] * LANES, LANES)
     conv = conv_ref[chunk_rows(chunk, length), :].T
     gated_ref[rows, :] = (q_ref[rows, :].astype(jnp.float32) * conv).astype(jnp.bfloat16)
-    leaving(chunk, places, gated_ref, out_ref, sems).start()
+    if start:
+        leaving(chunk, places, gated_ref, out_ref, sems).start()
 
 
 def local_kernel(
@@ -178,7 +179,10 @@
             else:
                 for i in range(SUBLANES):
                     fading = steps(i, fading)
-                    finish((half - 1) * SUBLANES + i, places, conv_ref, q_ref, gated_ref, out_ref, sems)
+                    if i > 0:
+                        leaving((half - 1) * SUBLANES + i - 1, places, gated_ref, out_ref, sems).start()
+                    finish((half - 1) * SUBLANES + i, places, conv_ref, q_ref, gated_ref, out_ref, sems, False)
+                leaving(half * SUBLANES - 1, places, gated_ref, out_ref, sems).start()
         for chunk in range(chunks - SUBLANES, chunks):
             finish(chunk, places, conv_ref, q_ref, gated_ref, out_ref, sems)
         for chunk in range(chunks):

time: 38.4 us -> 38.4 us (level)
  no operation moved by 1% of the time
where the time goes in v31:
time: 38.4 us; the launch traced here: 38 us
  blocking collectives  22.2 us (58%)
  Pallas kernels  7.89 us (21%)
  starting transfers between devices  5.61 us (15%)
  waiting for transfers between devices  2.25 us (6%)
    all_to_all x2, blocking collectives, all_to_all(): lax.all_to_all(pieces, 'seq', split_axis=0, concat_axis=0, axis_index_gro...  22.2 us
    pallas_call x5, Pallas kernels, call(): pl.pallas_call(kernel, out_shape=out_shape, in_specs=[pl.BlockSpec(memory...  7.89 us
    all_to_all x1, starting transfers between devices, all_to_all(): lax.all_to_all(pieces, 'seq', split_axis=0, concat_axis=0, axis_index_gro...  5.61 us
    all_to_all x1, waiting for transfers between devices, all_to_all(): lax.all_to_all(pieces, 'seq', split_axis=0, concat_axis=0, axis_index_gro...  2.25 us
  transfers between devices with their start and end apart: 1, of which 1 were waited for; matrix products, arithmetic and copies ran while one was open for 0% of the time, Pallas kernels for 7%

profile of v31, /device:TPU:2, one launch (start us, length us, event | category | flops | bytes accessed | tf_op | source)
XLA Modules:
  0.0 38.0 jit_solution(11860121799875566046)
XLA Ops:
  0.0 0.0 copy-start.1
  0.0 0.0 copy-start.2
  0.0 0.0 copy-start.3
  0.0 0.0 copy-start.4
  0.0 0.8 %shard_map.64 = f32[16,16,128]{2,1,0:T(8,128)S(1)} custom-call(f32[16,128]{1,0:T(8,128)} %bitcast.12), custom_call_target="tpu_custom_call" | custom-call | flops 10000000000 | bytes 8192 | tf_op jit(solution)/shard_map/pallas_call | solution.py:196
  0.8 11.1 %all_to_all.15 = f32[16,16,128]{2,1,0:T(8,128)S(1)} all-to-all(f32[16,16,128]{2,1,0:T(8,128)S(1)} %shard_map.64), channel_id=1, replica_groups={{22,6,30,14,28,12,26,10,24,8,20,4,18,2,16,0},{23,7,31,15,29,13,27,11,25..., dimensions={0} | all-to-all | bytes 262144 | tf_op jit(solution)/shard_map/all_to_all | solution.py:230
  12.0 0.0 copy-done.1
  12.0 0.0 copy-done.2
  12.0 0.0 copy-done.3
  12.0 0.0 copy-done.4
  12.0 1.5 %shard_map.65 = (f32[2048,128]{1,0:T(8,128)S(1)}, f32[512,128]{1,0:T(8,128)S(1)}) custom-call(f32[256,128]{1,0:T(8,128)S(1)} %bitcast.8, f32[16,128]{1,0:T(8,128)S(1)} %bitcast.13, f32[16,128]{1,0:T(8,128)S(1)} %bitcast.15, bf16[2048,128]{1,0:T(8,128)(2,1)S(1)} %copy-done.1, bf16[2048,128]{1,0:T(8,128)(2,1)S(1)} %copy-done.2), custom_call_target="tpu_custom_call" | custom-call | flops 8388608 | bytes 1196032 | tf_op jit(solution)/shard_map/pallas_call | solution.py:196
  13.5 0.0 copy-start
  13.5 11.1 %all_to_all.16.ends_ref = f32[16,32,128]{2,1,0:T(8,128)S(1)} all-to-all(f32[16,32,128]{2,1,0:T(8,128)S(1)} %bitcast.11), channel_id=1, replica_groups={{22,6,30,14,28,12,26,10,24,8,20,4,18,2,16,0},{23,7,31,15,29,13,27,11,25..., dimensions={0} | all-to-all | bytes 524288 | tf_op jit(solution)/shard_map/all_to_all | solution.py:230
  24.6 0.7 %shard_map.67 = f32[16,16,128]{2,1,0:T(8,128)} custom-call(f32[16,128]{1,0:T(8,128)S(1)} %bitcast.14, f32[16,32,128]{2,1,0:T(8,128)S(1)} %all_to_all.16.ends_ref), custom_call_target="tpu_custom_call" | custom-call | bytes 270336 | tf_op jit(solution)/shard_map/pallas_call | solution.py:196
  25.3 0.0 copy-start.5
  25.3 5.6 %all-to-all-start.2 = ((f32[16,16,128]{2,1,0:T(8,128)}), f32[16,16,128]{2,1,0:T(8,128)S(1)}, u32[]{:S(2)}, u32[]{:S(2)}) async-start(f32[16,16,128]{2,1,0:T(8,128)} %shard_map.67), calls=%async_computation.2 | async-start | bytes 262144 | tf_op jit(solution)/shard_map/all_to_all | solution.py:230
  30.9 0.0 copy-done
  30.9 0.0 copy-done.5
  30.9 2.6 %shard_map.66 = (f32[2048,128]{1,0:T(8,128)S(1)}, f32[2,2,16,8,128]{4,3,2,1,0:T(8,128)S(1)}, bf16[2048,128]{1,0:T(8,128)(2,1)}) custom-call(f32[256,128]{1,0:T(8,128)S(1)} %bitcast.9, f32[512,128]{1,0:T(8,128)S(1)} %bitcast.7, f32[2048,128]{1,0:T(8,128)S(1)} %get-tuple-element.11.series_ref, f32[16,128]{1,0:T(8,128)S(1)} %bitcast.16, ...), custom_call_target="tpu_custom_call" | custom-call | flops 16777216 | bytes 1974272 | tf_op jit(solution)/shard_map/pallas_call | solution.py:196
  33.5 2.2 %all-to-all-done.2 = f32[16,16,128]{2,1,0:T(8,128)S(1)} async-done(((f32[16,16,128]{2,1,0:T(8,128)}), f32[16,16,128]{2,1,0:T(8,128)S(1)}, u32[]{:S(2)}, u32[]{:S(2)}) %all-to-all-start.2) | async-done | bytes 131104 | tf_op jit(solution)/shard_map/all_to_all | solution.py:230
  35.8 2.3 %shard_map.68 = bf16[2048,128]{1,0:T(8,128)(2,1)} custom-call(f32[2,2,16,8,128]{4,3,2,1,0:T(8,128)S(1)} %get-tuple-element.12.dense_ref, f32[256,128]{1,0:T(8,128)S(1)} %bitcast.10, f32[2048,128]{1,0:T(8,128)S(1)} %get-tuple-element.13.local_ref, bf16[2048,128]{1,0:T(8,128)(2,1)S(1)} %copy-done, ...), custom_call_target="tpu_custom_call", output_to_operand_aliasing={{}: (4, {})} | custom-call | flops 8388608 | bytes 2490368 | tf_op jit(solution)/shard_map/pallas_call | solution.py:196
Async XLA Ops:
  0.0 12.0 %copy-start.1 = (bf16[2048,128]{1,0:T(8,128)(2,1)S(1)}, bf16[2048,128]{1,0:T(8,128)(2,1)}, u32[]{:S(2)}) copy-start(bf16[2048,128]{1,0:T(8,128)(2,1)} %k_ref.1) | copy-start | bytes 1572868
  0.0 12.0 %copy-start.2 = (bf16[2048,128]{1,0:T(8,128)(2,1)S(1)}, bf16[2048,128]{1,0:T(8,128)(2,1)}, u32[]{:S(2)}) copy-start(bf16[2048,128]{1,0:T(8,128)(2,1)} %v_ref.1) | copy-start | bytes 1572868
  0.0 12.0 %copy-start.3 = (f32[128,16]{0,1:T(8,128)S(1)}, f32[128,16]{0,1:T(8,128)}, u32[]{:S(2)}) copy-start(f32[128,16]{0,1:T(8,128)} %param.10) | copy-start | bytes 24580
  0.0 12.0 %copy-start.4 = (f32[128,16]{0,1:T(8,128)S(1)}, f32[128,16]{0,1:T(8,128)}, u32[]{:S(2)}) copy-start(f32[128,16]{0,1:T(8,128)} %param.9) | copy-start | bytes 24580
  13.5 17.4 %copy-start = (bf16[2048,128]{1,0:T(8,128)(2,1)S(1)}, bf16[2048,128]{1,0:T(8,128)(2,1)}, u32[]{:S(2)}) copy-start(bf16[2048,128]{1,0:T(8,128)(2,1)} %q_ref.3) | copy-start | bytes 1572868
  25.3 5.6 %copy-start.5 = (f32[2048]{0:T(1024)S(1)}, f32[2048]{0:T(1024)}, u32[]{:S(2)}) copy-start(f32[2048]{0:T(1024)} %param.11) | copy-start | bytes 24580
  25.3 10.5 %all-to-all-start.2 = ((f32[16,16,128]{2,1,0:T(8,128)}), f32[16,16,128]{2,1,0:T(8,128)S(1)}, u32[]{:S(2)}, u32[]{:S(2)}) async-start(f32[16,16,128]{2,1,0:T(8,128)} %shard_map.67), calls=%async_computation.2 | async-start | bytes 262144 | tf_op jit(solution)/shard_map/all_to_all | solution.py:230

commit v32 on v26

--- a/solution.py
+++ b/solution.py
@@ -76,12 +76,10 @@
             return tuple(state)
 
         state = (jnp.zeros((SUBLANES, LANES), jnp.float32),) * order
-        if half + 1 < halves:
-            for i in range(SUBLANES):
-                state = steps(i, state)
+        for i in range(SUBLANES):
+            state = steps(i, state)
+            if half + 1 < halves:
                 build((half + 1) * SUBLANES + i)
-        else:
-            state = lax.fori_loop(0, SUBLANES, steps, state)
         for r in range(order):
             state_ref[pl.ds(half * SUBLANES * 2 * order + r, SUBLANES, stride=2 * order), :] = state[r]
 

time: 38.4 us -> 38.3 us (level)
  no operation moved by 1% of the time
where the time goes in v32:
time: 38.3 us; the launch traced here: 38 us
  blocking collectives  22.2 us (58%)
  Pallas kernels  7.84 us (20%)
  starting transfers between devices  5.61 us (15%)
  waiting for transfers between devices  2.25 us (6%)
    all_to_all x2, blocking collectives, all_to_all(): lax.all_to_all(pieces, 'seq', split_axis=0, concat_axis=0, axis_index_gro...  22.2 us
    pallas_call x5, Pallas kernels, call(): pl.pallas_call(kernel, out_shape=out_shape, in_specs=[pl.BlockSpec(memory...  7.84 us
    all_to_all x1, starting transfers between devices, all_to_all(): lax.all_to_all(pieces, 'seq', split_axis=0, concat_axis=0, axis_index_gro...  5.61 us
    all_to_all x1, waiting for transfers between devices, all_to_all(): lax.all_to_all(pieces, 'seq', split_axis=0, concat_axis=0, axis_index_gro...  2.25 us
  transfers between devices with their start and end apart: 1, of which 1 were waited for; matrix products, arithmetic and copies ran while one was open for 0% of the time, Pallas kernels for 7%

profile of v32, /device:TPU:2, one launch (start us, length us, event | category | flops | bytes accessed | tf_op | source)
XLA Modules:
  0.0 38.0 jit_solution(16708345808364788491)
XLA Ops:
  0.0 0.0 copy-start.1
  0.0 0.0 copy-start.2
  0.0 0.0 copy-start.3
  0.0 0.0 copy-start.4
  0.0 0.8 %shard_map.64 = f32[16,16,128]{2,1,0:T(8,128)S(1)} custom-call(f32[16,128]{1,0:T(8,128)} %bitcast.12), custom_call_target="tpu_custom_call" | custom-call | flops 10000000000 | bytes 8192 | tf_op jit(solution)/shard_map/pallas_call | solution.py:190
  0.8 11.1 %all_to_all.15 = f32[16,16,128]{2,1,0:T(8,128)S(1)} all-to-all(f32[16,16,128]{2,1,0:T(8,128)S(1)} %shard_map.64), channel_id=1, replica_groups={{22,6,30,14,28,12,26,10,24,8,20,4,18,2,16,0},{23,7,31,15,29,13,27,11,25..., dimensions={0} | all-to-all | bytes 262144 | tf_op jit(solution)/shard_map/all_to_all | solution.py:224
  12.0 0.0 copy-done.1
  12.0 0.0 copy-done.2
  12.0 0.0 copy-done.3
  12.0 0.0 copy-done.4
  12.0 1.5 %shard_map.65 = (f32[2048,128]{1,0:T(8,128)S(1)}, f32[512,128]{1,0:T(8,128)S(1)}) custom-call(f32[256,128]{1,0:T(8,128)S(1)} %bitcast.8, f32[16,128]{1,0:T(8,128)S(1)} %bitcast.13, f32[16,128]{1,0:T(8,128)S(1)} %bitcast.15, bf16[2048,128]{1,0:T(8,128)(2,1)S(1)} %copy-done.1, bf16[2048,128]{1,0:T(8,128)(2,1)S(1)} %copy-done.2), custom_call_target="tpu_custom_call" | custom-call | flops 8388608 | bytes 1196032 | tf_op jit(solution)/shard_map/pallas_call | solution.py:190
  13.5 0.0 copy-start
  13.5 11.1 %all_to_all.16.ends_ref = f32[16,32,128]{2,1,0:T(8,128)S(1)} all-to-all(f32[16,32,128]{2,1,0:T(8,128)S(1)} %bitcast.11), channel_id=1, replica_groups={{22,6,30,14,28,12,26,10,24,8,20,4,18,2,16,0},{23,7,31,15,29,13,27,11,25..., dimensions={0} | all-to-all | bytes 524288 | tf_op jit(solution)/shard_map/all_to_all | solution.py:224
  24.6 0.7 %shard_map.67 = f32[16,16,128]{2,1,0:T(8,128)} custom-call(f32[16,128]{1,0:T(8,128)S(1)} %bitcast.14, f32[16,32,128]{2,1,0:T(8,128)S(1)} %all_to_all.16.ends_ref), custom_call_target="tpu_custom_call" | custom-call | bytes 270336 | tf_op jit(solution)/shard_map/pallas_call | solution.py:190
  25.2 0.0 copy-start.5
  25.2 5.6 %all-to-all-start.2 = ((f32[16,16,128]{2,1,0:T(8,128)}), f32[16,16,128]{2,1,0:T(8,128)S(1)}, u32[]{:S(2)}, u32[]{:S(2)}) async-start(f32[16,16,128]{2,1,0:T(8,128)} %shard_map.67), calls=%async_computation.2 | async-start | bytes 262144 | tf_op jit(solution)/shard_map/all_to_all | solution.py:224
  30.8 0.0 copy-done
  30.9 0.0 copy-done.5
  30.9 2.6 %shard_map.66 = (f32[2048,128]{1,0:T(8,128)S(1)}, f32[2,2,16,8,128]{4,3,2,1,0:T(8,128)S(1)}, bf16[2048,128]{1,0:T(8,128)(2,1)}) custom-call(f32[256,128]{1,0:T(8,128)S(1)} %bitcast.9, f32[512,128]{1,0:T(8,128)S(1)} %bitcast.7, f32[2048,128]{1,0:T(8,128)S(1)} %get-tuple-element.11.series_ref, f32[16,128]{1,0:T(8,128)S(1)} %bitcast.16, ...), custom_call_target="tpu_custom_call" | custom-call | flops 16777216 | bytes 1974272 | tf_op jit(solution)/shard_map/pallas_call | solution.py:190
  33.5 2.2 %all-to-all-done.2 = f32[16,16,128]{2,1,0:T(8,128)S(1)} async-done(((f32[16,16,128]{2,1,0:T(8,128)}), f32[16,16,128]{2,1,0:T(8,128)S(1)}, u32[]{:S(2)}, u32[]{:S(2)}) %all-to-all-start.2) | async-done | bytes 131104 | tf_op jit(solution)/shard_map/all_to_all | solution.py:224
  35.7 2.3 %shard_map.68 = bf16[2048,128]{1,0:T(8,128)(2,1)} custom-call(f32[2,2,16,8,128]{4,3,2,1,0:T(8,128)S(1)} %get-tuple-element.12.dense_ref, f32[256,128]{1,0:T(8,128)S(1)} %bitcast.10, f32[2048,128]{1,0:T(8,128)S(1)} %get-tuple-element.13.local_ref, bf16[2048,128]{1,0:T(8,128)(2,1)S(1)} %copy-done, ...), custom_call_target="tpu_custom_call", output_to_operand_aliasing={{}: (4, {})} | custom-call | flops 8388608 | bytes 2490368 | tf_op jit(solution)/shard_map/pallas_call | solution.py:190
Async XLA Ops:
  0.0 12.0 %copy-start.1 = (bf16[2048,128]{1,0:T(8,128)(2,1)S(1)}, bf16[2048,128]{1,0:T(8,128)(2,1)}, u32[]{:S(2)}) copy-start(bf16[2048,128]{1,0:T(8,128)(2,1)} %k_ref.1) | copy-start | bytes 1572868
  0.0 12.0 %copy-start.2 = (bf16[2048,128]{1,0:T(8,128)(2,1)S(1)}, bf16[2048,128]{1,0:T(8,128)(2,1)}, u32[]{:S(2)}) copy-start(bf16[2048,128]{1,0:T(8,128)(2,1)} %v_ref.1) | copy-start | bytes 1572868
  0.0 12.0 %copy-start.3 = (f32[128,16]{0,1:T(8,128)S(1)}, f32[128,16]{0,1:T(8,128)}, u32[]{:S(2)}) copy-start(f32[128,16]{0,1:T(8,128)} %param.10) | copy-start | bytes 24580
  0.0 12.0 %copy-start.4 = (f32[128,16]{0,1:T(8,128)S(1)}, f32[128,16]{0,1:T(8,128)}, u32[]{:S(2)}) copy-start(f32[128,16]{0,1:T(8,128)} %param.9) | copy-start | bytes 24580
  13.5 17.4 %copy-start = (bf16[2048,128]{1,0:T(8,128)(2,1)S(1)}, bf16[2048,128]{1,0:T(8,128)(2,1)}, u32[]{:S(2)}) copy-start(bf16[2048,128]{1,0:T(8,128)(2,1)} %q_ref.3) | copy-start | bytes 1572868
  25.2 5.6 %copy-start.5 = (f32[2048]{0:T(1024)S(1)}, f32[2048]{0:T(1024)}, u32[]{:S(2)}) copy-start(f32[2048]{0:T(1024)} %param.11) | copy-start | bytes 24580
  25.2 10.5 %all-to-all-start.2 = ((f32[16,16,128]{2,1,0:T(8,128)}), f32[16,16,128]{2,1,0:T(8,128)S(1)}, u32[]{:S(2)}, u32[]{:S(2)}) async-start(f32[16,16,128]{2,1,0:T(8,128)} %shard_map.67), calls=%async_computation.2 | async-start | bytes 262144 | tf_op jit(solution)/shard_map/all_to_all | solution.py:224
